TPU v7x, 128 devices: a whole 4x4x4 slice. The times are simulated.
128 devices in a mesh: cat: 32 (over y, z, core), tp: 4 (over x).
Axes of the slice: x: 4, y: 4, z: 4, core: 2. Of those that a mesh axis runs over, the one named last changes fastest.
Arguments:
- query_emb: bfloat16 [32768, 512], P('cat', 'tp'), may hold values from -100 to 100
- positive_emb: bfloat16 [32768, 512], P('cat', 'tp'), may hold values from -6 to 6
- item_hidden: bfloat16 [65536, 1024], P('cat', 'tp'), may hold values from -6 to 6
- item_weight: bfloat16 [1024, 512], P('tp'), may hold values from -0.1875 to 0.1875
- neg_blocks: int32 [128, 64], P('cat'), may hold values from 0 to 255, all different within a row
- block_home: int32 [256], replicated, may hold values from 0 to 255, each once
- sample_counts: int32 [65536], replicated, may hold values from 1 to 4096
Outputs:
- query_loss: float32 [32768], P('cat')
- query_grad: bfloat16 [32768, 512], P('cat', 'tp')
Inputs may be any that keep to these rules, and one draw needn't show every extreme that they name: `neg_blocks`: each row names 64 different catalog blocks. `block_home`: each storage position once.
All inputs are finite; a program needn't handle non-finite values.
Results may differ from a plain program's by a relative error of at most 0.012.
Values may be sent and summed in bfloat16 or wider, within the bound.
No kernel may reach another device: no remote copies, remote signals or barrier semaphores. Data moves between devices by JAX's collectives and lax.ppermute only.
A program may use at most 192 MiB of HBM per device.

v0:
```python
import math

import jax
import jax.numpy as jnp
from jax import lax
from jax.sharding import PartitionSpec as P

BLK = 256


def merged(value, axis, join):
    pieces = jax.tree.map(lambda part: lax.all_gather(part, axis), value)
    head = jax.tree.map(lambda part: part[0], pieces)
    tail = jax.tree.map(lambda part: part[1:], pieces)
    subtotal, _ = lax.scan(lambda subtotal, piece: (join(subtotal, piece), None), head, tail)
    return subtotal


def combine_pairs(first_pair, second_pair):
    max_first, sum_first = first_pair
    max_second, sum_second = second_pair
    new_max = jnp.maximum(max_first, max_second)
    new_sum = sum_first * jnp.exp(max_first - new_max) + sum_second * jnp.exp(max_second - new_max)
    return (new_max, new_sum)


def local(query_emb, positive_emb, item_hidden, item_weight, neg_blocks, block_home, sample_counts):
    tp_count = lax.axis_size("tp")
    tp_rank = lax.axis_index("tp")
    feat_width = item_weight.shape[1]
    hid_shard = item_hidden.shape[1]
    sub_rows = BLK // tp_count
    own_rows = item_hidden.shape[0]
    own_blocks = own_rows // BLK
    reordered = (
        item_hidden.reshape(own_blocks, tp_count, sub_rows, hid_shard)
        .transpose(1, 0, 2, 3)
        .reshape(own_rows, hid_shard)
    )
    item_vec = lax.psum_scatter(
        jnp.dot(reordered, item_weight, preferred_element_type=jnp.float32),
        "tp",
        scatter_dimension=0,
        tiled=True,
    ).astype(jnp.bfloat16)
    total_blocks = block_home.shape[0]
    log_table = jnp.log(sample_counts.astype(jnp.float32)).reshape(total_blocks, tp_count, sub_rows)
    my_logq = lax.dynamic_index_in_dim(log_table, tp_rank, 1, keepdims=False)
    query_full, positive_full = (
        lax.all_gather(query_emb, "tp", axis=1, tiled=True),
        lax.all_gather(positive_emb, "tp", axis=1, tiled=True),
    )
    qblock_count = neg_blocks.shape[0]
    query_rows = query_full.reshape(qblock_count, BLK, feat_width)
    score_scale = 2.0 / math.sqrt(feat_width)
    pos_score = score_scale * jnp.sum(
        query_full.astype(jnp.float32) * positive_full.astype(jnp.float32), axis=1
    ).reshape(qblock_count, BLK)
    matches = neg_blocks[:, :, None] == jnp.arange(total_blocks, dtype=jnp.int32)[None, None, :]
    home_ids = jnp.sum(jnp.where(matches, block_home[None, None, :], 0), axis=2)
    item_table = lax.all_gather(item_vec, "cat", axis=0, tiled=True).reshape(
        total_blocks, sub_rows, feat_width
    )
    picked = item_table[home_ids].reshape(qblock_count, -1, feat_width)
    picked_q = my_logq[home_ids].reshape(qblock_count, -1)
    scores = (
        score_scale
        * jnp.einsum("gqe,gke->gqk", query_rows, picked, preferred_element_type=jnp.float32)
        - picked_q[:, None, :]
    )
    run_max = jnp.max(scores, axis=2)
    run_sum = jnp.sum(jnp.exp(scores - run_max[..., None]), axis=2)
    run_max, run_sum = merged((run_max, run_sum), "tp", combine_pairs)
    joint_max = jnp.maximum(run_max, pos_score)
    log_total = joint_max + jnp.log(
        run_sum * jnp.exp(run_max - joint_max) + jnp.exp(pos_score - joint_max)
    )
    weights = jnp.exp(scores - log_total[..., None]).astype(jnp.bfloat16)
    weighted = jnp.einsum("gqk,gke->gqe", weights, picked, preferred_element_type=jnp.float32)
    flat_sum = weighted.reshape(qblock_count * BLK, feat_width)
    grad_share = lax.psum_scatter(
        flat_sum.astype(jnp.bfloat16), "tp", scatter_dimension=1, tiled=True
    ).astype(jnp.float32)
    pos_weight = jnp.exp(pos_score - log_total).reshape(-1)
    query_grad = score_scale * (
        grad_share + (pos_weight - 1.0)[:, None] * positive_emb.astype(jnp.float32)
    )
    query_loss = (log_total - pos_score).reshape(-1)
    return (query_loss, query_grad.astype(jnp.bfloat16))


def solution(mesh):
    placed = (
        P("cat", "tp"),
        P("cat", "tp"),
        P("cat", "tp"),
        P("tp", None),
        P("cat", None),
        P(),
        P(),
    )
    return jax.shard_map(
        local, mesh=mesh, in_specs=placed, out_specs=(P("cat"), P("cat", "tp")), check_vma=False
    )
```

profile of v0, /device:TPU:0, one launch (start us, length us, event | category | flops | bytes accessed | tf_op | source)
XLA Modules:
  0.0 297.7 jit_solution(12200659495050789672)
XLA Ops:
  7.3 1.4 copy.15
  8.6 2.7 fusion.17
  11.4 0.7 all-gather.10.cloned.1.call-update
  12.1 0.7 all-gather.12.cloned.1.call-update
  12.8 47.8 %reduce-scatter.5.cloned.1.call-done = f32[512,512]{1,0:T(8,128)} async-done(((f32[2048,512]{1,0:T(8,128)}), f32[512,512]{1,0:T(8,128)}) %reduce-scatter.5.cloned.1.call-update) | async-done | bytes 1048592 | tf_op jit(solution)/shard_map/reduce_scatter | solution.py:40
  60.7 2.1 convert_element_type.30
  62.9 0.2 select_reduce_fusion
  63.3 0.2 reshape.61
  63.6 0.7 gather_fusion.1
  64.5 23.6 %all-gather.10.cloned.1.call-done = bf16[1024,512]{1,0:T(8,128)(2,1)} async-done(((bf16[1024,128]{1,0:T(8,128)(2,1)}), bf16[1024,512]{1,0:T(8,128)(2,1)}) %all-gather.10.cloned.1.call-update) | async-done | bytes 1048592 | tf_op jit(solution)/shard_map/all_gather | solution.py:50
  88.1 28.6 %all-gather.12.cloned.1.call-done = bf16[1024,512]{1,0:T(8,128)(2,1)} async-done(((bf16[1024,128]{1,0:T(8,128)(2,1)}), bf16[1024,512]{1,0:T(8,128)(2,1)}) %all-gather.12.cloned.1.call-update) | async-done | bytes 1048592 | tf_op jit(solution)/shard_map/all_gather | solution.py:51
  116.7 1.9 multiply_reduce_fusion
  118.6 74.1 %all-gather.8.cloned.1.call-done = bf16[16384,512]{1,0:T(8,128)(2,1)} async-done(((bf16[512,512]{1,0:T(8,128)(2,1)}), bf16[16384,512]{1,0:T(8,128)(2,1)}) %all-gather.8.cloned.1.call-update) | async-done | bytes 16777232 | tf_op jit(solution)/shard_map/all_gather | solution.py:61
  192.7 15.6 %gather_fusion = bf16[256,64,512]{2,1,0:T(8,128)(2,1)} fusion(bf16[256,64,512]{2,1,0:T(8,128)(2,1)} %bitcast.63, s32[1024]{0:T(1024)S(1)} %pad_clamp_fusion), kind=kCustom, calls=%fused_computation | custom fusion | bytes 33555456 | tf_op jit(solution)/shard_map/gather | solution.py:64
  208.3 11.5 %bitcast_reduce_fusion = (f32[4,256]{1,0:T(4,128)S(1)}, f32[4,4096,256]{2,1,0:T(8,128)}) fusion(f32[4,4096]{1,0:T(4,128)S(1)} %sub.53, bf16[4,4096,512]{2,1,0:T(8,128)(2,1)} %bitcast.61, bf16[4,256,512]{2,1,0:T(8,128)(2,1)S(1)} %bitcast.68), kind=kOutput, calls=%fused_computation.9 | convolution fusion | flops 4307549184 | bytes 34672640 | tf_op jit(solution)/shard_map/gqe,gke->gqk/dot_general | solution.py:68
  219.9 7.7 %fusion.3 = f32[4,256]{1,0:T(4,128)S(1)} fusion(f32[4,4096,256]{2,1,0:T(8,128)} %get-tuple-element.47, f32[4,256]{1,0:T(4,128)S(1)} %get-tuple-element.46, f32[4,4096]{1,0:T(4,128)S(1)} %sub.53), kind=kLoop, calls=%fused_computation.11 | loop fusion | flops 16776192 | bytes 16850944 | tf_op jit(solution)/shard_map/reduce_sum | solution.py:72
  227.6 12.2 %all-gather.3 = f32[4,4,256]{2,1,0:T(4,128)S(1)} all-gather(f32[1,4,256]{2,1,0:T(4,128)S(1)} %bitcast.73), channel_id=3, replica_groups=mesh['cat'=32,'tp'=4] {'tp'}, dimensions={0}, use_global_device_ids=true | all-gather | bytes 20480 | tf_op jit(solution)/shard_map/all_gather | solution.py:12
  239.8 11.9 %all-gather.2 = f32[4,4,256]{2,1,0:T(4,128)S(1)} all-gather(f32[1,4,256]{2,1,0:T(4,128)S(1)} %bitcast.72), channel_id=2, replica_groups=mesh['cat'=32,'tp'=4] {'tp'}, dimensions={0}, use_global_device_ids=true | all-gather | bytes 20480 | tf_op jit(solution)/shard_map/all_gather | solution.py:12
  251.9 13.4 %fusion.11 = bf16[4,256,512]{2,1,0:T(8,128)(2,1)S(1)} fusion(bf16[4,4096,512]{2,1,0:T(8,128)(2,1)} %bitcast.62, f32[4,4096,256]{2,1,0:T(8,128)} %get-tuple-element.47, f32[4,256]{1,0:T(4,128)S(1)} %get-tuple-element.45, f32[4,4096]{1,0:T(4,128)S(1)} %sub.53), kind=kOutput, calls=%fused_computation.20 | convolution fusion | flops 4312268800 | bytes 34672640 | tf_op jit(solution)/shard_map/gqk,gke->gqe/dot_general | solution.py:79
  265.3 1.3 copy.18
  266.7 0.6 copy.20
  267.3 21.9 %reduce-scatter.7.cloned.1.call-done = bf16[128,1024]{1,0:T(8,128)(2,1)} async-done(((bf16[512,1024]{1,0:T(8,128)(2,1)}), bf16[128,1024]{1,0:T(8,128)(2,1)}) %reduce-scatter.7.cloned.1.call-update) | async-done | bytes 262160
  289.1 1.1 copy.19
  290.3 0.9 multiply_convert_fusion
  (39 shorter events, 0.9 us)
Async XLA Ops:
  7.2 1.5 copy-start
  7.2 55.7 %copy-start.5 = (s32[256]{0:T(256)S(1)}, s32[256]{0:T(256)}, u32[]{:S(2)}) copy-start(s32[256]{0:T(256)} %param.14) | copy-start | bytes 3076
  7.2 55.7 %copy-start.4 = (s32[4,64]{1,0:T(4,128)S(1)}, s32[4,64]{1,0:T(4,128)}, u32[]{:S(2)}) copy-start(s32[4,64]{1,0:T(4,128)} %param.13) | copy-start | bytes 3076
  7.2 56.0 %copy-start.3 = (s32[65536]{0:T(1024)S(1)}, s32[65536]{0:T(1024)}, u32[]{:S(2)}) copy-start(s32[65536]{0:T(1024)} %param.15) | copy-start | bytes 786436
  7.2 53.5 %reduce-scatter.5.cloned.1.call-start = ((), (), s32[]{:S(2)}) async-start(), calls=%async_computation.2 | async-start | bytes 5242880 | tf_op jit(solution)/shard_map/reduce_scatter | solution.py:40
  11.3 76.8 %all-gather.10.cloned.1.call-start = ((), (), s32[]{:S(2)}) async-start(), calls=%async_computation.4 | async-start | bytes 1310720 | tf_op jit(solution)/shard_map/all_gather | solution.py:50
  12.1 104.6 %all-gather.12.cloned.1.call-start = ((), (), s32[]{:S(2)}) async-start(), calls=%async_computation.5 | async-start | bytes 1310720 | tf_op jit(solution)/shard_map/all_gather | solution.py:51
  12.8 179.9 %all-gather.8.cloned.1.call-start = ((), (), s32[]{:S(2)}) async-start(), calls=%async_computation.3 | async-start | bytes 17301504 | tf_op jit(solution)/shard_map/all_gather | solution.py:61
  62.8 226.3 %reduce-scatter.7.cloned.1.call-start = ((), (), s32[]{:S(2)}) async-start(), calls=%async_computation.6 | async-start | bytes 1310720
  192.7 15.6 %copy-start.2 = (bf16[1024,512]{1,0:T(8,128)(2,1)S(1)}, bf16[1024,512]{1,0:T(8,128)(2,1)}, u32[]{:S(2)}) copy-start(bf16[1024,512]{1,0:T(8,128)(2,1)} %all-gather.10.cloned.1.call-done) | copy-start | bytes 3145732
  251.9 38.4 %copy-start.1 = (bf16[1024,128]{1,0:T(8,128)(2,1)S(1)}, bf16[1024,128]{1,0:T(8,128)(2,1)}, u32[]{:S(2)}) copy-start(bf16[1024,128]{1,0:T(8,128)(2,1)} %param.10) | copy-start | bytes 786436
Sparse Core Ops, SparseCore 0:
  11.4 49.2 reduce-scatter.4
  62.4 25.6 all-gather.9
  89.8 26.8 all-gather.11
  119.1 73.5 all-gather.7
  266.8 22.3 reduce-scatter.6
where the time goes:
time: 298 us
  waiting for transfers between devices  197 us (66%)
  matrix products  27.6 us (9%)
  blocking collectives  24.2 us (8%)
  local copies, waits for them, and re-layouts  21.3 us (7%)
  between operations  14 us (5%)
  other arithmetic  13 us (4%)
    all_gather x1, waiting for transfers between devices, local(): lax.all_gather(item_vec, 'cat', axis=0, tiled=True)  74.1 us
    reduce_scatter x1, waiting for transfers between devices, local(): lax.psum_scatter(jnp.dot(reordered, item_weight, preferred_element_type=j...  47.8 us
    all_gather x1, waiting for transfers between devices, local(): lax.all_gather(positive_emb, 'tp', axis=1, tiled=True)  28.6 us
    all_gather x2, blocking collectives, merged(): pieces = jax.tree.map(lambda part: lax.all_gather(part, axis), value)  24.2 us
    all_gather x1, waiting for transfers between devices, local(): lax.all_gather(query_emb, 'tp', axis=1, tiled=True)  23.6 us
    unnamed x6, waiting for transfers between devices  23.3 us
    gather x1, local copies, waits for them, and re-layouts, local(): picked = item_table[home_ids].reshape(qblock_count, -1, feat_width)  15.6 us
    dot_general x1, matrix products, local(): jnp.einsum('gqk,gke->gqe', weights, picked, preferred_element_type=jnp.fl...  13.4 us
  transfers between devices with their start and end apart: 5, of which 5 were waited for; matrix products, arithmetic and copies ran while one was open for 2% of the time, Pallas kernels for 0%

commit v1 on v0

v1 whole, which is shorter than its diff:
```python
import functools
import math

import jax
import jax.numpy as jnp
from jax import lax
from jax.experimental import pallas as pl
from jax.experimental.pallas import tpu as pltpu
from jax.sharding import PartitionSpec as P

BLK = 256
TP = 4
NY = 4
NZ = 4
E = 512
LOG2E = math.log2(math.e)
LN2 = math.log(2.0)
SCALE = 2.0 / math.sqrt(E)
LOW = -1e30
ROWS = BLK // TP // 2
NBD = 8
PICKS = 64
COLS = PICKS * ROWS
TILE = 512


def cat_perm(dy, dz, dc):
    def at(y, z, c):
        return ((y % NY) * NZ + z % NZ) * 2 + c % 2

    return [
        (at(y, z, c), at(y + dy, z + dz, c + dc))
        for y in range(NY)
        for z in range(NZ)
        for c in range(2)
    ]


def send(value, dy=0, dz=0, dc=0):
    return lax.ppermute(value, "cat", cat_perm(dy, dz, dc))


def send_x(value, d):
    return lax.ppermute(value, "tp", [(i, (i + d) % TP) for i in range(TP)])


def tower_kernel(core_ref, *refs):
    hidden = refs[0:4]
    weight = refs[4:8]
    keep_ref, give_ref, scratch = refs[8:]
    acc = jnp.dot(hidden[0][...], weight[0][...], preferred_element_type=jnp.float32)
    for d in range(1, 4):
        acc += jnp.dot(hidden[d][...], weight[d][...], preferred_element_type=jnp.float32)
    scratch[...] = acc.astype(jnp.bfloat16).reshape(scratch.shape)
    core = core_ref[0]
    keep_ref[...] = scratch[:, core]
    give_ref[...] = scratch[:, 1 - core]


def tower(core, hidden, weight):
    half = jax.ShapeDtypeStruct((NBD, ROWS, E), jnp.bfloat16)
    return pl.pallas_call(
        tower_kernel,
        out_shape=(half, half),
        in_specs=[pl.BlockSpec(memory_space=pltpu.SMEM)]
        + [pl.BlockSpec(memory_space=pltpu.VMEM)] * 8,
        out_specs=(pl.BlockSpec(memory_space=pltpu.VMEM),) * 2,
        scratch_shapes=[pltpu.VMEM((NBD, 2, ROWS, E), jnp.bfloat16)],
        compiler_params=pltpu.CompilerParams(vmem_limit_bytes=40 << 20),
        cost_estimate=pl.CostEstimate(
            flops=2 * 512 * 1024 * 512, bytes_accessed=3 << 20, transcendentals=0
        ),
        name="tower",
    )(core, *hidden, *weight)


PLACES = ((0, 32), (32, 32), (64, 16), (80, 16), (96, 32))
PLACES = PLACES + tuple((start + 128, size) for start, size in PLACES)


def one_block(q_ref, lq_ref, row_ref, table, picked, scores, first):
    for j in range(PICKS):
        picked[pl.ds(j * ROWS, ROWS), :] = table[row_ref[first + j]]
    query = jnp.concatenate([q_ref[s] for s in range(TP)], axis=1)
    top = jnp.full((BLK, 128), LOW, jnp.float32)
    for n in range(COLS // TILE):
        cols = pl.ds(n * TILE, TILE)
        part = lax.dot_general(
            query,
            picked[cols, :],
            (((1,), (1,)), ((), ())),
            preferred_element_type=jnp.float32,
        )
        part = part * (SCALE * LOG2E) - lq_ref[0, :, cols]
        scores[:, cols] = part
        for g in range(TILE // 128):
            top = jnp.maximum(top, part[:, g * 128 : (g + 1) * 128])
    top = jnp.max(top, axis=1, keepdims=True)
    total = jnp.zeros((BLK, 128), jnp.float32)
    acc = jnp.zeros((BLK, E), jnp.float32)
    for n in range(COLS // TILE):
        cols = pl.ds(n * TILE, TILE)
        weight = jnp.exp2(scores[:, cols] - top)
        for g in range(TILE // 128):
            total += weight[:, g * 128 : (g + 1) * 128]
        acc += jnp.dot(
            weight.astype(jnp.bfloat16), picked[cols, :], preferred_element_type=jnp.float32
        )
    return top, jnp.sum(total, axis=1, keepdims=True), acc


def rows_of(top, total):
    lane = lax.broadcasted_iota(jnp.int32, (BLK, 128), 1)
    both = jnp.where(lane == 0, top, jnp.where(lane == 1, total, 0.0))
    return jnp.transpose(both)[:8]


def fill(pieces, table, sems):
    copies = [
        pltpu.make_async_copy(piece, table.at[pl.ds(start, size)], sems.at[n])
        for n, (piece, (start, size)) in enumerate(zip(pieces, PLACES))
    ]
    for copy in copies:
        copy.start()
    for copy in copies:
        copy.wait()


def first_kernel(row_ref, q_ref, lq_ref, *refs):
    pieces = refs[:10]
    out_ref, stat_ref, table, picked, scores, sems = refs[10:]
    step = pl.program_id(0)

    @pl.when(step == 0)
    def _():
        fill(pieces, table, sems)

    top, total, acc = one_block(q_ref, lq_ref, row_ref, table, picked, scores, step * PICKS)
    out_ref[...] = acc.astype(jnp.bfloat16)
    stat_ref[0] = rows_of(top, total)


def second_kernel(row_ref, q_ref, lq_ref, *refs):
    pieces = refs[:10]
    other_ref, other_stat_ref, pos_ref = refs[10:13]
    out_ref, stat_ref, table, picked, scores, sems = refs[13:]
    step = pl.program_id(0)

    @pl.when(step == 0)
    def _():
        fill(pieces, table, sems)

    top, total, acc = one_block(q_ref, lq_ref, row_ref, table, picked, scores, step * PICKS)
    theirs = jnp.transpose(jnp.concatenate([other_stat_ref[0]] * 16, axis=0))
    their_top, their_total = theirs[:, 0:1], theirs[:, 1:2]
    joint = jnp.maximum(top, their_top)
    mine_by, theirs_by = jnp.exp2(top - joint), jnp.exp2(their_top - joint)
    acc = acc * mine_by + other_ref[...].astype(jnp.float32) * theirs_by
    for s in range(TP):
        out_ref[s] = acc[:, s * 128 : (s + 1) * 128].astype(jnp.bfloat16)
    stat = rows_of(joint, total * mine_by + their_total * theirs_by)
    row = lax.broadcasted_iota(jnp.int32, (8, BLK), 0)
    stat_ref[0] = jnp.where(row == 2, pos_ref[0], stat)


def attend(body, rows, query, lq, pieces, extra, out_shape, out_spec, name):
    blocks = lq.shape[0]
    stat_spec = pl.BlockSpec((1, 8, BLK), lambda i, r: (i, 0, 0))
    extra_specs = []
    if extra:
        extra_specs = [
            pl.BlockSpec((BLK, E), lambda i, r: (i, 0)),
            stat_spec,
            pl.BlockSpec((1, 1, BLK), lambda i, r: (i, 0, 0)),
        ]
    return pl.pallas_call(
        body,
        grid_spec=pltpu.PrefetchScalarGridSpec(
            num_scalar_prefetch=1,
            grid=(blocks,),
            in_specs=[
                pl.BlockSpec((TP, BLK, 128), lambda i, r: (0, i, 0)),
                pl.BlockSpec((1, 1, COLS), lambda i, r: (i, 0, 0)),
            ]
            + [pl.BlockSpec(memory_space=pl.ANY)] * 10
            + extra_specs,
            out_specs=(out_spec, stat_spec),
            scratch_shapes=[
                pltpu.VMEM((256, ROWS, E), jnp.bfloat16),
                pltpu.VMEM((COLS, E), jnp.bfloat16),
                pltpu.VMEM((BLK, COLS), jnp.float32),
                pltpu.SemaphoreType.DMA((10,)),
            ],
        ),
        out_shape=(out_shape, jax.ShapeDtypeStruct((blocks, 8, BLK), jnp.float32)),
        compiler_params=pltpu.CompilerParams(
            dimension_semantics=("arbitrary",), vmem_limit_bytes=48 << 20
        ),
        cost_estimate=pl.CostEstimate(
            flops=blocks * 4 * BLK * COLS * E,
            bytes_accessed=12 << 20,
            transcendentals=blocks * BLK * COLS,
        ),
        name=name,
    )(rows, query, lq, *pieces, *extra)


def last_kernel(*refs):
    parts, stats = refs[0:4], refs[4:8]
    positive_ref, loss_ref, grad_ref = refs[8:]
    stat = [ref[0] for ref in stats]
    pos = (stat[0][2:3] + stat[1][2:3] + stat[2][2:3] + stat[3][2:3]) * LOG2E
    joint = pos
    for one in stat:
        joint = jnp.maximum(joint, one[0:1])
    total = jnp.exp2(pos - joint)
    for one in stat:
        total += one[1:2] * jnp.exp2(one[0:1] - joint)
    log_total = joint + jnp.log(total) * LOG2E
    loss_ref[0] = (log_total - pos) * LN2
    factors = [jnp.exp2(one[0:1] - log_total) * SCALE for one in stat]
    factors.append((jnp.exp2(pos - log_total) - 1.0) * SCALE)
    row = lax.broadcasted_iota(jnp.int32, (128, BLK), 0)
    packed = jnp.zeros((128, BLK), jnp.float32)
    for n, factor in enumerate(factors):
        packed = jnp.where(row == n, factor, packed)
    by = jnp.transpose(packed)
    grad = by[:, 4:5] * positive_ref[...].astype(jnp.float32)
    for n in range(4):
        grad += by[:, n : n + 1] * parts[n][...].astype(jnp.float32)
    grad_ref[...] = grad.astype(jnp.bfloat16)


def last(parts, stats, positive):
    blocks = stats[0].shape[0]
    flat = pl.BlockSpec((BLK, 128), lambda i: (i, 0))
    stat_spec = pl.BlockSpec((1, 8, BLK), lambda i: (i, 0, 0))
    return pl.pallas_call(
        last_kernel,
        grid=(blocks,),
        in_specs=[flat] * 4 + [stat_spec] * 4 + [flat],
        out_specs=(pl.BlockSpec((1, 1, BLK), lambda i: (i, 0, 0)), flat),
        out_shape=(
            jax.ShapeDtypeStruct((blocks, 1, BLK), jnp.float32),
            jax.ShapeDtypeStruct((blocks * BLK, 128), jnp.bfloat16),
        ),
        compiler_params=pltpu.CompilerParams(vmem_limit_bytes=32 << 20),
        name="last",
    )(*parts, *stats, positive)


def spread(near, far):
    near_line = jnp.concatenate([near[None]] + [send(near, -d, 0)[None] for d in (1, 2, 3)])
    far_line = jnp.concatenate([far[None]] + [send(far, 0, -d)[None] for d in (1, 2, 3)])
    near_up, near_down = send(near_line, 0, 1), send(near_line, 0, -1)
    far_up, far_down = send(far_line, 1, 0), send(far_line, -1, 0)
    near_a, near_b = send(near_up[:2], 0, 1), send(near_down[2:], 0, -1)
    far_a, far_b = send(far_up[:2], 1, 0), send(far_down[2:], -1, 0)
    pieces = [near_line, near_down, near_a, near_b, near_up]
    pieces += [far_line, far_down, far_a, far_b, far_up]
    return [piece.reshape(-1, ROWS, E) for piece in pieces]


def local(query_emb, positive_emb, item_hidden, item_weight, neg_blocks, block_home, sample_counts):
    rank = lax.axis_index("tp")
    place = lax.axis_index("cat")
    core, my_z, my_y = place % 2, (place // 2) % NZ, place // (2 * NZ)
    qblocks = neg_blocks.shape[0]
    total_blocks = block_home.shape[0]

    hidden = item_hidden.reshape(NBD, TP, BLK // TP, -1)

    def piece(d):
        cut = lax.dynamic_index_in_dim(hidden, (rank + d) % TP, 1, keepdims=False)
        return cut.reshape(NBD * BLK // TP, -1)

    weights = [item_weight] + [send_x(item_weight, d) for d in (1, 2, 3)]
    hiddens = [piece(0)] + [send_x(piece(d), d) for d in (1, 2, 3)]
    keep, give = tower(core.reshape(1).astype(jnp.int32), hiddens, weights)
    pieces = spread(keep, send(give, 0, 0, 1))

    query = lax.all_gather(query_emb, "tp")
    other_query = send(query, 0, 0, 1)
    pos_part = SCALE * jnp.sum(
        query_emb.astype(jnp.float32) * positive_emb.astype(jnp.float32), axis=1
    ).reshape(qblocks, 1, BLK)

    picks = jnp.concatenate([send(neg_blocks, 0, 0, 1), neg_blocks])
    matches = picks[:, :, None] == jnp.arange(total_blocks, dtype=jnp.int32)[None, None, :]
    home = jnp.sum(jnp.where(matches, block_home[None, None, :], 0), axis=2)
    slot, owner = home % NBD, home // NBD
    dz = ((owner // 2) % NZ - my_z) % NZ
    dy = (owner // (2 * NZ) - my_y) % NY
    rows = jnp.where(
        owner % 2 == core, dz * 32 + dy * NBD + slot, 128 + dy * 32 + dz * NBD + slot
    ).astype(jnp.int32)
    log_table = (jnp.log(sample_counts.astype(jnp.float32)) * LOG2E).reshape(
        total_blocks, TP * 2, ROWS
    )
    my_log = lax.dynamic_index_in_dim(log_table, rank * 2 + core, 1, keepdims=False)
    lq = my_log[home].reshape(2 * qblocks, 1, COLS)

    theirs, their_stat = attend(
        first_kernel,
        rows[:qblocks].reshape(-1),
        other_query,
        lq[:qblocks],
        pieces,
        (),
        jax.ShapeDtypeStruct((qblocks * BLK, E), jnp.bfloat16),
        pl.BlockSpec((BLK, E), lambda i, r: (i, 0)),
        "attend_other",
    )
    from_other = send(theirs, 0, 0, 1)
    from_other_stat = send(their_stat, 0, 0, 1)
    mine, stat = attend(
        second_kernel,
        rows[qblocks:].reshape(-1),
        query,
        lq[qblocks:],
        pieces,
        (from_other, from_other_stat, pos_part),
        jax.ShapeDtypeStruct((TP, qblocks * BLK, 128), jnp.bfloat16),
        pl.BlockSpec((TP, BLK, 128), lambda i, r: (0, i, 0)),
        "attend_own",
    )

    def share(d):
        return lax.dynamic_index_in_dim(mine, (rank + d) % TP, 0, keepdims=False)

    stats = [stat] + [send_x(stat, d) for d in (1, 2, 3)]
    parts = [share(0)] + [send_x(share(d), d) for d in (1, 2, 3)]
    loss, grad = last(parts, stats, positive_emb)
    return loss.reshape(-1), grad


def solution(mesh):
    placed = (
        P("cat", "tp"),
        P("cat", "tp"),
        P("cat", "tp"),
        P("tp", None),
        P("cat", None),
        P(),
        P(),
    )
    return jax.shard_map(
        local, mesh=mesh, in_specs=placed, out_specs=(P("cat"), P("cat", "tp")), check_vma=False
    )
```

time: 298 us -> 168 us (0.56)
  waiting for transfers between devices: 197 us -> 60.1 us
  starting transfers between devices: 0.2 us -> 45.6 us
  matrix products: 27.6 us -> 0 us
  Pallas kernels: 0 us -> 25.8 us
  blocking collectives: 24.2 us -> 0 us
  other arithmetic: 13 us -> 1.87 us
    all_gather x3 -> x1, waiting for transfers between devices: 126 us -> 13.8 us  [local(): query = lax.all_gather(query_emb, 'tp')]
    reduce_scatter x1 -> x0, waiting for transfers between devices: 47.8 us -> none  [local(): lax.psum_scatter(jnp.dot(reordered, item_weight, preferred_element_type=j...]
    ppermute x0 -> x31, waiting for transfers between devices: none -> 46.3 us  [the longest x12 28.6 us: send_x(): return lax.ppermute(value, 'tp', [(i, (i + d) % TP) for i in range(TP)])]
    ppermute x0 -> x31, starting transfers between devices: none -> 45.5 us  [the longest x19 27.5 us: send(): return lax.ppermute(value, 'cat', cat_perm(dy, dz, dc))]
    dot_general x3 -> x0, matrix products: 27.6 us -> none  [the longest x1 13.4 us: local(): jnp.einsum('gqk,gke->gqe', weights, picked, preferred_element_type=jnp.fl...]
    pallas_call x0 -> x4, Pallas kernels: none -> 25.8 us  [the longest x2 22.3 us: attend(): pl.pallas_call(body, grid_spec=pltpu.PrefetchScalarGridSpec(num_scalar_pr...]
    all_gather x2 -> x0, blocking collectives: 24.2 us -> none  [merged(): pieces = jax.tree.map(lambda part: lax.all_gather(part, axis), value)]
    unnamed x6 -> x1, waiting for transfers between devices: 23.3 us -> 0.02 us
  transfers between devices with their start and end apart: 5 -> 32, of which waited for: 5 -> 15; matrix products, arithmetic and copies ran while one was open for 2% -> 9% of each run, Pallas kernels for 0% -> 0%
where the time goes in v1:
time: 168 us; the launch traced here: 166 us
  waiting for transfers between devices  60.1 us (36%)
  starting transfers between devices  45.6 us (27%)
  Pallas kernels  25.8 us (15%)
  local copies, waits for them, and re-layouts  18.8 us (11%)
  between operations  14.4 us (9%)
  other arithmetic  1.87 us (1%)
    ppermute x12, waiting for transfers between devices, send_x(): return lax.ppermute(value, 'tp', [(i, (i + d) % TP) for i in range(TP)])  28.6 us
    ppermute x19, starting transfers between devices, send(): return lax.ppermute(value, 'cat', cat_perm(dy, dz, dc))  27.5 us
    pallas_call x2, Pallas kernels, attend(): pl.pallas_call(body, grid_spec=pltpu.PrefetchScalarGridSpec(num_scalar_pr...  22.3 us
    ppermute x12, starting transfers between devices, send_x(): return lax.ppermute(value, 'tp', [(i, (i + d) % TP) for i in range(TP)])  18 us
    ppermute x19, waiting for transfers between devices, send(): return lax.ppermute(value, 'cat', cat_perm(dy, dz, dc))  17.7 us
    all_gather x1, waiting for transfers between devices, local(): query = lax.all_gather(query_emb, 'tp')  13.8 us
    unnamed x26, local copies, waits for them, and re-layouts  4.77 us
    slice x2, local copies, waits for them, and re-layouts, spread(): near_a, near_b = (send(near_up[:2], 0, 1), send(near_down[2:], 0, -1))  3.81 us
  transfers between devices with their start and end apart: 32, of which 15 were waited for; matrix products, arithmetic and copies ran while one was open for 9% of the time, Pallas kernels for 0%

profile of v1, /device:TPU:0, one launch (start us, length us, event | category | flops | bytes accessed | tf_op | source)
XLA Modules:
  0.0 166.4 jit_solution(7216405682443537516)
XLA Ops:
  10.2 2.7 %collective-permute-start.2 = (bf16[512,256]{1,0:T(8,128)(2,1)S(1)}, bf16[512,256]{1,0:T(8,128)(2,1)S(1)}, u32[]{:S(2)}, u32[]{:S(2)}) collective-permute-start(bf16[512,256]{1,0:T(8,128)(2,1)S(1)} %bitcast.62), channel_id=1, source_target_pairs={{0,2},{1,3},{2,0},{3,1},{4,6},{5,7},{6,4},{7,5},{8,10},{9,11},{10,... | collective-permute-start | bytes 786440 | tf_op jit(solution)/shard_map/ppermute | solution.py:44
  15.9 3.0 %collective-permute-done.1.refs_1_ = bf16[512,256]{1,0:T(8,128)(2,1)S(1)} collective-permute-done((bf16[512,256]{1,0:T(8,128)(2,1)S(1)}, bf16[512,256]{1,0:T(8,128)(2,1)S(1)}, u32[]{:S(2)}, u32[]{:S(2)}) %collective-permute-start.1) | collective-permute-done | bytes 262176 | tf_op jit(solution)/shard_map/ppermute | solution.py:44
  20.7 5.1 %collective-permute-done.2.refs_2_ = bf16[512,256]{1,0:T(8,128)(2,1)S(1)} collective-permute-done((bf16[512,256]{1,0:T(8,128)(2,1)S(1)}, bf16[512,256]{1,0:T(8,128)(2,1)S(1)}, u32[]{:S(2)}, u32[]{:S(2)}) %collective-permute-start.2) | collective-permute-done | bytes 262176 | tf_op jit(solution)/shard_map/ppermute | solution.py:44
  25.8 3.2 %collective-permute-done.4.refs_5_ = bf16[256,512]{1,0:T(8,128)(2,1)S(1)} collective-permute-done((bf16[256,512]{1,0:T(8,128)(2,1)S(1)}, bf16[256,512]{1,0:T(8,128)(2,1)S(1)}, u32[]{:S(2)}, u32[]{:S(2)}) %collective-permute-start.4) | collective-permute-done | bytes 262176 | tf_op jit(solution)/shard_map/ppermute | solution.py:44
  29.0 6.8 %collective-permute-done.5.refs_6_ = bf16[256,512]{1,0:T(8,128)(2,1)S(1)} collective-permute-done((bf16[256,512]{1,0:T(8,128)(2,1)S(1)}, bf16[256,512]{1,0:T(8,128)(2,1)S(1)}, u32[]{:S(2)}, u32[]{:S(2)}) %collective-permute-start.5) | collective-permute-done | bytes 262176 | tf_op jit(solution)/shard_map/ppermute | solution.py:44
  38.4 2.9 %collective-permute-start.8 = (bf16[8,32,512]{2,1,0:T(8,128)(2,1)S(1)}, bf16[8,32,512]{2,1,0:T(8,128)(2,1)S(1)}, u32[]{:S(2)}, u32[]{:S(2)}) collective-permute-start(bf16[8,32,512]{2,1,0:T(8,128)(2,1)S(1)} %get-tuple-element.10), channel_id=1, source_target_pairs={{0,64},{4,68},{8,72},{12,76},{16,80},{20,84},{24,88},{28,92},{32,9... | collective-permute-start | bytes 786440 | tf_op jit(solution)/shard_map/ppermute | solution.py:40
  44.6 3.6 %collective-permute-start.16 = (bf16[8,32,512]{2,1,0:T(8,128)(2,1)S(1)}, bf16[8,32,512]{2,1,0:T(8,128)(2,1)S(1)}, u32[]{:S(2)}, u32[]{:S(2)}) collective-permute-start(bf16[8,32,512]{2,1,0:T(8,128)(2,1)S(1)} %collective-permute-done.14), channel_id=1, source_target_pairs={{0,16},{4,20},{8,24},{12,28},{16,0},{20,4},{24,8},{28,12},{32,48},... | collective-permute-start | bytes 786440 | tf_op jit(solution)/shard_map/ppermute | solution.py:40
  48.1 2.6 %collective-permute-start.15 = (bf16[8,32,512]{2,1,0:T(8,128)(2,1)S(1)}, bf16[8,32,512]{2,1,0:T(8,128)(2,1)S(1)}, u32[]{:S(2)}, u32[]{:S(2)}) collective-permute-start(bf16[8,32,512]{2,1,0:T(8,128)(2,1)S(1)} %collective-permute-done.14), channel_id=1, source_target_pairs={{0,24},{4,28},{8,0},{12,4},{16,8},{20,12},{24,16},{28,20},{32,56},... | collective-permute-start | bytes 786440 | tf_op jit(solution)/shard_map/ppermute | solution.py:40
  50.8 2.8 %collective-permute-done.8 = bf16[8,32,512]{2,1,0:T(8,128)(2,1)S(1)} collective-permute-done((bf16[8,32,512]{2,1,0:T(8,128)(2,1)S(1)}, bf16[8,32,512]{2,1,0:T(8,128)(2,1)S(1)}, u32[]{:S(2)}, u32[]{:S(2)}) %collective-permute-start.8) | collective-permute-done | bytes 262176 | tf_op jit(solution)/shard_map/ppermute | solution.py:40
  53.7 4.1 %collective-permute-start.10 = (bf16[4,8,32,512]{3,2,1,0:T(8,128)(2,1)S(1)}, bf16[4,8,32,512]{3,2,1,0:T(8,128)(2,1)}, u32[]{:S(2)}, u32[]{:S(2)}) collective-permute-start(bf16[4,8,32,512]{3,2,1,0:T(8,128)(2,1)S(1)} %pad_maximum_fusion), channel_id=1, source_target_pairs={{0,24},{4,28},{8,0},{12,4},{16,8},{20,12},{24,16},{28,20},{32,56},... | collective-permute-start | bytes 3145736 | tf_op jit(solution)/shard_map/ppermute | solution.py:40
  61.5 2.0 %collective-permute-start.19 = (bf16[4,8,32,512]{3,2,1,0:T(8,128)(2,1)}, bf16[4,8,32,512]{3,2,1,0:T(8,128)(2,1)}, u32[]{:S(2)}, u32[]{:S(2)}) collective-permute-start(bf16[4,8,32,512]{3,2,1,0:T(8,128)(2,1)} %pad_maximum_fusion.1), channel_id=1, source_target_pairs={{0,32},{4,36},{8,40},{12,44},{16,48},{20,52},{24,56},{28,60},{32,6... | collective-permute-start | bytes 3145736 | tf_op jit(solution)/shard_map/ppermute | solution.py:40
  64.0 13.8 %all-gather.3.cloned.1.call-done = bf16[4096,128]{1,0:T(8,128)(2,1)} async-done(((bf16[1024,128]{1,0:T(8,128)(2,1)}), bf16[4096,128]{1,0:T(8,128)(2,1)}) %all-gather.3.cloned.1.call-update) | async-done | bytes 1048592 | tf_op jit(solution)/shard_map/all_gather | solution.py:282
  78.2 6.2 %collective-permute-done.11 = bf16[4,8,32,512]{3,2,1,0:T(8,128)(2,1)} collective-permute-done((bf16[4,8,32,512]{3,2,1,0:T(8,128)(2,1)S(1)}, bf16[4,8,32,512]{3,2,1,0:T(8,128)(2,1)}, u32[]{:S(2)}, u32[]{:S(2)}) %collective-permute-start.11) | collective-permute-done | bytes 1048608 | tf_op jit(solution)/shard_map/ppermute | solution.py:40
  88.2 3.2 %collective-permute-start.13 = (bf16[2,8,32,512]{3,2,1,0:T(8,128)(2,1)}, bf16[2,8,32,512]{3,2,1,0:T(8,128)(2,1)S(1)}, u32[]{:S(2)}, u32[]{:S(2)}) collective-permute-start(bf16[2,8,32,512]{3,2,1,0:T(8,128)(2,1)} %slice.48), channel_id=1, source_target_pairs={{0,24},{4,28},{8,0},{12,4},{16,8},{20,12},{24,16},{28,20},{32,56},... | collective-permute-start | bytes 1572872 | tf_op jit(solution)/shard_map/ppermute | solution.py:40
  93.3 1.9 %slice.50 = bf16[2,8,32,512]{3,2,1,0:T(8,128)(2,1)} slice(bf16[4,8,32,512]{3,2,1,0:T(8,128)(2,1)} %collective-permute-done.18), slice={[2:4], [0:8], [0:32], [0:512]} | slice | bytes 1048576 | tf_op jit(solution)/shard_map/slice | solution.py:258
  95.3 3.2 %collective-permute-start.21 = (bf16[2,8,32,512]{3,2,1,0:T(8,128)(2,1)}, bf16[2,8,32,512]{3,2,1,0:T(8,128)(2,1)}, u32[]{:S(2)}, u32[]{:S(2)}) collective-permute-start(bf16[2,8,32,512]{3,2,1,0:T(8,128)(2,1)} %slice.50), channel_id=1, source_target_pairs={{0,96},{4,100},{8,104},{12,108},{16,112},{20,116},{24,120},{28,124... | collective-permute-start | bytes 1572872 | tf_op jit(solution)/shard_map/ppermute | solution.py:40
  103.6 3.9 %collective-permute-done.20 = bf16[2,8,32,512]{3,2,1,0:T(8,128)(2,1)} collective-permute-done((bf16[2,8,32,512]{3,2,1,0:T(8,128)(2,1)}, bf16[2,8,32,512]{3,2,1,0:T(8,128)(2,1)}, u32[]{:S(2)}, u32[]{:S(2)}) %collective-permute-start.20) | collective-permute-done | bytes 524320 | tf_op jit(solution)/shard_map/ppermute | solution.py:40
  110.8 11.1 %attend_other.1 = (bf16[1024,512]{1,0:T(8,128)(2,1)}, f32[4,8,256]{2,1,0:T(8,128)S(1)}) custom-call(s32[256]{0:T(256)S(1)} %reshape.119.row_ref, bf16[4,1024,128]{2,1,0:T(8,128)(2,1)S(1)} %collective-permute-done.22.q_ref, f32[4,1,2048]{2,1,0:T(1,128)S(1)} %slice.43.lq_ref, bf16[32,32,512]{2,1,0:T(8,128)(2,1)S(1)} %bitcast.49, ...), custom_call_target="tpu_custom_call" | custom-call | flops 4294967296 | bytes 12582912 | tf_op jit(solution)/shard_map/attend_other/pallas_call | solution.py:176
  126.3 11.2 %attend_own.1 = (bf16[4,1024,128]{2,1,0:T(8,128)(2,1)S(1)}, f32[4,8,256]{2,1,0:T(8,128)S(1)}) custom-call(s32[256]{0:T(256)S(1)} %reshape.101.row_ref, bf16[4,1024,128]{2,1,0:T(8,128)(2,1)S(1)} %bitcast.54, f32[4,1,2048]{2,1,0:T(1,128)S(1)} %slice.42.lq_ref, bf16[32,32,512]{2,1,0:T(8,128)(2,1)S(1)} %bitcast.50, bf16[32,32,512]{2,1,0:T(8,128)(2,1)} %bitcast.14.refs_1_, ...), custom_call_target="tpu_custom_call" | custom-call | flops 4294967296 | bytes 12582912 | tf_op jit(solution)/shard_map/attend_own/pallas_call | solution.py:176
  138.9 2.4 %collective-permute-start.26 = (bf16[1024,128]{1,0:T(8,128)(2,1)S(1)}, bf16[1024,128]{1,0:T(8,128)(2,1)S(1)}, u32[]{:S(2)}, u32[]{:S(2)}) collective-permute-start(bf16[1024,128]{1,0:T(8,128)(2,1)S(1)} %get-tuple-element.19), channel_id=1, source_target_pairs={{0,2},{1,3},{2,0},{3,1},{4,6},{5,7},{6,4},{7,5},{8,10},{9,11},{10,... | collective-permute-start | bytes 786440 | tf_op jit(solution)/shard_map/ppermute | solution.py:44
  144.5 8.5 %collective-permute-done.28.refs_5_ = f32[4,8,256]{2,1,0:T(8,128)S(1)} collective-permute-done((f32[4,8,256]{2,1,0:T(8,128)S(1)}, f32[4,8,256]{2,1,0:T(8,128)S(1)}, u32[]{:S(2)}, u32[]{:S(2)}) %collective-permute-start.28) | collective-permute-done | bytes 32800 | tf_op jit(solution)/shard_map/ppermute | solution.py:44
  152.9 2.0 %collective-permute-start.30 = (f32[4,8,256]{2,1,0:T(8,128)S(1)}, f32[4,8,256]{2,1,0:T(8,128)S(1)}, u32[]{:S(2)}, u32[]{:S(2)}) collective-permute-start(f32[4,8,256]{2,1,0:T(8,128)S(1)} %get-tuple-element.15.refs_4_), channel_id=1, source_target_pairs={{0,3},{1,0},{2,1},{3,2},{4,7},{5,4},{6,5},{7,6},{8,11},{9,8},{10,9... | collective-permute-start | bytes 98312 | tf_op jit(solution)/shard_map/ppermute | solution.py:44
  154.9 1.9 %collective-permute-done.30.refs_7_ = f32[4,8,256]{2,1,0:T(8,128)S(1)} collective-permute-done((f32[4,8,256]{2,1,0:T(8,128)S(1)}, f32[4,8,256]{2,1,0:T(8,128)S(1)}, u32[]{:S(2)}, u32[]{:S(2)}) %collective-permute-start.30) | collective-permute-done | bytes 32800 | tf_op jit(solution)/shard_map/ppermute | solution.py:44
  156.9 2.7 %last.1 = (f32[4,1,256]{2,1,0:T(1,128)}, bf16[1024,128]{1,0:T(8,128)(2,1)}) custom-call(bf16[1024,128]{1,0:T(8,128)(2,1)S(1)} %get-tuple-element.21.refs_0_, bf16[1024,128]{1,0:T(8,128)(2,1)S(1)} %collective-permute-done.25.refs_1_, bf16[1024,128]{1,0:T(8,128)(2,1)S(1)} %collective-permute-done.26.refs_2_, ...), custom_call_target="tpu_custom_call" | custom-call | tf_op jit(solution)/shard_map/last/pallas_call | solution.py:238
  (97 shorter events, 41.2 us)
Async XLA Ops:
  7.2 70.6 %all-gather.3.cloned.1.call-start = ((), (), s32[]{:S(2)}) async-start(), calls=%async_computation | async-start | bytes 1310720 | tf_op jit(solution)/shard_map/all_gather | solution.py:282
  10.2 15.6 %collective-permute-start.2 = (bf16[512,256]{1,0:T(8,128)(2,1)S(1)}, bf16[512,256]{1,0:T(8,128)(2,1)S(1)}, u32[]{:S(2)}, u32[]{:S(2)}) collective-permute-start(bf16[512,256]{1,0:T(8,128)(2,1)S(1)} %bitcast.62), channel_id=1, source_target_pairs={{0,2},{1,3},{2,0},{3,1},{4,6},{5,7},{6,4},{7,5},{8,10},{9,11},{10,... | collective-permute-start | bytes 786440 | tf_op jit(solution)/shard_map/ppermute | solution.py:44
  13.0 12.8 %collective-permute-start.3 = (bf16[512,256]{1,0:T(8,128)(2,1)S(1)}, bf16[512,256]{1,0:T(8,128)(2,1)S(1)}, u32[]{:S(2)}, u32[]{:S(2)}) collective-permute-start(bf16[512,256]{1,0:T(8,128)(2,1)S(1)} %bitcast.61), channel_id=1, source_target_pairs={{0,3},{1,0},{2,1},{3,2},{4,7},{5,4},{6,5},{7,6},{8,11},{9,8},{10,9... | collective-permute-start | bytes 786440 | tf_op jit(solution)/shard_map/ppermute | solution.py:44
  14.4 14.6 %collective-permute-start.4 = (bf16[256,512]{1,0:T(8,128)(2,1)S(1)}, bf16[256,512]{1,0:T(8,128)(2,1)S(1)}, u32[]{:S(2)}, u32[]{:S(2)}) collective-permute-start(bf16[256,512]{1,0:T(8,128)(2,1)S(1)} %copy-done.1), channel_id=1, source_target_pairs={{0,1},{1,2},{2,3},{3,0},{4,5},{5,6},{6,7},{7,4},{8,9},{9,10},{10,1... | collective-permute-start | bytes 786440 | tf_op jit(solution)/shard_map/ppermute | solution.py:44
  15.0 20.9 %collective-permute-start.5 = (bf16[256,512]{1,0:T(8,128)(2,1)S(1)}, bf16[256,512]{1,0:T(8,128)(2,1)S(1)}, u32[]{:S(2)}, u32[]{:S(2)}) collective-permute-start(bf16[256,512]{1,0:T(8,128)(2,1)S(1)} %copy-done.1), channel_id=1, source_target_pairs={{0,2},{1,3},{2,0},{3,1},{4,6},{5,7},{6,4},{7,5},{8,10},{9,11},{10,... | collective-permute-start | bytes 786440 | tf_op jit(solution)/shard_map/ppermute | solution.py:44
  18.9 17.0 %collective-permute-start.6 = (bf16[256,512]{1,0:T(8,128)(2,1)S(1)}, bf16[256,512]{1,0:T(8,128)(2,1)S(1)}, u32[]{:S(2)}, u32[]{:S(2)}) collective-permute-start(bf16[256,512]{1,0:T(8,128)(2,1)S(1)} %copy-done.1), channel_id=1, source_target_pairs={{0,3},{1,0},{2,1},{3,2},{4,7},{5,4},{6,5},{7,6},{8,11},{9,8},{10,9... | collective-permute-start | bytes 786440 | tf_op jit(solution)/shard_map/ppermute | solution.py:44
  38.4 15.1 %collective-permute-start.8 = (bf16[8,32,512]{2,1,0:T(8,128)(2,1)S(1)}, bf16[8,32,512]{2,1,0:T(8,128)(2,1)S(1)}, u32[]{:S(2)}, u32[]{:S(2)}) collective-permute-start(bf16[8,32,512]{2,1,0:T(8,128)(2,1)S(1)} %get-tuple-element.10), channel_id=1, source_target_pairs={{0,64},{4,68},{8,72},{12,76},{16,80},{20,84},{24,88},{28,92},{32,9... | collective-permute-start | bytes 786440 | tf_op jit(solution)/shard_map/ppermute | solution.py:40
  41.3 12.2 %collective-permute-start.7 = (bf16[8,32,512]{2,1,0:T(8,128)(2,1)S(1)}, bf16[8,32,512]{2,1,0:T(8,128)(2,1)S(1)}, u32[]{:S(2)}, u32[]{:S(2)}) collective-permute-start(bf16[8,32,512]{2,1,0:T(8,128)(2,1)S(1)} %get-tuple-element.10), channel_id=1, source_target_pairs={{0,96},{4,100},{8,104},{12,108},{16,112},{20,116},{24,120},{28,124... | collective-permute-start | bytes 786440 | tf_op jit(solution)/shard_map/ppermute | solution.py:40
  42.6 15.1 %collective-permute-start.17 = (bf16[8,32,512]{2,1,0:T(8,128)(2,1)S(1)}, bf16[8,32,512]{2,1,0:T(8,128)(2,1)S(1)}, u32[]{:S(2)}, u32[]{:S(2)}) collective-permute-start(bf16[8,32,512]{2,1,0:T(8,128)(2,1)S(1)} %collective-permute-done.14), channel_id=1, source_target_pairs={{0,8},{4,12},{8,16},{12,20},{16,24},{20,28},{24,0},{28,4},{32,40},... | collective-permute-start | bytes 786440 | tf_op jit(solution)/shard_map/ppermute | solution.py:40
  44.6 15.0 %collective-permute-start.16 = (bf16[8,32,512]{2,1,0:T(8,128)(2,1)S(1)}, bf16[8,32,512]{2,1,0:T(8,128)(2,1)S(1)}, u32[]{:S(2)}, u32[]{:S(2)}) collective-permute-start(bf16[8,32,512]{2,1,0:T(8,128)(2,1)S(1)} %collective-permute-done.14), channel_id=1, source_target_pairs={{0,16},{4,20},{8,24},{12,28},{16,0},{20,4},{24,8},{28,12},{32,48},... | collective-permute-start | bytes 786440 | tf_op jit(solution)/shard_map/ppermute | solution.py:40
  48.1 12.2 %collective-permute-start.15 = (bf16[8,32,512]{2,1,0:T(8,128)(2,1)S(1)}, bf16[8,32,512]{2,1,0:T(8,128)(2,1)S(1)}, u32[]{:S(2)}, u32[]{:S(2)}) collective-permute-start(bf16[8,32,512]{2,1,0:T(8,128)(2,1)S(1)} %collective-permute-done.14), channel_id=1, source_target_pairs={{0,24},{4,28},{8,0},{12,4},{16,8},{20,12},{24,16},{28,20},{32,56},... | collective-permute-start | bytes 786440 | tf_op jit(solution)/shard_map/ppermute | solution.py:40
  53.7 32.6 %collective-permute-start.10 = (bf16[4,8,32,512]{3,2,1,0:T(8,128)(2,1)S(1)}, bf16[4,8,32,512]{3,2,1,0:T(8,128)(2,1)}, u32[]{:S(2)}, u32[]{:S(2)}) collective-permute-start(bf16[4,8,32,512]{3,2,1,0:T(8,128)(2,1)S(1)} %pad_maximum_fusion), channel_id=1, source_target_pairs={{0,24},{4,28},{8,0},{12,4},{16,8},{20,12},{24,16},{28,20},{32,56},... | collective-permute-start | bytes 3145736 | tf_op jit(solution)/shard_map/ppermute | solution.py:40
  57.8 26.6 %collective-permute-start.11 = (bf16[4,8,32,512]{3,2,1,0:T(8,128)(2,1)S(1)}, bf16[4,8,32,512]{3,2,1,0:T(8,128)(2,1)}, u32[]{:S(2)}, u32[]{:S(2)}) collective-permute-start(bf16[4,8,32,512]{3,2,1,0:T(8,128)(2,1)S(1)} %pad_maximum_fusion), channel_id=1, source_target_pairs={{0,8},{4,12},{8,16},{12,20},{16,24},{20,28},{24,0},{28,4},{32,40},... | collective-permute-start | bytes 3145736 | tf_op jit(solution)/shard_map/ppermute | solution.py:40
  61.5 31.9 %collective-permute-start.18 = (bf16[4,8,32,512]{3,2,1,0:T(8,128)(2,1)}, bf16[4,8,32,512]{3,2,1,0:T(8,128)(2,1)}, u32[]{:S(2)}, u32[]{:S(2)}) collective-permute-start(bf16[4,8,32,512]{3,2,1,0:T(8,128)(2,1)} %pad_maximum_fusion.1), channel_id=1, source_target_pairs={{0,96},{4,100},{8,104},{12,108},{16,112},{20,116},{24,120},{28,124... | collective-permute-start | bytes 3145736 | tf_op jit(solution)/shard_map/ppermute | solution.py:40
  61.5 30.0 %collective-permute-start.19 = (bf16[4,8,32,512]{3,2,1,0:T(8,128)(2,1)}, bf16[4,8,32,512]{3,2,1,0:T(8,128)(2,1)}, u32[]{:S(2)}, u32[]{:S(2)}) collective-permute-start(bf16[4,8,32,512]{3,2,1,0:T(8,128)(2,1)} %pad_maximum_fusion.1), channel_id=1, source_target_pairs={{0,32},{4,36},{8,40},{12,44},{16,48},{20,52},{24,56},{28,60},{32,6... | collective-permute-start | bytes 3145736 | tf_op jit(solution)/shard_map/ppermute | solution.py:40
  77.8 31.0 %collective-permute-start.22 = (bf16[4,1024,128]{2,1,0:T(8,128)(2,1)}, bf16[4,1024,128]{2,1,0:T(8,128)(2,1)S(1)}, u32[]{:S(2)}, u32[]{:S(2)}) collective-permute-start(bf16[4,1024,128]{2,1,0:T(8,128)(2,1)} %bitcast.53), channel_id=1, source_target_pairs={{0,4},{4,0},{8,12},{12,8},{16,20},{20,16},{24,28},{28,24},{32,36},... | collective-permute-start | bytes 3145736 | tf_op jit(solution)/shard_map/ppermute | solution.py:40
  86.3 15.7 %collective-permute-start.12 = (bf16[2,8,32,512]{3,2,1,0:T(8,128)(2,1)}, bf16[2,8,32,512]{3,2,1,0:T(8,128)(2,1)S(1)}, u32[]{:S(2)}, u32[]{:S(2)}) collective-permute-start(bf16[2,8,32,512]{3,2,1,0:T(8,128)(2,1)} %slice.47), channel_id=1, source_target_pairs={{0,8},{4,12},{8,16},{12,20},{16,24},{20,28},{24,0},{28,4},{32,40},... | collective-permute-start | bytes 1572872 | tf_op jit(solution)/shard_map/ppermute | solution.py:40
  88.2 14.6 %collective-permute-start.13 = (bf16[2,8,32,512]{3,2,1,0:T(8,128)(2,1)}, bf16[2,8,32,512]{3,2,1,0:T(8,128)(2,1)S(1)}, u32[]{:S(2)}, u32[]{:S(2)}) collective-permute-start(bf16[2,8,32,512]{3,2,1,0:T(8,128)(2,1)} %slice.48), channel_id=1, source_target_pairs={{0,24},{4,28},{8,0},{12,4},{16,8},{20,12},{24,16},{28,20},{32,56},... | collective-permute-start | bytes 1572872 | tf_op jit(solution)/shard_map/ppermute | solution.py:40
  93.3 14.2 %collective-permute-start.20 = (bf16[2,8,32,512]{3,2,1,0:T(8,128)(2,1)}, bf16[2,8,32,512]{3,2,1,0:T(8,128)(2,1)}, u32[]{:S(2)}, u32[]{:S(2)}) collective-permute-start(bf16[2,8,32,512]{3,2,1,0:T(8,128)(2,1)} %slice.49), channel_id=1, source_target_pairs={{0,32},{4,36},{8,40},{12,44},{16,48},{20,52},{24,56},{28,60},{32,6... | collective-permute-start | bytes 1572872 | tf_op jit(solution)/shard_map/ppermute | solution.py:40
  95.3 13.5 %collective-permute-start.21 = (bf16[2,8,32,512]{3,2,1,0:T(8,128)(2,1)}, bf16[2,8,32,512]{3,2,1,0:T(8,128)(2,1)}, u32[]{:S(2)}, u32[]{:S(2)}) collective-permute-start(bf16[2,8,32,512]{3,2,1,0:T(8,128)(2,1)} %slice.50), channel_id=1, source_target_pairs={{0,96},{4,100},{8,104},{12,108},{16,112},{20,116},{24,120},{28,124... | collective-permute-start | bytes 1572872 | tf_op jit(solution)/shard_map/ppermute | solution.py:40
  137.5 19.3 %collective-permute-start.25 = (bf16[1024,128]{1,0:T(8,128)(2,1)S(1)}, bf16[1024,128]{1,0:T(8,128)(2,1)S(1)}, u32[]{:S(2)}, u32[]{:S(2)}) collective-permute-start(bf16[1024,128]{1,0:T(8,128)(2,1)S(1)} %get-tuple-element.20), channel_id=1, source_target_pairs={{0,1},{1,2},{2,3},{3,0},{4,5},{5,6},{6,7},{7,4},{8,9},{9,10},{10,1... | collective-permute-start | bytes 786440 | tf_op jit(solution)/shard_map/ppermute | solution.py:44
  138.9 17.9 %collective-permute-start.26 = (bf16[1024,128]{1,0:T(8,128)(2,1)S(1)}, bf16[1024,128]{1,0:T(8,128)(2,1)S(1)}, u32[]{:S(2)}, u32[]{:S(2)}) collective-permute-start(bf16[1024,128]{1,0:T(8,128)(2,1)S(1)} %get-tuple-element.19), channel_id=1, source_target_pairs={{0,2},{1,3},{2,0},{3,1},{4,6},{5,7},{6,4},{7,5},{8,10},{9,11},{10,... | collective-permute-start | bytes 786440 | tf_op jit(solution)/shard_map/ppermute | solution.py:44
  141.3 15.6 %collective-permute-start.27 = (bf16[1024,128]{1,0:T(8,128)(2,1)S(1)}, bf16[1024,128]{1,0:T(8,128)(2,1)S(1)}, u32[]{:S(2)}, u32[]{:S(2)}) collective-permute-start(bf16[1024,128]{1,0:T(8,128)(2,1)S(1)} %get-tuple-element.18), channel_id=1, source_target_pairs={{0,3},{1,0},{2,1},{3,2},{4,7},{5,4},{6,5},{7,6},{8,11},{9,8},{10,9... | collective-permute-start | bytes 786440 | tf_op jit(solution)/shard_map/ppermute | solution.py:44
  143.3 11.6 %collective-permute-start.29 = (f32[4,8,256]{2,1,0:T(8,128)S(1)}, f32[4,8,256]{2,1,0:T(8,128)S(1)}, u32[]{:S(2)}, u32[]{:S(2)}) collective-permute-start(f32[4,8,256]{2,1,0:T(8,128)S(1)} %get-tuple-element.15.refs_4_), channel_id=1, source_target_pairs={{0,2},{1,3},{2,0},{3,1},{4,6},{5,7},{6,4},{7,5},{8,10},{9,11},{10,... | collective-permute-start | bytes 98312 | tf_op jit(solution)/shard_map/ppermute | solution.py:44
  (21 other events, 143.9 us)
Sparse Core Ops, SparseCore 0:
  50.9 26.8 all-gather.2

commit v2 on v1

v2 whole, which is shorter than its diff:
```python
import functools
import math

import jax
import jax.numpy as jnp
from jax import lax
from jax.experimental import pallas as pl
from jax.experimental.pallas import tpu as pltpu
from jax.sharding import PartitionSpec as P

BLK = 256
TP = 4
NY = 4
NZ = 4
E = 512
LOG2E = math.log2(math.e)
LN2 = math.log(2.0)
SCALE = 2.0 / math.sqrt(E)
LOW = -1e30
ROWS = BLK // TP // 2
NBD = 8
PICKS = 64
COLS = PICKS * ROWS
TILE = 512
HID = 1024
EXTRA = 32


def cat_perm(flip_y, flip_z, flip_c):
    def at(y, z, c):
        return (y * NZ + z) * 2 + c

    return [
        (at(y, z, c), at(y ^ flip_y, z ^ flip_z, c ^ flip_c))
        for y in range(NY)
        for z in range(NZ)
        for c in range(2)
    ]


def send(value, y=0, z=0, c=0):
    return lax.ppermute(value, "cat", cat_perm(y, z, c))


def send_x(value, d):
    return lax.ppermute(value, "tp", [(i, (i + d) % TP) for i in range(TP)])


def tower_kernel(core_ref, *refs):
    hidden = refs[0:4]
    mine, theirs = refs[4:8], refs[8]
    keep_ref, give_ref, scratch = refs[9:]
    core = core_ref[0]
    half = HID // TP // 2
    acc = jnp.zeros((NBD * 2 * ROWS, E), jnp.float32)
    for d in range(TP):
        low = jnp.where(core == 0, mine[d][...], theirs[d])
        high = jnp.where(core == 0, theirs[d], mine[d][...])
        acc += jnp.dot(hidden[d][:, :half], low, preferred_element_type=jnp.float32)
        acc += jnp.dot(hidden[d][:, half:], high, preferred_element_type=jnp.float32)
    scratch[...] = acc.astype(jnp.bfloat16).reshape(scratch.shape)
    keep_ref[...] = scratch[:, core]
    give_ref[...] = scratch[:, 1 - core]


def tower(core, hidden, mine, theirs):
    half = jax.ShapeDtypeStruct((NBD, ROWS, E), jnp.bfloat16)
    return pl.pallas_call(
        tower_kernel,
        out_shape=(half, half),
        in_specs=[pl.BlockSpec(memory_space=pltpu.SMEM)]
        + [pl.BlockSpec(memory_space=pltpu.VMEM)] * 9,
        out_specs=(pl.BlockSpec(memory_space=pltpu.VMEM),) * 2,
        scratch_shapes=[pltpu.VMEM((NBD, 2, ROWS, E), jnp.bfloat16)],
        compiler_params=pltpu.CompilerParams(vmem_limit_bytes=40 << 20),
        cost_estimate=pl.CostEstimate(
            flops=2 * 512 * 1024 * 512, bytes_accessed=3 << 20, transcendentals=0
        ),
        name="tower",
    )(core, *hidden, *mine, theirs)


PIECES = 16


def one_block(rank, q_ref, lq_ref, row_ref, table, picked, scores, first):
    for j in range(PICKS):
        picked[pl.ds(j * ROWS, ROWS), :] = table[row_ref[first + j]]
    query = jnp.concatenate(
        [q_ref[lax.rem(rank + TP - s, TP)] for s in range(TP)], axis=1
    )
    top = jnp.full((BLK, 128), LOW, jnp.float32)
    for n in range(COLS // TILE):
        cols = pl.ds(n * TILE, TILE)
        part = lax.dot_general(
            query,
            picked[cols, :],
            (((1,), (1,)), ((), ())),
            preferred_element_type=jnp.float32,
        )
        part = part * (SCALE * LOG2E) - lq_ref[0, :, cols]
        scores[:, cols] = part
        for g in range(TILE // 128):
            top = jnp.maximum(top, part[:, g * 128 : (g + 1) * 128])
    top = jnp.max(top, axis=1, keepdims=True)
    total = jnp.zeros((BLK, 128), jnp.float32)
    acc = jnp.zeros((BLK, E), jnp.float32)
    for n in range(COLS // TILE):
        cols = pl.ds(n * TILE, TILE)
        weight = jnp.exp2(scores[:, cols] - top)
        for g in range(TILE // 128):
            total += weight[:, g * 128 : (g + 1) * 128]
        acc += jnp.dot(
            weight.astype(jnp.bfloat16), picked[cols, :], preferred_element_type=jnp.float32
        )
    return top, jnp.sum(total, axis=1, keepdims=True), acc


def rows_of(top, total):
    lane = lax.broadcasted_iota(jnp.int32, (BLK, 128), 1)
    both = jnp.where(lane == 0, top, jnp.where(lane == 1, total, 0.0))
    return jnp.transpose(both)[:8]


def fill(pieces, table, sems):
    size = table.shape[0] // PIECES
    copies = [
        pltpu.make_async_copy(piece, table.at[pl.ds(n * size, size)], sems.at[n])
        for n, piece in enumerate(pieces)
    ]
    for copy in copies:
        copy.start()
    for copy in copies:
        copy.wait()


def first_kernel(row_ref, rank_ref, q_ref, lq_ref, *refs):
    pieces = refs[:PIECES]
    out_ref, stat_ref, table, picked, scores, sems = refs[PIECES:]
    step = pl.program_id(0)

    @pl.when(step == 0)
    def _():
        fill(pieces, table, sems)

    top, total, acc = one_block(rank_ref[0], q_ref, lq_ref, row_ref, table, picked, scores, step * PICKS)
    out_ref[...] = acc.astype(jnp.bfloat16)
    stat_ref[0] = rows_of(top, total)


def split_rows(row):
    out = []
    for _ in range(3):
        part = row.astype(jnp.bfloat16).astype(jnp.float32)
        out += [part[:, :128], part[:, 128:]]
        row = row - part
    return out


def joined_row(rows):
    halves = [rows[n : n + 1] + (rows[n + 2 : n + 3] + rows[n + 4 : n + 5]) for n in range(2)]
    return jnp.concatenate(halves, axis=1)


def second_kernel(row_ref, rank_ref, q_ref, lq_ref, *refs):
    pieces = refs[:PIECES]
    other_ref, other_stat_ref, pos_ref = refs[PIECES : PIECES + 3]
    outs = refs[PIECES + 3 : PIECES + 7]
    table, picked, scores, sems, quarters = refs[PIECES + 7 :]
    step = pl.program_id(0)

    @pl.when(step == 0)
    def _():
        fill(pieces, table, sems)

    top, total, acc = one_block(rank_ref[0], q_ref, lq_ref, row_ref, table, picked, scores, step * PICKS)
    theirs = jnp.transpose(jnp.concatenate([other_stat_ref[0]] * 16, axis=0))
    their_top, their_total = theirs[:, 0:1], theirs[:, 1:2]
    joint = jnp.maximum(top, their_top)
    mine_by, theirs_by = jnp.exp2(top - joint), jnp.exp2(their_top - joint)
    acc = acc * mine_by + other_ref[...].astype(jnp.float32) * theirs_by
    for s in range(TP):
        quarters[s] = acc[:, s * 128 : (s + 1) * 128].astype(jnp.bfloat16)
    stat = rows_of(joint, total * mine_by + their_total * theirs_by)
    rows = split_rows(stat[0:1]) + split_rows(stat[1:2]) + split_rows(pos_ref[0])
    rows.append(jnp.zeros((EXTRA - len(rows), 128), jnp.float32))
    tail = jnp.concatenate(rows, axis=0).astype(jnp.bfloat16)
    for d in range(TP):
        outs[d][0, :BLK] = quarters[lax.rem(rank_ref[0] + d, TP)]
        outs[d][0, BLK:] = tail


def attend(body, scalars, query, lq, pieces, extra, outs, out_specs, scratch, name):
    blocks = lq.shape[0]
    extra_specs = []
    if extra:
        extra_specs = [
            pl.BlockSpec((BLK, E), lambda i, *_: (i, 0)),
            pl.BlockSpec((1, 8, BLK), lambda i, *_: (i, 0, 0)),
            pl.BlockSpec((1, 1, BLK), lambda i, *_: (i, 0, 0)),
        ]
    return pl.pallas_call(
        body,
        grid_spec=pltpu.PrefetchScalarGridSpec(
            num_scalar_prefetch=len(scalars),
            grid=(blocks,),
            in_specs=[
                pl.BlockSpec((TP, BLK, 128), lambda i, *_: (0, i, 0)),
                pl.BlockSpec((1, 1, COLS), lambda i, *_: (i, 0, 0)),
            ]
            + [pl.BlockSpec(memory_space=pl.ANY)] * PIECES
            + extra_specs,
            out_specs=out_specs,
            scratch_shapes=[
                pltpu.VMEM((256, ROWS, E), jnp.bfloat16),
                pltpu.VMEM((COLS, E), jnp.bfloat16),
                pltpu.VMEM((BLK, COLS), jnp.float32),
                pltpu.SemaphoreType.DMA((PIECES,)),
            ]
            + scratch,
        ),
        out_shape=outs,
        compiler_params=pltpu.CompilerParams(
            dimension_semantics=("arbitrary",), vmem_limit_bytes=58 << 20
        ),
        cost_estimate=pl.CostEstimate(
            flops=blocks * 4 * BLK * COLS * E,
            bytes_accessed=12 << 20,
            transcendentals=blocks * BLK * COLS,
        ),
        name=name,
    )(*scalars, query, lq, *pieces, *extra)


def last_kernel(*refs):
    parts, positive_ref, loss_ref, grad_ref = refs[0:4], *refs[4:]
    tails = [ref[0, BLK:].astype(jnp.float32) for ref in parts]
    tops = [joined_row(tail[0:6]) for tail in tails]
    totals = [joined_row(tail[6:12]) for tail in tails]
    shares = [joined_row(tail[12:18]) for tail in tails]
    pos = (shares[0] + shares[1] + shares[2] + shares[3]) * LOG2E
    joint = pos
    for top in tops:
        joint = jnp.maximum(joint, top)
    total = jnp.exp2(pos - joint)
    for top, one in zip(tops, totals):
        total += one * jnp.exp2(top - joint)
    log_total = joint + jnp.log(total) * LOG2E
    loss_ref[0] = (log_total - pos) * LN2
    factors = [jnp.exp2(top - log_total) * SCALE for top in tops]
    factors.append((jnp.exp2(pos - log_total) - 1.0) * SCALE)
    row = lax.broadcasted_iota(jnp.int32, (128, BLK), 0)
    packed = jnp.zeros((128, BLK), jnp.float32)
    for n, factor in enumerate(factors):
        packed = jnp.where(row == n, factor, packed)
    by = jnp.transpose(packed)
    grad = by[:, 4:5] * positive_ref[...].astype(jnp.float32)
    for n in range(4):
        grad += by[:, n : n + 1] * parts[n][0, :BLK].astype(jnp.float32)
    grad_ref[...] = grad.astype(jnp.bfloat16)


def last(parts, positive):
    blocks = parts[0].shape[0]
    flat = pl.BlockSpec((BLK, 128), lambda i: (i, 0))
    return pl.pallas_call(
        last_kernel,
        grid=(blocks,),
        in_specs=[pl.BlockSpec((1, BLK + EXTRA, 128), lambda i: (i, 0, 0))] * 4 + [flat],
        out_specs=(pl.BlockSpec((1, 1, BLK), lambda i: (i, 0, 0)), flat),
        out_shape=(
            jax.ShapeDtypeStruct((blocks, 1, BLK), jnp.float32),
            jax.ShapeDtypeStruct((blocks * BLK, 128), jnp.bfloat16),
        ),
        compiler_params=pltpu.CompilerParams(vmem_limit_bytes=32 << 20),
        name="last",
    )(*parts, positive)


STREAMS = (
    (("y", 1), ("y", 3), ("z", 1), ("z", 3)),
    (("y", 3), ("y", 1), ("z", 3), ("z", 1)),
    (("z", 1), ("z", 3), ("y", 1), ("y", 3)),
    (("z", 3), ("z", 1), ("y", 3), ("y", 1)),
)


def spread(near, far):
    held = [near[: NBD // 2], near[NBD // 2 :], far[: NBD // 2], far[NBD // 2 :]]
    for step in range(2):
        got = [send(h, **{st[step][0]: st[step][1]}) for h, st in zip(held, STREAMS)]
        held = [jnp.concatenate([h, g]) for h, g in zip(held, got)]
    third = [send(h, **{st[2][0]: st[2][1]}) for h, st in zip(held, STREAMS)]
    fourth = [send(h, **{st[3][0]: st[3][1]}) for h, st in zip(held, STREAMS)]
    fifth = [send(h, **{st[3][0]: st[3][1]}) for h, st in zip(third, STREAMS)]
    pieces = []
    for four in zip(held, third, fourth, fifth):
        pieces += list(four)
    return pieces, held[0]


def place_of(flipped, first):
    return jnp.where(
        flipped == 0, 0, jnp.where(flipped == 2, 3, jnp.where(flipped == first, 1, 2))
    )


def local(query_emb, positive_emb, item_hidden, item_weight, neg_blocks, block_home, sample_counts):
    rank = lax.axis_index("tp")
    place = lax.axis_index("cat")
    core, my_z, my_y = place % 2, (place // 2) % NZ, place // (2 * NZ)
    qblocks = neg_blocks.shape[0]
    total_blocks = block_home.shape[0]

    hidden = item_hidden.reshape(NBD, TP, BLK // TP, -1)

    def piece(d):
        cut = lax.dynamic_index_in_dim(hidden, (rank + d) % TP, 1, keepdims=False)
        return cut.reshape(NBD * BLK // TP, -1)

    core_id = core.reshape(1).astype(jnp.int32)
    half = lax.dynamic_slice_in_dim(item_weight, core * (HID // TP // 2), HID // TP // 2, 0)
    mine_w = [half] + [send_x(half, d) for d in (1, 2, 3)]
    theirs_w = send(jnp.stack(mine_w), c=1)
    hiddens = [piece(0)] + [send_x(piece(d), d) for d in (1, 2, 3)]
    keep, give = tower(core_id, hiddens, mine_w, theirs_w)
    pieces, mark = spread(keep, send(give, c=1))

    late_query, _ = lax.optimization_barrier((query_emb, mark))
    rank_id = rank.reshape(1).astype(jnp.int32)
    query = jnp.stack([late_query] + [send_x(late_query, d) for d in (1, 2, 3)])
    other_query = send(query, c=1)
    pos_part = SCALE * jnp.sum(
        query_emb.astype(jnp.float32) * positive_emb.astype(jnp.float32), axis=1
    ).reshape(qblocks, 1, BLK)

    picks = jnp.concatenate([send(neg_blocks, c=1), neg_blocks])
    matches = picks[:, :, None] == jnp.arange(total_blocks, dtype=jnp.int32)[None, None, :]
    home = jnp.sum(jnp.where(matches, block_home[None, None, :], 0), axis=2)
    slot, owner = home % NBD, home // NBD
    flip_z = ((owner // 2) % NZ) ^ my_z
    flip_y = (owner // (2 * NZ)) ^ my_y
    late = slot // (NBD // 2)
    at_y = place_of(flip_y, jnp.where(late == 0, 1, 3))
    at_z = place_of(flip_z, jnp.where(late == 0, 1, 3))
    near = owner % 2 == core
    rows = jnp.where(near, at_z * 4 + at_y, 128 // 4 + at_y * 4 + at_z)
    rows = (rows * 4 + late * 64 + slot % 4).astype(jnp.int32)
    log_table = (jnp.log(sample_counts.astype(jnp.float32)) * LOG2E).reshape(
        total_blocks, TP * 2, ROWS
    )
    my_log = lax.dynamic_index_in_dim(log_table, rank * 2 + core, 1, keepdims=False)
    lq = my_log[home].reshape(2 * qblocks, 1, COLS)

    bf16 = jnp.bfloat16
    theirs, their_stat = attend(
        first_kernel,
        (rows[:qblocks].reshape(-1), rank_id),
        other_query,
        lq[:qblocks],
        pieces,
        (),
        (
            jax.ShapeDtypeStruct((qblocks * BLK, E), bf16),
            jax.ShapeDtypeStruct((qblocks, 8, BLK), jnp.float32),
        ),
        (
            pl.BlockSpec((BLK, E), lambda i, *_: (i, 0)),
            pl.BlockSpec((1, 8, BLK), lambda i, *_: (i, 0, 0)),
        ),
        [],
        "attend_other",
    )
    from_other = send(theirs, c=1)
    from_other_stat = send(their_stat, c=1)
    shares = attend(
        second_kernel,
        (rows[qblocks:].reshape(-1), rank_id),
        query,
        lq[qblocks:],
        pieces,
        (from_other, from_other_stat, pos_part),
        (jax.ShapeDtypeStruct((qblocks, BLK + EXTRA, 128), bf16),) * TP,
        (pl.BlockSpec((1, BLK + EXTRA, 128), lambda i, *_: (i, 0, 0)),) * TP,
        [pltpu.VMEM((TP, BLK, 128), bf16)],
        "attend_own",
    )
    parts = [shares[0]] + [send_x(shares[d], d) for d in (1, 2, 3)]
    loss, grad = last(parts, positive_emb)
    return loss.reshape(-1), grad


def solution(mesh):
    placed = (
        P("cat", "tp"),
        P("cat", "tp"),
        P("cat", "tp"),
        P("tp", None),
        P("cat", None),
        P(),
        P(),
    )
    return jax.shard_map(
        local, mesh=mesh, in_specs=placed, out_specs=(P("cat"), P("cat", "tp")), check_vma=False
    )
```

time: 168 us -> 165 us (0.982)
  between operations: 14.4 us -> 1.07 us
  local copies, waits for them, and re-layouts: 18.8 us -> 8.32 us
  other arithmetic: 1.87 us -> 9.29 us
  starting transfers between devices: 45.6 us -> 53 us
  Pallas kernels: 25.8 us -> 30 us
  waiting for transfers between devices: 60.1 us -> 62.6 us
    all_gather x1 -> x0, waiting for transfers between devices: 13.8 us -> none  [local(): query = lax.all_gather(query_emb, 'tp')]
    ppermute x19 -> x26, starting transfers between devices: 27.5 us -> 35.8 us  [send(): return lax.ppermute(value, 'cat', cat_perm(y, z, c))]
    ppermute x12, waiting for transfers between devices: 28.6 us -> 36.8 us  [send_x(): return lax.ppermute(value, 'tp', [(i, (i + d) % TP) for i in range(TP)])]
    ppermute x19 -> x26, waiting for transfers between devices: 17.7 us -> 25.8 us  [send(): return lax.ppermute(value, 'cat', cat_perm(y, z, c))]
    slice x4 -> x2, local copies, waits for them, and re-layouts: 7.62 us -> 0.04 us  [spread(): held = [near[:NBD // 2], near[NBD // 2:], far[:NBD // 2], far[NBD // 2:]]]
    concatenate x3 -> x9, other arithmetic: 1.24 us -> 6.83 us  [the longest x8 6.82 us: spread(): held = [jnp.concatenate([h, g]) for h, g in zip(held, got)]]
    pallas_call x2, Pallas kernels: 22.3 us -> 26 us  [attend(): pl.pallas_call(body, grid_spec=pltpu.PrefetchScalarGridSpec(num_scalar_pr...]
    unnamed x26 -> x30, local copies, waits for them, and re-layouts: 4.77 us -> 3.98 us
  transfers between devices with their start and end apart: 32 -> 38, of which waited for: 15 -> 19; matrix products, arithmetic and copies ran while one was open for 9% -> 8% of each run, Pallas kernels for 0% -> 0%
where the time goes in v2:
time: 165 us; the launch traced here: 164 us
  waiting for transfers between devices  62.6 us (38%)
  starting transfers between devices  53 us (32%)
  Pallas kernels  30 us (18%)
  other arithmetic  9.29 us (6%)
  local copies, waits for them, and re-layouts  8.32 us (5%)
    ppermute x12, waiting for transfers between devices, send_x(): return lax.ppermute(value, 'tp', [(i, (i + d) % TP) for i in range(TP)])  36.8 us
    ppermute x26, starting transfers between devices, send(): return lax.ppermute(value, 'cat', cat_perm(y, z, c))  35.8 us
    pallas_call x2, Pallas kernels, attend(): pl.pallas_call(body, grid_spec=pltpu.PrefetchScalarGridSpec(num_scalar_pr...  26 us
    ppermute x26, waiting for transfers between devices, send(): return lax.ppermute(value, 'cat', cat_perm(y, z, c))  25.8 us
    ppermute x12, starting transfers between devices, send_x(): return lax.ppermute(value, 'tp', [(i, (i + d) % TP) for i in range(TP)])  17.1 us
    concatenate x8, other arithmetic, spread(): held = [jnp.concatenate([h, g]) for h, g in zip(held, got)]  6.82 us
    unnamed x30, local copies, waits for them, and re-layouts  3.98 us
  transfers between devices with their start and end apart: 38, of which 19 were waited for; matrix products, arithmetic and copies ran while one was open for 8% of the time, Pallas kernels for 0%

profile of v2, /device:TPU:0, one launch (start us, length us, event | category | flops | bytes accessed | tf_op | source)
XLA Modules:
  0.0 164.2 jit_solution(7528519641011414711)
XLA Ops:
  1.6 2.9 %collective-permute-start.6 = (bf16[128,512]{1,0:T(8,128)(2,1)S(1)}, bf16[128,512]{1,0:T(8,128)(2,1)S(1)}, u32[]{:S(2)}, u32[]{:S(2)}) collective-permute-start(bf16[128,512]{1,0:T(8,128)(2,1)S(1)} %constant_dynamic-slice_fusion.1.refs_4_), channel_id=1, source_target_pairs={{0,3},{1,0},{2,1},{3,2},{4,7},{5,4},{6,5},{7,6},{8,11},{9,8},{10,9... | collective-permute-start | bytes 393224 | tf_op jit(solution)/shard_map/ppermute | solution.py:46
  6.2 3.9 %collective-permute-done.6.refs_7_ = bf16[128,512]{1,0:T(8,128)(2,1)S(1)} collective-permute-done((bf16[128,512]{1,0:T(8,128)(2,1)S(1)}, bf16[128,512]{1,0:T(8,128)(2,1)S(1)}, u32[]{:S(2)}, u32[]{:S(2)}) %collective-permute-start.6) | collective-permute-done | bytes 131104 | tf_op jit(solution)/shard_map/ppermute | solution.py:46
  10.1 2.3 %collective-permute-done.5.refs_6_ = bf16[128,512]{1,0:T(8,128)(2,1)S(1)} collective-permute-done((bf16[128,512]{1,0:T(8,128)(2,1)S(1)}, bf16[128,512]{1,0:T(8,128)(2,1)S(1)}, u32[]{:S(2)}, u32[]{:S(2)}) %collective-permute-start.5) | collective-permute-done | bytes 131104 | tf_op jit(solution)/shard_map/ppermute | solution.py:46
  17.0 7.8 %collective-permute-done.2.refs_2_ = bf16[512,256]{1,0:T(8,128)(2,1)S(1)} collective-permute-done((bf16[512,256]{1,0:T(8,128)(2,1)S(1)}, bf16[512,256]{1,0:T(8,128)(2,1)S(1)}, u32[]{:S(2)}, u32[]{:S(2)}) %collective-permute-start.2) | collective-permute-done | bytes 262176 | tf_op jit(solution)/shard_map/ppermute | solution.py:46
  24.8 3.0 %collective-permute-done.3.refs_3_ = bf16[512,256]{1,0:T(8,128)(2,1)S(1)} collective-permute-done((bf16[512,256]{1,0:T(8,128)(2,1)S(1)}, bf16[512,256]{1,0:T(8,128)(2,1)S(1)}, u32[]{:S(2)}, u32[]{:S(2)}) %collective-permute-start.3) | collective-permute-done | bytes 262176 | tf_op jit(solution)/shard_map/ppermute | solution.py:46
  37.3 3.1 %collective-permute-start.9 = (bf16[8,32,512]{2,1,0:T(8,128)(2,1)S(1)}, bf16[8,32,512]{2,1,0:T(8,128)(2,1)S(1)}, u32[]{:S(2)}, u32[]{:S(2)}) collective-permute-start(bf16[8,32,512]{2,1,0:T(8,128)(2,1)S(1)} %pad_maximum_fusion.6), channel_id=1, source_target_pairs={{0,96},{4,100},{8,104},{12,108},{16,112},{20,116},{24,120},{28,124... | collective-permute-start | bytes 786440 | tf_op jit(solution)/shard_map/ppermute | solution.py:42
  40.5 4.1 %collective-permute-start.27 = (bf16[4,32,512]{2,1,0:T(8,128)(2,1)S(1)}, bf16[4,32,512]{2,1,0:T(8,128)(2,1)S(1)}, u32[]{:S(2)}, u32[]{:S(2)}) collective-permute-start(bf16[4,32,512]{2,1,0:T(8,128)(2,1)S(1)} %get-tuple-element.30), channel_id=1, source_target_pairs={{0,24},{4,28},{8,16},{12,20},{16,8},{20,12},{24,0},{28,4},{32,56},... | collective-permute-start | bytes 393224 | tf_op jit(solution)/shard_map/ppermute | solution.py:42
  51.5 2.5 %collective-permute-start.23 = (bf16[8,32,512]{2,1,0:T(8,128)(2,1)}, bf16[8,32,512]{2,1,0:T(8,128)(2,1)}, u32[]{:S(2)}, u32[]{:S(2)}) collective-permute-start(bf16[8,32,512]{2,1,0:T(8,128)(2,1)} %pad_maximum_fusion.8), channel_id=1, source_target_pairs={{0,24},{4,28},{8,16},{12,20},{16,8},{20,12},{24,0},{28,4},{32,56},... | collective-permute-start | bytes 786440 | tf_op jit(solution)/shard_map/ppermute | solution.py:42
  59.0 3.2 %collective-permute-start.18 = (bf16[16,32,512]{2,1,0:T(8,128)(2,1)S(1)}, bf16[16,32,512]{2,1,0:T(8,128)(2,1)}, u32[]{:S(2)}, u32[]{:S(2)}) collective-permute-start(bf16[16,32,512]{2,1,0:T(8,128)(2,1)S(1)} %pad_maximum_fusion.3.refs_4_), channel_id=1, source_target_pairs={{0,24},{4,28},{8,16},{12,20},{16,8},{20,12},{24,0},{28,4},{32,56},... | collective-permute-start | bytes 1572872 | tf_op jit(solution)/shard_map/ppermute | solution.py:42
  68.0 3.3 %collective-permute-done.10 = bf16[1024,128]{1,0:T(8,128)(2,1)S(1)} collective-permute-done((bf16[1024,128]{1,0:T(8,128)(2,1)S(1)}, bf16[1024,128]{1,0:T(8,128)(2,1)S(1)}, u32[]{:S(2)}, u32[]{:S(2)}) %collective-permute-start.10) | collective-permute-done | bytes 262176 | tf_op jit(solution)/shard_map/ppermute | solution.py:46
  71.3 2.9 %collective-permute-start.25 = (bf16[16,32,512]{2,1,0:T(8,128)(2,1)}, bf16[16,32,512]{2,1,0:T(8,128)(2,1)}, u32[]{:S(2)}, u32[]{:S(2)}) collective-permute-start(bf16[16,32,512]{2,1,0:T(8,128)(2,1)} %pad_maximum_fusion.4.refs_8_), channel_id=1, source_target_pairs={{0,96},{4,100},{8,104},{12,108},{16,112},{20,116},{24,120},{28,124... | collective-permute-start | bytes 1572872 | tf_op jit(solution)/shard_map/ppermute | solution.py:42
  77.5 4.8 %collective-permute-done.19.refs_6_ = bf16[16,32,512]{2,1,0:T(8,128)(2,1)} collective-permute-done((bf16[16,32,512]{2,1,0:T(8,128)(2,1)S(1)}, bf16[16,32,512]{2,1,0:T(8,128)(2,1)}, u32[]{:S(2)}, u32[]{:S(2)}) %collective-permute-start.19) | collective-permute-done | bytes 524320 | tf_op jit(solution)/shard_map/ppermute | solution.py:42
  82.3 3.0 %collective-permute-start.29 = (bf16[16,32,512]{2,1,0:T(8,128)(2,1)}, bf16[16,32,512]{2,1,0:T(8,128)(2,1)}, u32[]{:S(2)}, u32[]{:S(2)}) collective-permute-start(bf16[16,32,512]{2,1,0:T(8,128)(2,1)} %pad_maximum_fusion.5.refs_12_), channel_id=1, source_target_pairs={{0,96},{4,100},{8,104},{12,108},{16,112},{20,116},{24,120},{28,124... | collective-permute-start | bytes 1572872 | tf_op jit(solution)/shard_map/ppermute | solution.py:42
  85.7 2.6 %collective-permute-start.15 = (bf16[16,32,512]{2,1,0:T(8,128)(2,1)}, bf16[16,32,512]{2,1,0:T(8,128)(2,1)S(1)}, u32[]{:S(2)}, u32[]{:S(2)}) collective-permute-start(bf16[16,32,512]{2,1,0:T(8,128)(2,1)} %collective-permute-done.13.refs_1_), channel_id=1, source_target_pairs={{0,24},{4,28},{8,16},{12,20},{16,8},{20,12},{24,0},{28,4},{32,56},... | collective-permute-start | bytes 1572872 | tf_op jit(solution)/shard_map/ppermute | solution.py:42
  88.3 2.3 %collective-permute-done.24.refs_9_ = bf16[16,32,512]{2,1,0:T(8,128)(2,1)} collective-permute-done((bf16[16,32,512]{2,1,0:T(8,128)(2,1)}, bf16[16,32,512]{2,1,0:T(8,128)(2,1)}, u32[]{:S(2)}, u32[]{:S(2)}) %collective-permute-start.24) | collective-permute-done | bytes 524320 | tf_op jit(solution)/shard_map/ppermute | solution.py:42
  91.6 5.9 %collective-permute-done.30.refs_14_ = bf16[16,32,512]{2,1,0:T(8,128)(2,1)} collective-permute-done((bf16[16,32,512]{2,1,0:T(8,128)(2,1)}, bf16[16,32,512]{2,1,0:T(8,128)(2,1)}, u32[]{:S(2)}, u32[]{:S(2)}) %collective-permute-start.30) | collective-permute-done | bytes 524320 | tf_op jit(solution)/shard_map/ppermute | solution.py:42
  97.6 2.3 %collective-permute-start.26 = (bf16[16,32,512]{2,1,0:T(8,128)(2,1)}, bf16[16,32,512]{2,1,0:T(8,128)(2,1)}, u32[]{:S(2)}, u32[]{:S(2)}) collective-permute-start(bf16[16,32,512]{2,1,0:T(8,128)(2,1)} %collective-permute-done.24.refs_9_), channel_id=1, source_target_pairs={{0,96},{4,100},{8,104},{12,108},{16,112},{20,116},{24,120},{28,124... | collective-permute-start | bytes 1572872 | tf_op jit(solution)/shard_map/ppermute | solution.py:42
  102.7 7.3 %collective-permute-done.26.refs_11_ = bf16[16,32,512]{2,1,0:T(8,128)(2,1)} collective-permute-done((bf16[16,32,512]{2,1,0:T(8,128)(2,1)}, bf16[16,32,512]{2,1,0:T(8,128)(2,1)}, u32[]{:S(2)}, u32[]{:S(2)}) %collective-permute-start.26) | collective-permute-done | bytes 524320 | tf_op jit(solution)/shard_map/ppermute | solution.py:42
  111.4 12.9 %attend_other.1 = (bf16[1024,512]{1,0:T(8,128)(2,1)}, f32[4,8,256]{2,1,0:T(8,128)}) custom-call(s32[256]{0:T(256)} %reshape.83.row_ref, s32[1]{0:T(128)} %bitcast.rank_ref, bf16[4,1024,128]{2,1,0:T(8,128)(2,1)} %collective-permute-done.32.q_ref, f32[4,1,2048]{2,1,0:T(1,128)} %slice.43.lq_ref, bf16[16,32,512]{2,1,0:T(8,128)(2,1)} %copy-done.6, ...), custom_call_target="tpu_custom_call" | custom-call | flops 4294967296 | bytes 12582912 | tf_op jit(solution)/shard_map/attend_other/pallas_call | solution.py:202
  128.2 13.1 %attend_own.1 = (bf16[4,288,128]{2,1,0:T(8,128)(2,1)}, bf16[4,288,128]{2,1,0:T(8,128)(2,1)}, bf16[4,288,128]{2,1,0:T(8,128)(2,1)}, bf16[4,288,128]{2,1,0:T(8,128)(2,1)}) custom-call(s32[256]{0:T(256)} %reshape.74.row_ref, s32[1]{0:T(128)} %bitcast.rank_ref, bf16[4,1024,128]{2,1,0:T(8,128)(2,1)} %copy-done.4, f32[4,1,2048]{2,1,0:T(1,128)} %slice.42.lq_ref, ...), custom_call_target="tpu_custom_call" | custom-call | flops 4294967296 | bytes 12582912 | tf_op jit(solution)/shard_map/attend_own/pallas_call | solution.py:202
  142.9 4.0 %collective-permute-start.36 = (bf16[4,288,128]{2,1,0:T(8,128)(2,1)}, bf16[4,288,128]{2,1,0:T(8,128)(2,1)S(1)}, u32[]{:S(2)}, u32[]{:S(2)}) collective-permute-start(bf16[4,288,128]{2,1,0:T(8,128)(2,1)} %get-tuple-element.20), channel_id=1, source_target_pairs={{0,2},{1,3},{2,0},{3,1},{4,6},{5,7},{6,4},{7,5},{8,10},{9,11},{10,... | collective-permute-start | bytes 884744 | tf_op jit(solution)/shard_map/ppermute | solution.py:46
  147.5 5.6 %collective-permute-done.35.refs_1_ = bf16[4,288,128]{2,1,0:T(8,128)(2,1)S(1)} collective-permute-done((bf16[4,288,128]{2,1,0:T(8,128)(2,1)}, bf16[4,288,128]{2,1,0:T(8,128)(2,1)S(1)}, u32[]{:S(2)}, u32[]{:S(2)}) %collective-permute-start.35) | collective-permute-done | bytes 294944 | tf_op jit(solution)/shard_map/ppermute | solution.py:46
  153.0 7.5 %collective-permute-done.36.refs_2_ = bf16[4,288,128]{2,1,0:T(8,128)(2,1)S(1)} collective-permute-done((bf16[4,288,128]{2,1,0:T(8,128)(2,1)}, bf16[4,288,128]{2,1,0:T(8,128)(2,1)S(1)}, u32[]{:S(2)}, u32[]{:S(2)}) %collective-permute-start.36) | collective-permute-done | bytes 294944 | tf_op jit(solution)/shard_map/ppermute | solution.py:46
  161.5 2.7 %last.1 = (f32[4,1,256]{2,1,0:T(1,128)}, bf16[1024,128]{1,0:T(8,128)(2,1)}) custom-call(bf16[4,288,128]{2,1,0:T(8,128)(2,1)S(1)} %copy-done.2, bf16[4,288,128]{2,1,0:T(8,128)(2,1)S(1)} %collective-permute-done.35.refs_1_, bf16[4,288,128]{2,1,0:T(8,128)(2,1)S(1)} %collective-permute-done.36.refs_2_, bf16[4,288,128]{2,1,0:T(8,128)(2,1)S(1)} %collective-permute-done.37.refs_3_, ...), custom_call_target="tpu_custom_call" | custom-call | tf_op jit(solution)/shard_map/last/pallas_call | solution.py:266
  (119 shorter events, 50.2 us)
Async XLA Ops:
  13.9 16.1 %collective-permute-start.7 = (bf16[4,128,512]{2,1,0:T(8,128)(2,1)S(1)}, bf16[4,128,512]{2,1,0:T(8,128)(2,1)S(1)}, u32[]{:S(2)}, u32[]{:S(2)}) collective-permute-start(bf16[4,128,512]{2,1,0:T(8,128)(2,1)S(1)} %pad_maximum_fusion.1), channel_id=1, source_target_pairs={{0,4},{4,0},{8,12},{12,8},{16,20},{20,16},{24,28},{28,24},{32,36},... | collective-permute-start | bytes 1572872 | tf_op jit(solution)/shard_map/ppermute | solution.py:42
  14.1 10.7 %collective-permute-start.2 = (bf16[512,256]{1,0:T(8,128)(2,1)S(1)}, bf16[512,256]{1,0:T(8,128)(2,1)S(1)}, u32[]{:S(2)}, u32[]{:S(2)}) collective-permute-start(bf16[512,256]{1,0:T(8,128)(2,1)S(1)} %bitcast.40), channel_id=1, source_target_pairs={{0,2},{1,3},{2,0},{3,1},{4,6},{5,7},{6,4},{7,5},{8,10},{9,11},{10,... | collective-permute-start | bytes 786440 | tf_op jit(solution)/shard_map/ppermute | solution.py:46
  15.0 12.9 %collective-permute-start.3 = (bf16[512,256]{1,0:T(8,128)(2,1)S(1)}, bf16[512,256]{1,0:T(8,128)(2,1)S(1)}, u32[]{:S(2)}, u32[]{:S(2)}) collective-permute-start(bf16[512,256]{1,0:T(8,128)(2,1)S(1)} %bitcast.39), channel_id=1, source_target_pairs={{0,3},{1,0},{2,1},{3,2},{4,7},{5,4},{6,5},{7,6},{8,11},{9,8},{10,9... | collective-permute-start | bytes 786440 | tf_op jit(solution)/shard_map/ppermute | solution.py:46
  16.1 13.8 %collective-permute-start.1 = (bf16[512,256]{1,0:T(8,128)(2,1)S(1)}, bf16[512,256]{1,0:T(8,128)(2,1)S(1)}, u32[]{:S(2)}, u32[]{:S(2)}) collective-permute-start(bf16[512,256]{1,0:T(8,128)(2,1)S(1)} %bitcast.38), channel_id=1, source_target_pairs={{0,1},{1,2},{2,3},{3,0},{4,5},{5,6},{6,7},{7,4},{8,9},{9,10},{10,1... | collective-permute-start | bytes 786440 | tf_op jit(solution)/shard_map/ppermute | solution.py:46
  33.0 11.6 %collective-permute-start.16 = (bf16[4,32,512]{2,1,0:T(8,128)(2,1)S(1)}, bf16[4,32,512]{2,1,0:T(8,128)(2,1)S(1)}, u32[]{:S(2)}, u32[]{:S(2)}) collective-permute-start(bf16[4,32,512]{2,1,0:T(8,128)(2,1)S(1)} %get-tuple-element.32), channel_id=1, source_target_pairs={{0,96},{4,100},{8,104},{12,108},{16,112},{20,116},{24,120},{28,124... | collective-permute-start | bytes 393224 | tf_op jit(solution)/shard_map/ppermute | solution.py:42
  46.7 10.2 %collective-permute-start.12 = (bf16[1024,128]{1,0:T(8,128)(2,1)S(1)}, bf16[1024,128]{1,0:T(8,128)(2,1)}, u32[]{:S(2)}, u32[]{:S(2)}) collective-permute-start(bf16[1024,128]{1,0:T(8,128)(2,1)S(1)} %copy-done.5), channel_id=1, source_target_pairs={{0,3},{1,0},{2,1},{3,2},{4,7},{5,4},{6,5},{7,6},{8,11},{9,8},{10,9... | collective-permute-start | bytes 786440 | tf_op jit(solution)/shard_map/ppermute | solution.py:46
  47.4 10.7 %collective-permute-start.11 = (bf16[1024,128]{1,0:T(8,128)(2,1)S(1)}, bf16[1024,128]{1,0:T(8,128)(2,1)}, u32[]{:S(2)}, u32[]{:S(2)}) collective-permute-start(bf16[1024,128]{1,0:T(8,128)(2,1)S(1)} %copy-done.5), channel_id=1, source_target_pairs={{0,2},{1,3},{2,0},{3,1},{4,6},{5,7},{6,4},{7,5},{8,10},{9,11},{10,... | collective-permute-start | bytes 786440 | tf_op jit(solution)/shard_map/ppermute | solution.py:46
  51.5 10.8 %collective-permute-start.23 = (bf16[8,32,512]{2,1,0:T(8,128)(2,1)}, bf16[8,32,512]{2,1,0:T(8,128)(2,1)}, u32[]{:S(2)}, u32[]{:S(2)}) collective-permute-start(bf16[8,32,512]{2,1,0:T(8,128)(2,1)} %pad_maximum_fusion.8), channel_id=1, source_target_pairs={{0,24},{4,28},{8,16},{12,20},{16,8},{20,12},{24,0},{28,4},{32,56},... | collective-permute-start | bytes 786440 | tf_op jit(solution)/shard_map/ppermute | solution.py:42
  56.2 19.1 %collective-permute-start.14 = (bf16[16,32,512]{2,1,0:T(8,128)(2,1)S(1)}, bf16[16,32,512]{2,1,0:T(8,128)(2,1)}, u32[]{:S(2)}, u32[]{:S(2)}) collective-permute-start(bf16[16,32,512]{2,1,0:T(8,128)(2,1)S(1)} %pad_maximum_fusion.2.refs_0_), channel_id=1, source_target_pairs={{0,24},{4,28},{8,16},{12,20},{16,8},{20,12},{24,0},{28,4},{32,56},... | collective-permute-start | bytes 1572872 | tf_op jit(solution)/shard_map/ppermute | solution.py:42
  56.9 18.5 %collective-permute-start.13 = (bf16[16,32,512]{2,1,0:T(8,128)(2,1)S(1)}, bf16[16,32,512]{2,1,0:T(8,128)(2,1)}, u32[]{:S(2)}, u32[]{:S(2)}) collective-permute-start(bf16[16,32,512]{2,1,0:T(8,128)(2,1)S(1)} %pad_maximum_fusion.2.refs_0_), channel_id=1, source_target_pairs={{0,8},{4,12},{8,0},{12,4},{16,24},{20,28},{24,16},{28,20},{32,40},... | collective-permute-start | bytes 1572872 | tf_op jit(solution)/shard_map/ppermute | solution.py:42
  58.0 24.2 %collective-permute-start.19 = (bf16[16,32,512]{2,1,0:T(8,128)(2,1)S(1)}, bf16[16,32,512]{2,1,0:T(8,128)(2,1)}, u32[]{:S(2)}, u32[]{:S(2)}) collective-permute-start(bf16[16,32,512]{2,1,0:T(8,128)(2,1)S(1)} %pad_maximum_fusion.3.refs_4_), channel_id=1, source_target_pairs={{0,8},{4,12},{8,0},{12,4},{16,24},{20,28},{24,16},{28,20},{32,40},... | collective-permute-start | bytes 1572872 | tf_op jit(solution)/shard_map/ppermute | solution.py:42
  59.0 26.3 %collective-permute-start.18 = (bf16[16,32,512]{2,1,0:T(8,128)(2,1)S(1)}, bf16[16,32,512]{2,1,0:T(8,128)(2,1)}, u32[]{:S(2)}, u32[]{:S(2)}) collective-permute-start(bf16[16,32,512]{2,1,0:T(8,128)(2,1)S(1)} %pad_maximum_fusion.3.refs_4_), channel_id=1, source_target_pairs={{0,24},{4,28},{8,16},{12,20},{16,8},{20,12},{24,0},{28,4},{32,56},... | collective-permute-start | bytes 1572872 | tf_op jit(solution)/shard_map/ppermute | solution.py:42
  71.3 14.4 %collective-permute-start.25 = (bf16[16,32,512]{2,1,0:T(8,128)(2,1)}, bf16[16,32,512]{2,1,0:T(8,128)(2,1)}, u32[]{:S(2)}, u32[]{:S(2)}) collective-permute-start(bf16[16,32,512]{2,1,0:T(8,128)(2,1)} %pad_maximum_fusion.4.refs_8_), channel_id=1, source_target_pairs={{0,96},{4,100},{8,104},{12,108},{16,112},{20,116},{24,120},{28,124... | collective-permute-start | bytes 1572872 | tf_op jit(solution)/shard_map/ppermute | solution.py:42
  75.4 15.3 %collective-permute-start.24 = (bf16[16,32,512]{2,1,0:T(8,128)(2,1)}, bf16[16,32,512]{2,1,0:T(8,128)(2,1)}, u32[]{:S(2)}, u32[]{:S(2)}) collective-permute-start(bf16[16,32,512]{2,1,0:T(8,128)(2,1)} %pad_maximum_fusion.4.refs_8_), channel_id=1, source_target_pairs={{0,32},{4,36},{8,40},{12,44},{16,48},{20,52},{24,56},{28,60},{32,0... | collective-permute-start | bytes 1572872 | tf_op jit(solution)/shard_map/ppermute | solution.py:42
  75.5 22.1 %collective-permute-start.30 = (bf16[16,32,512]{2,1,0:T(8,128)(2,1)}, bf16[16,32,512]{2,1,0:T(8,128)(2,1)}, u32[]{:S(2)}, u32[]{:S(2)}) collective-permute-start(bf16[16,32,512]{2,1,0:T(8,128)(2,1)} %pad_maximum_fusion.5.refs_12_), channel_id=1, source_target_pairs={{0,32},{4,36},{8,40},{12,44},{16,48},{20,52},{24,56},{28,60},{32,0... | collective-permute-start | bytes 1572872 | tf_op jit(solution)/shard_map/ppermute | solution.py:42
  82.3 17.5 %collective-permute-start.29 = (bf16[16,32,512]{2,1,0:T(8,128)(2,1)}, bf16[16,32,512]{2,1,0:T(8,128)(2,1)}, u32[]{:S(2)}, u32[]{:S(2)}) collective-permute-start(bf16[16,32,512]{2,1,0:T(8,128)(2,1)} %pad_maximum_fusion.5.refs_12_), channel_id=1, source_target_pairs={{0,96},{4,100},{8,104},{12,108},{16,112},{20,116},{24,120},{28,124... | collective-permute-start | bytes 1572872 | tf_op jit(solution)/shard_map/ppermute | solution.py:42
  85.2 17.4 %collective-permute-start.32 = (bf16[4,1024,128]{2,1,0:T(8,128)(2,1)S(1)}, bf16[4,1024,128]{2,1,0:T(8,128)(2,1)}, u32[]{:S(2)}, u32[]{:S(2)}) collective-permute-start(bf16[4,1024,128]{2,1,0:T(8,128)(2,1)S(1)} %pad_maximum_fusion.q_ref), channel_id=1, source_target_pairs={{0,4},{4,0},{8,12},{12,8},{16,20},{20,16},{24,28},{28,24},{32,36},... | collective-permute-start | bytes 3145736 | tf_op jit(solution)/shard_map/ppermute | solution.py:42
  85.7 16.6 %collective-permute-start.15 = (bf16[16,32,512]{2,1,0:T(8,128)(2,1)}, bf16[16,32,512]{2,1,0:T(8,128)(2,1)S(1)}, u32[]{:S(2)}, u32[]{:S(2)}) collective-permute-start(bf16[16,32,512]{2,1,0:T(8,128)(2,1)} %collective-permute-done.13.refs_1_), channel_id=1, source_target_pairs={{0,24},{4,28},{8,16},{12,20},{16,8},{20,12},{24,0},{28,4},{32,56},... | collective-permute-start | bytes 1572872 | tf_op jit(solution)/shard_map/ppermute | solution.py:42
  90.6 12.1 %collective-permute-start.20 = (bf16[16,32,512]{2,1,0:T(8,128)(2,1)}, bf16[16,32,512]{2,1,0:T(8,128)(2,1)}, u32[]{:S(2)}, u32[]{:S(2)}) collective-permute-start(bf16[16,32,512]{2,1,0:T(8,128)(2,1)} %collective-permute-done.18.refs_5_), channel_id=1, source_target_pairs={{0,8},{4,12},{8,0},{12,4},{16,24},{20,28},{24,16},{28,20},{32,40},... | collective-permute-start | bytes 1572872 | tf_op jit(solution)/shard_map/ppermute | solution.py:42
  97.6 12.4 %collective-permute-start.26 = (bf16[16,32,512]{2,1,0:T(8,128)(2,1)}, bf16[16,32,512]{2,1,0:T(8,128)(2,1)}, u32[]{:S(2)}, u32[]{:S(2)}) collective-permute-start(bf16[16,32,512]{2,1,0:T(8,128)(2,1)} %collective-permute-done.24.refs_9_), channel_id=1, source_target_pairs={{0,96},{4,100},{8,104},{12,108},{16,112},{20,116},{24,120},{28,124... | collective-permute-start | bytes 1572872 | tf_op jit(solution)/shard_map/ppermute | solution.py:42
  99.8 11.6 %collective-permute-start.31 = (bf16[16,32,512]{2,1,0:T(8,128)(2,1)}, bf16[16,32,512]{2,1,0:T(8,128)(2,1)}, u32[]{:S(2)}, u32[]{:S(2)}) collective-permute-start(bf16[16,32,512]{2,1,0:T(8,128)(2,1)} %collective-permute-done.29.refs_13_), channel_id=1, source_target_pairs={{0,32},{4,36},{8,40},{12,44},{16,48},{20,52},{24,56},{28,60},{32,0... | collective-permute-start | bytes 1572872 | tf_op jit(solution)/shard_map/ppermute | solution.py:42
  141.3 11.7 %collective-permute-start.35 = (bf16[4,288,128]{2,1,0:T(8,128)(2,1)}, bf16[4,288,128]{2,1,0:T(8,128)(2,1)S(1)}, u32[]{:S(2)}, u32[]{:S(2)}) collective-permute-start(bf16[4,288,128]{2,1,0:T(8,128)(2,1)} %get-tuple-element.19), channel_id=1, source_target_pairs={{0,1},{1,2},{2,3},{3,0},{4,5},{5,6},{6,7},{7,4},{8,9},{9,10},{10,1... | collective-permute-start | bytes 884744 | tf_op jit(solution)/shard_map/ppermute | solution.py:46
  142.9 17.6 %collective-permute-start.36 = (bf16[4,288,128]{2,1,0:T(8,128)(2,1)}, bf16[4,288,128]{2,1,0:T(8,128)(2,1)S(1)}, u32[]{:S(2)}, u32[]{:S(2)}) collective-permute-start(bf16[4,288,128]{2,1,0:T(8,128)(2,1)} %get-tuple-element.20), channel_id=1, source_target_pairs={{0,2},{1,3},{2,0},{3,1},{4,6},{5,7},{6,4},{7,5},{8,10},{9,11},{10,... | collective-permute-start | bytes 884744 | tf_op jit(solution)/shard_map/ppermute | solution.py:46
  146.8 13.7 %collective-permute-start.37 = (bf16[4,288,128]{2,1,0:T(8,128)(2,1)}, bf16[4,288,128]{2,1,0:T(8,128)(2,1)S(1)}, u32[]{:S(2)}, u32[]{:S(2)}) collective-permute-start(bf16[4,288,128]{2,1,0:T(8,128)(2,1)} %get-tuple-element.21), channel_id=1, source_target_pairs={{0,3},{1,0},{2,1},{3,2},{4,7},{5,4},{6,5},{7,6},{8,11},{9,8},{10,9... | collective-permute-start | bytes 884744 | tf_op jit(solution)/shard_map/ppermute | solution.py:46
  (29 other events, 201.1 us)

commit v3 on v2

--- a/solution.py
+++ b/solution.py
@@ -49,7 +49,7 @@
 def tower_kernel(core_ref, *refs):
     hidden = refs[0:4]
     mine, theirs = refs[4:8], refs[8]
-    keep_ref, give_ref, scratch = refs[9:]
+    out_ref = refs[9]
     core = core_ref[0]
     half = HID // TP // 2
     acc = jnp.zeros((NBD * 2 * ROWS, E), jnp.float32)
@@ -58,20 +58,16 @@
         high = jnp.where(core == 0, theirs[d], mine[d][...])
         acc += jnp.dot(hidden[d][:, :half], low, preferred_element_type=jnp.float32)
         acc += jnp.dot(hidden[d][:, half:], high, preferred_element_type=jnp.float32)
-    scratch[...] = acc.astype(jnp.bfloat16).reshape(scratch.shape)
-    keep_ref[...] = scratch[:, core]
-    give_ref[...] = scratch[:, 1 - core]
+    out_ref[...] = acc.astype(jnp.bfloat16).reshape(out_ref.shape)
 
 
 def tower(core, hidden, mine, theirs):
-    half = jax.ShapeDtypeStruct((NBD, ROWS, E), jnp.bfloat16)
     return pl.pallas_call(
         tower_kernel,
-        out_shape=(half, half),
+        out_shape=jax.ShapeDtypeStruct((2 * NBD, ROWS, E), jnp.bfloat16),
         in_specs=[pl.BlockSpec(memory_space=pltpu.SMEM)]
         + [pl.BlockSpec(memory_space=pltpu.VMEM)] * 9,
-        out_specs=(pl.BlockSpec(memory_space=pltpu.VMEM),) * 2,
-        scratch_shapes=[pltpu.VMEM((NBD, 2, ROWS, E), jnp.bfloat16)],
+        out_specs=pl.BlockSpec(memory_space=pltpu.VMEM),
         compiler_params=pltpu.CompilerParams(vmem_limit_bytes=40 << 20),
         cost_estimate=pl.CostEstimate(
             flops=2 * 512 * 1024 * 512, bytes_accessed=3 << 20, transcendentals=0
@@ -80,7 +76,7 @@
     )(core, *hidden, *mine, theirs)
 
 
-PIECES = 16
+PIECES = 8
 
 
 def one_block(rank, q_ref, lq_ref, row_ref, table, picked, scores, first):
@@ -285,18 +281,22 @@
 )
 
 
-def spread(near, far):
-    held = [near[: NBD // 2], near[NBD // 2 :], far[: NBD // 2], far[NBD // 2 :]]
-    for step in range(2):
+def together(*values):
+    return list(lax.optimization_barrier(tuple(values)))
+
+
+def spread(items, query):
+    held = [items[n * 4 : n * 4 + 4] for n in range(4)]
+    queries = [query]
+    for step in range(4):
         got = [send(h, **{st[step][0]: st[step][1]}) for h, st in zip(held, STREAMS)]
-        held = [jnp.concatenate([h, g]) for h, g in zip(held, got)]
-    third = [send(h, **{st[2][0]: st[2][1]}) for h, st in zip(held, STREAMS)]
-    fourth = [send(h, **{st[3][0]: st[3][1]}) for h, st in zip(held, STREAMS)]
-    fifth = [send(h, **{st[3][0]: st[3][1]}) for h, st in zip(third, STREAMS)]
-    pieces = []
-    for four in zip(held, third, fourth, fifth):
-        pieces += list(four)
-    return pieces, held[0]
+        if step == 3:
+            break
+        got = together(*got, send_x(query, step + 1), query)
+        queries.append(got[4])
+        query = got[5]
+        held = together(*[jnp.concatenate([h, g]) for h, g in zip(held, got)])
+    return held, got, jnp.stack(queries)
 
 
 def place_of(flipped, first):
@@ -312,23 +312,27 @@
     qblocks = neg_blocks.shape[0]
     total_blocks = block_home.shape[0]
 
-    hidden = item_hidden.reshape(NBD, TP, BLK // TP, -1)
+    core_id = core.reshape(1).astype(jnp.int32)
+    rank_id = rank.reshape(1).astype(jnp.int32)
+    hidden = item_hidden.reshape(NBD, TP, 2, ROWS, -1)
+    keep = lax.dynamic_index_in_dim(hidden, core, 2, keepdims=False)
+    give = lax.dynamic_index_in_dim(hidden, 1 - core, 2, keepdims=False)
+    half = lax.dynamic_slice_in_dim(item_weight, core * (HID // TP // 2), HID // TP // 2, 0)
+    swapped = send(give, c=1)
+    mine_w = [half] + [send_x(half, d) for d in (1, 2, 3)]
+    both = jnp.concatenate([keep, swapped])
 
     def piece(d):
-        cut = lax.dynamic_index_in_dim(hidden, (rank + d) % TP, 1, keepdims=False)
-        return cut.reshape(NBD * BLK // TP, -1)
-
-    core_id = core.reshape(1).astype(jnp.int32)
-    half = lax.dynamic_slice_in_dim(item_weight, core * (HID // TP // 2), HID // TP // 2, 0)
-    mine_w = [half] + [send_x(half, d) for d in (1, 2, 3)]
+        cut = lax.dynamic_index_in_dim(both, (rank + d) % TP, 1, keepdims=False)
+        return cut.reshape(2 * NBD * ROWS, -1)
+
+    hiddens = [piece(0)] + [send_x(piece(d), d) for d in (1, 2, 3)]
     theirs_w = send(jnp.stack(mine_w), c=1)
-    hiddens = [piece(0)] + [send_x(piece(d), d) for d in (1, 2, 3)]
-    keep, give = tower(core_id, hiddens, mine_w, theirs_w)
-    pieces, mark = spread(keep, send(give, c=1))
-
-    late_query, _ = lax.optimization_barrier((query_emb, mark))
-    rank_id = rank.reshape(1).astype(jnp.int32)
-    query = jnp.stack([late_query] + [send_x(late_query, d) for d in (1, 2, 3)])
+    items, late_query = together(tower(core_id, hiddens, mine_w, theirs_w), query_emb)
+    held, got, query = spread(items, late_query)
+    pieces = []
+    for pair in zip(held, got):
+        pieces += list(pair)
     other_query = send(query, c=1)
     pos_part = SCALE * jnp.sum(
         query_emb.astype(jnp.float32) * positive_emb.astype(jnp.float32), axis=1

time: 165 us -> 158 us (0.958)
  starting transfers between devices: 53 us -> 40.4 us
  other arithmetic: 9.29 us -> 13.3 us
    ppermute x26 -> x22, starting transfers between devices: 35.8 us -> 24.7 us  [send(): return lax.ppermute(value, 'cat', cat_perm(y, z, c))]
    unnamed x30 -> x26, local copies, waits for them, and re-layouts: 3.98 us -> 2.61 us
    ppermute x26 -> x22, waiting for transfers between devices: 25.8 us -> 26.8 us  [send(): return lax.ppermute(value, 'cat', cat_perm(y, z, c))]
    concatenate x8 -> x11, other arithmetic: 6.82 us -> 7.29 us  [the longest x10 7.19 us: spread(): held = together(*[jnp.concatenate([h, g]) for h, g in zip(held, got)])]
  transfers between devices with their start and end apart: 38 -> 34, of which waited for: 19 -> 19; matrix products, arithmetic and copies ran while one was open for 8% -> 7% of each run, Pallas kernels for 0% -> 0%
where the time goes in v3:
time: 158 us; the launch traced here: 157 us
  waiting for transfers between devices  63.4 us (40%)
  starting transfers between devices  40.4 us (26%)
  Pallas kernels  29.8 us (19%)
  other arithmetic  13.3 us (8%)
  local copies, waits for them, and re-layouts  9.3 us (6%)
    ppermute x12, waiting for transfers between devices, send_x(): return lax.ppermute(value, 'tp', [(i, (i + d) % TP) for i in range(TP)])  36.6 us
    ppermute x22, waiting for transfers between devices, send(): return lax.ppermute(value, 'cat', cat_perm(y, z, c))  26.8 us
    pallas_call x2, Pallas kernels, attend(): pl.pallas_call(body, grid_spec=pltpu.PrefetchScalarGridSpec(num_scalar_pr...  25.8 us
    ppermute x22, starting transfers between devices, send(): return lax.ppermute(value, 'cat', cat_perm(y, z, c))  24.7 us
    ppermute x12, starting transfers between devices, send_x(): return lax.ppermute(value, 'tp', [(i, (i + d) % TP) for i in range(TP)])  15.7 us
    concatenate x10, other arithmetic, spread(): held = together(*[jnp.concatenate([h, g]) for h, g in zip(held, got)])  7.19 us
  transfers between devices with their start and end apart: 34, of which 19 were waited for; matrix products, arithmetic and copies ran while one was open for 7% of the time, Pallas kernels for 0%

profile of v3, /device:TPU:0, one launch (start us, length us, event | category | flops | bytes accessed | tf_op | source)
XLA Modules:
  0.0 157.1 jit_solution(6694217514396420863)
XLA Ops:
  2.2 2.9 %collective-permute-start.7 = (bf16[128,512]{1,0:T(8,128)(2,1)S(1)}, bf16[128,512]{1,0:T(8,128)(2,1)S(1)}, u32[]{:S(2)}, u32[]{:S(2)}) collective-permute-start(bf16[128,512]{1,0:T(8,128)(2,1)S(1)} %constant_dynamic-slice_fusion.1.refs_4_), channel_id=1, source_target_pairs={{0,3},{1,0},{2,1},{3,2},{4,7},{5,4},{6,5},{7,6},{8,11},{9,8},{10,9... | collective-permute-start | bytes 393224 | tf_op jit(solution)/shard_map/ppermute | solution.py:46
  6.8 4.5 %collective-permute-done.7.refs_7_ = bf16[128,512]{1,0:T(8,128)(2,1)S(1)} collective-permute-done((bf16[128,512]{1,0:T(8,128)(2,1)S(1)}, bf16[128,512]{1,0:T(8,128)(2,1)S(1)}, u32[]{:S(2)}, u32[]{:S(2)}) %collective-permute-start.7) | collective-permute-done | bytes 131104 | tf_op jit(solution)/shard_map/ppermute | solution.py:46
  13.0 2.0 %collective-permute-done.5.refs_5_ = bf16[128,512]{1,0:T(8,128)(2,1)S(1)} collective-permute-done((bf16[128,512]{1,0:T(8,128)(2,1)S(1)}, bf16[128,512]{1,0:T(8,128)(2,1)S(1)}, u32[]{:S(2)}, u32[]{:S(2)}) %collective-permute-start.5) | collective-permute-done | bytes 131104 | tf_op jit(solution)/shard_map/ppermute | solution.py:46
  19.0 6.3 %collective-permute-done.4.refs_3_ = bf16[512,256]{1,0:T(8,128)(2,1)S(1)} collective-permute-done((bf16[512,256]{1,0:T(8,128)(2,1)S(1)}, bf16[512,256]{1,0:T(8,128)(2,1)S(1)}, u32[]{:S(2)}, u32[]{:S(2)}) %collective-permute-start.4) | collective-permute-done | bytes 262176 | tf_op jit(solution)/shard_map/ppermute | solution.py:46
  25.2 6.8 %collective-permute-done.2.refs_1_ = bf16[512,256]{1,0:T(8,128)(2,1)S(1)} collective-permute-done((bf16[512,256]{1,0:T(8,128)(2,1)S(1)}, bf16[512,256]{1,0:T(8,128)(2,1)S(1)}, u32[]{:S(2)}, u32[]{:S(2)}) %collective-permute-start.2) | collective-permute-done | bytes 262176 | tf_op jit(solution)/shard_map/ppermute | solution.py:46
  33.4 4.1 %collective-permute-start.12 = (bf16[4,32,512]{2,1,0:T(8,128)(2,1)S(1)}, bf16[4,32,512]{2,1,0:T(8,128)(2,1)S(1)}, u32[]{:S(2)}, u32[]{:S(2)}) collective-permute-start(bf16[4,32,512]{2,1,0:T(8,128)(2,1)S(1)} %get-tuple-element.86), channel_id=1, source_target_pairs={{0,24},{4,28},{8,16},{12,20},{16,8},{20,12},{24,0},{28,4},{32,56},... | collective-permute-start | bytes 393224 | tf_op jit(solution)/shard_map/ppermute | solution.py:42
  37.5 3.0 %collective-permute-start.10 = (bf16[4,32,512]{2,1,0:T(8,128)(2,1)S(1)}, bf16[4,32,512]{2,1,0:T(8,128)(2,1)S(1)}, u32[]{:S(2)}, u32[]{:S(2)}) collective-permute-start(bf16[4,32,512]{2,1,0:T(8,128)(2,1)S(1)} %get-tuple-element.88), channel_id=1, source_target_pairs={{0,96},{4,100},{8,104},{12,108},{16,112},{20,116},{24,120},{28,124... | collective-permute-start | bytes 393224 | tf_op jit(solution)/shard_map/ppermute | solution.py:42
  47.5 2.8 %collective-permute-start.16 = (bf16[8,32,512]{2,1,0:T(8,128)(2,1)S(1)}, bf16[8,32,512]{2,1,0:T(8,128)(2,1)S(1)}, u32[]{:S(2)}, u32[]{:S(2)}) collective-permute-start(bf16[8,32,512]{2,1,0:T(8,128)(2,1)S(1)} %get-tuple-element.50), channel_id=1, source_target_pairs={{0,24},{4,28},{8,16},{12,20},{16,8},{20,12},{24,0},{28,4},{32,56},... | collective-permute-start | bytes 786440 | tf_op jit(solution)/shard_map/ppermute | solution.py:42
  56.8 1.8 %collective-permute-done.18 = bf16[1024,128]{1,0:T(8,128)(2,1)} collective-permute-done((bf16[1024,128]{1,0:T(8,128)(2,1)}, bf16[1024,128]{1,0:T(8,128)(2,1)}, u32[]{:S(2)}, u32[]{:S(2)}) %collective-permute-start.18) | collective-permute-done | bytes 262176 | tf_op jit(solution)/shard_map/ppermute | solution.py:46
  58.8 2.5 %collective-permute-start.23 = (bf16[1024,128]{1,0:T(8,128)(2,1)}, bf16[1024,128]{1,0:T(8,128)(2,1)}, u32[]{:S(2)}, u32[]{:S(2)}) collective-permute-start(bf16[1024,128]{1,0:T(8,128)(2,1)} %param.7), channel_id=1, source_target_pairs={{0,3},{1,0},{2,1},{3,2},{4,7},{5,4},{6,5},{7,6},{8,11},{9,8},{10,9... | collective-permute-start | bytes 786440 | tf_op jit(solution)/shard_map/ppermute | solution.py:46
  61.8 3.7 %collective-permute-start.20 = (bf16[16,32,512]{2,1,0:T(8,128)(2,1)S(1)}, bf16[16,32,512]{2,1,0:T(8,128)(2,1)}, u32[]{:S(2)}, u32[]{:S(2)}) collective-permute-start(bf16[16,32,512]{2,1,0:T(8,128)(2,1)S(1)} %pad_maximum_fusion.7), channel_id=1, source_target_pairs={{0,24},{4,28},{8,16},{12,20},{16,8},{20,12},{24,0},{28,4},{32,56},... | collective-permute-start | bytes 1572872 | tf_op jit(solution)/shard_map/ppermute | solution.py:42
  65.5 2.3 %collective-permute-start.21 = (bf16[16,32,512]{2,1,0:T(8,128)(2,1)S(1)}, bf16[16,32,512]{2,1,0:T(8,128)(2,1)}, u32[]{:S(2)}, u32[]{:S(2)}) collective-permute-start(bf16[16,32,512]{2,1,0:T(8,128)(2,1)S(1)} %pad_maximum_fusion.8), channel_id=1, source_target_pairs={{0,32},{4,36},{8,40},{12,44},{16,48},{20,52},{24,56},{28,60},{32,0... | collective-permute-start | bytes 1572872 | tf_op jit(solution)/shard_map/ppermute | solution.py:42
  67.8 2.3 %collective-permute-start.22 = (bf16[16,32,512]{2,1,0:T(8,128)(2,1)S(1)}, bf16[16,32,512]{2,1,0:T(8,128)(2,1)}, u32[]{:S(2)}, u32[]{:S(2)}) collective-permute-start(bf16[16,32,512]{2,1,0:T(8,128)(2,1)S(1)} %pad_maximum_fusion.9), channel_id=1, source_target_pairs={{0,96},{4,100},{8,104},{12,108},{16,112},{20,116},{24,120},{28,124... | collective-permute-start | bytes 1572872 | tf_op jit(solution)/shard_map/ppermute | solution.py:42
  72.3 2.3 %collective-permute-done.20 = bf16[16,32,512]{2,1,0:T(8,128)(2,1)} collective-permute-done((bf16[16,32,512]{2,1,0:T(8,128)(2,1)S(1)}, bf16[16,32,512]{2,1,0:T(8,128)(2,1)}, u32[]{:S(2)}, u32[]{:S(2)}) %collective-permute-start.20) | collective-permute-done | bytes 524320 | tf_op jit(solution)/shard_map/ppermute | solution.py:42
  75.1 3.2 %collective-permute-done.22 = bf16[16,32,512]{2,1,0:T(8,128)(2,1)} collective-permute-done((bf16[16,32,512]{2,1,0:T(8,128)(2,1)S(1)}, bf16[16,32,512]{2,1,0:T(8,128)(2,1)}, u32[]{:S(2)}, u32[]{:S(2)}) %collective-permute-start.22) | collective-permute-done | bytes 524320 | tf_op jit(solution)/shard_map/ppermute | solution.py:42
  79.4 2.5 %pad_maximum_fusion.2.refs_2_ = bf16[32,32,512]{2,1,0:T(8,128)(2,1)} fusion(bf16[16,32,512]{2,1,0:T(8,128)(2,1)} %collective-permute-done.20, bf16[16,32,512]{2,1,0:T(8,128)(2,1)S(1)} %pad_maximum_fusion.7), kind=kLoop, calls=%fused_computation.11 | loop fusion | flops 524288 | bytes 2097152 | tf_op jit(solution)/shard_map/concatenate | solution.py:298
  81.9 2.1 %pad_maximum_fusion.3.refs_4_ = bf16[32,32,512]{2,1,0:T(8,128)(2,1)} fusion(bf16[16,32,512]{2,1,0:T(8,128)(2,1)} %collective-permute-done.21, bf16[16,32,512]{2,1,0:T(8,128)(2,1)S(1)} %pad_maximum_fusion.8), kind=kLoop, calls=%fused_computation.12 | loop fusion | flops 524288 | bytes 2097152 | tf_op jit(solution)/shard_map/concatenate | solution.py:298
  86.5 2.3 %collective-permute-start.26 = (bf16[32,32,512]{2,1,0:T(8,128)(2,1)}, bf16[32,32,512]{2,1,0:T(8,128)(2,1)}, u32[]{:S(2)}, u32[]{:S(2)}) collective-permute-start(bf16[32,32,512]{2,1,0:T(8,128)(2,1)} %pad_maximum_fusion.3.refs_4_), channel_id=1, source_target_pairs={{0,96},{4,100},{8,104},{12,108},{16,112},{20,116},{24,120},{28,124... | collective-permute-start | bytes 3145736 | tf_op jit(solution)/shard_map/ppermute | solution.py:42
  88.9 2.2 %pad_maximum_fusion.q_ref = bf16[4,1024,128]{2,1,0:T(8,128)(2,1)} fusion(bf16[1,1024,128]{2,1,0:T(8,128)(2,1)} %bitcast.16, bf16[1,1024,128]{2,1,0:T(8,128)(2,1)} %bitcast.15, bf16[1,1024,128]{2,1,0:T(8,128)(2,1)S(1)} %bitcast.40, bf16[1,1024,128]{2,1,0:T(8,128)(2,1)} %bitcast.13), kind=kLoop, calls=%fused_computation.9 | loop fusion | flops 1572864 | bytes 2097152 | tf_op jit(solution)/shard_map/stack | solution.py:299
  94.0 10.2 %collective-permute-done.24.refs_1_ = bf16[32,32,512]{2,1,0:T(8,128)(2,1)} collective-permute-done((bf16[32,32,512]{2,1,0:T(8,128)(2,1)S(1)}, bf16[32,32,512]{2,1,0:T(8,128)(2,1)}, u32[]{:S(2)}, u32[]{:S(2)}) %collective-permute-start.24) | collective-permute-done | bytes 1048608 | tf_op jit(solution)/shard_map/ppermute | solution.py:42
  105.4 12.8 %attend_other.1 = (bf16[1024,512]{1,0:T(8,128)(2,1)}, f32[4,8,256]{2,1,0:T(8,128)}) custom-call(s32[256]{0:T(256)} %reshape.83.row_ref, s32[1]{0:T(128)} %bitcast.rank_ref, bf16[4,1024,128]{2,1,0:T(8,128)(2,1)} %collective-permute-done.28.q_ref, f32[4,1,2048]{2,1,0:T(1,128)} %slice.43.lq_ref, bf16[32,32,512]{2,1,0:T(8,128)(2,1)} %copy-done.3, ...), custom_call_target="tpu_custom_call" | custom-call | flops 4294967296 | bytes 12582912 | tf_op jit(solution)/shard_map/attend_other/pallas_call | solution.py:198
  123.0 13.0 %attend_own.1 = (bf16[4,288,128]{2,1,0:T(8,128)(2,1)}, bf16[4,288,128]{2,1,0:T(8,128)(2,1)}, bf16[4,288,128]{2,1,0:T(8,128)(2,1)}, bf16[4,288,128]{2,1,0:T(8,128)(2,1)}) custom-call(s32[256]{0:T(256)} %reshape.74.row_ref, s32[1]{0:T(128)} %bitcast.rank_ref, bf16[4,1024,128]{2,1,0:T(8,128)(2,1)} %pad_maximum_fusion.q_ref, f32[4,1,2048]{2,1,0:T(1,128)} %slice.42.lq_ref, ...), custom_call_target="tpu_custom_call" | custom-call | flops 4294967296 | bytes 12582912 | tf_op jit(solution)/shard_map/attend_own/pallas_call | solution.py:198
  139.9 12.9 %collective-permute-done.31.refs_1_ = bf16[4,288,128]{2,1,0:T(8,128)(2,1)S(1)} collective-permute-done((bf16[4,288,128]{2,1,0:T(8,128)(2,1)}, bf16[4,288,128]{2,1,0:T(8,128)(2,1)S(1)}, u32[]{:S(2)}, u32[]{:S(2)}) %collective-permute-start.31) | collective-permute-done | bytes 294944 | tf_op jit(solution)/shard_map/ppermute | solution.py:46
  154.4 2.7 %last.1 = (f32[4,1,256]{2,1,0:T(1,128)}, bf16[1024,128]{1,0:T(8,128)(2,1)}) custom-call(bf16[4,288,128]{2,1,0:T(8,128)(2,1)S(1)} %copy-done.2, bf16[4,288,128]{2,1,0:T(8,128)(2,1)S(1)} %collective-permute-done.31.refs_1_, bf16[4,288,128]{2,1,0:T(8,128)(2,1)S(1)} %collective-permute-done.32.refs_2_, bf16[4,288,128]{2,1,0:T(8,128)(2,1)S(1)} %collective-permute-done.33.refs_3_, ...), custom_call_target="tpu_custom_call" | custom-call | tf_op jit(solution)/shard_map/last/pallas_call | solution.py:262
  (111 shorter events, 44.7 us)
Async XLA Ops:
  2.1 13.9 %collective-permute-start.1 = (bf16[8,4,32,256]{3,2,0,1:T(8,128)(2,1)S(1)}, bf16[8,4,32,256]{3,2,0,1:T(8,128)(2,1)S(1)}, u32[]{:S(2)}, u32[]{:S(2)}) collective-permute-start(bf16[8,4,32,256]{3,2,0,1:T(8,128)(2,1)S(1)} %bitcast.36), channel_id=1, source_target_pairs={{0,4},{4,0},{8,12},{12,8},{16,20},{20,16},{24,28},{28,24},{32,36},... | collective-permute-start | bytes 1572872 | tf_op jit(solution)/shard_map/ppermute | solution.py:42
  2.2 9.1 %collective-permute-start.7 = (bf16[128,512]{1,0:T(8,128)(2,1)S(1)}, bf16[128,512]{1,0:T(8,128)(2,1)S(1)}, u32[]{:S(2)}, u32[]{:S(2)}) collective-permute-start(bf16[128,512]{1,0:T(8,128)(2,1)S(1)} %constant_dynamic-slice_fusion.1.refs_4_), channel_id=1, source_target_pairs={{0,3},{1,0},{2,1},{3,2},{4,7},{5,4},{6,5},{7,6},{8,11},{9,8},{10,9... | collective-permute-start | bytes 393224 | tf_op jit(solution)/shard_map/ppermute | solution.py:46
  5.1 7.9 %collective-permute-start.6 = (bf16[128,512]{1,0:T(8,128)(2,1)S(1)}, bf16[128,512]{1,0:T(8,128)(2,1)S(1)}, u32[]{:S(2)}, u32[]{:S(2)}) collective-permute-start(bf16[128,512]{1,0:T(8,128)(2,1)S(1)} %constant_dynamic-slice_fusion.1.refs_4_), channel_id=1, source_target_pairs={{0,2},{1,3},{2,0},{3,1},{4,6},{5,7},{6,4},{7,5},{8,10},{9,11},{10,... | collective-permute-start | bytes 393224 | tf_op jit(solution)/shard_map/ppermute | solution.py:46
  5.9 9.1 %collective-permute-start.5 = (bf16[128,512]{1,0:T(8,128)(2,1)S(1)}, bf16[128,512]{1,0:T(8,128)(2,1)S(1)}, u32[]{:S(2)}, u32[]{:S(2)}) collective-permute-start(bf16[128,512]{1,0:T(8,128)(2,1)S(1)} %constant_dynamic-slice_fusion.1.refs_4_), channel_id=1, source_target_pairs={{0,1},{1,2},{2,3},{3,0},{4,5},{5,6},{6,7},{7,4},{8,9},{9,10},{10,1... | collective-permute-start | bytes 393224 | tf_op jit(solution)/shard_map/ppermute | solution.py:46
  16.1 9.2 %collective-permute-start.4 = (bf16[512,256]{1,0:T(8,128)(2,1)S(1)}, bf16[512,256]{1,0:T(8,128)(2,1)S(1)}, u32[]{:S(2)}, u32[]{:S(2)}) collective-permute-start(bf16[512,256]{1,0:T(8,128)(2,1)S(1)} %bitcast.39), channel_id=1, source_target_pairs={{0,3},{1,0},{2,1},{3,2},{4,7},{5,4},{6,5},{7,6},{8,11},{9,8},{10,9... | collective-permute-start | bytes 786440 | tf_op jit(solution)/shard_map/ppermute | solution.py:46
  16.7 15.3 %collective-permute-start.2 = (bf16[512,256]{1,0:T(8,128)(2,1)S(1)}, bf16[512,256]{1,0:T(8,128)(2,1)S(1)}, u32[]{:S(2)}, u32[]{:S(2)}) collective-permute-start(bf16[512,256]{1,0:T(8,128)(2,1)S(1)} %bitcast.38), channel_id=1, source_target_pairs={{0,1},{1,2},{2,3},{3,0},{4,5},{5,6},{6,7},{7,4},{8,9},{9,10},{10,1... | collective-permute-start | bytes 786440 | tf_op jit(solution)/shard_map/ppermute | solution.py:46
  18.2 13.8 %collective-permute-start.3 = (bf16[512,256]{1,0:T(8,128)(2,1)S(1)}, bf16[512,256]{1,0:T(8,128)(2,1)S(1)}, u32[]{:S(2)}, u32[]{:S(2)}) collective-permute-start(bf16[512,256]{1,0:T(8,128)(2,1)S(1)} %bitcast.37), channel_id=1, source_target_pairs={{0,2},{1,3},{2,0},{3,1},{4,6},{5,7},{6,4},{7,5},{8,10},{9,11},{10,... | collective-permute-start | bytes 786440 | tf_op jit(solution)/shard_map/ppermute | solution.py:46
  33.2 12.2 %collective-permute-start.13 = (bf16[1024,128]{1,0:T(8,128)(2,1)}, bf16[1024,128]{1,0:T(8,128)(2,1)S(1)}, u32[]{:S(2)}, u32[]{:S(2)}) collective-permute-start(bf16[1024,128]{1,0:T(8,128)(2,1)} %param.7), channel_id=1, source_target_pairs={{0,1},{1,2},{2,3},{3,0},{4,5},{5,6},{6,7},{7,4},{8,9},{9,10},{10,1... | collective-permute-start | bytes 786440 | tf_op jit(solution)/shard_map/ppermute | solution.py:46
  46.2 7.7 %collective-permute-start.14 = (bf16[8,32,512]{2,1,0:T(8,128)(2,1)S(1)}, bf16[8,32,512]{2,1,0:T(8,128)(2,1)S(1)}, u32[]{:S(2)}, u32[]{:S(2)}) collective-permute-start(bf16[8,32,512]{2,1,0:T(8,128)(2,1)S(1)} %get-tuple-element.48), channel_id=1, source_target_pairs={{0,96},{4,100},{8,104},{12,108},{16,112},{20,116},{24,120},{28,124... | collective-permute-start | bytes 786440 | tf_op jit(solution)/shard_map/ppermute | solution.py:42
  50.4 8.2 %collective-permute-start.18 = (bf16[1024,128]{1,0:T(8,128)(2,1)}, bf16[1024,128]{1,0:T(8,128)(2,1)}, u32[]{:S(2)}, u32[]{:S(2)}) collective-permute-start(bf16[1024,128]{1,0:T(8,128)(2,1)} %param.7), channel_id=1, source_target_pairs={{0,2},{1,3},{2,0},{3,1},{4,6},{5,7},{6,4},{7,5},{8,10},{9,11},{10,... | collective-permute-start | bytes 786440 | tf_op jit(solution)/shard_map/ppermute | solution.py:46
  53.9 13.9 %collective-permute-start = (s32[4,64]{1,0:T(4,128)S(1)}, s32[4,64]{1,0:T(4,128)S(1)}, u32[]{:S(2)}, u32[]{:S(2)}) collective-permute-start(s32[4,64]{1,0:T(4,128)S(1)} %copy-done.8), channel_id=1, source_target_pairs={{0,4},{4,0},{8,12},{12,8},{16,20},{20,16},{24,28},{28,24},{32,36},... | collective-permute-start | bytes 3080 | tf_op jit(solution)/shard_map/ppermute | solution.py:42
  58.8 13.4 %collective-permute-start.23 = (bf16[1024,128]{1,0:T(8,128)(2,1)}, bf16[1024,128]{1,0:T(8,128)(2,1)}, u32[]{:S(2)}, u32[]{:S(2)}) collective-permute-start(bf16[1024,128]{1,0:T(8,128)(2,1)} %param.7), channel_id=1, source_target_pairs={{0,3},{1,0},{2,1},{3,2},{4,7},{5,4},{6,5},{7,6},{8,11},{9,8},{10,9... | collective-permute-start | bytes 786440 | tf_op jit(solution)/shard_map/ppermute | solution.py:46
  61.3 11.0 %collective-permute-start.19 = (bf16[16,32,512]{2,1,0:T(8,128)(2,1)S(1)}, bf16[16,32,512]{2,1,0:T(8,128)(2,1)}, u32[]{:S(2)}, u32[]{:S(2)}) collective-permute-start(bf16[16,32,512]{2,1,0:T(8,128)(2,1)S(1)} %pad_maximum_fusion.6), channel_id=1, source_target_pairs={{0,8},{4,12},{8,0},{12,4},{16,24},{20,28},{24,16},{28,20},{32,40},... | collective-permute-start | bytes 1572872 | tf_op jit(solution)/shard_map/ppermute | solution.py:42
  61.8 12.8 %collective-permute-start.20 = (bf16[16,32,512]{2,1,0:T(8,128)(2,1)S(1)}, bf16[16,32,512]{2,1,0:T(8,128)(2,1)}, u32[]{:S(2)}, u32[]{:S(2)}) collective-permute-start(bf16[16,32,512]{2,1,0:T(8,128)(2,1)S(1)} %pad_maximum_fusion.7), channel_id=1, source_target_pairs={{0,24},{4,28},{8,16},{12,20},{16,8},{20,12},{24,0},{28,4},{32,56},... | collective-permute-start | bytes 1572872 | tf_op jit(solution)/shard_map/ppermute | solution.py:42
  65.5 9.6 %collective-permute-start.21 = (bf16[16,32,512]{2,1,0:T(8,128)(2,1)S(1)}, bf16[16,32,512]{2,1,0:T(8,128)(2,1)}, u32[]{:S(2)}, u32[]{:S(2)}) collective-permute-start(bf16[16,32,512]{2,1,0:T(8,128)(2,1)S(1)} %pad_maximum_fusion.8), channel_id=1, source_target_pairs={{0,32},{4,36},{8,40},{12,44},{16,48},{20,52},{24,56},{28,60},{32,0... | collective-permute-start | bytes 1572872 | tf_op jit(solution)/shard_map/ppermute | solution.py:42
  67.8 10.5 %collective-permute-start.22 = (bf16[16,32,512]{2,1,0:T(8,128)(2,1)S(1)}, bf16[16,32,512]{2,1,0:T(8,128)(2,1)}, u32[]{:S(2)}, u32[]{:S(2)}) collective-permute-start(bf16[16,32,512]{2,1,0:T(8,128)(2,1)S(1)} %pad_maximum_fusion.9), channel_id=1, source_target_pairs={{0,96},{4,100},{8,104},{12,108},{16,112},{20,116},{24,120},{28,124... | collective-permute-start | bytes 1572872 | tf_op jit(solution)/shard_map/ppermute | solution.py:42
  85.2 19.0 %collective-permute-start.24 = (bf16[32,32,512]{2,1,0:T(8,128)(2,1)S(1)}, bf16[32,32,512]{2,1,0:T(8,128)(2,1)}, u32[]{:S(2)}, u32[]{:S(2)}) collective-permute-start(bf16[32,32,512]{2,1,0:T(8,128)(2,1)S(1)} %pad_maximum_fusion.1.refs_0_), channel_id=1, source_target_pairs={{0,24},{4,28},{8,16},{12,20},{16,8},{20,12},{24,0},{28,4},{32,56},... | collective-permute-start | bytes 3145736 | tf_op jit(solution)/shard_map/ppermute | solution.py:42
  85.3 18.9 %collective-permute-start.25 = (bf16[32,32,512]{2,1,0:T(8,128)(2,1)}, bf16[32,32,512]{2,1,0:T(8,128)(2,1)}, u32[]{:S(2)}, u32[]{:S(2)}) collective-permute-start(bf16[32,32,512]{2,1,0:T(8,128)(2,1)} %pad_maximum_fusion.2.refs_2_), channel_id=1, source_target_pairs={{0,8},{4,12},{8,0},{12,4},{16,24},{20,28},{24,16},{28,20},{32,40},... | collective-permute-start | bytes 3145736 | tf_op jit(solution)/shard_map/ppermute | solution.py:42
  86.5 18.8 %collective-permute-start.26 = (bf16[32,32,512]{2,1,0:T(8,128)(2,1)}, bf16[32,32,512]{2,1,0:T(8,128)(2,1)}, u32[]{:S(2)}, u32[]{:S(2)}) collective-permute-start(bf16[32,32,512]{2,1,0:T(8,128)(2,1)} %pad_maximum_fusion.3.refs_4_), channel_id=1, source_target_pairs={{0,96},{4,100},{8,104},{12,108},{16,112},{20,116},{24,120},{28,124... | collective-permute-start | bytes 3145736 | tf_op jit(solution)/shard_map/ppermute | solution.py:42
  88.9 16.5 %collective-permute-start.27 = (bf16[32,32,512]{2,1,0:T(8,128)(2,1)S(1)}, bf16[32,32,512]{2,1,0:T(8,128)(2,1)}, u32[]{:S(2)}, u32[]{:S(2)}) collective-permute-start(bf16[32,32,512]{2,1,0:T(8,128)(2,1)S(1)} %pad_maximum_fusion.4.refs_6_), channel_id=1, source_target_pairs={{0,32},{4,36},{8,40},{12,44},{16,48},{20,52},{24,56},{28,60},{32,0... | collective-permute-start | bytes 3145736 | tf_op jit(solution)/shard_map/ppermute | solution.py:42
  91.1 14.2 %collective-permute-start.28 = (bf16[4,1024,128]{2,1,0:T(8,128)(2,1)}, bf16[4,1024,128]{2,1,0:T(8,128)(2,1)}, u32[]{:S(2)}, u32[]{:S(2)}) collective-permute-start(bf16[4,1024,128]{2,1,0:T(8,128)(2,1)} %pad_maximum_fusion.q_ref), channel_id=1, source_target_pairs={{0,4},{4,0},{8,12},{12,8},{16,20},{20,16},{24,28},{28,24},{32,36},... | collective-permute-start | bytes 3145736 | tf_op jit(solution)/shard_map/ppermute | solution.py:42
  136.0 16.8 %collective-permute-start.31 = (bf16[4,288,128]{2,1,0:T(8,128)(2,1)}, bf16[4,288,128]{2,1,0:T(8,128)(2,1)S(1)}, u32[]{:S(2)}, u32[]{:S(2)}) collective-permute-start(bf16[4,288,128]{2,1,0:T(8,128)(2,1)} %get-tuple-element.75), channel_id=1, source_target_pairs={{0,1},{1,2},{2,3},{3,0},{4,5},{5,6},{6,7},{7,4},{8,9},{9,10},{10,1... | collective-permute-start | bytes 884744 | tf_op jit(solution)/shard_map/ppermute | solution.py:46
  136.9 15.9 %collective-permute-start.32 = (bf16[4,288,128]{2,1,0:T(8,128)(2,1)}, bf16[4,288,128]{2,1,0:T(8,128)(2,1)S(1)}, u32[]{:S(2)}, u32[]{:S(2)}) collective-permute-start(bf16[4,288,128]{2,1,0:T(8,128)(2,1)} %get-tuple-element.76), channel_id=1, source_target_pairs={{0,2},{1,3},{2,0},{3,1},{4,6},{5,7},{6,4},{7,5},{8,10},{9,11},{10,... | collective-permute-start | bytes 884744 | tf_op jit(solution)/shard_map/ppermute | solution.py:46
  138.3 15.1 %collective-permute-start.33 = (bf16[4,288,128]{2,1,0:T(8,128)(2,1)}, bf16[4,288,128]{2,1,0:T(8,128)(2,1)S(1)}, u32[]{:S(2)}, u32[]{:S(2)}) collective-permute-start(bf16[4,288,128]{2,1,0:T(8,128)(2,1)} %get-tuple-element.77), channel_id=1, source_target_pairs={{0,3},{1,0},{2,1},{3,2},{4,7},{5,4},{6,5},{7,6},{8,11},{9,8},{10,9... | collective-permute-start | bytes 884744 | tf_op jit(solution)/shard_map/ppermute | solution.py:46
  (23 other events, 110.1 us)

commit v4 on v3

--- a/solution.py
+++ b/solution.py
@@ -217,7 +217,7 @@
         ),
         out_shape=outs,
         compiler_params=pltpu.CompilerParams(
-            dimension_semantics=("arbitrary",), vmem_limit_bytes=58 << 20
+            dimension_semantics=("arbitrary",), vmem_limit_bytes=24 << 20
         ),
         cost_estimate=pl.CostEstimate(
             flops=blocks * 4 * BLK * COLS * E,
@@ -327,8 +327,11 @@
         return cut.reshape(2 * NBD * ROWS, -1)
 
     hiddens = [piece(0)] + [send_x(piece(d), d) for d in (1, 2, 3)]
-    theirs_w = send(jnp.stack(mine_w), c=1)
-    items, late_query = together(tower(core_id, hiddens, mine_w, theirs_w), query_emb)
+    theirs_w = send(together(jnp.stack(mine_w), hiddens[1], hiddens[3])[0], c=1)
+    picks = jnp.concatenate([send(neg_blocks, c=1), neg_blocks])
+    items, late_query, picks = together(
+        tower(core_id, hiddens, mine_w, theirs_w), query_emb, picks
+    )
     held, got, query = spread(items, late_query)
     pieces = []
     for pair in zip(held, got):
@@ -338,7 +341,6 @@
         query_emb.astype(jnp.float32) * positive_emb.astype(jnp.float32), axis=1
     ).reshape(qblocks, 1, BLK)
 
-    picks = jnp.concatenate([send(neg_blocks, c=1), neg_blocks])
     matches = picks[:, :, None] == jnp.arange(total_blocks, dtype=jnp.int32)[None, None, :]
     home = jnp.sum(jnp.where(matches, block_home[None, None, :], 0), axis=2)
     slot, owner = home % NBD, home // NBD
@@ -356,12 +358,18 @@
     my_log = lax.dynamic_index_in_dim(log_table, rank * 2 + core, 1, keepdims=False)
     lq = my_log[home].reshape(2 * qblocks, 1, COLS)
 
+    first_rows, own_rows = rows[:qblocks].reshape(-1), rows[qblocks:].reshape(-1)
+    first_lq, own_lq = lq[:qblocks], lq[qblocks:]
+    pieces[-1], pos_part, first_rows, own_rows, first_lq, own_lq = together(
+        pieces[-1], pos_part, first_rows, own_rows, first_lq, own_lq
+    )
+
     bf16 = jnp.bfloat16
     theirs, their_stat = attend(
         first_kernel,
-        (rows[:qblocks].reshape(-1), rank_id),
+        (first_rows, rank_id),
         other_query,
-        lq[:qblocks],
+        first_lq,
         pieces,
         (),
         (
@@ -379,9 +387,9 @@
     from_other_stat = send(their_stat, c=1)
     shares = attend(
         second_kernel,
-        (rows[qblocks:].reshape(-1), rank_id),
+        (own_rows, rank_id),
         query,
-        lq[qblocks:],
+        own_lq,
         pieces,
         (from_other, from_other_stat, pos_part),
         (jax.ShapeDtypeStruct((qblocks, BLK + EXTRA, 128), bf16),) * TP,

time: 158 us -> 150 us (0.949)
  other arithmetic: 13.3 us -> 8.63 us
  local copies, waits for them, and re-layouts: 9.3 us -> 13.9 us
  Pallas kernels: 29.8 us -> 26 us
  starting transfers between devices: 40.4 us -> 36.7 us
    pallas_call x2, Pallas kernels: 25.8 us -> 22 us  [attend(): pl.pallas_call(body, grid_spec=pltpu.PrefetchScalarGridSpec(num_scalar_pr...]
    ppermute x22, starting transfers between devices: 24.7 us -> 21.9 us  [send(): return lax.ppermute(value, 'cat', cat_perm(y, z, c))]
    slice x4, local copies, waits for them, and re-layouts: 1.49 us -> 4.01 us  [the longest x3 4.01 us: local(): first_lq, own_lq = (lq[:qblocks], lq[qblocks:])]
  transfers between devices with their start and end apart: 34 -> 34, of which waited for: 19 -> 22; matrix products, arithmetic and copies ran while one was open for 7% -> 8% of each run, Pallas kernels for 0% -> 0%
where the time goes in v4:
time: 150 us; the launch traced here: 149 us
  waiting for transfers between devices  62.7 us (42%)
  starting transfers between devices  36.7 us (24%)
  Pallas kernels  26 us (17%)
  local copies, waits for them, and re-layouts  13.9 us (9%)
  other arithmetic  8.63 us (6%)
    ppermute x12, waiting for transfers between devices, send_x(): return lax.ppermute(value, 'tp', [(i, (i + d) % TP) for i in range(TP)])  37 us
    ppermute x22, waiting for transfers between devices, send(): return lax.ppermute(value, 'cat', cat_perm(y, z, c))  25.7 us
    pallas_call x2, Pallas kernels, attend(): pl.pallas_call(body, grid_spec=pltpu.PrefetchScalarGridSpec(num_scalar_pr...  22 us
    ppermute x22, starting transfers between devices, send(): return lax.ppermute(value, 'cat', cat_perm(y, z, c))  21.9 us
    ppermute x12, starting transfers between devices, send_x(): return lax.ppermute(value, 'tp', [(i, (i + d) % TP) for i in range(TP)])  14.8 us
    concatenate x10, other arithmetic, spread(): held = together(*[jnp.concatenate([h, g]) for h, g in zip(held, got)])  6.03 us
    slice x3, local copies, waits for them, and re-layouts, local(): first_lq, own_lq = (lq[:qblocks], lq[qblocks:])  4.01 us
  transfers between devices with their start and end apart: 34, of which 22 were waited for; matrix products, arithmetic and copies ran while one was open for 8% of the time, Pallas kernels for 0%

profile of v4, /device:TPU:0, one launch (start us, length us, event | category | flops | bytes accessed | tf_op | source)
XLA Modules:
  0.0 149.2 jit_solution(9878827017439602528)
XLA Ops:
  4.1 2.9 %collective-permute-start.3 = (bf16[512,256]{1,0:T(8,128)(2,1)S(1)}, bf16[512,256]{1,0:T(8,128)(2,1)S(1)}, u32[]{:S(2)}, u32[]{:S(2)}) collective-permute-start(bf16[512,256]{1,0:T(8,128)(2,1)S(1)} %bitcast.41), channel_id=1, source_target_pairs={{0,3},{1,0},{2,1},{3,2},{4,7},{5,4},{6,5},{7,6},{8,11},{9,8},{10,9... | collective-permute-start | bytes 786440 | tf_op jit(solution)/shard_map/ppermute | solution.py:46
  7.1 3.3 %collective-permute-start.6 = (bf16[128,512]{1,0:T(8,128)(2,1)S(1)}, bf16[128,512]{1,0:T(8,128)(2,1)S(1)}, u32[]{:S(2)}, u32[]{:S(2)}) collective-permute-start(bf16[128,512]{1,0:T(8,128)(2,1)S(1)} %constant_dynamic-slice_fusion.1.refs_4_), channel_id=1, source_target_pairs={{0,3},{1,0},{2,1},{3,2},{4,7},{5,4},{6,5},{7,6},{8,11},{9,8},{10,9... | collective-permute-start | bytes 393224 | tf_op jit(solution)/shard_map/ppermute | solution.py:46
  11.3 7.2 %collective-permute-done.6.refs_7_ = bf16[128,512]{1,0:T(8,128)(2,1)S(1)} collective-permute-done((bf16[128,512]{1,0:T(8,128)(2,1)S(1)}, bf16[128,512]{1,0:T(8,128)(2,1)S(1)}, u32[]{:S(2)}, u32[]{:S(2)}) %collective-permute-start.6) | collective-permute-done | bytes 131104 | tf_op jit(solution)/shard_map/ppermute | solution.py:46
  19.3 2.6 %collective-permute-done.4.refs_5_ = bf16[128,512]{1,0:T(8,128)(2,1)S(1)} collective-permute-done((bf16[128,512]{1,0:T(8,128)(2,1)S(1)}, bf16[128,512]{1,0:T(8,128)(2,1)S(1)}, u32[]{:S(2)}, u32[]{:S(2)}) %collective-permute-start.4) | collective-permute-done | bytes 131104 | tf_op jit(solution)/shard_map/ppermute | solution.py:46
  24.1 8.3 %collective-permute-done.2.refs_2_ = bf16[512,256]{1,0:T(8,128)(2,1)S(1)} collective-permute-done((bf16[512,256]{1,0:T(8,128)(2,1)S(1)}, bf16[512,256]{1,0:T(8,128)(2,1)S(1)}, u32[]{:S(2)}, u32[]{:S(2)}) %collective-permute-start.2) | collective-permute-done | bytes 262176 | tf_op jit(solution)/shard_map/ppermute | solution.py:46
  33.8 4.1 %collective-permute-start.12 = (bf16[4,32,512]{2,1,0:T(8,128)(2,1)S(1)}, bf16[4,32,512]{2,1,0:T(8,128)(2,1)S(1)}, u32[]{:S(2)}, u32[]{:S(2)}) collective-permute-start(bf16[4,32,512]{2,1,0:T(8,128)(2,1)S(1)} %get-tuple-element.102), channel_id=1, source_target_pairs={{0,24},{4,28},{8,16},{12,20},{16,8},{20,12},{24,0},{28,4},{32,56},... | collective-permute-start | bytes 393224 | tf_op jit(solution)/shard_map/ppermute | solution.py:42
  37.9 3.0 %collective-permute-start.10 = (bf16[4,32,512]{2,1,0:T(8,128)(2,1)S(1)}, bf16[4,32,512]{2,1,0:T(8,128)(2,1)S(1)}, u32[]{:S(2)}, u32[]{:S(2)}) collective-permute-start(bf16[4,32,512]{2,1,0:T(8,128)(2,1)S(1)} %get-tuple-element.104), channel_id=1, source_target_pairs={{0,96},{4,100},{8,104},{12,108},{16,112},{20,116},{24,120},{28,124... | collective-permute-start | bytes 393224 | tf_op jit(solution)/shard_map/ppermute | solution.py:42
  44.1 1.8 %collective-permute-done.9 = bf16[4,32,512]{2,1,0:T(8,128)(2,1)S(1)} collective-permute-done((bf16[4,32,512]{2,1,0:T(8,128)(2,1)S(1)}, bf16[4,32,512]{2,1,0:T(8,128)(2,1)S(1)}, u32[]{:S(2)}, u32[]{:S(2)}) %collective-permute-start.9) | collective-permute-done | bytes 131104 | tf_op jit(solution)/shard_map/ppermute | solution.py:42
  47.9 2.9 %collective-permute-start.16 = (bf16[8,32,512]{2,1,0:T(8,128)(2,1)S(1)}, bf16[8,32,512]{2,1,0:T(8,128)(2,1)S(1)}, u32[]{:S(2)}, u32[]{:S(2)}) collective-permute-start(bf16[8,32,512]{2,1,0:T(8,128)(2,1)S(1)} %get-tuple-element.58), channel_id=1, source_target_pairs={{0,24},{4,28},{8,16},{12,20},{16,8},{20,12},{24,0},{28,4},{32,56},... | collective-permute-start | bytes 786440 | tf_op jit(solution)/shard_map/ppermute | solution.py:42
  51.7 2.7 %collective-permute-done.14 = bf16[8,32,512]{2,1,0:T(8,128)(2,1)S(1)} collective-permute-done((bf16[8,32,512]{2,1,0:T(8,128)(2,1)S(1)}, bf16[8,32,512]{2,1,0:T(8,128)(2,1)S(1)}, u32[]{:S(2)}, u32[]{:S(2)}) %collective-permute-start.14) | collective-permute-done | bytes 262176 | tf_op jit(solution)/shard_map/ppermute | solution.py:42
  59.6 2.1 %collective-permute-start.19 = (bf16[16,32,512]{2,1,0:T(8,128)(2,1)S(1)}, bf16[16,32,512]{2,1,0:T(8,128)(2,1)}, u32[]{:S(2)}, u32[]{:S(2)}) collective-permute-start(bf16[16,32,512]{2,1,0:T(8,128)(2,1)S(1)} %pad_maximum_fusion.6), channel_id=1, source_target_pairs={{0,8},{4,12},{8,0},{12,4},{16,24},{20,28},{24,16},{28,20},{32,40},... | collective-permute-start | bytes 1572872 | tf_op jit(solution)/shard_map/ppermute | solution.py:42
  62.1 2.0 %collective-permute-start.21 = (bf16[16,32,512]{2,1,0:T(8,128)(2,1)S(1)}, bf16[16,32,512]{2,1,0:T(8,128)(2,1)}, u32[]{:S(2)}, u32[]{:S(2)}) collective-permute-start(bf16[16,32,512]{2,1,0:T(8,128)(2,1)S(1)} %pad_maximum_fusion.8), channel_id=1, source_target_pairs={{0,32},{4,36},{8,40},{12,44},{16,48},{20,52},{24,56},{28,60},{32,0... | collective-permute-start | bytes 1572872 | tf_op jit(solution)/shard_map/ppermute | solution.py:42
  64.1 2.0 %collective-permute-start.22 = (bf16[16,32,512]{2,1,0:T(8,128)(2,1)S(1)}, bf16[16,32,512]{2,1,0:T(8,128)(2,1)}, u32[]{:S(2)}, u32[]{:S(2)}) collective-permute-start(bf16[16,32,512]{2,1,0:T(8,128)(2,1)S(1)} %pad_maximum_fusion.9), channel_id=1, source_target_pairs={{0,96},{4,100},{8,104},{12,108},{16,112},{20,116},{24,120},{28,124... | collective-permute-start | bytes 1572872 | tf_op jit(solution)/shard_map/ppermute | solution.py:42
  67.7 3.3 %collective-permute-start.23 = (bf16[1024,128]{1,0:T(8,128)(2,1)S(1)}, bf16[1024,128]{1,0:T(8,128)(2,1)S(1)}, u32[]{:S(2)}, u32[]{:S(2)}) collective-permute-start(bf16[1024,128]{1,0:T(8,128)(2,1)S(1)} %copy-done.7), channel_id=1, source_target_pairs={{0,3},{1,0},{2,1},{3,2},{4,7},{5,4},{6,5},{7,6},{8,11},{9,8},{10,9... | collective-permute-start | bytes 786440 | tf_op jit(solution)/shard_map/ppermute | solution.py:46
  72.4 2.5 %collective-permute-done.23 = bf16[1024,128]{1,0:T(8,128)(2,1)S(1)} collective-permute-done((bf16[1024,128]{1,0:T(8,128)(2,1)S(1)}, bf16[1024,128]{1,0:T(8,128)(2,1)S(1)}, u32[]{:S(2)}, u32[]{:S(2)}) %collective-permute-start.23) | collective-permute-done | bytes 262176 | tf_op jit(solution)/shard_map/ppermute | solution.py:46
  79.2 2.2 %pad_maximum_fusion.3.refs_6_ = bf16[32,32,512]{2,1,0:T(8,128)(2,1)} fusion(bf16[16,32,512]{2,1,0:T(8,128)(2,1)} %collective-permute-done.22, bf16[16,32,512]{2,1,0:T(8,128)(2,1)S(1)} %copy-done.6), kind=kLoop, calls=%fused_computation.12 | loop fusion | flops 524288 | bytes 2097152 | tf_op jit(solution)/shard_map/concatenate | solution.py:298
  81.4 2.0 %collective-permute-start.25 = (bf16[32,32,512]{2,1,0:T(8,128)(2,1)S(1)}, bf16[32,32,512]{2,1,0:T(8,128)(2,1)}, u32[]{:S(2)}, u32[]{:S(2)}) collective-permute-start(bf16[32,32,512]{2,1,0:T(8,128)(2,1)S(1)} %pad_maximum_fusion.refs_0_), channel_id=1, source_target_pairs={{0,24},{4,28},{8,16},{12,20},{16,8},{20,12},{24,0},{28,4},{32,56},... | collective-permute-start | bytes 3145736 | tf_op jit(solution)/shard_map/ppermute | solution.py:42
  93.3 7.2 %collective-permute-done.24.refs_7_ = bf16[32,32,512]{2,1,0:T(8,128)(2,1)} collective-permute-done((bf16[32,32,512]{2,1,0:T(8,128)(2,1)}, bf16[32,32,512]{2,1,0:T(8,128)(2,1)}, u32[]{:S(2)}, u32[]{:S(2)}) %collective-permute-start.24) | collective-permute-done | bytes 1048608 | tf_op jit(solution)/shard_map/ppermute | solution.py:42
  104.3 10.9 %attend_other.1 = (bf16[1024,512]{1,0:T(8,128)(2,1)S(1)}, f32[4,8,256]{2,1,0:T(8,128)S(1)}) custom-call(s32[256]{0:T(256)S(1)} %reshape.80.row_ref, s32[1]{0:T(128)} %bitcast.15.rank_ref, bf16[4,1024,128]{2,1,0:T(8,128)(2,1)} %collective-permute-done.28.q_ref, f32[4,1,2048]{2,1,0:T(1,128)S(1)} %copy.17.lq_ref, ...), custom_call_target="tpu_custom_call" | custom-call | flops 4294967296 | bytes 12582912 | tf_op jit(solution)/shard_map/attend_other/pallas_call | solution.py:198
  115.9 2.1 %collective-permute-done.30.refs_9_ = f32[4,8,256]{2,1,0:T(8,128)S(1)} collective-permute-done((f32[4,8,256]{2,1,0:T(8,128)S(1)}, f32[4,8,256]{2,1,0:T(8,128)S(1)}, u32[]{:S(2)}, u32[]{:S(2)}) %collective-permute-start.30) | collective-permute-done | bytes 32800 | tf_op jit(solution)/shard_map/ppermute | solution.py:42
  118.0 11.1 %attend_own.1 = (bf16[4,288,128]{2,1,0:T(8,128)(2,1)S(1)}, bf16[4,288,128]{2,1,0:T(8,128)(2,1)S(1)}, bf16[4,288,128]{2,1,0:T(8,128)(2,1)S(1)}, bf16[4,288,128]{2,1,0:T(8,128)(2,1)S(1)}) custom-call(s32[256]{0:T(256)S(1)} %reshape.81.row_ref, s32[1]{0:T(128)} %bitcast.15.rank_ref, bf16[4,1024,128]{2,1,0:T(8,128)(2,1)} %pad_maximum_fusion.4.q_ref, ...), custom_call_target="tpu_custom_call" | custom-call | flops 4294967296 | bytes 12582912 | tf_op jit(solution)/shard_map/attend_own/pallas_call | solution.py:198
  129.2 2.8 %collective-permute-start.32 = (bf16[4,288,128]{2,1,0:T(8,128)(2,1)S(1)}, bf16[4,288,128]{2,1,0:T(8,128)(2,1)S(1)}, u32[]{:S(2)}, u32[]{:S(2)}) collective-permute-start(bf16[4,288,128]{2,1,0:T(8,128)(2,1)S(1)} %get-tuple-element.92), channel_id=1, source_target_pairs={{0,2},{1,3},{2,0},{3,1},{4,6},{5,7},{6,4},{7,5},{8,10},{9,11},{10,... | collective-permute-start | bytes 884744 | tf_op jit(solution)/shard_map/ppermute | solution.py:46
  132.4 13.4 %collective-permute-done.31.refs_1_ = bf16[4,288,128]{2,1,0:T(8,128)(2,1)S(1)} collective-permute-done((bf16[4,288,128]{2,1,0:T(8,128)(2,1)S(1)}, bf16[4,288,128]{2,1,0:T(8,128)(2,1)S(1)}, u32[]{:S(2)}, u32[]{:S(2)}) %collective-permute-start.31) | collective-permute-done | bytes 294944 | tf_op jit(solution)/shard_map/ppermute | solution.py:46
  146.4 2.7 %last.1 = (f32[4,1,256]{2,1,0:T(1,128)}, bf16[1024,128]{1,0:T(8,128)(2,1)}) custom-call(bf16[4,288,128]{2,1,0:T(8,128)(2,1)S(1)} %get-tuple-element.90.refs_0_, bf16[4,288,128]{2,1,0:T(8,128)(2,1)S(1)} %collective-permute-done.31.refs_1_, bf16[4,288,128]{2,1,0:T(8,128)(2,1)S(1)} %collective-permute-done.32.refs_2_, ...), custom_call_target="tpu_custom_call" | custom-call | tf_op jit(solution)/shard_map/last/pallas_call | solution.py:262
  (125 shorter events, 42.7 us)
Async XLA Ops:
  4.1 17.9 %collective-permute-start.3 = (bf16[512,256]{1,0:T(8,128)(2,1)S(1)}, bf16[512,256]{1,0:T(8,128)(2,1)S(1)}, u32[]{:S(2)}, u32[]{:S(2)}) collective-permute-start(bf16[512,256]{1,0:T(8,128)(2,1)S(1)} %bitcast.41), channel_id=1, source_target_pairs={{0,3},{1,0},{2,1},{3,2},{4,7},{5,4},{6,5},{7,6},{8,11},{9,8},{10,9... | collective-permute-start | bytes 786440 | tf_op jit(solution)/shard_map/ppermute | solution.py:46
  7.1 15.0 %collective-permute-start.1 = (bf16[512,256]{1,0:T(8,128)(2,1)S(1)}, bf16[512,256]{1,0:T(8,128)(2,1)S(1)}, u32[]{:S(2)}, u32[]{:S(2)}) collective-permute-start(bf16[512,256]{1,0:T(8,128)(2,1)S(1)} %bitcast.40), channel_id=1, source_target_pairs={{0,1},{1,2},{2,3},{3,0},{4,5},{5,6},{6,7},{7,4},{8,9},{9,10},{10,1... | collective-permute-start | bytes 786440 | tf_op jit(solution)/shard_map/ppermute | solution.py:46
  7.1 11.5 %collective-permute-start.6 = (bf16[128,512]{1,0:T(8,128)(2,1)S(1)}, bf16[128,512]{1,0:T(8,128)(2,1)S(1)}, u32[]{:S(2)}, u32[]{:S(2)}) collective-permute-start(bf16[128,512]{1,0:T(8,128)(2,1)S(1)} %constant_dynamic-slice_fusion.1.refs_4_), channel_id=1, source_target_pairs={{0,3},{1,0},{2,1},{3,2},{4,7},{5,4},{6,5},{7,6},{8,11},{9,8},{10,9... | collective-permute-start | bytes 393224 | tf_op jit(solution)/shard_map/ppermute | solution.py:46
  10.4 8.9 %collective-permute-start.5 = (bf16[128,512]{1,0:T(8,128)(2,1)S(1)}, bf16[128,512]{1,0:T(8,128)(2,1)S(1)}, u32[]{:S(2)}, u32[]{:S(2)}) collective-permute-start(bf16[128,512]{1,0:T(8,128)(2,1)S(1)} %constant_dynamic-slice_fusion.1.refs_4_), channel_id=1, source_target_pairs={{0,2},{1,3},{2,0},{3,1},{4,6},{5,7},{6,4},{7,5},{8,10},{9,11},{10,... | collective-permute-start | bytes 393224 | tf_op jit(solution)/shard_map/ppermute | solution.py:46
  10.4 11.6 %collective-permute-start.4 = (bf16[128,512]{1,0:T(8,128)(2,1)S(1)}, bf16[128,512]{1,0:T(8,128)(2,1)S(1)}, u32[]{:S(2)}, u32[]{:S(2)}) collective-permute-start(bf16[128,512]{1,0:T(8,128)(2,1)S(1)} %constant_dynamic-slice_fusion.1.refs_4_), channel_id=1, source_target_pairs={{0,1},{1,2},{2,3},{3,0},{4,5},{5,6},{6,7},{7,4},{8,9},{9,10},{10,1... | collective-permute-start | bytes 393224 | tf_op jit(solution)/shard_map/ppermute | solution.py:46
  22.1 10.3 %collective-permute-start.7 = (bf16[4,128,512]{2,1,0:T(8,128)(2,1)S(1)}, bf16[4,128,512]{2,1,0:T(8,128)(2,1)S(1)}, u32[]{:S(2)}, u32[]{:S(2)}) collective-permute-start(bf16[4,128,512]{2,1,0:T(8,128)(2,1)S(1)} %pad_maximum_fusion.5), channel_id=1, source_target_pairs={{0,4},{4,0},{8,12},{12,8},{16,20},{20,16},{24,28},{28,24},{32,36},... | collective-permute-start | bytes 1572872 | tf_op jit(solution)/shard_map/ppermute | solution.py:42
  22.2 10.2 %collective-permute-start.2 = (bf16[512,256]{1,0:T(8,128)(2,1)S(1)}, bf16[512,256]{1,0:T(8,128)(2,1)S(1)}, u32[]{:S(2)}, u32[]{:S(2)}) collective-permute-start(bf16[512,256]{1,0:T(8,128)(2,1)S(1)} %bitcast.39), channel_id=1, source_target_pairs={{0,2},{1,3},{2,0},{3,1},{4,6},{5,7},{6,4},{7,5},{8,10},{9,11},{10,... | collective-permute-start | bytes 786440 | tf_op jit(solution)/shard_map/ppermute | solution.py:46
  33.6 12.2 %collective-permute-start.13 = (bf16[1024,128]{1,0:T(8,128)(2,1)S(1)}, bf16[1024,128]{1,0:T(8,128)(2,1)S(1)}, u32[]{:S(2)}, u32[]{:S(2)}) collective-permute-start(bf16[1024,128]{1,0:T(8,128)(2,1)S(1)} %copy-done.7), channel_id=1, source_target_pairs={{0,1},{1,2},{2,3},{3,0},{4,5},{5,6},{6,7},{7,4},{8,9},{9,10},{10,1... | collective-permute-start | bytes 786440 | tf_op jit(solution)/shard_map/ppermute | solution.py:46
  33.8 7.4 %collective-permute-start.12 = (bf16[4,32,512]{2,1,0:T(8,128)(2,1)S(1)}, bf16[4,32,512]{2,1,0:T(8,128)(2,1)S(1)}, u32[]{:S(2)}, u32[]{:S(2)}) collective-permute-start(bf16[4,32,512]{2,1,0:T(8,128)(2,1)S(1)} %get-tuple-element.102), channel_id=1, source_target_pairs={{0,24},{4,28},{8,16},{12,20},{16,8},{20,12},{24,0},{28,4},{32,56},... | collective-permute-start | bytes 393224 | tf_op jit(solution)/shard_map/ppermute | solution.py:42
  46.6 7.7 %collective-permute-start.14 = (bf16[8,32,512]{2,1,0:T(8,128)(2,1)S(1)}, bf16[8,32,512]{2,1,0:T(8,128)(2,1)S(1)}, u32[]{:S(2)}, u32[]{:S(2)}) collective-permute-start(bf16[8,32,512]{2,1,0:T(8,128)(2,1)S(1)} %get-tuple-element.56), channel_id=1, source_target_pairs={{0,96},{4,100},{8,104},{12,108},{16,112},{20,116},{24,120},{28,124... | collective-permute-start | bytes 786440 | tf_op jit(solution)/shard_map/ppermute | solution.py:42
  47.9 7.7 %collective-permute-start.16 = (bf16[8,32,512]{2,1,0:T(8,128)(2,1)S(1)}, bf16[8,32,512]{2,1,0:T(8,128)(2,1)S(1)}, u32[]{:S(2)}, u32[]{:S(2)}) collective-permute-start(bf16[8,32,512]{2,1,0:T(8,128)(2,1)S(1)} %get-tuple-element.58), channel_id=1, source_target_pairs={{0,24},{4,28},{8,16},{12,20},{16,8},{20,12},{24,0},{28,4},{32,56},... | collective-permute-start | bytes 786440 | tf_op jit(solution)/shard_map/ppermute | solution.py:42
  50.8 7.9 %collective-permute-start.18 = (bf16[1024,128]{1,0:T(8,128)(2,1)S(1)}, bf16[1024,128]{1,0:T(8,128)(2,1)S(1)}, u32[]{:S(2)}, u32[]{:S(2)}) collective-permute-start(bf16[1024,128]{1,0:T(8,128)(2,1)S(1)} %copy-done.7), channel_id=1, source_target_pairs={{0,2},{1,3},{2,0},{3,1},{4,6},{5,7},{6,4},{7,5},{8,10},{9,11},{10,... | collective-permute-start | bytes 786440 | tf_op jit(solution)/shard_map/ppermute | solution.py:46
  59.6 15.3 %collective-permute-start.19 = (bf16[16,32,512]{2,1,0:T(8,128)(2,1)S(1)}, bf16[16,32,512]{2,1,0:T(8,128)(2,1)}, u32[]{:S(2)}, u32[]{:S(2)}) collective-permute-start(bf16[16,32,512]{2,1,0:T(8,128)(2,1)S(1)} %pad_maximum_fusion.6), channel_id=1, source_target_pairs={{0,8},{4,12},{8,0},{12,4},{16,24},{20,28},{24,16},{28,20},{32,40},... | collective-permute-start | bytes 1572872 | tf_op jit(solution)/shard_map/ppermute | solution.py:42
  61.7 13.2 %collective-permute-start.20 = (bf16[16,32,512]{2,1,0:T(8,128)(2,1)S(1)}, bf16[16,32,512]{2,1,0:T(8,128)(2,1)}, u32[]{:S(2)}, u32[]{:S(2)}) collective-permute-start(bf16[16,32,512]{2,1,0:T(8,128)(2,1)S(1)} %pad_maximum_fusion.7), channel_id=1, source_target_pairs={{0,24},{4,28},{8,16},{12,20},{16,8},{20,12},{24,0},{28,4},{32,56},... | collective-permute-start | bytes 1572872 | tf_op jit(solution)/shard_map/ppermute | solution.py:42
  62.1 12.8 %collective-permute-start.21 = (bf16[16,32,512]{2,1,0:T(8,128)(2,1)S(1)}, bf16[16,32,512]{2,1,0:T(8,128)(2,1)}, u32[]{:S(2)}, u32[]{:S(2)}) collective-permute-start(bf16[16,32,512]{2,1,0:T(8,128)(2,1)S(1)} %pad_maximum_fusion.8), channel_id=1, source_target_pairs={{0,32},{4,36},{8,40},{12,44},{16,48},{20,52},{24,56},{28,60},{32,0... | collective-permute-start | bytes 1572872 | tf_op jit(solution)/shard_map/ppermute | solution.py:42
  64.1 10.8 %collective-permute-start.22 = (bf16[16,32,512]{2,1,0:T(8,128)(2,1)S(1)}, bf16[16,32,512]{2,1,0:T(8,128)(2,1)}, u32[]{:S(2)}, u32[]{:S(2)}) collective-permute-start(bf16[16,32,512]{2,1,0:T(8,128)(2,1)S(1)} %pad_maximum_fusion.9), channel_id=1, source_target_pairs={{0,96},{4,100},{8,104},{12,108},{16,112},{20,116},{24,120},{28,124... | collective-permute-start | bytes 1572872 | tf_op jit(solution)/shard_map/ppermute | solution.py:42
  81.4 19.1 %collective-permute-start.24 = (bf16[32,32,512]{2,1,0:T(8,128)(2,1)}, bf16[32,32,512]{2,1,0:T(8,128)(2,1)}, u32[]{:S(2)}, u32[]{:S(2)}) collective-permute-start(bf16[32,32,512]{2,1,0:T(8,128)(2,1)} %pad_maximum_fusion.3.refs_6_), channel_id=1, source_target_pairs={{0,32},{4,36},{8,40},{12,44},{16,48},{20,52},{24,56},{28,60},{32,0... | collective-permute-start | bytes 3145736 | tf_op jit(solution)/shard_map/ppermute | solution.py:42
  81.4 20.7 %collective-permute-start.25 = (bf16[32,32,512]{2,1,0:T(8,128)(2,1)S(1)}, bf16[32,32,512]{2,1,0:T(8,128)(2,1)}, u32[]{:S(2)}, u32[]{:S(2)}) collective-permute-start(bf16[32,32,512]{2,1,0:T(8,128)(2,1)S(1)} %pad_maximum_fusion.refs_0_), channel_id=1, source_target_pairs={{0,24},{4,28},{8,16},{12,20},{16,8},{20,12},{24,0},{28,4},{32,56},... | collective-permute-start | bytes 3145736 | tf_op jit(solution)/shard_map/ppermute | solution.py:42
  83.5 19.6 %collective-permute-start.26 = (bf16[32,32,512]{2,1,0:T(8,128)(2,1)S(1)}, bf16[32,32,512]{2,1,0:T(8,128)(2,1)}, u32[]{:S(2)}, u32[]{:S(2)}) collective-permute-start(bf16[32,32,512]{2,1,0:T(8,128)(2,1)S(1)} %pad_maximum_fusion.1.refs_2_), channel_id=1, source_target_pairs={{0,8},{4,12},{8,0},{12,4},{16,24},{20,28},{24,16},{28,20},{32,40},... | collective-permute-start | bytes 3145736 | tf_op jit(solution)/shard_map/ppermute | solution.py:42
  83.5 20.8 %collective-permute-start.27 = (bf16[32,32,512]{2,1,0:T(8,128)(2,1)S(1)}, bf16[32,32,512]{2,1,0:T(8,128)(2,1)}, u32[]{:S(2)}, u32[]{:S(2)}) collective-permute-start(bf16[32,32,512]{2,1,0:T(8,128)(2,1)S(1)} %pad_maximum_fusion.2.refs_4_), channel_id=1, source_target_pairs={{0,96},{4,100},{8,104},{12,108},{16,112},{20,116},{24,120},{28,124... | collective-permute-start | bytes 3145736 | tf_op jit(solution)/shard_map/ppermute | solution.py:42
  85.8 18.5 %collective-permute-start.28 = (bf16[4,1024,128]{2,1,0:T(8,128)(2,1)}, bf16[4,1024,128]{2,1,0:T(8,128)(2,1)}, u32[]{:S(2)}, u32[]{:S(2)}) collective-permute-start(bf16[4,1024,128]{2,1,0:T(8,128)(2,1)} %pad_maximum_fusion.4.q_ref), channel_id=1, source_target_pairs={{0,4},{4,0},{8,12},{12,8},{16,20},{20,16},{24,28},{28,24},{32,36},... | collective-permute-start | bytes 3145736 | tf_op jit(solution)/shard_map/ppermute | solution.py:42
  129.1 16.7 %collective-permute-start.31 = (bf16[4,288,128]{2,1,0:T(8,128)(2,1)S(1)}, bf16[4,288,128]{2,1,0:T(8,128)(2,1)S(1)}, u32[]{:S(2)}, u32[]{:S(2)}) collective-permute-start(bf16[4,288,128]{2,1,0:T(8,128)(2,1)S(1)} %get-tuple-element.91), channel_id=1, source_target_pairs={{0,1},{1,2},{2,3},{3,0},{4,5},{5,6},{6,7},{7,4},{8,9},{9,10},{10,1... | collective-permute-start | bytes 884744 | tf_op jit(solution)/shard_map/ppermute | solution.py:46
  129.2 16.6 %collective-permute-start.32 = (bf16[4,288,128]{2,1,0:T(8,128)(2,1)S(1)}, bf16[4,288,128]{2,1,0:T(8,128)(2,1)S(1)}, u32[]{:S(2)}, u32[]{:S(2)}) collective-permute-start(bf16[4,288,128]{2,1,0:T(8,128)(2,1)S(1)} %get-tuple-element.92), channel_id=1, source_target_pairs={{0,2},{1,3},{2,0},{3,1},{4,6},{5,7},{6,4},{7,5},{8,10},{9,11},{10,... | collective-permute-start | bytes 884744 | tf_op jit(solution)/shard_map/ppermute | solution.py:46
  132.0 14.4 %collective-permute-start.33 = (bf16[4,288,128]{2,1,0:T(8,128)(2,1)S(1)}, bf16[4,288,128]{2,1,0:T(8,128)(2,1)S(1)}, u32[]{:S(2)}, u32[]{:S(2)}) collective-permute-start(bf16[4,288,128]{2,1,0:T(8,128)(2,1)S(1)} %get-tuple-element.93), channel_id=1, source_target_pairs={{0,3},{1,0},{2,1},{3,2},{4,7},{5,4},{6,5},{7,6},{8,11},{9,8},{10,9... | collective-permute-start | bytes 884744 | tf_op jit(solution)/shard_map/ppermute | solution.py:46
  (29 other events, 141.3 us)

commit v5 on v4

v5 whole, which is shorter than its diff:
```python
import functools
import math

import jax
import jax.numpy as jnp
from jax import lax
from jax.experimental import pallas as pl
from jax.experimental.pallas import tpu as pltpu
from jax.sharding import PartitionSpec as P

BLK = 256
TP = 4
NY = 4
NZ = 4
E = 512
LOG2E = math.log2(math.e)
LN2 = math.log(2.0)
SCALE = 2.0 / math.sqrt(E)
LOW = -1e30
ROWS = BLK // TP // 2
NBD = 8
PICKS = 64
COLS = PICKS * ROWS
TILE = 512
HID = 1024
EXTRA = 32


def cat_perm(flip_y, flip_z, flip_c):
    def at(y, z, c):
        return (y * NZ + z) * 2 + c

    return [
        (at(y, z, c), at(y ^ flip_y, z ^ flip_z, c ^ flip_c))
        for y in range(NY)
        for z in range(NZ)
        for c in range(2)
    ]


def send(value, y=0, z=0, c=0):
    return lax.ppermute(value, "cat", cat_perm(y, z, c))


def send_x(value, d):
    return lax.ppermute(value, "tp", [(i, (i + d) % TP) for i in range(TP)])


def tower_kernel(core_ref, *refs):
    hidden = refs[0:4]
    mine, theirs = refs[4:8], refs[8]
    out_ref = refs[9]
    core = core_ref[0]
    half = HID // TP // 2
    acc = jnp.zeros((NBD * 2 * ROWS, E), jnp.float32)
    for d in range(TP):
        low = jnp.where(core == 0, mine[d][...], theirs[d])
        high = jnp.where(core == 0, theirs[d], mine[d][...])
        acc += jnp.dot(hidden[d][:, :half], low, preferred_element_type=jnp.float32)
        acc += jnp.dot(hidden[d][:, half:], high, preferred_element_type=jnp.float32)
    out_ref[...] = acc.astype(jnp.bfloat16).reshape(out_ref.shape)


def tower(core, hidden, mine, theirs):
    return pl.pallas_call(
        tower_kernel,
        out_shape=jax.ShapeDtypeStruct((2 * NBD, ROWS, E), jnp.bfloat16),
        in_specs=[pl.BlockSpec(memory_space=pltpu.SMEM)]
        + [pl.BlockSpec(memory_space=pltpu.VMEM)] * 9,
        out_specs=pl.BlockSpec(memory_space=pltpu.VMEM),
        compiler_params=pltpu.CompilerParams(vmem_limit_bytes=40 << 20),
        cost_estimate=pl.CostEstimate(
            flops=2 * 512 * 1024 * 512, bytes_accessed=3 << 20, transcendentals=0
        ),
        name="tower",
    )(core, *hidden, *mine, theirs)


PART = 2


def one_block(rank, block, base, q_ref, lq_ref, row_ref, table, picked, scores):
    for j in range(PICKS):
        picked[pl.ds(j * ROWS, ROWS), :] = table[row_ref[(base + block) * PICKS + j]]
    here = pl.ds(pl.multiple_of(block * BLK, BLK), BLK)
    query = jnp.concatenate([q_ref[lax.rem(rank + TP - s, TP), here] for s in range(TP)], axis=1)
    top = jnp.full((BLK, 128), LOW, jnp.float32)
    for n in range(COLS // TILE):
        cols = pl.ds(n * TILE, TILE)
        part = lax.dot_general(
            query,
            picked[cols, :],
            (((1,), (1,)), ((), ())),
            preferred_element_type=jnp.float32,
        )
        part = part * (SCALE * LOG2E) - lq_ref[pl.ds(base + block, 1), cols]
        scores[:, cols] = part
        for g in range(TILE // 128):
            top = jnp.maximum(top, part[:, g * 128 : (g + 1) * 128])
    top = jnp.max(top, axis=1, keepdims=True)
    total = jnp.zeros((BLK, 128), jnp.float32)
    acc = jnp.zeros((BLK, E), jnp.float32)
    for n in range(COLS // TILE):
        cols = pl.ds(n * TILE, TILE)
        weight = jnp.exp2(scores[:, cols] - top)
        for g in range(TILE // 128):
            total += weight[:, g * 128 : (g + 1) * 128]
        acc += jnp.dot(
            weight.astype(jnp.bfloat16), picked[cols, :], preferred_element_type=jnp.float32
        )
    return top, jnp.sum(total, axis=1, keepdims=True), acc


def rows_of(top, total):
    lane = lax.broadcasted_iota(jnp.int32, (BLK, 128), 1)
    both = jnp.where(lane == 0, top, jnp.where(lane == 1, total, 0.0))
    return jnp.transpose(both)[:8]


def pack_kernel(places, *refs):
    count = len(places)
    pieces, table, sems = refs[:count], refs[-2], refs[-1]
    copies = [
        pltpu.make_async_copy(piece, table.at[pl.ds(place * 16, 16)], sems.at[n])
        for n, (piece, place) in enumerate(zip(pieces, places))
    ]
    for copy in copies:
        copy.start()
    for copy in copies:
        copy.wait()


def pack(pieces, places):
    return pl.pallas_call(
        functools.partial(pack_kernel, places),
        out_shape=jax.ShapeDtypeStruct((256, ROWS, E), jnp.bfloat16),
        in_specs=[pl.BlockSpec(memory_space=pl.ANY)] * len(pieces),
        out_specs=pl.BlockSpec(memory_space=pltpu.VMEM),
        scratch_shapes=[pltpu.SemaphoreType.DMA((len(pieces),))],
        compiler_params=pltpu.CompilerParams(vmem_limit_bytes=12 << 20),
        cost_estimate=pl.CostEstimate(flops=0, bytes_accessed=16 << 20, transcendentals=0),
        name="pack",
    )(*pieces)


def first_kernel(start, row_ref, rank_ref, q_ref, lq_ref, table, *refs):
    out_ref, stat_ref, picked, scores = refs

    @pl.loop(0, PART)
    def _(n):
        top, total, acc = one_block(
            rank_ref[0], start + n, 0, q_ref, lq_ref, row_ref, table, picked, scores
        )
        out_ref[n] = acc.astype(jnp.bfloat16)
        stat_ref[n] = rows_of(top, total)


def split_rows(row):
    out = []
    for _ in range(3):
        part = row.astype(jnp.bfloat16).astype(jnp.float32)
        out += [part[:, :128], part[:, 128:]]
        row = row - part
    return out


def joined_row(rows):
    halves = [rows[n : n + 1] + (rows[n + 2 : n + 3] + rows[n + 4 : n + 5]) for n in range(2)]
    return jnp.concatenate(halves, axis=1)


def second_kernel(start, row_ref, rank_ref, q_ref, lq_ref, table, *refs):
    other_ref, other_stat_ref, pos_ref = refs[:3]
    outs = refs[3:7]
    picked, scores, quarters = refs[7:]

    @pl.loop(0, PART)
    def _(n):
        top, total, acc = one_block(
            rank_ref[0], start + n, 2 * PART, q_ref, lq_ref, row_ref, table, picked, scores
        )
        theirs = jnp.transpose(jnp.concatenate([other_stat_ref[n]] * 16, axis=0))
        their_top, their_total = theirs[:, 0:1], theirs[:, 1:2]
        joint = jnp.maximum(top, their_top)
        mine_by, theirs_by = jnp.exp2(top - joint), jnp.exp2(their_top - joint)
        acc = acc * mine_by + other_ref[n].astype(jnp.float32) * theirs_by
        for s in range(TP):
            quarters[s] = acc[:, s * 128 : (s + 1) * 128].astype(jnp.bfloat16)
        stat = rows_of(joint, total * mine_by + their_total * theirs_by)
        rows = split_rows(stat[0:1]) + split_rows(stat[1:2]) + split_rows(pos_ref[start + n])
        rows.append(jnp.zeros((EXTRA - len(rows), 128), jnp.float32))
        tail = jnp.concatenate(rows, axis=0).astype(jnp.bfloat16)
        for d in range(TP):
            outs[d][n, :BLK] = quarters[lax.rem(rank_ref[0] + d, TP)]
            outs[d][n, BLK:] = tail


def attend(body, start, scalars, inputs, outs, scratch, name):
    vmem = pl.BlockSpec(memory_space=pltpu.VMEM)
    return pl.pallas_call(
        functools.partial(body, start),
        in_specs=[pl.BlockSpec(memory_space=pltpu.SMEM)] * len(scalars) + [vmem] * len(inputs),
        out_specs=(vmem,) * len(outs),
        out_shape=outs,
        scratch_shapes=[
            pltpu.VMEM((COLS, E), jnp.bfloat16),
            pltpu.VMEM((BLK, COLS), jnp.float32),
        ]
        + scratch,
        compiler_params=pltpu.CompilerParams(vmem_limit_bytes=32 << 20),
        cost_estimate=pl.CostEstimate(
            flops=PART * 4 * BLK * COLS * E,
            bytes_accessed=2 << 20,
            transcendentals=PART * BLK * COLS,
        ),
        name=name,
    )(*scalars, *inputs)


def last_kernel(*refs):
    positive_ref, loss_ref, grad_ref = refs[8:]
    for block in range(2 * PART):
        parts = refs[0:4] if block < PART else refs[4:8]
        finish(parts, block % PART, block, positive_ref, loss_ref, grad_ref)


def finish(parts, n, block, positive_ref, loss_ref, grad_ref):
    here = pl.ds(block * BLK, BLK)
    tails = [ref[n, BLK:].astype(jnp.float32) for ref in parts]
    tops = [joined_row(tail[0:6]) for tail in tails]
    totals = [joined_row(tail[6:12]) for tail in tails]
    shares = [joined_row(tail[12:18]) for tail in tails]
    pos = (shares[0] + shares[1] + shares[2] + shares[3]) * LOG2E
    joint = pos
    for top in tops:
        joint = jnp.maximum(joint, top)
    total = jnp.exp2(pos - joint)
    for top, one in zip(tops, totals):
        total += one * jnp.exp2(top - joint)
    log_total = joint + jnp.log(total) * LOG2E
    loss_ref[block] = (log_total - pos) * LN2
    factors = [jnp.exp2(top - log_total) * SCALE for top in tops]
    factors.append((jnp.exp2(pos - log_total) - 1.0) * SCALE)
    row = lax.broadcasted_iota(jnp.int32, (128, BLK), 0)
    packed = jnp.zeros((128, BLK), jnp.float32)
    for at, factor in enumerate(factors):
        packed = jnp.where(row == at, factor, packed)
    by = jnp.transpose(packed)
    grad = by[:, 4:5] * positive_ref[here].astype(jnp.float32)
    for s in range(4):
        grad += by[:, s : s + 1] * parts[s][n, :BLK].astype(jnp.float32)
    grad_ref[here] = grad.astype(jnp.bfloat16)


def last(parts, positive):
    vmem = pl.BlockSpec(memory_space=pltpu.VMEM)
    blocks = positive.shape[0] // BLK
    return pl.pallas_call(
        last_kernel,
        in_specs=[vmem] * 9,
        out_specs=(vmem, vmem),
        out_shape=(
            jax.ShapeDtypeStruct((blocks, 1, BLK), jnp.float32),
            jax.ShapeDtypeStruct((blocks * BLK, 128), jnp.bfloat16),
        ),
        compiler_params=pltpu.CompilerParams(vmem_limit_bytes=16 << 20),
        name="last",
    )(*parts, positive)


STREAMS = (
    (("y", 1), ("y", 3), ("z", 1), ("z", 3)),
    (("y", 3), ("y", 1), ("z", 3), ("z", 1)),
    (("z", 1), ("z", 3), ("y", 1), ("y", 3)),
    (("z", 3), ("z", 1), ("y", 3), ("y", 1)),
)


def together(*values):
    return list(lax.optimization_barrier(tuple(values)))


def spread(items, query):
    held = [items[n * 4 : n * 4 + 4] for n in range(4)]
    queries = [query]
    for step in range(3):
        got = [send(h, **{st[step][0]: st[step][1]}) for h, st in zip(held, STREAMS)]
        got = together(*got, send_x(query, step + 1), query)
        queries.append(got[4])
        query = got[5]
        if step < 2:
            held = together(*[jnp.concatenate([h, g]) for h, g in zip(held, got)])
    third = got[:4]
    fourth = [send(h, **{st[3][0]: st[3][1]}) for h, st in zip(held, STREAMS)]
    fifth = [send(h, **{st[3][0]: st[3][1]}) for h, st in zip(third, STREAMS)]
    places = (0, 4, 8, 12, 1, 5, 9, 13, 2, 6, 10, 14, 3, 7, 11, 15)
    table = pack(held + third + fourth + fifth, places)
    return table, jnp.stack(queries)


def place_of(flipped, first):
    return jnp.where(
        flipped == 0, 0, jnp.where(flipped == 2, 3, jnp.where(flipped == first, 1, 2))
    )


def local(query_emb, positive_emb, item_hidden, item_weight, neg_blocks, block_home, sample_counts):
    rank = lax.axis_index("tp")
    place = lax.axis_index("cat")
    core, my_z, my_y = place % 2, (place // 2) % NZ, place // (2 * NZ)
    qblocks = neg_blocks.shape[0]
    total_blocks = block_home.shape[0]

    core_id = core.reshape(1).astype(jnp.int32)
    rank_id = rank.reshape(1).astype(jnp.int32)
    hidden = item_hidden.reshape(NBD, TP, 2, ROWS, -1)
    keep = lax.dynamic_index_in_dim(hidden, core, 2, keepdims=False)
    give = lax.dynamic_index_in_dim(hidden, 1 - core, 2, keepdims=False)
    half = lax.dynamic_slice_in_dim(item_weight, core * (HID // TP // 2), HID // TP // 2, 0)
    swapped = send(give, c=1)
    mine_w = [half] + [send_x(half, d) for d in (1, 2, 3)]
    both = jnp.concatenate([keep, swapped])

    def piece(d):
        cut = lax.dynamic_index_in_dim(both, (rank + d) % TP, 1, keepdims=False)
        return cut.reshape(2 * NBD * ROWS, -1)

    hiddens = [piece(0)] + [send_x(piece(d), d) for d in (1, 2, 3)]
    theirs_w = send(together(jnp.stack(mine_w), hiddens[1], hiddens[3])[0], c=1)
    picks = jnp.concatenate([send(neg_blocks, c=1), neg_blocks])
    items, late_query, picks = together(
        tower(core_id, hiddens, mine_w, theirs_w), query_emb, picks
    )
    table, query = spread(items, late_query)
    other_query = send(query, c=1)
    pos_part = SCALE * jnp.sum(
        query_emb.astype(jnp.float32) * positive_emb.astype(jnp.float32), axis=1
    ).reshape(qblocks, 1, BLK)

    matches = picks[:, :, None] == jnp.arange(total_blocks, dtype=jnp.int32)[None, None, :]
    home = jnp.sum(jnp.where(matches, block_home[None, None, :], 0), axis=2)
    slot, owner = home % NBD, home // NBD
    flip_z = ((owner // 2) % NZ) ^ my_z
    flip_y = (owner // (2 * NZ)) ^ my_y
    late = slot // (NBD // 2)
    at_y = place_of(flip_y, jnp.where(late == 0, 1, 3))
    at_z = place_of(flip_z, jnp.where(late == 0, 1, 3))
    near = owner % 2 == core
    rows = jnp.where(near, at_z * 4 + at_y, 128 // 4 + at_y * 4 + at_z)
    rows = (rows * 4 + late * 64 + slot % 4).astype(jnp.int32)
    log_table = (jnp.log(sample_counts.astype(jnp.float32)) * LOG2E).reshape(
        total_blocks, TP * 2, ROWS
    )
    my_log = lax.dynamic_index_in_dim(log_table, rank * 2 + core, 1, keepdims=False)
    lq = my_log[home].reshape(2 * qblocks, COLS)

    rows = rows.reshape(-1)
    table, pos_part, rows, lq = together(table, pos_part, rows, lq)

    raw = (
        jax.ShapeDtypeStruct((PART, BLK, E), jnp.bfloat16),
        jax.ShapeDtypeStruct((PART, 8, BLK), jnp.float32),
    )
    share = jax.ShapeDtypeStruct((PART, BLK + EXTRA, 128), jnp.bfloat16)
    others = []
    for start in (0, PART):
        made = attend(
            first_kernel,
            start,
            (rows, rank_id),
            (other_query, lq, table),
            raw,
            [],
            "attend_other",
        )
        others.append([send(one, c=1) for one in made])
    parts = []
    for start, other in zip((0, PART), others):
        shares = attend(
            second_kernel,
            start,
            (rows, rank_id),
            (query, lq, table, *other, pos_part),
            (share,) * TP,
            [pltpu.VMEM((TP, BLK, 128), jnp.bfloat16)],
            "attend_own",
        )
        parts += [shares[0]] + [send_x(shares[d], d) for d in (1, 2, 3)]
    loss, grad = last(parts, positive_emb)
    return loss.reshape(-1), grad


def solution(mesh):
    placed = (
        P("cat", "tp"),
        P("cat", "tp"),
        P("cat", "tp"),
        P("tp", None),
        P("cat", None),
        P(),
        P(),
    )
    return jax.shard_map(
        local, mesh=mesh, in_specs=placed, out_specs=(P("cat"), P("cat", "tp")), check_vma=False
    )
```

time: 150 us -> 146 us (0.973)
  starting transfers between devices: 36.7 us -> 54.1 us
  waiting for transfers between devices: 62.7 us -> 45.6 us
  Pallas kernels: 26 us -> 21.4 us
    ppermute x12 -> x15, waiting for transfers between devices: 37 us -> 23.3 us  [send_x(): return lax.ppermute(value, 'tp', [(i, (i + d) % TP) for i in range(TP)])]
    ppermute x12 -> x15, starting transfers between devices: 14.8 us -> 26.4 us  [send_x(): return lax.ppermute(value, 'tp', [(i, (i + d) % TP) for i in range(TP)])]
    ppermute x22 -> x28, starting transfers between devices: 21.9 us -> 27.7 us  [send(): return lax.ppermute(value, 'cat', cat_perm(y, z, c))]
    pallas_call x3 -> x6, Pallas kernels: 24.8 us -> 20.2 us  [the longest x4 15.7 us: attend(): pl.pallas_call(functools.partial(body, start), in_specs=[pl.BlockSpec(mem...]
    concatenate x10 -> x6, other arithmetic: 6.03 us -> 1.89 us  [spread(): held = together(*[jnp.concatenate([h, g]) for h, g in zip(held, got)])]
    slice x4 -> x0, local copies, waits for them, and re-layouts: 4.01 us -> none  [the longest x3 4.01 us: local(): first_lq, own_lq = (lq[:qblocks], lq[qblocks:])]
    ppermute x22 -> x28, waiting for transfers between devices: 25.7 us -> 22.3 us  [send(): return lax.ppermute(value, 'cat', cat_perm(y, z, c))]
    unnamed x38 -> x28, local copies, waits for them, and re-layouts: 2.58 us -> 5.83 us
  transfers between devices with their start and end apart: 34 -> 43, of which waited for: 22 -> 19; matrix products, arithmetic and copies ran while one was open for 8% -> 9% of each run, Pallas kernels for 0% -> 10%
where the time goes in v5:
time: 146 us; the launch traced here: 145 us
  starting transfers between devices  54.1 us (37%)
  waiting for transfers between devices  45.6 us (31%)
  Pallas kernels  21.4 us (15%)
  local copies, waits for them, and re-layouts  15.3 us (10%)
  other arithmetic  7.38 us (5%)
    ppermute x28, starting transfers between devices, send(): return lax.ppermute(value, 'cat', cat_perm(y, z, c))  27.7 us
    ppermute x15, starting transfers between devices, send_x(): return lax.ppermute(value, 'tp', [(i, (i + d) % TP) for i in range(TP)])  26.4 us
    ppermute x15, waiting for transfers between devices, send_x(): return lax.ppermute(value, 'tp', [(i, (i + d) % TP) for i in range(TP)])  23.3 us
    ppermute x28, waiting for transfers between devices, send(): return lax.ppermute(value, 'cat', cat_perm(y, z, c))  22.3 us
    pallas_call x4, Pallas kernels, attend(): pl.pallas_call(functools.partial(body, start), in_specs=[pl.BlockSpec(mem...  15.7 us
    unnamed x28, local copies, waits for them, and re-layouts  5.83 us
  transfers between devices with their start and end apart: 43, of which 19 were waited for; matrix products, arithmetic and copies ran while one was open for 9% of the time, Pallas kernels for 10%

profile of v5, /device:TPU:0, one launch (start us, length us, event | category | flops | bytes accessed | tf_op | source)
XLA Modules:
  0.0 145.0 jit_solution(17223894572222559717)
XLA Ops:
  7.9 2.7 %collective-permute-start.5 = (bf16[128,512]{1,0:T(8,128)(2,1)S(1)}, bf16[128,512]{1,0:T(8,128)(2,1)S(1)}, u32[]{:S(2)}, u32[]{:S(2)}) collective-permute-start(bf16[128,512]{1,0:T(8,128)(2,1)S(1)} %constant_dynamic-slice_fusion.1.refs_4_), channel_id=1, source_target_pairs={{0,2},{1,3},{2,0},{3,1},{4,6},{5,7},{6,4},{7,5},{8,10},{9,11},{10,... | collective-permute-start | bytes 393224 | tf_op jit(solution)/shard_map/ppermute | solution.py:46
  12.1 4.5 %collective-permute-done.4.refs_5_ = bf16[128,512]{1,0:T(8,128)(2,1)S(1)} collective-permute-done((bf16[128,512]{1,0:T(8,128)(2,1)S(1)}, bf16[128,512]{1,0:T(8,128)(2,1)S(1)}, u32[]{:S(2)}, u32[]{:S(2)}) %collective-permute-start.4) | collective-permute-done | bytes 131104 | tf_op jit(solution)/shard_map/ppermute | solution.py:46
  16.6 3.9 %collective-permute-done.5.refs_6_ = bf16[128,512]{1,0:T(8,128)(2,1)S(1)} collective-permute-done((bf16[128,512]{1,0:T(8,128)(2,1)S(1)}, bf16[128,512]{1,0:T(8,128)(2,1)S(1)}, u32[]{:S(2)}, u32[]{:S(2)}) %collective-permute-start.5) | collective-permute-done | bytes 131104 | tf_op jit(solution)/shard_map/ppermute | solution.py:46
  24.6 6.3 %collective-permute-done.2.refs_2_ = bf16[512,256]{1,0:T(8,128)(2,1)S(1)} collective-permute-done((bf16[512,256]{1,0:T(8,128)(2,1)S(1)}, bf16[512,256]{1,0:T(8,128)(2,1)S(1)}, u32[]{:S(2)}, u32[]{:S(2)}) %collective-permute-start.2) | collective-permute-done | bytes 262176 | tf_op jit(solution)/shard_map/ppermute | solution.py:46
  34.4 2.2 %collective-permute-start.10 = (bf16[4,32,512]{2,1,0:T(8,128)(2,1)S(1)}, bf16[4,32,512]{2,1,0:T(8,128)(2,1)S(1)}, u32[]{:S(2)}, u32[]{:S(2)}) collective-permute-start(bf16[4,32,512]{2,1,0:T(8,128)(2,1)S(1)} %get-tuple-element.104), channel_id=1, source_target_pairs={{0,96},{4,100},{8,104},{12,108},{16,112},{20,116},{24,120},{28,124... | collective-permute-start | bytes 393224 | tf_op jit(solution)/shard_map/ppermute | solution.py:42
  38.5 2.5 %collective-permute-start.12 = (bf16[4,32,512]{2,1,0:T(8,128)(2,1)S(1)}, bf16[4,32,512]{2,1,0:T(8,128)(2,1)S(1)}, u32[]{:S(2)}, u32[]{:S(2)}) collective-permute-start(bf16[4,32,512]{2,1,0:T(8,128)(2,1)S(1)} %get-tuple-element.102), channel_id=1, source_target_pairs={{0,24},{4,28},{8,16},{12,20},{16,8},{20,12},{24,0},{28,4},{32,56},... | collective-permute-start | bytes 393224 | tf_op jit(solution)/shard_map/ppermute | solution.py:42
  41.6 3.1 %collective-permute-done.12 = bf16[4,32,512]{2,1,0:T(8,128)(2,1)S(1)} collective-permute-done((bf16[4,32,512]{2,1,0:T(8,128)(2,1)S(1)}, bf16[4,32,512]{2,1,0:T(8,128)(2,1)S(1)}, u32[]{:S(2)}, u32[]{:S(2)}) %collective-permute-start.12) | collective-permute-done | bytes 131104 | tf_op jit(solution)/shard_map/ppermute | solution.py:42
  46.0 2.7 %collective-permute-start.16 = (bf16[8,32,512]{2,1,0:T(8,128)(2,1)S(1)}, bf16[8,32,512]{2,1,0:T(8,128)(2,1)S(1)}, u32[]{:S(2)}, u32[]{:S(2)}) collective-permute-start(bf16[8,32,512]{2,1,0:T(8,128)(2,1)S(1)} %get-tuple-element.58), channel_id=1, source_target_pairs={{0,24},{4,28},{8,16},{12,20},{16,8},{20,12},{24,0},{28,4},{32,56},... | collective-permute-start | bytes 786440 | tf_op jit(solution)/shard_map/ppermute | solution.py:42
  48.7 2.7 %collective-permute-start.18 = (bf16[1024,128]{1,0:T(8,128)(2,1)S(1)}, bf16[1024,128]{1,0:T(8,128)(2,1)S(1)}, u32[]{:S(2)}, u32[]{:S(2)}) collective-permute-start(bf16[1024,128]{1,0:T(8,128)(2,1)S(1)} %copy-done.10), channel_id=1, source_target_pairs={{0,2},{1,3},{2,0},{3,1},{4,6},{5,7},{6,4},{7,5},{8,10},{9,11},{10,... | collective-permute-start | bytes 786440 | tf_op jit(solution)/shard_map/ppermute | solution.py:46
  65.8 2.7 %collective-permute-start.23 = (bf16[1024,128]{1,0:T(8,128)(2,1)}, bf16[1024,128]{1,0:T(8,128)(2,1)}, u32[]{:S(2)}, u32[]{:S(2)}) collective-permute-start(bf16[1024,128]{1,0:T(8,128)(2,1)} %param.7), channel_id=1, source_target_pairs={{0,3},{1,0},{2,1},{3,2},{4,7},{5,4},{6,5},{7,6},{8,11},{9,8},{10,9... | collective-permute-start | bytes 786440 | tf_op jit(solution)/shard_map/ppermute | solution.py:46
  70.3 2.2 %reshape.76 = f32[256,8,32]{2,1,0:T(8,128)} reshape(f32[65536]{0:T(1024)} %log_multiply_fusion) | data formatting | bytes 524288 | tf_op jit(solution)/shard_map/reshape | solution.py:351
  74.5 2.5 %collective-permute-start.24 = (bf16[16,32,512]{2,1,0:T(8,128)(2,1)S(1)}, bf16[16,32,512]{2,1,0:T(8,128)(2,1)}, u32[]{:S(2)}, u32[]{:S(2)}) collective-permute-start(bf16[16,32,512]{2,1,0:T(8,128)(2,1)S(1)} %pad_maximum_fusion.2.refs_0_), channel_id=1, source_target_pairs={{0,24},{4,28},{8,16},{12,20},{16,8},{20,12},{24,0},{28,4},{32,56},... | collective-permute-start | bytes 1572872 | tf_op jit(solution)/shard_map/ppermute | solution.py:42
  82.3 2.7 %collective-permute-done.24.refs_8_ = bf16[16,32,512]{2,1,0:T(8,128)(2,1)} collective-permute-done((bf16[16,32,512]{2,1,0:T(8,128)(2,1)S(1)}, bf16[16,32,512]{2,1,0:T(8,128)(2,1)}, u32[]{:S(2)}, u32[]{:S(2)}) %collective-permute-start.24) | collective-permute-done | bytes 524320 | tf_op jit(solution)/shard_map/ppermute | solution.py:42
  85.0 2.5 %collective-permute-start.28 = (bf16[16,32,512]{2,1,0:T(8,128)(2,1)}, bf16[16,32,512]{2,1,0:T(8,128)(2,1)}, u32[]{:S(2)}, u32[]{:S(2)}) collective-permute-start(bf16[16,32,512]{2,1,0:T(8,128)(2,1)} %copy-done.2), channel_id=1, source_target_pairs={{0,24},{4,28},{8,16},{12,20},{16,8},{20,12},{24,0},{28,4},{32,56},... | collective-permute-start | bytes 1572872 | tf_op jit(solution)/shard_map/ppermute | solution.py:42
  89.0 2.5 %gather_fusion = f32[512,32]{1,0:T(8,128)} fusion(f32[256,32]{1,0:T(8,128)} %bitcast.35, s32[1024]{0:T(1024)S(1)} %pad_clamp_fusion), kind=kCustom, calls=%fused_computation | custom fusion | bytes 133120 | tf_op jit(solution)/shard_map/gather | solution.py:355
  92.7 5.5 %collective-permute-done.28.refs_12_ = bf16[16,32,512]{2,1,0:T(8,128)(2,1)} collective-permute-done((bf16[16,32,512]{2,1,0:T(8,128)(2,1)}, bf16[16,32,512]{2,1,0:T(8,128)(2,1)}, u32[]{:S(2)}, u32[]{:S(2)}) %collective-permute-start.28) | collective-permute-done | bytes 524320 | tf_op jit(solution)/shard_map/ppermute | solution.py:42
  104.8 2.7 %pack.1.table = bf16[256,32,512]{2,1,0:T(8,128)(2,1)S(1)} custom-call(bf16[16,32,512]{2,1,0:T(8,128)(2,1)S(1)} %pad_maximum_fusion.2.refs_0_, bf16[16,32,512]{2,1,0:T(8,128)(2,1)S(1)} %pad_maximum_fusion.3.refs_1_, bf16[16,32,512]{2,1,0:T(8,128)(2,1)} %pad_maximum_fusion.4.refs_2_, bf16[16,32,512]{2,1,0:T(8,128)(2,1)} %pad_maximum_fusion.5.refs_3_, ...), custom_call_target="tpu_custom_call" | custom-call | bytes 16777216 | tf_op jit(solution)/shard_map/pack/pallas_call | solution.py:134
  107.5 3.9 %attend_other.2 = (bf16[2,256,512]{2,1,0:T(8,128)(2,1)S(1)}, f32[2,8,256]{2,1,0:T(8,128)S(1)}) custom-call(s32[512]{0:T(512)S(1)} %fusion.9.row_ref, s32[1]{0:T(128)} %bitcast.15.rank_ref, bf16[4,1024,128]{2,1,0:T(8,128)(2,1)S(1)} %collective-permute-done.32.q_ref, f32[8,2048]{1,0:T(8,128)S(1)} %reshape.77.lq_ref, bf16[256,32,512]{2,1,0:T(8,128)(2,1)S(1)} %pack.1.table), custom_call_target="tpu_custom_call" | custom-call | flops 2147483648 | bytes 2097152 | tf_op jit(solution)/shard_map/attend_other/pallas_call | solution.py:200
  111.5 3.9 %attend_other.3 = (bf16[2,256,512]{2,1,0:T(8,128)(2,1)S(1)}, f32[2,8,256]{2,1,0:T(8,128)S(1)}) custom-call(s32[512]{0:T(512)S(1)} %fusion.9.row_ref, s32[1]{0:T(128)} %bitcast.15.rank_ref, bf16[4,1024,128]{2,1,0:T(8,128)(2,1)S(1)} %collective-permute-done.32.q_ref, f32[8,2048]{1,0:T(8,128)S(1)} %reshape.77.lq_ref, bf16[256,32,512]{2,1,0:T(8,128)(2,1)S(1)} %pack.1.table), custom_call_target="tpu_custom_call" | custom-call | flops 2147483648 | bytes 2097152 | tf_op jit(solution)/shard_map/attend_other/pallas_call | solution.py:200
  117.5 4.0 %attend_own.2 = (bf16[2,288,128]{2,1,0:T(8,128)(2,1)S(1)}, bf16[2,288,128]{2,1,0:T(8,128)(2,1)S(1)}, bf16[2,288,128]{2,1,0:T(8,128)(2,1)S(1)}, bf16[2,288,128]{2,1,0:T(8,128)(2,1)S(1)}) custom-call(s32[512]{0:T(512)S(1)} %fusion.9.row_ref, s32[1]{0:T(128)} %bitcast.15.rank_ref, bf16[4,1024,128]{2,1,0:T(8,128)(2,1)S(1)} %pad_maximum_fusion.q_ref, ...), custom_call_target="tpu_custom_call" | custom-call | flops 2147483648 | bytes 2097152 | tf_op jit(solution)/shard_map/attend_own/pallas_call | solution.py:200
  122.7 3.7 %collective-permute-start.36 = (bf16[2,288,128]{2,1,0:T(8,128)(2,1)S(1)}, bf16[2,288,128]{2,1,0:T(8,128)(2,1)S(1)}, u32[]{:S(2)}, u32[]{:S(2)}) collective-permute-start(bf16[2,288,128]{2,1,0:T(8,128)(2,1)S(1)} %get-tuple-element.86), channel_id=1, source_target_pairs={{0,2},{1,3},{2,0},{3,1},{4,6},{5,7},{6,4},{7,5},{8,10},{9,11},{10,... | collective-permute-start | bytes 442376 | tf_op jit(solution)/shard_map/ppermute | solution.py:46
  126.5 2.4 %collective-permute-start.37 = (bf16[2,288,128]{2,1,0:T(8,128)(2,1)S(1)}, bf16[2,288,128]{2,1,0:T(8,128)(2,1)S(1)}, u32[]{:S(2)}, u32[]{:S(2)}) collective-permute-start(bf16[2,288,128]{2,1,0:T(8,128)(2,1)S(1)} %get-tuple-element.87), channel_id=1, source_target_pairs={{0,3},{1,0},{2,1},{3,2},{4,7},{5,4},{6,5},{7,6},{8,11},{9,8},{10,9... | collective-permute-start | bytes 442376 | tf_op jit(solution)/shard_map/ppermute | solution.py:46
  128.8 4.0 %attend_own.3 = (bf16[2,288,128]{2,1,0:T(8,128)(2,1)S(1)}, bf16[2,288,128]{2,1,0:T(8,128)(2,1)S(1)}, bf16[2,288,128]{2,1,0:T(8,128)(2,1)S(1)}, bf16[2,288,128]{2,1,0:T(8,128)(2,1)S(1)}) custom-call(s32[512]{0:T(512)S(1)} %fusion.9.row_ref, s32[1]{0:T(128)} %bitcast.15.rank_ref, bf16[4,1024,128]{2,1,0:T(8,128)(2,1)S(1)} %pad_maximum_fusion.q_ref, ...), custom_call_target="tpu_custom_call" | custom-call | flops 2147483648 | bytes 2097152 | tf_op jit(solution)/shard_map/attend_own/pallas_call | solution.py:200
  136.1 6.4 %collective-permute-done.40.refs_5_ = bf16[2,288,128]{2,1,0:T(8,128)(2,1)S(1)} collective-permute-done((bf16[2,288,128]{2,1,0:T(8,128)(2,1)S(1)}, bf16[2,288,128]{2,1,0:T(8,128)(2,1)S(1)}, u32[]{:S(2)}, u32[]{:S(2)}) %collective-permute-start.40) | collective-permute-done | bytes 147488 | tf_op jit(solution)/shard_map/ppermute | solution.py:46
  (126 shorter events, 61.5 us)
Async XLA Ops:
  4.2 16.4 %collective-permute-start.1 = (bf16[512,256]{1,0:T(8,128)(2,1)S(1)}, bf16[512,256]{1,0:T(8,128)(2,1)S(1)}, u32[]{:S(2)}, u32[]{:S(2)}) collective-permute-start(bf16[512,256]{1,0:T(8,128)(2,1)S(1)} %bitcast.42), channel_id=1, source_target_pairs={{0,1},{1,2},{2,3},{3,0},{4,5},{5,6},{6,7},{7,4},{8,9},{9,10},{10,1... | collective-permute-start | bytes 786440 | tf_op jit(solution)/shard_map/ppermute | solution.py:46
  5.8 14.8 %collective-permute-start.3 = (bf16[512,256]{1,0:T(8,128)(2,1)S(1)}, bf16[512,256]{1,0:T(8,128)(2,1)S(1)}, u32[]{:S(2)}, u32[]{:S(2)}) collective-permute-start(bf16[512,256]{1,0:T(8,128)(2,1)S(1)} %bitcast.41), channel_id=1, source_target_pairs={{0,3},{1,0},{2,1},{3,2},{4,7},{5,4},{6,5},{7,6},{8,11},{9,8},{10,9... | collective-permute-start | bytes 786440 | tf_op jit(solution)/shard_map/ppermute | solution.py:46
  7.9 12.6 %collective-permute-start.5 = (bf16[128,512]{1,0:T(8,128)(2,1)S(1)}, bf16[128,512]{1,0:T(8,128)(2,1)S(1)}, u32[]{:S(2)}, u32[]{:S(2)}) collective-permute-start(bf16[128,512]{1,0:T(8,128)(2,1)S(1)} %constant_dynamic-slice_fusion.1.refs_4_), channel_id=1, source_target_pairs={{0,2},{1,3},{2,0},{3,1},{4,6},{5,7},{6,4},{7,5},{8,10},{9,11},{10,... | collective-permute-start | bytes 393224 | tf_op jit(solution)/shard_map/ppermute | solution.py:46
  10.7 9.8 %collective-permute-start.6 = (bf16[128,512]{1,0:T(8,128)(2,1)S(1)}, bf16[128,512]{1,0:T(8,128)(2,1)S(1)}, u32[]{:S(2)}, u32[]{:S(2)}) collective-permute-start(bf16[128,512]{1,0:T(8,128)(2,1)S(1)} %constant_dynamic-slice_fusion.1.refs_4_), channel_id=1, source_target_pairs={{0,3},{1,0},{2,1},{3,2},{4,7},{5,4},{6,5},{7,6},{8,11},{9,8},{10,9... | collective-permute-start | bytes 393224 | tf_op jit(solution)/shard_map/ppermute | solution.py:46
  20.6 10.3 %collective-permute-start.7 = (bf16[4,128,512]{2,1,0:T(8,128)(2,1)S(1)}, bf16[4,128,512]{2,1,0:T(8,128)(2,1)S(1)}, u32[]{:S(2)}, u32[]{:S(2)}) collective-permute-start(bf16[4,128,512]{2,1,0:T(8,128)(2,1)S(1)} %pad_maximum_fusion.1), channel_id=1, source_target_pairs={{0,4},{4,0},{8,12},{12,8},{16,20},{20,16},{24,28},{28,24},{32,36},... | collective-permute-start | bytes 1572872 | tf_op jit(solution)/shard_map/ppermute | solution.py:42
  20.7 10.2 %collective-permute-start.2 = (bf16[512,256]{1,0:T(8,128)(2,1)S(1)}, bf16[512,256]{1,0:T(8,128)(2,1)S(1)}, u32[]{:S(2)}, u32[]{:S(2)}) collective-permute-start(bf16[512,256]{1,0:T(8,128)(2,1)S(1)} %bitcast.40), channel_id=1, source_target_pairs={{0,2},{1,3},{2,0},{3,1},{4,6},{5,7},{6,4},{7,5},{8,10},{9,11},{10,... | collective-permute-start | bytes 786440 | tf_op jit(solution)/shard_map/ppermute | solution.py:46
  32.2 12.5 %collective-permute-start.13 = (bf16[1024,128]{1,0:T(8,128)(2,1)S(1)}, bf16[1024,128]{1,0:T(8,128)(2,1)S(1)}, u32[]{:S(2)}, u32[]{:S(2)}) collective-permute-start(bf16[1024,128]{1,0:T(8,128)(2,1)S(1)} %copy-done.10), channel_id=1, source_target_pairs={{0,1},{1,2},{2,3},{3,0},{4,5},{5,6},{6,7},{7,4},{8,9},{9,10},{10,1... | collective-permute-start | bytes 786440 | tf_op jit(solution)/shard_map/ppermute | solution.py:46
  59.1 18.0 %collective-permute-start.19 = (bf16[16,32,512]{2,1,0:T(8,128)(2,1)S(1)}, bf16[16,32,512]{2,1,0:T(8,128)(2,1)S(1)}, u32[]{:S(2)}, u32[]{:S(2)}) collective-permute-start(bf16[16,32,512]{2,1,0:T(8,128)(2,1)S(1)} %pad_maximum_fusion.2.refs_0_), channel_id=1, source_target_pairs={{0,8},{4,12},{8,0},{12,4},{16,24},{20,28},{24,16},{28,20},{32,40},... | collective-permute-start | bytes 1572872 | tf_op jit(solution)/shard_map/ppermute | solution.py:42
  61.1 16.0 %collective-permute-start.20 = (bf16[16,32,512]{2,1,0:T(8,128)(2,1)S(1)}, bf16[16,32,512]{2,1,0:T(8,128)(2,1)S(1)}, u32[]{:S(2)}, u32[]{:S(2)}) collective-permute-start(bf16[16,32,512]{2,1,0:T(8,128)(2,1)S(1)} %pad_maximum_fusion.3.refs_1_), channel_id=1, source_target_pairs={{0,24},{4,28},{8,16},{12,20},{16,8},{20,12},{24,0},{28,4},{32,56},... | collective-permute-start | bytes 1572872 | tf_op jit(solution)/shard_map/ppermute | solution.py:42
  61.6 16.6 %collective-permute-start.21 = (bf16[16,32,512]{2,1,0:T(8,128)(2,1)}, bf16[16,32,512]{2,1,0:T(8,128)(2,1)S(1)}, u32[]{:S(2)}, u32[]{:S(2)}) collective-permute-start(bf16[16,32,512]{2,1,0:T(8,128)(2,1)} %pad_maximum_fusion.4.refs_2_), channel_id=1, source_target_pairs={{0,32},{4,36},{8,40},{12,44},{16,48},{20,52},{24,56},{28,60},{32,0... | collective-permute-start | bytes 1572872 | tf_op jit(solution)/shard_map/ppermute | solution.py:42
  63.6 14.6 %collective-permute-start.22 = (bf16[16,32,512]{2,1,0:T(8,128)(2,1)}, bf16[16,32,512]{2,1,0:T(8,128)(2,1)S(1)}, u32[]{:S(2)}, u32[]{:S(2)}) collective-permute-start(bf16[16,32,512]{2,1,0:T(8,128)(2,1)} %pad_maximum_fusion.5.refs_3_), channel_id=1, source_target_pairs={{0,96},{4,100},{8,104},{12,108},{16,112},{20,116},{24,120},{28,124... | collective-permute-start | bytes 1572872 | tf_op jit(solution)/shard_map/ppermute | solution.py:42
  74.5 10.5 %collective-permute-start.24 = (bf16[16,32,512]{2,1,0:T(8,128)(2,1)S(1)}, bf16[16,32,512]{2,1,0:T(8,128)(2,1)}, u32[]{:S(2)}, u32[]{:S(2)}) collective-permute-start(bf16[16,32,512]{2,1,0:T(8,128)(2,1)S(1)} %pad_maximum_fusion.2.refs_0_), channel_id=1, source_target_pairs={{0,24},{4,28},{8,16},{12,20},{16,8},{20,12},{24,0},{28,4},{32,56},... | collective-permute-start | bytes 1572872 | tf_op jit(solution)/shard_map/ppermute | solution.py:42
  77.0 10.5 %collective-permute-start.25 = (bf16[16,32,512]{2,1,0:T(8,128)(2,1)S(1)}, bf16[16,32,512]{2,1,0:T(8,128)(2,1)}, u32[]{:S(2)}, u32[]{:S(2)}) collective-permute-start(bf16[16,32,512]{2,1,0:T(8,128)(2,1)S(1)} %pad_maximum_fusion.3.refs_1_), channel_id=1, source_target_pairs={{0,8},{4,12},{8,0},{12,4},{16,24},{20,28},{24,16},{28,20},{32,40},... | collective-permute-start | bytes 1572872 | tf_op jit(solution)/shard_map/ppermute | solution.py:42
  77.1 10.8 %collective-permute-start.26 = (bf16[16,32,512]{2,1,0:T(8,128)(2,1)}, bf16[16,32,512]{2,1,0:T(8,128)(2,1)}, u32[]{:S(2)}, u32[]{:S(2)}) collective-permute-start(bf16[16,32,512]{2,1,0:T(8,128)(2,1)} %pad_maximum_fusion.4.refs_2_), channel_id=1, source_target_pairs={{0,96},{4,100},{8,104},{12,108},{16,112},{20,116},{24,120},{28,124... | collective-permute-start | bytes 1572872 | tf_op jit(solution)/shard_map/ppermute | solution.py:42
  78.2 10.7 %collective-permute-start.27 = (bf16[16,32,512]{2,1,0:T(8,128)(2,1)}, bf16[16,32,512]{2,1,0:T(8,128)(2,1)}, u32[]{:S(2)}, u32[]{:S(2)}) collective-permute-start(bf16[16,32,512]{2,1,0:T(8,128)(2,1)} %pad_maximum_fusion.5.refs_3_), channel_id=1, source_target_pairs={{0,32},{4,36},{8,40},{12,44},{16,48},{20,52},{24,56},{28,60},{32,0... | collective-permute-start | bytes 1572872 | tf_op jit(solution)/shard_map/ppermute | solution.py:42
  80.5 27.0 %collective-permute-start.32 = (bf16[4,1024,128]{2,1,0:T(8,128)(2,1)S(1)}, bf16[4,1024,128]{2,1,0:T(8,128)(2,1)S(1)}, u32[]{:S(2)}, u32[]{:S(2)}) collective-permute-start(bf16[4,1024,128]{2,1,0:T(8,128)(2,1)S(1)} %pad_maximum_fusion.q_ref), channel_id=1, source_target_pairs={{0,4},{4,0},{8,12},{12,8},{16,20},{20,16},{24,28},{28,24},{32,36},... | collective-permute-start | bytes 3145736 | tf_op jit(solution)/shard_map/ppermute | solution.py:42
  85.0 13.1 %collective-permute-start.28 = (bf16[16,32,512]{2,1,0:T(8,128)(2,1)}, bf16[16,32,512]{2,1,0:T(8,128)(2,1)}, u32[]{:S(2)}, u32[]{:S(2)}) collective-permute-start(bf16[16,32,512]{2,1,0:T(8,128)(2,1)} %copy-done.2), channel_id=1, source_target_pairs={{0,24},{4,28},{8,16},{12,20},{16,8},{20,12},{24,0},{28,4},{32,56},... | collective-permute-start | bytes 1572872 | tf_op jit(solution)/shard_map/ppermute | solution.py:42
  87.5 10.6 %collective-permute-start.29 = (bf16[16,32,512]{2,1,0:T(8,128)(2,1)}, bf16[16,32,512]{2,1,0:T(8,128)(2,1)}, u32[]{:S(2)}, u32[]{:S(2)}) collective-permute-start(bf16[16,32,512]{2,1,0:T(8,128)(2,1)} %copy-done.4), channel_id=1, source_target_pairs={{0,8},{4,12},{8,0},{12,4},{16,24},{20,28},{24,16},{28,20},{32,40},... | collective-permute-start | bytes 1572872 | tf_op jit(solution)/shard_map/ppermute | solution.py:42
  87.8 12.0 %collective-permute-start.30 = (bf16[16,32,512]{2,1,0:T(8,128)(2,1)}, bf16[16,32,512]{2,1,0:T(8,128)(2,1)}, u32[]{:S(2)}, u32[]{:S(2)}) collective-permute-start(bf16[16,32,512]{2,1,0:T(8,128)(2,1)} %copy-done.6), channel_id=1, source_target_pairs={{0,96},{4,100},{8,104},{12,108},{16,112},{20,116},{24,120},{28,124... | collective-permute-start | bytes 1572872 | tf_op jit(solution)/shard_map/ppermute | solution.py:42
  88.9 11.7 %collective-permute-start.31 = (bf16[16,32,512]{2,1,0:T(8,128)(2,1)}, bf16[16,32,512]{2,1,0:T(8,128)(2,1)}, u32[]{:S(2)}, u32[]{:S(2)}) collective-permute-start(bf16[16,32,512]{2,1,0:T(8,128)(2,1)} %copy-done.8), channel_id=1, source_target_pairs={{0,32},{4,36},{8,40},{12,44},{16,48},{20,52},{24,56},{28,60},{32,0... | collective-permute-start | bytes 1572872 | tf_op jit(solution)/shard_map/ppermute | solution.py:42
  115.4 13.5 %collective-permute-start.38 = (bf16[2,256,512]{2,1,0:T(8,128)(2,1)S(1)}, bf16[2,256,512]{2,1,0:T(8,128)(2,1)S(1)}, u32[]{:S(2)}, u32[]{:S(2)}) collective-permute-start(bf16[2,256,512]{2,1,0:T(8,128)(2,1)S(1)} %get-tuple-element.88), channel_id=1, source_target_pairs={{0,4},{4,0},{8,12},{12,8},{16,20},{20,16},{24,28},{28,24},{32,36},... | collective-permute-start | bytes 1572872 | tf_op jit(solution)/shard_map/ppermute | solution.py:42
  116.0 12.8 %collective-permute-start.39 = (f32[2,8,256]{2,1,0:T(8,128)S(1)}, f32[2,8,256]{2,1,0:T(8,128)S(1)}, u32[]{:S(2)}, u32[]{:S(2)}) collective-permute-start(f32[2,8,256]{2,1,0:T(8,128)S(1)} %get-tuple-element.89), channel_id=1, source_target_pairs={{0,4},{4,0},{8,12},{12,8},{16,20},{20,16},{24,28},{28,24},{32,36},... | collective-permute-start | bytes 49160 | tf_op jit(solution)/shard_map/ppermute | solution.py:42
  121.5 12.9 %collective-permute-start.35 = (bf16[2,288,128]{2,1,0:T(8,128)(2,1)S(1)}, bf16[2,288,128]{2,1,0:T(8,128)(2,1)S(1)}, u32[]{:S(2)}, u32[]{:S(2)}) collective-permute-start(bf16[2,288,128]{2,1,0:T(8,128)(2,1)S(1)} %get-tuple-element.85), channel_id=1, source_target_pairs={{0,1},{1,2},{2,3},{3,0},{4,5},{5,6},{6,7},{7,4},{8,9},{9,10},{10,1... | collective-permute-start | bytes 442376 | tf_op jit(solution)/shard_map/ppermute | solution.py:46
  122.7 13.4 %collective-permute-start.36 = (bf16[2,288,128]{2,1,0:T(8,128)(2,1)S(1)}, bf16[2,288,128]{2,1,0:T(8,128)(2,1)S(1)}, u32[]{:S(2)}, u32[]{:S(2)}) collective-permute-start(bf16[2,288,128]{2,1,0:T(8,128)(2,1)S(1)} %get-tuple-element.86), channel_id=1, source_target_pairs={{0,2},{1,3},{2,0},{3,1},{4,6},{5,7},{6,4},{7,5},{8,10},{9,11},{10,... | collective-permute-start | bytes 442376 | tf_op jit(solution)/shard_map/ppermute | solution.py:46
  (33 other events, 291.2 us)

commit v6 on v5

--- a/solution.py
+++ b/solution.py
@@ -82,7 +82,7 @@
 def one_block(rank, block, base, q_ref, lq_ref, row_ref, table, picked, scores):
     for j in range(PICKS):
         picked[pl.ds(j * ROWS, ROWS), :] = table[row_ref[(base + block) * PICKS + j]]
-    here = pl.ds(pl.multiple_of(block * BLK, BLK), BLK)
+    here = pl.ds(block * BLK, BLK)
     query = jnp.concatenate([q_ref[lax.rem(rank + TP - s, TP), here] for s in range(TP)], axis=1)
     top = jnp.full((BLK, 128), LOW, jnp.float32)
     for n in range(COLS // TILE):
@@ -130,26 +130,28 @@
         copy.wait()
 
 
-def pack(pieces, places):
+def pack(pieces, places, table=None):
+    given = () if table is None else (table,)
+    vmem = pl.BlockSpec(memory_space=pltpu.VMEM)
     return pl.pallas_call(
         functools.partial(pack_kernel, places),
         out_shape=jax.ShapeDtypeStruct((256, ROWS, E), jnp.bfloat16),
-        in_specs=[pl.BlockSpec(memory_space=pl.ANY)] * len(pieces),
-        out_specs=pl.BlockSpec(memory_space=pltpu.VMEM),
+        in_specs=[pl.BlockSpec(memory_space=pl.ANY)] * len(pieces) + [vmem] * len(given),
+        out_specs=vmem,
         scratch_shapes=[pltpu.SemaphoreType.DMA((len(pieces),))],
-        compiler_params=pltpu.CompilerParams(vmem_limit_bytes=12 << 20),
-        cost_estimate=pl.CostEstimate(flops=0, bytes_accessed=16 << 20, transcendentals=0),
+        input_output_aliases={len(pieces): 0} if given else {},
+        compiler_params=pltpu.CompilerParams(vmem_limit_bytes=20 << 20),
+        cost_estimate=pl.CostEstimate(flops=0, bytes_accessed=8 << 20, transcendentals=0),
         name="pack",
-    )(*pieces)
+    )(*pieces, *given)
 
 
 def first_kernel(start, row_ref, rank_ref, q_ref, lq_ref, table, *refs):
     out_ref, stat_ref, picked, scores = refs
 
-    @pl.loop(0, PART)
-    def _(n):
+    for n in range(PART):
         top, total, acc = one_block(
-            rank_ref[0], start + n, 0, q_ref, lq_ref, row_ref, table, picked, scores
+            rank_ref[0], start + n, 0, q_ref, lq_ref, row_ref, table, picked.at[n], scores.at[n]
         )
         out_ref[n] = acc.astype(jnp.bfloat16)
         stat_ref[n] = rows_of(top, total)
@@ -174,10 +176,9 @@
     outs = refs[3:7]
     picked, scores, quarters = refs[7:]
 
-    @pl.loop(0, PART)
-    def _(n):
+    for n in range(PART):
         top, total, acc = one_block(
-            rank_ref[0], start + n, 2 * PART, q_ref, lq_ref, row_ref, table, picked, scores
+            rank_ref[0], start + n, 2 * PART, q_ref, lq_ref, row_ref, table, picked.at[n], scores.at[n]
         )
         theirs = jnp.transpose(jnp.concatenate([other_stat_ref[n]] * 16, axis=0))
         their_top, their_total = theirs[:, 0:1], theirs[:, 1:2]
@@ -203,8 +204,8 @@
         out_specs=(vmem,) * len(outs),
         out_shape=outs,
         scratch_shapes=[
-            pltpu.VMEM((COLS, E), jnp.bfloat16),
-            pltpu.VMEM((BLK, COLS), jnp.float32),
+            pltpu.VMEM((PART, COLS, E), jnp.bfloat16),
+            pltpu.VMEM((PART, BLK, COLS), jnp.float32),
         ]
         + scratch,
         compiler_params=pltpu.CompilerParams(vmem_limit_bytes=32 << 20),
@@ -285,16 +286,20 @@
     queries = [query]
     for step in range(3):
         got = [send(h, **{st[step][0]: st[step][1]}) for h, st in zip(held, STREAMS)]
-        got = together(*got, send_x(query, step + 1), query)
-        queries.append(got[4])
-        query = got[5]
+        if step > 0:
+            queries.append(send_x(query, step))
+            got.append(queries.pop())
+        got = together(*got, query)
+        query = got.pop()
+        queries += got[4:]
         if step < 2:
             held = together(*[jnp.concatenate([h, g]) for h, g in zip(held, got)])
+    queries.append(send_x(query, 3))
     third = got[:4]
     fourth = [send(h, **{st[3][0]: st[3][1]}) for h, st in zip(held, STREAMS)]
     fifth = [send(h, **{st[3][0]: st[3][1]}) for h, st in zip(third, STREAMS)]
-    places = (0, 4, 8, 12, 1, 5, 9, 13, 2, 6, 10, 14, 3, 7, 11, 15)
-    table = pack(held + third + fourth + fifth, places)
+    table = pack(held + third, (0, 4, 8, 12, 1, 5, 9, 13))
+    table = pack(fourth + fifth, (2, 6, 10, 14, 3, 7, 11, 15), table)
     return table, jnp.stack(queries)
 
 
@@ -348,11 +353,9 @@
     near = owner % 2 == core
     rows = jnp.where(near, at_z * 4 + at_y, 128 // 4 + at_y * 4 + at_z)
     rows = (rows * 4 + late * 64 + slot % 4).astype(jnp.int32)
-    log_table = (jnp.log(sample_counts.astype(jnp.float32)) * LOG2E).reshape(
-        total_blocks, TP * 2, ROWS
-    )
-    my_log = lax.dynamic_index_in_dim(log_table, rank * 2 + core, 1, keepdims=False)
-    lq = my_log[home].reshape(2 * qblocks, COLS)
+    count_rows = sample_counts.reshape(2 * total_blocks, 128)[home.reshape(-1) * 2 + rank // 2]
+    counts = lax.dynamic_slice_in_dim(count_rows, (rank % 2 * 2 + core) * ROWS, ROWS, 1)
+    lq = (jnp.log(counts.astype(jnp.float32)) * LOG2E).reshape(2 * qblocks, COLS)
 
     rows = rows.reshape(-1)
     table, pos_part, rows, lq = together(table, pos_part, rows, lq)

time: 146 us -> 140 us (0.959)
  starting transfers between devices: 54.1 us -> 49.1 us
  waiting for transfers between devices: 45.6 us -> 49.4 us
  local copies, waits for them, and re-layouts: 15.3 us -> 12 us
  other arithmetic: 7.38 us -> 5.27 us
    ppermute x15, waiting for transfers between devices: 23.3 us -> 30.9 us  [send_x(): return lax.ppermute(value, 'tp', [(i, (i + d) % TP) for i in range(TP)])]
    ppermute x15, starting transfers between devices: 26.4 us -> 20.5 us  [send_x(): return lax.ppermute(value, 'tp', [(i, (i + d) % TP) for i in range(TP)])]
    ppermute x28, waiting for transfers between devices: 22.3 us -> 18.5 us  [send(): return lax.ppermute(value, 'cat', cat_perm(y, z, c))]
    reshape x2 -> x1, local copies, waits for them, and re-layouts: 3.33 us -> 1.09 us  [local(): (jnp.log(counts.astype(jnp.float32)) * LOG2E).reshape(2 * qblocks, COLS)]
    dynamic_slice x1 -> x0, local copies, waits for them, and re-layouts: 1.99 us -> none  [local(): lax.dynamic_index_in_dim(log_table, rank * 2 + core, 1, keepdims=False)]
    pallas_call x1 -> x2, Pallas kernels: 2.71 us -> 3.57 us  [pack(): pl.pallas_call(functools.partial(pack_kernel, places), out_shape=jax.Shap...]
    unnamed x28 -> x26, local copies, waits for them, and re-layouts: 5.83 us -> 6.64 us
  transfers between devices with their start and end apart: 43 -> 43, of which waited for: 19 -> 18; matrix products, arithmetic and copies ran while one was open for 9% -> 5% of each run, Pallas kernels for 10% -> 10%
where the time goes in v6:
time: 140 us; the launch traced here: 138 us
  waiting for transfers between devices  49.4 us (35%)
  starting transfers between devices  49.1 us (35%)
  Pallas kernels  20.9 us (15%)
  local copies, waits for them, and re-layouts  12 us (9%)
  other arithmetic  5.27 us (4%)
    ppermute x15, waiting for transfers between devices, send_x(): return lax.ppermute(value, 'tp', [(i, (i + d) % TP) for i in range(TP)])  30.9 us
    ppermute x28, starting transfers between devices, send(): return lax.ppermute(value, 'cat', cat_perm(y, z, c))  28.7 us
    ppermute x15, starting transfers between devices, send_x(): return lax.ppermute(value, 'tp', [(i, (i + d) % TP) for i in range(TP)])  20.5 us
    ppermute x28, waiting for transfers between devices, send(): return lax.ppermute(value, 'cat', cat_perm(y, z, c))  18.5 us
    pallas_call x4, Pallas kernels, attend(): pl.pallas_call(functools.partial(body, start), in_specs=[pl.BlockSpec(mem...  14.3 us
    unnamed x26, local copies, waits for them, and re-layouts  6.64 us
    pallas_call x2, Pallas kernels, pack(): pl.pallas_call(functools.partial(pack_kernel, places), out_shape=jax.Shap...  3.57 us
  transfers between devices with their start and end apart: 43, of which 18 were waited for; matrix products, arithmetic and copies ran while one was open for 5% of the time, Pallas kernels for 10%

profile of v6, /device:TPU:0, one launch (start us, length us, event | category | flops | bytes accessed | tf_op | source)
XLA Modules:
  0.0 137.9 jit_solution(12636442202128297355)
XLA Ops:
  7.9 2.7 %collective-permute-start.5 = (bf16[128,512]{1,0:T(8,128)(2,1)S(1)}, bf16[128,512]{1,0:T(8,128)(2,1)S(1)}, u32[]{:S(2)}, u32[]{:S(2)}) collective-permute-start(bf16[128,512]{1,0:T(8,128)(2,1)S(1)} %constant_dynamic-slice_fusion.refs_4_), channel_id=1, source_target_pairs={{0,2},{1,3},{2,0},{3,1},{4,6},{5,7},{6,4},{7,5},{8,10},{9,11},{10,... | collective-permute-start | bytes 393224 | tf_op jit(solution)/shard_map/ppermute | solution.py:46
  12.1 4.5 %collective-permute-done.4.refs_5_ = bf16[128,512]{1,0:T(8,128)(2,1)S(1)} collective-permute-done((bf16[128,512]{1,0:T(8,128)(2,1)S(1)}, bf16[128,512]{1,0:T(8,128)(2,1)S(1)}, u32[]{:S(2)}, u32[]{:S(2)}) %collective-permute-start.4) | collective-permute-done | bytes 131104 | tf_op jit(solution)/shard_map/ppermute | solution.py:46
  16.6 3.9 %collective-permute-done.5.refs_6_ = bf16[128,512]{1,0:T(8,128)(2,1)S(1)} collective-permute-done((bf16[128,512]{1,0:T(8,128)(2,1)S(1)}, bf16[128,512]{1,0:T(8,128)(2,1)S(1)}, u32[]{:S(2)}, u32[]{:S(2)}) %collective-permute-start.5) | collective-permute-done | bytes 131104 | tf_op jit(solution)/shard_map/ppermute | solution.py:46
  24.6 6.3 %collective-permute-done.2.refs_2_ = bf16[512,256]{1,0:T(8,128)(2,1)S(1)} collective-permute-done((bf16[512,256]{1,0:T(8,128)(2,1)S(1)}, bf16[512,256]{1,0:T(8,128)(2,1)S(1)}, u32[]{:S(2)}, u32[]{:S(2)}) %collective-permute-start.2) | collective-permute-done | bytes 262176 | tf_op jit(solution)/shard_map/ppermute | solution.py:46
  33.9 2.2 %collective-permute-start.10 = (bf16[4,32,512]{2,1,0:T(8,128)(2,1)S(1)}, bf16[4,32,512]{2,1,0:T(8,128)(2,1)S(1)}, u32[]{:S(2)}, u32[]{:S(2)}) collective-permute-start(bf16[4,32,512]{2,1,0:T(8,128)(2,1)S(1)} %get-tuple-element.104), channel_id=1, source_target_pairs={{0,96},{4,100},{8,104},{12,108},{16,112},{20,116},{24,120},{28,124... | collective-permute-start | bytes 393224 | tf_op jit(solution)/shard_map/ppermute | solution.py:42
  38.0 2.5 %collective-permute-start.12 = (bf16[4,32,512]{2,1,0:T(8,128)(2,1)S(1)}, bf16[4,32,512]{2,1,0:T(8,128)(2,1)S(1)}, u32[]{:S(2)}, u32[]{:S(2)}) collective-permute-start(bf16[4,32,512]{2,1,0:T(8,128)(2,1)S(1)} %get-tuple-element.102), channel_id=1, source_target_pairs={{0,24},{4,28},{8,16},{12,20},{16,8},{20,12},{24,0},{28,4},{32,56},... | collective-permute-start | bytes 393224 | tf_op jit(solution)/shard_map/ppermute | solution.py:42
  41.0 3.1 %collective-permute-done.12 = bf16[4,32,512]{2,1,0:T(8,128)(2,1)S(1)} collective-permute-done((bf16[4,32,512]{2,1,0:T(8,128)(2,1)S(1)}, bf16[4,32,512]{2,1,0:T(8,128)(2,1)S(1)}, u32[]{:S(2)}, u32[]{:S(2)}) %collective-permute-start.12) | collective-permute-done | bytes 131104 | tf_op jit(solution)/shard_map/ppermute | solution.py:42
  45.4 2.5 %collective-permute-start.15 = (bf16[8,32,512]{2,1,0:T(8,128)(2,1)S(1)}, bf16[8,32,512]{2,1,0:T(8,128)(2,1)S(1)}, u32[]{:S(2)}, u32[]{:S(2)}) collective-permute-start(bf16[8,32,512]{2,1,0:T(8,128)(2,1)S(1)} %get-tuple-element.58), channel_id=1, source_target_pairs={{0,24},{4,28},{8,16},{12,20},{16,8},{20,12},{24,0},{28,4},{32,56},... | collective-permute-start | bytes 786440 | tf_op jit(solution)/shard_map/ppermute | solution.py:42
  48.4 3.5 %collective-permute-done.13 = bf16[8,32,512]{2,1,0:T(8,128)(2,1)S(1)} collective-permute-done((bf16[8,32,512]{2,1,0:T(8,128)(2,1)S(1)}, bf16[8,32,512]{2,1,0:T(8,128)(2,1)S(1)}, u32[]{:S(2)}, u32[]{:S(2)}) %collective-permute-start.13) | collective-permute-done | bytes 262176 | tf_op jit(solution)/shard_map/ppermute | solution.py:42
  60.0 2.0 %collective-permute-start.24 = (bf16[16,32,512]{2,1,0:T(8,128)(2,1)}, bf16[16,32,512]{2,1,0:T(8,128)(2,1)S(1)}, u32[]{:S(2)}, u32[]{:S(2)}) collective-permute-start(bf16[16,32,512]{2,1,0:T(8,128)(2,1)} %pad_maximum_fusion.4.refs_2_), channel_id=1, source_target_pairs={{0,32},{4,36},{8,40},{12,44},{16,48},{20,52},{24,56},{28,60},{32,0... | collective-permute-start | bytes 1572872 | tf_op jit(solution)/shard_map/ppermute | solution.py:42
  62.0 2.2 %collective-permute-start.25 = (bf16[16,32,512]{2,1,0:T(8,128)(2,1)}, bf16[16,32,512]{2,1,0:T(8,128)(2,1)S(1)}, u32[]{:S(2)}, u32[]{:S(2)}) collective-permute-start(bf16[16,32,512]{2,1,0:T(8,128)(2,1)} %pad_maximum_fusion.5.refs_3_), channel_id=1, source_target_pairs={{0,96},{4,100},{8,104},{12,108},{16,112},{20,116},{24,120},{28,124... | collective-permute-start | bytes 1572872 | tf_op jit(solution)/shard_map/ppermute | solution.py:42
  64.8 7.3 %collective-permute-done.26 = bf16[1024,128]{1,0:T(8,128)(2,1)S(1)} collective-permute-done((bf16[1024,128]{1,0:T(8,128)(2,1)S(1)}, bf16[1024,128]{1,0:T(8,128)(2,1)S(1)}, u32[]{:S(2)}, u32[]{:S(2)}) %collective-permute-start.26) | collective-permute-done | bytes 262176 | tf_op jit(solution)/shard_map/ppermute | solution.py:46
  75.6 2.6 %collective-permute-start.18 = (bf16[16,32,512]{2,1,0:T(8,128)(2,1)S(1)}, bf16[16,32,512]{2,1,0:T(8,128)(2,1)}, u32[]{:S(2)}, u32[]{:S(2)}) collective-permute-start(bf16[16,32,512]{2,1,0:T(8,128)(2,1)S(1)} %pad_maximum_fusion.2.refs_0_), channel_id=1, source_target_pairs={{0,24},{4,28},{8,16},{12,20},{16,8},{20,12},{24,0},{28,4},{32,56},... | collective-permute-start | bytes 1572872 | tf_op jit(solution)/shard_map/ppermute | solution.py:42
  81.7 4.5 %collective-permute-done.18.refs_0_ = bf16[16,32,512]{2,1,0:T(8,128)(2,1)} collective-permute-done((bf16[16,32,512]{2,1,0:T(8,128)(2,1)S(1)}, bf16[16,32,512]{2,1,0:T(8,128)(2,1)}, u32[]{:S(2)}, u32[]{:S(2)}) %collective-permute-start.18) | collective-permute-done | bytes 524320 | tf_op jit(solution)/shard_map/ppermute | solution.py:42
  86.2 2.5 %collective-permute-start.27 = (bf16[16,32,512]{2,1,0:T(8,128)(2,1)}, bf16[16,32,512]{2,1,0:T(8,128)(2,1)}, u32[]{:S(2)}, u32[]{:S(2)}) collective-permute-start(bf16[16,32,512]{2,1,0:T(8,128)(2,1)} %copy-done.3), channel_id=1, source_target_pairs={{0,24},{4,28},{8,16},{12,20},{16,8},{20,12},{24,0},{28,4},{32,56},... | collective-permute-start | bytes 1572872 | tf_op jit(solution)/shard_map/ppermute | solution.py:42
  90.9 2.6 %gather_fusion = s32[512,128]{1,0:T(8,128)} fusion(s32[512,128]{1,0:T(8,128)} %bitcast.32, s32[1024]{0:T(1024)S(1)} %pad_clamp_fusion), kind=kCustom, calls=%fused_computation | custom fusion | bytes 526336 | tf_op jit(solution)/shard_map/gather | solution.py:356
  102.0 2.2 %pack.3.table = bf16[256,32,512]{2,1,0:T(8,128)(2,1)S(1)} custom-call(bf16[16,32,512]{2,1,0:T(8,128)(2,1)} %collective-permute-done.18.refs_0_, bf16[16,32,512]{2,1,0:T(8,128)(2,1)} %collective-permute-done.19.refs_1_, bf16[16,32,512]{2,1,0:T(8,128)(2,1)} %collective-permute-done.20.refs_2_, ...), custom_call_target="tpu_custom_call", output_to_operand_aliasing={{}: (8, {})} | custom-call | bytes 8388608 | tf_op jit(solution)/shard_map/pack/pallas_call | solution.py:136
  104.3 3.4 %attend_other.2 = (bf16[2,256,512]{2,1,0:T(8,128)(2,1)S(1)}, f32[2,8,256]{2,1,0:T(8,128)S(1)}) custom-call(s32[512]{0:T(512)S(1)} %fusion.9.row_ref, s32[1]{0:T(128)} %bitcast.15.rank_ref, bf16[4,1024,128]{2,1,0:T(8,128)(2,1)S(1)} %collective-permute-done.32.q_ref, f32[8,2048]{1,0:T(8,128)S(1)} %reshape.91.lq_ref, bf16[256,32,512]{2,1,0:T(8,128)(2,1)S(1)} %pack.3.table), custom_call_target="tpu_custom_call" | custom-call | flops 2147483648 | bytes 2097152 | tf_op jit(solution)/shard_map/attend_other/pallas_call | solution.py:201
  107.8 3.4 %attend_other.3 = (bf16[2,256,512]{2,1,0:T(8,128)(2,1)S(1)}, f32[2,8,256]{2,1,0:T(8,128)S(1)}) custom-call(s32[512]{0:T(512)S(1)} %fusion.9.row_ref, s32[1]{0:T(128)} %bitcast.15.rank_ref, bf16[4,1024,128]{2,1,0:T(8,128)(2,1)S(1)} %collective-permute-done.32.q_ref, f32[8,2048]{1,0:T(8,128)S(1)} %reshape.91.lq_ref, bf16[256,32,512]{2,1,0:T(8,128)(2,1)S(1)} %pack.3.table), custom_call_target="tpu_custom_call" | custom-call | flops 2147483648 | bytes 2097152 | tf_op jit(solution)/shard_map/attend_other/pallas_call | solution.py:201
  113.4 3.7 %attend_own.2 = (bf16[2,288,128]{2,1,0:T(8,128)(2,1)S(1)}, bf16[2,288,128]{2,1,0:T(8,128)(2,1)S(1)}, bf16[2,288,128]{2,1,0:T(8,128)(2,1)S(1)}, bf16[2,288,128]{2,1,0:T(8,128)(2,1)S(1)}) custom-call(s32[512]{0:T(512)S(1)} %fusion.9.row_ref, s32[1]{0:T(128)} %bitcast.15.rank_ref, bf16[4,1024,128]{2,1,0:T(8,128)(2,1)S(1)} %pad_maximum_fusion.q_ref, ...), custom_call_target="tpu_custom_call" | custom-call | flops 2147483648 | bytes 2097152 | tf_op jit(solution)/shard_map/attend_own/pallas_call | solution.py:201
  119.0 2.8 %collective-permute-start.37 = (bf16[2,288,128]{2,1,0:T(8,128)(2,1)S(1)}, bf16[2,288,128]{2,1,0:T(8,128)(2,1)S(1)}, u32[]{:S(2)}, u32[]{:S(2)}) collective-permute-start(bf16[2,288,128]{2,1,0:T(8,128)(2,1)S(1)} %get-tuple-element.87), channel_id=1, source_target_pairs={{0,3},{1,0},{2,1},{3,2},{4,7},{5,4},{6,5},{7,6},{8,11},{9,8},{10,9... | collective-permute-start | bytes 442376 | tf_op jit(solution)/shard_map/ppermute | solution.py:46
  121.8 3.7 %attend_own.3 = (bf16[2,288,128]{2,1,0:T(8,128)(2,1)S(1)}, bf16[2,288,128]{2,1,0:T(8,128)(2,1)S(1)}, bf16[2,288,128]{2,1,0:T(8,128)(2,1)S(1)}, bf16[2,288,128]{2,1,0:T(8,128)(2,1)S(1)}) custom-call(s32[512]{0:T(512)S(1)} %fusion.9.row_ref, s32[1]{0:T(128)} %bitcast.15.rank_ref, bf16[4,1024,128]{2,1,0:T(8,128)(2,1)S(1)} %pad_maximum_fusion.q_ref, ...), custom_call_target="tpu_custom_call" | custom-call | flops 2147483648 | bytes 2097152 | tf_op jit(solution)/shard_map/attend_own/pallas_call | solution.py:201
  125.6 2.8 %collective-permute-start.41 = (bf16[2,288,128]{2,1,0:T(8,128)(2,1)S(1)}, bf16[2,288,128]{2,1,0:T(8,128)(2,1)S(1)}, u32[]{:S(2)}, u32[]{:S(2)}) collective-permute-start(bf16[2,288,128]{2,1,0:T(8,128)(2,1)S(1)} %get-tuple-element.92), channel_id=1, source_target_pairs={{0,2},{1,3},{2,0},{3,1},{4,6},{5,7},{6,4},{7,5},{8,10},{9,11},{10,... | collective-permute-start | bytes 442376 | tf_op jit(solution)/shard_map/ppermute | solution.py:46
  129.8 5.7 %collective-permute-done.40.refs_5_ = bf16[2,288,128]{2,1,0:T(8,128)(2,1)S(1)} collective-permute-done((bf16[2,288,128]{2,1,0:T(8,128)(2,1)S(1)}, bf16[2,288,128]{2,1,0:T(8,128)(2,1)S(1)}, u32[]{:S(2)}, u32[]{:S(2)}) %collective-permute-start.40) | collective-permute-done | bytes 147488 | tf_op jit(solution)/shard_map/ppermute | solution.py:46
  (124 shorter events, 53.9 us)
Async XLA Ops:
  4.2 16.4 %collective-permute-start.1 = (bf16[512,256]{1,0:T(8,128)(2,1)S(1)}, bf16[512,256]{1,0:T(8,128)(2,1)S(1)}, u32[]{:S(2)}, u32[]{:S(2)}) collective-permute-start(bf16[512,256]{1,0:T(8,128)(2,1)S(1)} %bitcast.39), channel_id=1, source_target_pairs={{0,1},{1,2},{2,3},{3,0},{4,5},{5,6},{6,7},{7,4},{8,9},{9,10},{10,1... | collective-permute-start | bytes 786440 | tf_op jit(solution)/shard_map/ppermute | solution.py:46
  5.8 14.8 %collective-permute-start.3 = (bf16[512,256]{1,0:T(8,128)(2,1)S(1)}, bf16[512,256]{1,0:T(8,128)(2,1)S(1)}, u32[]{:S(2)}, u32[]{:S(2)}) collective-permute-start(bf16[512,256]{1,0:T(8,128)(2,1)S(1)} %bitcast.38), channel_id=1, source_target_pairs={{0,3},{1,0},{2,1},{3,2},{4,7},{5,4},{6,5},{7,6},{8,11},{9,8},{10,9... | collective-permute-start | bytes 786440 | tf_op jit(solution)/shard_map/ppermute | solution.py:46
  7.9 12.6 %collective-permute-start.5 = (bf16[128,512]{1,0:T(8,128)(2,1)S(1)}, bf16[128,512]{1,0:T(8,128)(2,1)S(1)}, u32[]{:S(2)}, u32[]{:S(2)}) collective-permute-start(bf16[128,512]{1,0:T(8,128)(2,1)S(1)} %constant_dynamic-slice_fusion.refs_4_), channel_id=1, source_target_pairs={{0,2},{1,3},{2,0},{3,1},{4,6},{5,7},{6,4},{7,5},{8,10},{9,11},{10,... | collective-permute-start | bytes 393224 | tf_op jit(solution)/shard_map/ppermute | solution.py:46
  20.6 10.3 %collective-permute-start.7 = (bf16[4,128,512]{2,1,0:T(8,128)(2,1)S(1)}, bf16[4,128,512]{2,1,0:T(8,128)(2,1)S(1)}, u32[]{:S(2)}, u32[]{:S(2)}) collective-permute-start(bf16[4,128,512]{2,1,0:T(8,128)(2,1)S(1)} %pad_maximum_fusion.1), channel_id=1, source_target_pairs={{0,4},{4,0},{8,12},{12,8},{16,20},{20,16},{24,28},{28,24},{32,36},... | collective-permute-start | bytes 1572872 | tf_op jit(solution)/shard_map/ppermute | solution.py:42
  20.7 10.2 %collective-permute-start.2 = (bf16[512,256]{1,0:T(8,128)(2,1)S(1)}, bf16[512,256]{1,0:T(8,128)(2,1)S(1)}, u32[]{:S(2)}, u32[]{:S(2)}) collective-permute-start(bf16[512,256]{1,0:T(8,128)(2,1)S(1)} %bitcast.37), channel_id=1, source_target_pairs={{0,2},{1,3},{2,0},{3,1},{4,6},{5,7},{6,4},{7,5},{8,10},{9,11},{10,... | collective-permute-start | bytes 786440 | tf_op jit(solution)/shard_map/ppermute | solution.py:46
  57.3 14.8 %collective-permute-start.22 = (bf16[16,32,512]{2,1,0:T(8,128)(2,1)S(1)}, bf16[16,32,512]{2,1,0:T(8,128)(2,1)S(1)}, u32[]{:S(2)}, u32[]{:S(2)}) collective-permute-start(bf16[16,32,512]{2,1,0:T(8,128)(2,1)S(1)} %pad_maximum_fusion.2.refs_0_), channel_id=1, source_target_pairs={{0,8},{4,12},{8,0},{12,4},{16,24},{20,28},{24,16},{28,20},{32,40},... | collective-permute-start | bytes 1572872 | tf_op jit(solution)/shard_map/ppermute | solution.py:42
  59.3 12.8 %collective-permute-start.23 = (bf16[16,32,512]{2,1,0:T(8,128)(2,1)S(1)}, bf16[16,32,512]{2,1,0:T(8,128)(2,1)S(1)}, u32[]{:S(2)}, u32[]{:S(2)}) collective-permute-start(bf16[16,32,512]{2,1,0:T(8,128)(2,1)S(1)} %pad_maximum_fusion.3.refs_1_), channel_id=1, source_target_pairs={{0,24},{4,28},{8,16},{12,20},{16,8},{20,12},{24,0},{28,4},{32,56},... | collective-permute-start | bytes 1572872 | tf_op jit(solution)/shard_map/ppermute | solution.py:42
  60.0 12.9 %collective-permute-start.24 = (bf16[16,32,512]{2,1,0:T(8,128)(2,1)}, bf16[16,32,512]{2,1,0:T(8,128)(2,1)S(1)}, u32[]{:S(2)}, u32[]{:S(2)}) collective-permute-start(bf16[16,32,512]{2,1,0:T(8,128)(2,1)} %pad_maximum_fusion.4.refs_2_), channel_id=1, source_target_pairs={{0,32},{4,36},{8,40},{12,44},{16,48},{20,52},{24,56},{28,60},{32,0... | collective-permute-start | bytes 1572872 | tf_op jit(solution)/shard_map/ppermute | solution.py:42
  62.0 11.7 %collective-permute-start.25 = (bf16[16,32,512]{2,1,0:T(8,128)(2,1)}, bf16[16,32,512]{2,1,0:T(8,128)(2,1)S(1)}, u32[]{:S(2)}, u32[]{:S(2)}) collective-permute-start(bf16[16,32,512]{2,1,0:T(8,128)(2,1)} %pad_maximum_fusion.5.refs_3_), channel_id=1, source_target_pairs={{0,96},{4,100},{8,104},{12,108},{16,112},{20,116},{24,120},{28,124... | collective-permute-start | bytes 1572872 | tf_op jit(solution)/shard_map/ppermute | solution.py:42
  75.6 10.6 %collective-permute-start.18 = (bf16[16,32,512]{2,1,0:T(8,128)(2,1)S(1)}, bf16[16,32,512]{2,1,0:T(8,128)(2,1)}, u32[]{:S(2)}, u32[]{:S(2)}) collective-permute-start(bf16[16,32,512]{2,1,0:T(8,128)(2,1)S(1)} %pad_maximum_fusion.2.refs_0_), channel_id=1, source_target_pairs={{0,24},{4,28},{8,16},{12,20},{16,8},{20,12},{24,0},{28,4},{32,56},... | collective-permute-start | bytes 1572872 | tf_op jit(solution)/shard_map/ppermute | solution.py:42
  78.2 10.5 %collective-permute-start.19 = (bf16[16,32,512]{2,1,0:T(8,128)(2,1)S(1)}, bf16[16,32,512]{2,1,0:T(8,128)(2,1)}, u32[]{:S(2)}, u32[]{:S(2)}) collective-permute-start(bf16[16,32,512]{2,1,0:T(8,128)(2,1)S(1)} %pad_maximum_fusion.3.refs_1_), channel_id=1, source_target_pairs={{0,8},{4,12},{8,0},{12,4},{16,24},{20,28},{24,16},{28,20},{32,40},... | collective-permute-start | bytes 1572872 | tf_op jit(solution)/shard_map/ppermute | solution.py:42
  78.2 11.0 %collective-permute-start.20 = (bf16[16,32,512]{2,1,0:T(8,128)(2,1)}, bf16[16,32,512]{2,1,0:T(8,128)(2,1)}, u32[]{:S(2)}, u32[]{:S(2)}) collective-permute-start(bf16[16,32,512]{2,1,0:T(8,128)(2,1)} %pad_maximum_fusion.4.refs_2_), channel_id=1, source_target_pairs={{0,96},{4,100},{8,104},{12,108},{16,112},{20,116},{24,120},{28,124... | collective-permute-start | bytes 1572872 | tf_op jit(solution)/shard_map/ppermute | solution.py:42
  79.6 11.3 %collective-permute-start.21 = (bf16[16,32,512]{2,1,0:T(8,128)(2,1)}, bf16[16,32,512]{2,1,0:T(8,128)(2,1)}, u32[]{:S(2)}, u32[]{:S(2)}) collective-permute-start(bf16[16,32,512]{2,1,0:T(8,128)(2,1)} %pad_maximum_fusion.5.refs_3_), channel_id=1, source_target_pairs={{0,32},{4,36},{8,40},{12,44},{16,48},{20,52},{24,56},{28,60},{32,0... | collective-permute-start | bytes 1572872 | tf_op jit(solution)/shard_map/ppermute | solution.py:42
  81.1 23.2 %collective-permute-start.32 = (bf16[4,1024,128]{2,1,0:T(8,128)(2,1)S(1)}, bf16[4,1024,128]{2,1,0:T(8,128)(2,1)S(1)}, u32[]{:S(2)}, u32[]{:S(2)}) collective-permute-start(bf16[4,1024,128]{2,1,0:T(8,128)(2,1)S(1)} %pad_maximum_fusion.q_ref), channel_id=1, source_target_pairs={{0,4},{4,0},{8,12},{12,8},{16,20},{20,16},{24,28},{28,24},{32,36},... | collective-permute-start | bytes 3145736 | tf_op jit(solution)/shard_map/ppermute | solution.py:42
  86.2 15.8 %collective-permute-start.27 = (bf16[16,32,512]{2,1,0:T(8,128)(2,1)}, bf16[16,32,512]{2,1,0:T(8,128)(2,1)}, u32[]{:S(2)}, u32[]{:S(2)}) collective-permute-start(bf16[16,32,512]{2,1,0:T(8,128)(2,1)} %copy-done.3), channel_id=1, source_target_pairs={{0,24},{4,28},{8,16},{12,20},{16,8},{20,12},{24,0},{28,4},{32,56},... | collective-permute-start | bytes 1572872 | tf_op jit(solution)/shard_map/ppermute | solution.py:42
  88.7 13.3 %collective-permute-start.28 = (bf16[16,32,512]{2,1,0:T(8,128)(2,1)}, bf16[16,32,512]{2,1,0:T(8,128)(2,1)}, u32[]{:S(2)}, u32[]{:S(2)}) collective-permute-start(bf16[16,32,512]{2,1,0:T(8,128)(2,1)} %copy-done.5), channel_id=1, source_target_pairs={{0,8},{4,12},{8,0},{12,4},{16,24},{20,28},{24,16},{28,20},{32,40},... | collective-permute-start | bytes 1572872 | tf_op jit(solution)/shard_map/ppermute | solution.py:42
  89.2 12.9 %collective-permute-start.29 = (bf16[16,32,512]{2,1,0:T(8,128)(2,1)}, bf16[16,32,512]{2,1,0:T(8,128)(2,1)}, u32[]{:S(2)}, u32[]{:S(2)}) collective-permute-start(bf16[16,32,512]{2,1,0:T(8,128)(2,1)} %copy-done.7), channel_id=1, source_target_pairs={{0,96},{4,100},{8,104},{12,108},{16,112},{20,116},{24,120},{28,124... | collective-permute-start | bytes 1572872 | tf_op jit(solution)/shard_map/ppermute | solution.py:42
  90.8 11.2 %collective-permute-start.30 = (bf16[16,32,512]{2,1,0:T(8,128)(2,1)}, bf16[16,32,512]{2,1,0:T(8,128)(2,1)}, u32[]{:S(2)}, u32[]{:S(2)}) collective-permute-start(bf16[16,32,512]{2,1,0:T(8,128)(2,1)} %copy-done.9), channel_id=1, source_target_pairs={{0,32},{4,36},{8,40},{12,44},{16,48},{20,52},{24,56},{28,60},{32,0... | collective-permute-start | bytes 1572872 | tf_op jit(solution)/shard_map/ppermute | solution.py:42
  111.3 10.5 %collective-permute-start.38 = (bf16[2,256,512]{2,1,0:T(8,128)(2,1)S(1)}, bf16[2,256,512]{2,1,0:T(8,128)(2,1)S(1)}, u32[]{:S(2)}, u32[]{:S(2)}) collective-permute-start(bf16[2,256,512]{2,1,0:T(8,128)(2,1)S(1)} %get-tuple-element.88), channel_id=1, source_target_pairs={{0,4},{4,0},{8,12},{12,8},{16,20},{20,16},{24,28},{28,24},{32,36},... | collective-permute-start | bytes 1572872 | tf_op jit(solution)/shard_map/ppermute | solution.py:42
  117.1 11.2 %collective-permute-start.35 = (bf16[2,288,128]{2,1,0:T(8,128)(2,1)S(1)}, bf16[2,288,128]{2,1,0:T(8,128)(2,1)S(1)}, u32[]{:S(2)}, u32[]{:S(2)}) collective-permute-start(bf16[2,288,128]{2,1,0:T(8,128)(2,1)S(1)} %get-tuple-element.85), channel_id=1, source_target_pairs={{0,1},{1,2},{2,3},{3,0},{4,5},{5,6},{6,7},{7,4},{8,9},{9,10},{10,1... | collective-permute-start | bytes 442376 | tf_op jit(solution)/shard_map/ppermute | solution.py:46
  119.0 10.8 %collective-permute-start.36 = (bf16[2,288,128]{2,1,0:T(8,128)(2,1)S(1)}, bf16[2,288,128]{2,1,0:T(8,128)(2,1)S(1)}, u32[]{:S(2)}, u32[]{:S(2)}) collective-permute-start(bf16[2,288,128]{2,1,0:T(8,128)(2,1)S(1)} %get-tuple-element.86), channel_id=1, source_target_pairs={{0,2},{1,3},{2,0},{3,1},{4,6},{5,7},{6,4},{7,5},{8,10},{9,11},{10,... | collective-permute-start | bytes 442376 | tf_op jit(solution)/shard_map/ppermute | solution.py:46
  119.0 10.8 %collective-permute-start.37 = (bf16[2,288,128]{2,1,0:T(8,128)(2,1)S(1)}, bf16[2,288,128]{2,1,0:T(8,128)(2,1)S(1)}, u32[]{:S(2)}, u32[]{:S(2)}) collective-permute-start(bf16[2,288,128]{2,1,0:T(8,128)(2,1)S(1)} %get-tuple-element.87), channel_id=1, source_target_pairs={{0,3},{1,0},{2,1},{3,2},{4,7},{5,4},{6,5},{7,6},{8,11},{9,8},{10,9... | collective-permute-start | bytes 442376 | tf_op jit(solution)/shard_map/ppermute | solution.py:46
  125.5 10.0 %collective-permute-start.40 = (bf16[2,288,128]{2,1,0:T(8,128)(2,1)S(1)}, bf16[2,288,128]{2,1,0:T(8,128)(2,1)S(1)}, u32[]{:S(2)}, u32[]{:S(2)}) collective-permute-start(bf16[2,288,128]{2,1,0:T(8,128)(2,1)S(1)} %get-tuple-element.91), channel_id=1, source_target_pairs={{0,1},{1,2},{2,3},{3,0},{4,5},{5,6},{6,7},{7,4},{8,9},{9,10},{10,1... | collective-permute-start | bytes 442376 | tf_op jit(solution)/shard_map/ppermute | solution.py:46
  125.6 9.9 %collective-permute-start.41 = (bf16[2,288,128]{2,1,0:T(8,128)(2,1)S(1)}, bf16[2,288,128]{2,1,0:T(8,128)(2,1)S(1)}, u32[]{:S(2)}, u32[]{:S(2)}) collective-permute-start(bf16[2,288,128]{2,1,0:T(8,128)(2,1)S(1)} %get-tuple-element.92), channel_id=1, source_target_pairs={{0,2},{1,3},{2,0},{3,1},{4,6},{5,7},{6,4},{7,5},{8,10},{9,11},{10,... | collective-permute-start | bytes 442376 | tf_op jit(solution)/shard_map/ppermute | solution.py:46
  (32 other events, 369.2 us)

commit v7 on v6

--- a/solution.py
+++ b/solution.py
@@ -136,7 +136,7 @@
     return pl.pallas_call(
         functools.partial(pack_kernel, places),
         out_shape=jax.ShapeDtypeStruct((256, ROWS, E), jnp.bfloat16),
-        in_specs=[pl.BlockSpec(memory_space=pl.ANY)] * len(pieces) + [vmem] * len(given),
+        in_specs=[pl.BlockSpec(memory_space=pltpu.HBM)] * len(pieces) + [vmem] * len(given),
         out_specs=vmem,
         scratch_shapes=[pltpu.SemaphoreType.DMA((len(pieces),))],
         input_output_aliases={len(pieces): 0} if given else {},
@@ -269,44 +269,49 @@
     )(*parts, positive)
 
 
-STREAMS = (
-    (("y", 1), ("y", 3), ("z", 1), ("z", 3)),
-    (("y", 3), ("y", 1), ("z", 3), ("z", 1)),
-    (("z", 1), ("z", 3), ("y", 1), ("y", 3)),
-    (("z", 3), ("z", 1), ("y", 3), ("y", 1)),
-)
-
-
 def together(*values):
     return list(lax.optimization_barrier(tuple(values)))
 
 
 def spread(items, query):
-    held = [items[n * 4 : n * 4 + 4] for n in range(4)]
-    queries = [query]
-    for step in range(3):
-        got = [send(h, **{st[step][0]: st[step][1]}) for h, st in zip(held, STREAMS)]
-        if step > 0:
-            queries.append(send_x(query, step))
-            got.append(queries.pop())
-        got = together(*got, query)
-        query = got.pop()
-        queries += got[4:]
-        if step < 2:
-            held = together(*[jnp.concatenate([h, g]) for h, g in zip(held, got)])
-    queries.append(send_x(query, 3))
-    third = got[:4]
-    fourth = [send(h, **{st[3][0]: st[3][1]}) for h, st in zip(held, STREAMS)]
-    fifth = [send(h, **{st[3][0]: st[3][1]}) for h, st in zip(third, STREAMS)]
-    table = pack(held + third, (0, 4, 8, 12, 1, 5, 9, 13))
-    table = pack(fourth + fifth, (2, 6, 10, 14, 3, 7, 11, 15), table)
-    return table, jnp.stack(queries)
-
-
-def place_of(flipped, first):
-    return jnp.where(
-        flipped == 0, 0, jnp.where(flipped == 2, 3, jnp.where(flipped == first, 1, 2))
-    )
+    near, far = items[:NBD], items[NBD:]
+    near_1, far_1 = together(send(near, y=1), send(far, z=1))
+    near, far = together(jnp.concatenate([near, near_1]), jnp.concatenate([far, far_1]))
+    near_b, far_b, near_z1, far_y1, query_1, query = together(
+        send(near, y=3),
+        send(far, z=3),
+        send(near, z=1),
+        send(far, y=1),
+        send_x(query, 1),
+        query,
+    )
+    near_b1, near_b3, far_b1, far_b3, query_2, query = together(
+        send(near_b, z=1),
+        send(near_b, z=3),
+        send(far_b, y=1),
+        send(far_b, y=3),
+        send_x(query, 2),
+        query,
+    )
+    near_z3, far_y3, near_b31, far_b31, last_near, last_far, query_3 = together(
+        send(near, z=3),
+        send(far, y=3),
+        send(near_b3, z=1),
+        send(far_b3, y=1),
+        near_z1,
+        far_y1,
+        send_x(query, 3),
+    )
+    near_z13, far_y13 = send(last_near, z=3), send(last_far, y=3)
+    early = [near, near_b, near_z1, near_b1, near_b3, far, far_b, far_y1, far_b1, far_b3]
+    table = pack(early, (0, 1, 2, 3, 5, 8, 9, 10, 11, 13))
+    late = [near_z3, near_z13, near_b31, far_y3, far_y13, far_b31]
+    table = pack(late, (4, 6, 7, 12, 14, 15), table)
+    return table, jnp.stack([query, query_1, query_2, query_3])
+
+
+def place_of(flipped):
+    return jnp.where(flipped >= 2, 5 - flipped, flipped)
 
 
 def local(query_emb, positive_emb, item_hidden, item_weight, neg_blocks, block_home, sample_counts):
@@ -331,7 +336,7 @@
         return cut.reshape(2 * NBD * ROWS, -1)
 
     hiddens = [piece(0)] + [send_x(piece(d), d) for d in (1, 2, 3)]
-    theirs_w = send(together(jnp.stack(mine_w), hiddens[1], hiddens[3])[0], c=1)
+    theirs_w = send(together(jnp.stack(mine_w), hiddens[1], hiddens[2])[0], c=1)
     picks = jnp.concatenate([send(neg_blocks, c=1), neg_blocks])
     items, late_query, picks = together(
         tower(core_id, hiddens, mine_w, theirs_w), query_emb, picks
@@ -347,12 +352,10 @@
     slot, owner = home % NBD, home // NBD
     flip_z = ((owner // 2) % NZ) ^ my_z
     flip_y = (owner // (2 * NZ)) ^ my_y
-    late = slot // (NBD // 2)
-    at_y = place_of(flip_y, jnp.where(late == 0, 1, 3))
-    at_z = place_of(flip_z, jnp.where(late == 0, 1, 3))
+    at_y, at_z = place_of(flip_y), place_of(flip_z)
     near = owner % 2 == core
-    rows = jnp.where(near, at_z * 4 + at_y, 128 // 4 + at_y * 4 + at_z)
-    rows = (rows * 4 + late * 64 + slot % 4).astype(jnp.int32)
+    rows = jnp.where(near, at_z * 4 + at_y, 16 + at_y * 4 + at_z)
+    rows = (rows * NBD + slot).astype(jnp.int32)
     count_rows = sample_counts.reshape(2 * total_blocks, 128)[home.reshape(-1) * 2 + rank // 2]
     counts = lax.dynamic_slice_in_dim(count_rows, (rank % 2 * 2 + core) * ROWS, ROWS, 1)
     lq = (jnp.log(counts.astype(jnp.float32)) * LOG2E).reshape(2 * qblocks, COLS)

time: 140 us -> 147 us (1.050)
  waiting for transfers between devices: 49.4 us -> 59.5 us
  starting transfers between devices: 49.1 us -> 42 us
  local copies, waits for them, and re-layouts: 12 us -> 19 us
  other arithmetic: 5.27 us -> 3.48 us
    ppermute x15, waiting for transfers between devices: 30.9 us -> 39.7 us  [send_x(): return lax.ppermute(value, 'tp', [(i, (i + d) % TP) for i in range(TP)])]
    unnamed x26 -> x50, local copies, waits for them, and re-layouts: 6.64 us -> 13.7 us
    ppermute x28 -> x24, starting transfers between devices: 28.7 us -> 22.5 us  [send(): return lax.ppermute(value, 'cat', cat_perm(y, z, c))]
    concatenate x6 -> x1, other arithmetic: 1.88 us -> 0.09 us  [spread(): jnp.concatenate([near, near_1])]
    ppermute x28 -> x24, waiting for transfers between devices: 18.5 us -> 19.8 us  [send(): return lax.ppermute(value, 'cat', cat_perm(y, z, c))]
  transfers between devices with their start and end apart: 43 -> 39, of which waited for: 18 -> 19; matrix products, arithmetic and copies ran while one was open for 5% -> 5% of each run, Pallas kernels for 10% -> 10%
where the time goes in v7:
time: 147 us; the launch traced here: 146 us
  waiting for transfers between devices  59.5 us (40%)
  starting transfers between devices  42 us (29%)
  Pallas kernels  21.1 us (14%)
  local copies, waits for them, and re-layouts  19 us (13%)
  other arithmetic  3.48 us (2%)
    ppermute x15, waiting for transfers between devices, send_x(): return lax.ppermute(value, 'tp', [(i, (i + d) % TP) for i in range(TP)])  39.7 us
    ppermute x24, starting transfers between devices, send(): return lax.ppermute(value, 'cat', cat_perm(y, z, c))  22.5 us
    ppermute x24, waiting for transfers between devices, send(): return lax.ppermute(value, 'cat', cat_perm(y, z, c))  19.8 us
    ppermute x15, starting transfers between devices, send_x(): return lax.ppermute(value, 'tp', [(i, (i + d) % TP) for i in range(TP)])  19.6 us
    pallas_call x4, Pallas kernels, attend(): pl.pallas_call(functools.partial(body, start), in_specs=[pl.BlockSpec(mem...  15.3 us
    unnamed x50, local copies, waits for them, and re-layouts  13.7 us
  transfers between devices with their start and end apart: 39, of which 19 were waited for; matrix products, arithmetic and copies ran while one was open for 5% of the time, Pallas kernels for 10%

profile of v7, /device:TPU:0, one launch (start us, length us, event | category | flops | bytes accessed | tf_op | source)
XLA Modules:
  0.0 146.3 jit_solution(5570339802527743162)
XLA Ops:
  5.8 2.7 %collective-permute-start.2 = (bf16[512,256]{1,0:T(8,128)(2,1)S(1)}, bf16[512,256]{1,0:T(8,128)(2,1)S(1)}, u32[]{:S(2)}, u32[]{:S(2)}) collective-permute-start(bf16[512,256]{1,0:T(8,128)(2,1)S(1)} %bitcast.38), channel_id=1, source_target_pairs={{0,2},{1,3},{2,0},{3,1},{4,6},{5,7},{6,4},{7,5},{8,10},{9,11},{10,... | collective-permute-start | bytes 786440 | tf_op jit(solution)/shard_map/ppermute | solution.py:46
  8.7 2.9 %collective-permute-start.5 = (bf16[128,512]{1,0:T(8,128)(2,1)S(1)}, bf16[128,512]{1,0:T(8,128)(2,1)S(1)}, u32[]{:S(2)}, u32[]{:S(2)}) collective-permute-start(bf16[128,512]{1,0:T(8,128)(2,1)S(1)} %constant_dynamic-slice_fusion.refs_4_), channel_id=1, source_target_pairs={{0,2},{1,3},{2,0},{3,1},{4,6},{5,7},{6,4},{7,5},{8,10},{9,11},{10,... | collective-permute-start | bytes 393224 | tf_op jit(solution)/shard_map/ppermute | solution.py:46
  12.1 10.1 %collective-permute-done.4.refs_5_ = bf16[128,512]{1,0:T(8,128)(2,1)S(1)} collective-permute-done((bf16[128,512]{1,0:T(8,128)(2,1)S(1)}, bf16[128,512]{1,0:T(8,128)(2,1)S(1)}, u32[]{:S(2)}, u32[]{:S(2)}) %collective-permute-start.4) | collective-permute-done | bytes 131104 | tf_op jit(solution)/shard_map/ppermute | solution.py:46
  22.3 3.9 %collective-permute-done.5.refs_6_ = bf16[128,512]{1,0:T(8,128)(2,1)S(1)} collective-permute-done((bf16[128,512]{1,0:T(8,128)(2,1)S(1)}, bf16[128,512]{1,0:T(8,128)(2,1)S(1)}, u32[]{:S(2)}, u32[]{:S(2)}) %collective-permute-start.5) | collective-permute-done | bytes 131104 | tf_op jit(solution)/shard_map/ppermute | solution.py:46
  29.2 5.9 %collective-permute-done.3.refs_3_ = bf16[512,256]{1,0:T(8,128)(2,1)S(1)} collective-permute-done((bf16[512,256]{1,0:T(8,128)(2,1)S(1)}, bf16[512,256]{1,0:T(8,128)(2,1)S(1)}, u32[]{:S(2)}, u32[]{:S(2)}) %collective-permute-start.3) | collective-permute-done | bytes 262176 | tf_op jit(solution)/shard_map/ppermute | solution.py:46
  38.0 1.9 %collective-permute-start.10 = (bf16[8,32,512]{2,1,0:T(8,128)(2,1)S(1)}, bf16[8,32,512]{2,1,0:T(8,128)(2,1)S(1)}, u32[]{:S(2)}, u32[]{:S(2)}) collective-permute-start(bf16[8,32,512]{2,1,0:T(8,128)(2,1)S(1)} %get-tuple-element.98), channel_id=1, source_target_pairs={{0,8},{4,12},{8,0},{12,4},{16,24},{20,28},{24,16},{28,20},{32,40},... | collective-permute-start | bytes 786440 | tf_op jit(solution)/shard_map/ppermute | solution.py:42
  40.0 4.4 %collective-permute-done.9 = bf16[8,32,512]{2,1,0:T(8,128)(2,1)S(1)} collective-permute-done((bf16[8,32,512]{2,1,0:T(8,128)(2,1)S(1)}, bf16[8,32,512]{2,1,0:T(8,128)(2,1)S(1)}, u32[]{:S(2)}, u32[]{:S(2)}) %collective-permute-start.9) | collective-permute-done | bytes 262176 | tf_op jit(solution)/shard_map/ppermute | solution.py:42
  45.9 2.3 %collective-permute-start.13 = (bf16[16,32,512]{2,1,0:T(8,128)(2,1)S(1)}, bf16[16,32,512]{2,1,0:T(8,128)(2,1)S(1)}, u32[]{:S(2)}, u32[]{:S(2)}) collective-permute-start(bf16[16,32,512]{2,1,0:T(8,128)(2,1)S(1)} %get-tuple-element.51.refs_0_), channel_id=1, source_target_pairs={{0,96},{4,100},{8,104},{12,108},{16,112},{20,116},{24,120},{28,124... | collective-permute-start | bytes 1572872 | tf_op jit(solution)/shard_map/ppermute | solution.py:42
  48.1 3.9 %collective-permute-start.14 = (bf16[16,32,512]{2,1,0:T(8,128)(2,1)S(1)}, bf16[16,32,512]{2,1,0:T(8,128)(2,1)S(1)}, u32[]{:S(2)}, u32[]{:S(2)}) collective-permute-start(bf16[16,32,512]{2,1,0:T(8,128)(2,1)S(1)} %get-tuple-element.52.refs_5_), channel_id=1, source_target_pairs={{0,24},{4,28},{8,16},{12,20},{16,8},{20,12},{24,0},{28,4},{32,56},... | collective-permute-start | bytes 1572872 | tf_op jit(solution)/shard_map/ppermute | solution.py:42
  52.7 7.6 %collective-permute-done.17 = bf16[1024,128]{1,0:T(8,128)(2,1)S(1)} collective-permute-done((bf16[1024,128]{1,0:T(8,128)(2,1)S(1)}, bf16[1024,128]{1,0:T(8,128)(2,1)S(1)}, u32[]{:S(2)}, u32[]{:S(2)}) %collective-permute-start.17) | collective-permute-done | bytes 262176 | tf_op jit(solution)/shard_map/ppermute | solution.py:46
  60.3 2.0 %collective-permute-done.14.refs_6_ = bf16[16,32,512]{2,1,0:T(8,128)(2,1)S(1)} collective-permute-done((bf16[16,32,512]{2,1,0:T(8,128)(2,1)S(1)}, bf16[16,32,512]{2,1,0:T(8,128)(2,1)S(1)}, u32[]{:S(2)}, u32[]{:S(2)}) %collective-permute-start.14) | collective-permute-done | bytes 524320 | tf_op jit(solution)/shard_map/ppermute | solution.py:42
  70.0 7.1 %collective-permute-done.22 = bf16[1024,128]{1,0:T(8,128)(2,1)S(1)} collective-permute-done((bf16[1024,128]{1,0:T(8,128)(2,1)S(1)}, bf16[1024,128]{1,0:T(8,128)(2,1)S(1)}, u32[]{:S(2)}, u32[]{:S(2)}) %collective-permute-start.22) | collective-permute-done | bytes 262176 | tf_op jit(solution)/shard_map/ppermute | solution.py:46
  77.1 2.9 %collective-permute-start.11 = (bf16[16,32,512]{2,1,0:T(8,128)(2,1)S(1)}, bf16[16,32,512]{2,1,0:T(8,128)(2,1)S(1)}, u32[]{:S(2)}, u32[]{:S(2)}) collective-permute-start(bf16[16,32,512]{2,1,0:T(8,128)(2,1)S(1)} %get-tuple-element.51.refs_0_), channel_id=1, source_target_pairs={{0,24},{4,28},{8,16},{12,20},{16,8},{20,12},{24,0},{28,4},{32,56},... | collective-permute-start | bytes 1572872 | tf_op jit(solution)/shard_map/ppermute | solution.py:42
  80.8 2.3 %collective-permute-start.12 = (bf16[16,32,512]{2,1,0:T(8,128)(2,1)S(1)}, bf16[16,32,512]{2,1,0:T(8,128)(2,1)S(1)}, u32[]{:S(2)}, u32[]{:S(2)}) collective-permute-start(bf16[16,32,512]{2,1,0:T(8,128)(2,1)S(1)} %get-tuple-element.52.refs_5_), channel_id=1, source_target_pairs={{0,96},{4,100},{8,104},{12,108},{16,112},{20,116},{24,120},{28,124... | collective-permute-start | bytes 1572872 | tf_op jit(solution)/shard_map/ppermute | solution.py:42
  89.1 2.1 %collective-permute-done.12.refs_3_ = bf16[16,32,512]{2,1,0:T(8,128)(2,1)S(1)} collective-permute-done((bf16[16,32,512]{2,1,0:T(8,128)(2,1)S(1)}, bf16[16,32,512]{2,1,0:T(8,128)(2,1)S(1)}, u32[]{:S(2)}, u32[]{:S(2)}) %collective-permute-start.12) | collective-permute-done | bytes 524320 | tf_op jit(solution)/shard_map/ppermute | solution.py:42
  96.9 2.6 %gather_fusion = s32[512,128]{1,0:T(8,128)} fusion(s32[512,128]{1,0:T(8,128)} %bitcast.32, s32[1024]{0:T(1024)S(1)} %pad_clamp_fusion), kind=kCustom, calls=%fused_computation | custom fusion | bytes 526336 | tf_op jit(solution)/shard_map/gather | solution.py:359
  112.8 3.7 %attend_other.2 = (bf16[2,256,512]{2,1,0:T(8,128)(2,1)S(1)}, f32[2,8,256]{2,1,0:T(8,128)S(1)}) custom-call(s32[512]{0:T(512)S(1)} %fusion.9.row_ref, s32[1]{0:T(128)} %bitcast.15.rank_ref, bf16[4,1024,128]{2,1,0:T(8,128)(2,1)S(1)} %collective-permute-done.28.q_ref, f32[8,2048]{1,0:T(8,128)S(1)} %reshape.91.lq_ref, bf16[256,32,512]{2,1,0:T(8,128)(2,1)S(1)} %pack.3.table), custom_call_target="tpu_custom_call" | custom-call | flops 2147483648 | bytes 2097152 | tf_op jit(solution)/shard_map/attend_other/pallas_call | solution.py:201
  116.6 3.7 %attend_other.3 = (bf16[2,256,512]{2,1,0:T(8,128)(2,1)S(1)}, f32[2,8,256]{2,1,0:T(8,128)S(1)}) custom-call(s32[512]{0:T(512)S(1)} %fusion.9.row_ref, s32[1]{0:T(128)} %bitcast.15.rank_ref, bf16[4,1024,128]{2,1,0:T(8,128)(2,1)S(1)} %collective-permute-done.28.q_ref, f32[8,2048]{1,0:T(8,128)S(1)} %reshape.91.lq_ref, bf16[256,32,512]{2,1,0:T(8,128)(2,1)S(1)} %pack.3.table), custom_call_target="tpu_custom_call" | custom-call | flops 2147483648 | bytes 2097152 | tf_op jit(solution)/shard_map/attend_other/pallas_call | solution.py:201
  122.5 3.9 %attend_own.2 = (bf16[2,288,128]{2,1,0:T(8,128)(2,1)S(1)}, bf16[2,288,128]{2,1,0:T(8,128)(2,1)S(1)}, bf16[2,288,128]{2,1,0:T(8,128)(2,1)S(1)}, bf16[2,288,128]{2,1,0:T(8,128)(2,1)S(1)}) custom-call(s32[512]{0:T(512)S(1)} %fusion.9.row_ref, s32[1]{0:T(128)} %bitcast.15.rank_ref, bf16[4,1024,128]{2,1,0:T(8,128)(2,1)S(1)} %pad_maximum_fusion.q_ref, ...), custom_call_target="tpu_custom_call" | custom-call | flops 2147483648 | bytes 2097152 | tf_op jit(solution)/shard_map/attend_own/pallas_call | solution.py:201
  126.5 3.3 %collective-permute-start.32 = (bf16[2,288,128]{2,1,0:T(8,128)(2,1)S(1)}, bf16[2,288,128]{2,1,0:T(8,128)(2,1)S(1)}, u32[]{:S(2)}, u32[]{:S(2)}) collective-permute-start(bf16[2,288,128]{2,1,0:T(8,128)(2,1)S(1)} %get-tuple-element.82), channel_id=1, source_target_pairs={{0,2},{1,3},{2,0},{3,1},{4,6},{5,7},{6,4},{7,5},{8,10},{9,11},{10,... | collective-permute-start | bytes 442376 | tf_op jit(solution)/shard_map/ppermute | solution.py:46
  129.9 3.9 %attend_own.3 = (bf16[2,288,128]{2,1,0:T(8,128)(2,1)S(1)}, bf16[2,288,128]{2,1,0:T(8,128)(2,1)S(1)}, bf16[2,288,128]{2,1,0:T(8,128)(2,1)S(1)}, bf16[2,288,128]{2,1,0:T(8,128)(2,1)S(1)}) custom-call(s32[512]{0:T(512)S(1)} %fusion.9.row_ref, s32[1]{0:T(128)} %bitcast.15.rank_ref, bf16[4,1024,128]{2,1,0:T(8,128)(2,1)S(1)} %pad_maximum_fusion.q_ref, ...), custom_call_target="tpu_custom_call" | custom-call | flops 2147483648 | bytes 2097152 | tf_op jit(solution)/shard_map/attend_own/pallas_call | solution.py:201
  133.9 2.0 %collective-permute-start.36 = (bf16[2,288,128]{2,1,0:T(8,128)(2,1)S(1)}, bf16[2,288,128]{2,1,0:T(8,128)(2,1)S(1)}, u32[]{:S(2)}, u32[]{:S(2)}) collective-permute-start(bf16[2,288,128]{2,1,0:T(8,128)(2,1)S(1)} %get-tuple-element.87), channel_id=1, source_target_pairs={{0,1},{1,2},{2,3},{3,0},{4,5},{5,6},{6,7},{7,4},{8,9},{9,10},{10,1... | collective-permute-start | bytes 442376 | tf_op jit(solution)/shard_map/ppermute | solution.py:46
  136.8 2.5 %collective-permute-start.38 = (bf16[2,288,128]{2,1,0:T(8,128)(2,1)S(1)}, bf16[2,288,128]{2,1,0:T(8,128)(2,1)S(1)}, u32[]{:S(2)}, u32[]{:S(2)}) collective-permute-start(bf16[2,288,128]{2,1,0:T(8,128)(2,1)S(1)} %get-tuple-element.89), channel_id=1, source_target_pairs={{0,3},{1,0},{2,1},{3,2},{4,7},{5,4},{6,5},{7,6},{8,11},{9,8},{10,9... | collective-permute-start | bytes 442376 | tf_op jit(solution)/shard_map/ppermute | solution.py:46
  139.3 4.5 %collective-permute-done.36.refs_5_ = bf16[2,288,128]{2,1,0:T(8,128)(2,1)S(1)} collective-permute-done((bf16[2,288,128]{2,1,0:T(8,128)(2,1)S(1)}, bf16[2,288,128]{2,1,0:T(8,128)(2,1)S(1)}, u32[]{:S(2)}, u32[]{:S(2)}) %collective-permute-start.36) | collective-permute-done | bytes 147488 | tf_op jit(solution)/shard_map/ppermute | solution.py:46
  (135 shorter events, 53.0 us)
Async XLA Ops:
  4.2 22.1 %collective-permute-start.1 = (bf16[512,256]{1,0:T(8,128)(2,1)S(1)}, bf16[512,256]{1,0:T(8,128)(2,1)S(1)}, u32[]{:S(2)}, u32[]{:S(2)}) collective-permute-start(bf16[512,256]{1,0:T(8,128)(2,1)S(1)} %bitcast.39), channel_id=1, source_target_pairs={{0,1},{1,2},{2,3},{3,0},{4,5},{5,6},{6,7},{7,4},{8,9},{9,10},{10,1... | collective-permute-start | bytes 786440 | tf_op jit(solution)/shard_map/ppermute | solution.py:46
  5.8 20.4 %collective-permute-start.2 = (bf16[512,256]{1,0:T(8,128)(2,1)S(1)}, bf16[512,256]{1,0:T(8,128)(2,1)S(1)}, u32[]{:S(2)}, u32[]{:S(2)}) collective-permute-start(bf16[512,256]{1,0:T(8,128)(2,1)S(1)} %bitcast.38), channel_id=1, source_target_pairs={{0,2},{1,3},{2,0},{3,1},{4,6},{5,7},{6,4},{7,5},{8,10},{9,11},{10,... | collective-permute-start | bytes 786440 | tf_op jit(solution)/shard_map/ppermute | solution.py:46
  8.6 13.7 %collective-permute-start.4 = (bf16[128,512]{1,0:T(8,128)(2,1)S(1)}, bf16[128,512]{1,0:T(8,128)(2,1)S(1)}, u32[]{:S(2)}, u32[]{:S(2)}) collective-permute-start(bf16[128,512]{1,0:T(8,128)(2,1)S(1)} %constant_dynamic-slice_fusion.refs_4_), channel_id=1, source_target_pairs={{0,1},{1,2},{2,3},{3,0},{4,5},{5,6},{6,7},{7,4},{8,9},{9,10},{10,1... | collective-permute-start | bytes 393224 | tf_op jit(solution)/shard_map/ppermute | solution.py:46
  8.7 17.5 %collective-permute-start.5 = (bf16[128,512]{1,0:T(8,128)(2,1)S(1)}, bf16[128,512]{1,0:T(8,128)(2,1)S(1)}, u32[]{:S(2)}, u32[]{:S(2)}) collective-permute-start(bf16[128,512]{1,0:T(8,128)(2,1)S(1)} %constant_dynamic-slice_fusion.refs_4_), channel_id=1, source_target_pairs={{0,2},{1,3},{2,0},{3,1},{4,6},{5,7},{6,4},{7,5},{8,10},{9,11},{10,... | collective-permute-start | bytes 393224 | tf_op jit(solution)/shard_map/ppermute | solution.py:46
  11.6 14.6 %collective-permute-start.6 = (bf16[128,512]{1,0:T(8,128)(2,1)S(1)}, bf16[128,512]{1,0:T(8,128)(2,1)S(1)}, u32[]{:S(2)}, u32[]{:S(2)}) collective-permute-start(bf16[128,512]{1,0:T(8,128)(2,1)S(1)} %constant_dynamic-slice_fusion.refs_4_), channel_id=1, source_target_pairs={{0,3},{1,0},{2,1},{3,2},{4,7},{5,4},{6,5},{7,6},{8,11},{9,8},{10,9... | collective-permute-start | bytes 393224 | tf_op jit(solution)/shard_map/ppermute | solution.py:46
  45.9 14.4 %collective-permute-start.13 = (bf16[16,32,512]{2,1,0:T(8,128)(2,1)S(1)}, bf16[16,32,512]{2,1,0:T(8,128)(2,1)S(1)}, u32[]{:S(2)}, u32[]{:S(2)}) collective-permute-start(bf16[16,32,512]{2,1,0:T(8,128)(2,1)S(1)} %get-tuple-element.51.refs_0_), channel_id=1, source_target_pairs={{0,96},{4,100},{8,104},{12,108},{16,112},{20,116},{24,120},{28,124... | collective-permute-start | bytes 1572872 | tf_op jit(solution)/shard_map/ppermute | solution.py:42
  48.1 14.1 %collective-permute-start.14 = (bf16[16,32,512]{2,1,0:T(8,128)(2,1)S(1)}, bf16[16,32,512]{2,1,0:T(8,128)(2,1)S(1)}, u32[]{:S(2)}, u32[]{:S(2)}) collective-permute-start(bf16[16,32,512]{2,1,0:T(8,128)(2,1)S(1)} %get-tuple-element.52.refs_5_), channel_id=1, source_target_pairs={{0,24},{4,28},{8,16},{12,20},{16,8},{20,12},{24,0},{28,4},{32,56},... | collective-permute-start | bytes 1572872 | tf_op jit(solution)/shard_map/ppermute | solution.py:42
  52.0 12.1 %collective-permute-start.15 = (bf16[16,32,512]{2,1,0:T(8,128)(2,1)S(1)}, bf16[16,32,512]{2,1,0:T(8,128)(2,1)}, u32[]{:S(2)}, u32[]{:S(2)}) collective-permute-start(bf16[16,32,512]{2,1,0:T(8,128)(2,1)S(1)} %get-tuple-element.51.refs_0_), channel_id=1, source_target_pairs={{0,8},{4,12},{8,0},{12,4},{16,24},{20,28},{24,16},{28,20},{32,40},... | collective-permute-start | bytes 1572872 | tf_op jit(solution)/shard_map/ppermute | solution.py:42
  52.0 12.1 %collective-permute-start.16 = (bf16[16,32,512]{2,1,0:T(8,128)(2,1)S(1)}, bf16[16,32,512]{2,1,0:T(8,128)(2,1)}, u32[]{:S(2)}, u32[]{:S(2)}) collective-permute-start(bf16[16,32,512]{2,1,0:T(8,128)(2,1)S(1)} %get-tuple-element.52.refs_5_), channel_id=1, source_target_pairs={{0,32},{4,36},{8,40},{12,44},{16,48},{20,52},{24,56},{28,60},{32,0... | collective-permute-start | bytes 1572872 | tf_op jit(solution)/shard_map/ppermute | solution.py:42
  64.1 15.9 %collective-permute-start.18 = (bf16[16,32,512]{2,1,0:T(8,128)(2,1)S(1)}, bf16[16,32,512]{2,1,0:T(8,128)(2,1)S(1)}, u32[]{:S(2)}, u32[]{:S(2)}) collective-permute-start(bf16[16,32,512]{2,1,0:T(8,128)(2,1)S(1)} %collective-permute-done.13.refs_1_), channel_id=1, source_target_pairs={{0,8},{4,12},{8,0},{12,4},{16,24},{20,28},{24,16},{28,20},{32,40},... | collective-permute-start | bytes 1572872 | tf_op jit(solution)/shard_map/ppermute | solution.py:42
  65.6 17.5 %collective-permute-start.19 = (bf16[16,32,512]{2,1,0:T(8,128)(2,1)S(1)}, bf16[16,32,512]{2,1,0:T(8,128)(2,1)S(1)}, u32[]{:S(2)}, u32[]{:S(2)}) collective-permute-start(bf16[16,32,512]{2,1,0:T(8,128)(2,1)S(1)} %collective-permute-done.13.refs_1_), channel_id=1, source_target_pairs={{0,24},{4,28},{8,16},{12,20},{16,8},{20,12},{24,0},{28,4},{32,56},... | collective-permute-start | bytes 1572872 | tf_op jit(solution)/shard_map/ppermute | solution.py:42
  66.7 16.4 %collective-permute-start.20 = (bf16[16,32,512]{2,1,0:T(8,128)(2,1)S(1)}, bf16[16,32,512]{2,1,0:T(8,128)(2,1)S(1)}, u32[]{:S(2)}, u32[]{:S(2)}) collective-permute-start(bf16[16,32,512]{2,1,0:T(8,128)(2,1)S(1)} %collective-permute-done.14.refs_6_), channel_id=1, source_target_pairs={{0,32},{4,36},{8,40},{12,44},{16,48},{20,52},{24,56},{28,60},{32,0... | collective-permute-start | bytes 1572872 | tf_op jit(solution)/shard_map/ppermute | solution.py:42
  67.4 16.5 %collective-permute-start.21 = (bf16[16,32,512]{2,1,0:T(8,128)(2,1)S(1)}, bf16[16,32,512]{2,1,0:T(8,128)(2,1)S(1)}, u32[]{:S(2)}, u32[]{:S(2)}) collective-permute-start(bf16[16,32,512]{2,1,0:T(8,128)(2,1)S(1)} %collective-permute-done.14.refs_6_), channel_id=1, source_target_pairs={{0,96},{4,100},{8,104},{12,108},{16,112},{20,116},{24,120},{28,124... | collective-permute-start | bytes 1572872 | tf_op jit(solution)/shard_map/ppermute | solution.py:42
  77.1 11.1 %collective-permute-start.11 = (bf16[16,32,512]{2,1,0:T(8,128)(2,1)S(1)}, bf16[16,32,512]{2,1,0:T(8,128)(2,1)S(1)}, u32[]{:S(2)}, u32[]{:S(2)}) collective-permute-start(bf16[16,32,512]{2,1,0:T(8,128)(2,1)S(1)} %get-tuple-element.51.refs_0_), channel_id=1, source_target_pairs={{0,24},{4,28},{8,16},{12,20},{16,8},{20,12},{24,0},{28,4},{32,56},... | collective-permute-start | bytes 1572872 | tf_op jit(solution)/shard_map/ppermute | solution.py:42
  80.8 10.4 %collective-permute-start.12 = (bf16[16,32,512]{2,1,0:T(8,128)(2,1)S(1)}, bf16[16,32,512]{2,1,0:T(8,128)(2,1)S(1)}, u32[]{:S(2)}, u32[]{:S(2)}) collective-permute-start(bf16[16,32,512]{2,1,0:T(8,128)(2,1)S(1)} %get-tuple-element.52.refs_5_), channel_id=1, source_target_pairs={{0,96},{4,100},{8,104},{12,108},{16,112},{20,116},{24,120},{28,124... | collective-permute-start | bytes 1572872 | tf_op jit(solution)/shard_map/ppermute | solution.py:42
  83.9 10.0 %collective-permute-start.24 = (bf16[16,32,512]{2,1,0:T(8,128)(2,1)S(1)}, bf16[16,32,512]{2,1,0:T(8,128)(2,1)S(1)}, u32[]{:S(2)}, u32[]{:S(2)}) collective-permute-start(bf16[16,32,512]{2,1,0:T(8,128)(2,1)S(1)} %collective-permute-done.21.refs_9_), channel_id=1, source_target_pairs={{0,32},{4,36},{8,40},{12,44},{16,48},{20,52},{24,56},{28,60},{32,0... | collective-permute-start | bytes 1572872 | tf_op jit(solution)/shard_map/ppermute | solution.py:42
  94.8 18.0 %collective-permute-start.28 = (bf16[4,1024,128]{2,1,0:T(8,128)(2,1)S(1)}, bf16[4,1024,128]{2,1,0:T(8,128)(2,1)S(1)}, u32[]{:S(2)}, u32[]{:S(2)}) collective-permute-start(bf16[4,1024,128]{2,1,0:T(8,128)(2,1)S(1)} %pad_maximum_fusion.q_ref), channel_id=1, source_target_pairs={{0,4},{4,0},{8,12},{12,8},{16,20},{20,16},{24,28},{28,24},{32,36},... | collective-permute-start | bytes 3145736 | tf_op jit(solution)/shard_map/ppermute | solution.py:42
  95.4 15.8 %collective-permute-start.26 = (bf16[16,32,512]{2,1,0:T(8,128)(2,1)}, bf16[16,32,512]{2,1,0:T(8,128)(2,1)}, u32[]{:S(2)}, u32[]{:S(2)}) collective-permute-start(bf16[16,32,512]{2,1,0:T(8,128)(2,1)} %collective-permute-done.15.refs_2_), channel_id=1, source_target_pairs={{0,24},{4,28},{8,16},{12,20},{16,8},{20,12},{24,0},{28,4},{32,56},... | collective-permute-start | bytes 1572872 | tf_op jit(solution)/shard_map/ppermute | solution.py:42
  95.7 15.8 %collective-permute-start.27 = (bf16[16,32,512]{2,1,0:T(8,128)(2,1)}, bf16[16,32,512]{2,1,0:T(8,128)(2,1)}, u32[]{:S(2)}, u32[]{:S(2)}) collective-permute-start(bf16[16,32,512]{2,1,0:T(8,128)(2,1)} %collective-permute-done.16.refs_7_), channel_id=1, source_target_pairs={{0,96},{4,100},{8,104},{12,108},{16,112},{20,116},{24,120},{28,124... | collective-permute-start | bytes 1572872 | tf_op jit(solution)/shard_map/ppermute | solution.py:42
  120.3 9.6 %collective-permute-start.34 = (bf16[2,256,512]{2,1,0:T(8,128)(2,1)S(1)}, bf16[2,256,512]{2,1,0:T(8,128)(2,1)S(1)}, u32[]{:S(2)}, u32[]{:S(2)}) collective-permute-start(bf16[2,256,512]{2,1,0:T(8,128)(2,1)S(1)} %get-tuple-element.84), channel_id=1, source_target_pairs={{0,4},{4,0},{8,12},{12,8},{16,20},{20,16},{24,28},{28,24},{32,36},... | collective-permute-start | bytes 1572872 | tf_op jit(solution)/shard_map/ppermute | solution.py:42
  126.4 10.4 %collective-permute-start.31 = (bf16[2,288,128]{2,1,0:T(8,128)(2,1)S(1)}, bf16[2,288,128]{2,1,0:T(8,128)(2,1)S(1)}, u32[]{:S(2)}, u32[]{:S(2)}) collective-permute-start(bf16[2,288,128]{2,1,0:T(8,128)(2,1)S(1)} %get-tuple-element.81), channel_id=1, source_target_pairs={{0,1},{1,2},{2,3},{3,0},{4,5},{5,6},{6,7},{7,4},{8,9},{9,10},{10,1... | collective-permute-start | bytes 442376 | tf_op jit(solution)/shard_map/ppermute | solution.py:46
  126.5 12.8 %collective-permute-start.32 = (bf16[2,288,128]{2,1,0:T(8,128)(2,1)S(1)}, bf16[2,288,128]{2,1,0:T(8,128)(2,1)S(1)}, u32[]{:S(2)}, u32[]{:S(2)}) collective-permute-start(bf16[2,288,128]{2,1,0:T(8,128)(2,1)S(1)} %get-tuple-element.82), channel_id=1, source_target_pairs={{0,2},{1,3},{2,0},{3,1},{4,6},{5,7},{6,4},{7,5},{8,10},{9,11},{10,... | collective-permute-start | bytes 442376 | tf_op jit(solution)/shard_map/ppermute | solution.py:46
  129.8 9.5 %collective-permute-start.33 = (bf16[2,288,128]{2,1,0:T(8,128)(2,1)S(1)}, bf16[2,288,128]{2,1,0:T(8,128)(2,1)S(1)}, u32[]{:S(2)}, u32[]{:S(2)}) collective-permute-start(bf16[2,288,128]{2,1,0:T(8,128)(2,1)S(1)} %get-tuple-element.83), channel_id=1, source_target_pairs={{0,3},{1,0},{2,1},{3,2},{4,7},{5,4},{6,5},{7,6},{8,11},{9,8},{10,9... | collective-permute-start | bytes 442376 | tf_op jit(solution)/shard_map/ppermute | solution.py:46
  133.9 9.9 %collective-permute-start.36 = (bf16[2,288,128]{2,1,0:T(8,128)(2,1)S(1)}, bf16[2,288,128]{2,1,0:T(8,128)(2,1)S(1)}, u32[]{:S(2)}, u32[]{:S(2)}) collective-permute-start(bf16[2,288,128]{2,1,0:T(8,128)(2,1)S(1)} %get-tuple-element.87), channel_id=1, source_target_pairs={{0,1},{1,2},{2,3},{3,0},{4,5},{5,6},{6,7},{7,4},{8,9},{9,10},{10,1... | collective-permute-start | bytes 442376 | tf_op jit(solution)/shard_map/ppermute | solution.py:46
  (40 other events, 426.0 us)

commit v8 on v6

--- a/solution.py
+++ b/solution.py
@@ -286,15 +286,11 @@
     queries = [query]
     for step in range(3):
         got = [send(h, **{st[step][0]: st[step][1]}) for h, st in zip(held, STREAMS)]
-        if step > 0:
-            queries.append(send_x(query, step))
-            got.append(queries.pop())
-        got = together(*got, query)
-        query = got.pop()
-        queries += got[4:]
+        got = together(*got, send_x(query, step + 1), query)
+        queries.append(got[4])
+        query = got[5]
         if step < 2:
             held = together(*[jnp.concatenate([h, g]) for h, g in zip(held, got)])
-    queries.append(send_x(query, 3))
     third = got[:4]
     fourth = [send(h, **{st[3][0]: st[3][1]}) for h, st in zip(held, STREAMS)]
     fifth = [send(h, **{st[3][0]: st[3][1]}) for h, st in zip(third, STREAMS)]

time: 140 us -> 140 us (level); the launches traced: 138 us -> 140 us
  starting transfers between devices: 49.1 us -> 60.1 us
  waiting for transfers between devices: 49.4 us -> 42.1 us
  local copies, waits for them, and re-layouts: 12 us -> 10.3 us
    ppermute x28, starting transfers between devices: 28.7 us -> 34.7 us  [send(): return lax.ppermute(value, 'cat', cat_perm(y, z, c))]
    ppermute x15, starting transfers between devices: 20.5 us -> 25.4 us  [send_x(): return lax.ppermute(value, 'tp', [(i, (i + d) % TP) for i in range(TP)])]
    ppermute x15, waiting for transfers between devices: 30.9 us -> 26.9 us  [send_x(): return lax.ppermute(value, 'tp', [(i, (i + d) % TP) for i in range(TP)])]
    ppermute x28, waiting for transfers between devices: 18.5 us -> 15.1 us  [send(): return lax.ppermute(value, 'cat', cat_perm(y, z, c))]
    unnamed x26, local copies, waits for them, and re-layouts: 6.64 us -> 5 us
where the time goes in v8:
time: 140 us
  starting transfers between devices  60.1 us (43%)
  waiting for transfers between devices  42.1 us (30%)
  Pallas kernels  20.9 us (15%)
  local copies, waits for them, and re-layouts  10.3 us (7%)
  other arithmetic  5.29 us (4%)
    ppermute x28, starting transfers between devices, send(): return lax.ppermute(value, 'cat', cat_perm(y, z, c))  34.7 us
    ppermute x15, waiting for transfers between devices, send_x(): return lax.ppermute(value, 'tp', [(i, (i + d) % TP) for i in range(TP)])  26.9 us
    ppermute x15, starting transfers between devices, send_x(): return lax.ppermute(value, 'tp', [(i, (i + d) % TP) for i in range(TP)])  25.4 us
    ppermute x28, waiting for transfers between devices, send(): return lax.ppermute(value, 'cat', cat_perm(y, z, c))  15.1 us
    pallas_call x4, Pallas kernels, attend(): pl.pallas_call(functools.partial(body, start), in_specs=[pl.BlockSpec(mem...  14.3 us
    unnamed x26, local copies, waits for them, and re-layouts  5 us
    pallas_call x2, Pallas kernels, pack(): pl.pallas_call(functools.partial(pack_kernel, places), out_shape=jax.Shap...  3.57 us
  transfers between devices with their start and end apart: 43, of which 18 were waited for; matrix products, arithmetic and copies ran while one was open for 5% of the time, Pallas kernels for 10%

profile of v8, /device:TPU:0, one launch (start us, length us, event | category | flops | bytes accessed | tf_op | source)
XLA Modules:
  0.0 139.9 jit_solution(1566523086565498302)
XLA Ops:
  7.9 2.7 %collective-permute-start.5 = (bf16[128,512]{1,0:T(8,128)(2,1)S(1)}, bf16[128,512]{1,0:T(8,128)(2,1)S(1)}, u32[]{:S(2)}, u32[]{:S(2)}) collective-permute-start(bf16[128,512]{1,0:T(8,128)(2,1)S(1)} %constant_dynamic-slice_fusion.refs_4_), channel_id=1, source_target_pairs={{0,2},{1,3},{2,0},{3,1},{4,6},{5,7},{6,4},{7,5},{8,10},{9,11},{10,... | collective-permute-start | bytes 393224 | tf_op jit(solution)/shard_map/ppermute | solution.py:46
  12.1 4.5 %collective-permute-done.4.refs_5_ = bf16[128,512]{1,0:T(8,128)(2,1)S(1)} collective-permute-done((bf16[128,512]{1,0:T(8,128)(2,1)S(1)}, bf16[128,512]{1,0:T(8,128)(2,1)S(1)}, u32[]{:S(2)}, u32[]{:S(2)}) %collective-permute-start.4) | collective-permute-done | bytes 131104 | tf_op jit(solution)/shard_map/ppermute | solution.py:46
  16.6 3.9 %collective-permute-done.5.refs_6_ = bf16[128,512]{1,0:T(8,128)(2,1)S(1)} collective-permute-done((bf16[128,512]{1,0:T(8,128)(2,1)S(1)}, bf16[128,512]{1,0:T(8,128)(2,1)S(1)}, u32[]{:S(2)}, u32[]{:S(2)}) %collective-permute-start.5) | collective-permute-done | bytes 131104 | tf_op jit(solution)/shard_map/ppermute | solution.py:46
  24.6 6.3 %collective-permute-done.2.refs_2_ = bf16[512,256]{1,0:T(8,128)(2,1)S(1)} collective-permute-done((bf16[512,256]{1,0:T(8,128)(2,1)S(1)}, bf16[512,256]{1,0:T(8,128)(2,1)S(1)}, u32[]{:S(2)}, u32[]{:S(2)}) %collective-permute-start.2) | collective-permute-done | bytes 262176 | tf_op jit(solution)/shard_map/ppermute | solution.py:46
  34.4 2.2 %collective-permute-start.10 = (bf16[4,32,512]{2,1,0:T(8,128)(2,1)S(1)}, bf16[4,32,512]{2,1,0:T(8,128)(2,1)S(1)}, u32[]{:S(2)}, u32[]{:S(2)}) collective-permute-start(bf16[4,32,512]{2,1,0:T(8,128)(2,1)S(1)} %get-tuple-element.104), channel_id=1, source_target_pairs={{0,96},{4,100},{8,104},{12,108},{16,112},{20,116},{24,120},{28,124... | collective-permute-start | bytes 393224 | tf_op jit(solution)/shard_map/ppermute | solution.py:42
  38.5 2.5 %collective-permute-start.12 = (bf16[4,32,512]{2,1,0:T(8,128)(2,1)S(1)}, bf16[4,32,512]{2,1,0:T(8,128)(2,1)S(1)}, u32[]{:S(2)}, u32[]{:S(2)}) collective-permute-start(bf16[4,32,512]{2,1,0:T(8,128)(2,1)S(1)} %get-tuple-element.102), channel_id=1, source_target_pairs={{0,24},{4,28},{8,16},{12,20},{16,8},{20,12},{24,0},{28,4},{32,56},... | collective-permute-start | bytes 393224 | tf_op jit(solution)/shard_map/ppermute | solution.py:42
  41.6 3.1 %collective-permute-done.12 = bf16[4,32,512]{2,1,0:T(8,128)(2,1)S(1)} collective-permute-done((bf16[4,32,512]{2,1,0:T(8,128)(2,1)S(1)}, bf16[4,32,512]{2,1,0:T(8,128)(2,1)S(1)}, u32[]{:S(2)}, u32[]{:S(2)}) %collective-permute-start.12) | collective-permute-done | bytes 131104 | tf_op jit(solution)/shard_map/ppermute | solution.py:42
  46.0 2.7 %collective-permute-start.16 = (bf16[8,32,512]{2,1,0:T(8,128)(2,1)S(1)}, bf16[8,32,512]{2,1,0:T(8,128)(2,1)S(1)}, u32[]{:S(2)}, u32[]{:S(2)}) collective-permute-start(bf16[8,32,512]{2,1,0:T(8,128)(2,1)S(1)} %get-tuple-element.58), channel_id=1, source_target_pairs={{0,24},{4,28},{8,16},{12,20},{16,8},{20,12},{24,0},{28,4},{32,56},... | collective-permute-start | bytes 786440 | tf_op jit(solution)/shard_map/ppermute | solution.py:42
  48.7 2.7 %collective-permute-start.18 = (bf16[1024,128]{1,0:T(8,128)(2,1)S(1)}, bf16[1024,128]{1,0:T(8,128)(2,1)S(1)}, u32[]{:S(2)}, u32[]{:S(2)}) collective-permute-start(bf16[1024,128]{1,0:T(8,128)(2,1)S(1)} %copy-done.11), channel_id=1, source_target_pairs={{0,2},{1,3},{2,0},{3,1},{4,6},{5,7},{6,4},{7,5},{8,10},{9,11},{10,... | collective-permute-start | bytes 786440 | tf_op jit(solution)/shard_map/ppermute | solution.py:46
  62.9 2.2 %collective-permute-start.26 = (bf16[16,32,512]{2,1,0:T(8,128)(2,1)}, bf16[16,32,512]{2,1,0:T(8,128)(2,1)S(1)}, u32[]{:S(2)}, u32[]{:S(2)}) collective-permute-start(bf16[16,32,512]{2,1,0:T(8,128)(2,1)} %pad_maximum_fusion.5.refs_3_), channel_id=1, source_target_pairs={{0,96},{4,100},{8,104},{12,108},{16,112},{20,116},{24,120},{28,124... | collective-permute-start | bytes 1572872 | tf_op jit(solution)/shard_map/ppermute | solution.py:42
  65.1 2.7 %collective-permute-start.27 = (bf16[1024,128]{1,0:T(8,128)(2,1)S(1)}, bf16[1024,128]{1,0:T(8,128)(2,1)S(1)}, u32[]{:S(2)}, u32[]{:S(2)}) collective-permute-start(bf16[1024,128]{1,0:T(8,128)(2,1)S(1)} %copy-done.11), channel_id=1, source_target_pairs={{0,3},{1,0},{2,1},{3,2},{4,7},{5,4},{6,5},{7,6},{8,11},{9,8},{10,9... | collective-permute-start | bytes 786440 | tf_op jit(solution)/shard_map/ppermute | solution.py:46
  68.1 3.7 %collective-permute-done.27 = bf16[1024,128]{1,0:T(8,128)(2,1)S(1)} collective-permute-done((bf16[1024,128]{1,0:T(8,128)(2,1)S(1)}, bf16[1024,128]{1,0:T(8,128)(2,1)S(1)}, u32[]{:S(2)}, u32[]{:S(2)}) %collective-permute-start.27) | collective-permute-done | bytes 262176 | tf_op jit(solution)/shard_map/ppermute | solution.py:46
  71.7 2.5 %collective-permute-start.19 = (bf16[16,32,512]{2,1,0:T(8,128)(2,1)S(1)}, bf16[16,32,512]{2,1,0:T(8,128)(2,1)}, u32[]{:S(2)}, u32[]{:S(2)}) collective-permute-start(bf16[16,32,512]{2,1,0:T(8,128)(2,1)S(1)} %pad_maximum_fusion.2.refs_0_), channel_id=1, source_target_pairs={{0,24},{4,28},{8,16},{12,20},{16,8},{20,12},{24,0},{28,4},{32,56},... | collective-permute-start | bytes 1572872 | tf_op jit(solution)/shard_map/ppermute | solution.py:42
  75.5 3.4 %collective-permute-start.22 = (bf16[16,32,512]{2,1,0:T(8,128)(2,1)}, bf16[16,32,512]{2,1,0:T(8,128)(2,1)}, u32[]{:S(2)}, u32[]{:S(2)}) collective-permute-start(bf16[16,32,512]{2,1,0:T(8,128)(2,1)} %pad_maximum_fusion.5.refs_3_), channel_id=1, source_target_pairs={{0,32},{4,36},{8,40},{12,44},{16,48},{20,52},{24,56},{28,60},{32,0... | collective-permute-start | bytes 1572872 | tf_op jit(solution)/shard_map/ppermute | solution.py:42
  80.4 2.7 %collective-permute-done.19.refs_0_ = bf16[16,32,512]{2,1,0:T(8,128)(2,1)} collective-permute-done((bf16[16,32,512]{2,1,0:T(8,128)(2,1)S(1)}, bf16[16,32,512]{2,1,0:T(8,128)(2,1)}, u32[]{:S(2)}, u32[]{:S(2)}) %collective-permute-start.19) | collective-permute-done | bytes 524320 | tf_op jit(solution)/shard_map/ppermute | solution.py:42
  87.1 4.3 %collective-permute-start.31 = (bf16[16,32,512]{2,1,0:T(8,128)(2,1)}, bf16[16,32,512]{2,1,0:T(8,128)(2,1)}, u32[]{:S(2)}, u32[]{:S(2)}) collective-permute-start(bf16[16,32,512]{2,1,0:T(8,128)(2,1)} %copy-done.9), channel_id=1, source_target_pairs={{0,32},{4,36},{8,40},{12,44},{16,48},{20,52},{24,56},{28,60},{32,0... | collective-permute-start | bytes 1572872 | tf_op jit(solution)/shard_map/ppermute | solution.py:42
  91.5 2.6 %gather_fusion = s32[512,128]{1,0:T(8,128)} fusion(s32[512,128]{1,0:T(8,128)} %bitcast.32, s32[1024]{0:T(1024)S(1)} %pad_clamp_fusion), kind=kCustom, calls=%fused_computation | custom fusion | bytes 526336 | tf_op jit(solution)/shard_map/gather | solution.py:352
  102.6 2.2 %pack.3.table = bf16[256,32,512]{2,1,0:T(8,128)(2,1)S(1)} custom-call(bf16[16,32,512]{2,1,0:T(8,128)(2,1)} %collective-permute-done.19.refs_0_, bf16[16,32,512]{2,1,0:T(8,128)(2,1)} %collective-permute-done.20.refs_1_, bf16[16,32,512]{2,1,0:T(8,128)(2,1)} %collective-permute-done.21.refs_2_, ...), custom_call_target="tpu_custom_call", output_to_operand_aliasing={{}: (8, {})} | custom-call | bytes 8388608 | tf_op jit(solution)/shard_map/pack/pallas_call | solution.py:136
  104.8 3.4 %attend_other.2 = (bf16[2,256,512]{2,1,0:T(8,128)(2,1)S(1)}, f32[2,8,256]{2,1,0:T(8,128)S(1)}) custom-call(s32[512]{0:T(512)S(1)} %fusion.9.row_ref, s32[1]{0:T(128)} %bitcast.15.rank_ref, bf16[4,1024,128]{2,1,0:T(8,128)(2,1)S(1)} %collective-permute-done.32.q_ref, f32[8,2048]{1,0:T(8,128)S(1)} %reshape.91.lq_ref, bf16[256,32,512]{2,1,0:T(8,128)(2,1)S(1)} %pack.3.table), custom_call_target="tpu_custom_call" | custom-call | flops 2147483648 | bytes 2097152 | tf_op jit(solution)/shard_map/attend_other/pallas_call | solution.py:201
  108.3 3.4 %attend_other.3 = (bf16[2,256,512]{2,1,0:T(8,128)(2,1)S(1)}, f32[2,8,256]{2,1,0:T(8,128)S(1)}) custom-call(s32[512]{0:T(512)S(1)} %fusion.9.row_ref, s32[1]{0:T(128)} %bitcast.15.rank_ref, bf16[4,1024,128]{2,1,0:T(8,128)(2,1)S(1)} %collective-permute-done.32.q_ref, f32[8,2048]{1,0:T(8,128)S(1)} %reshape.91.lq_ref, bf16[256,32,512]{2,1,0:T(8,128)(2,1)S(1)} %pack.3.table), custom_call_target="tpu_custom_call" | custom-call | flops 2147483648 | bytes 2097152 | tf_op jit(solution)/shard_map/attend_other/pallas_call | solution.py:201
  113.9 3.7 %attend_own.2 = (bf16[2,288,128]{2,1,0:T(8,128)(2,1)S(1)}, bf16[2,288,128]{2,1,0:T(8,128)(2,1)S(1)}, bf16[2,288,128]{2,1,0:T(8,128)(2,1)S(1)}, bf16[2,288,128]{2,1,0:T(8,128)(2,1)S(1)}) custom-call(s32[512]{0:T(512)S(1)} %fusion.9.row_ref, s32[1]{0:T(128)} %bitcast.15.rank_ref, bf16[4,1024,128]{2,1,0:T(8,128)(2,1)S(1)} %pad_maximum_fusion.q_ref, ...), custom_call_target="tpu_custom_call" | custom-call | flops 2147483648 | bytes 2097152 | tf_op jit(solution)/shard_map/attend_own/pallas_call | solution.py:201
  121.5 2.5 %collective-permute-start.37 = (bf16[2,288,128]{2,1,0:T(8,128)(2,1)S(1)}, bf16[2,288,128]{2,1,0:T(8,128)(2,1)S(1)}, u32[]{:S(2)}, u32[]{:S(2)}) collective-permute-start(bf16[2,288,128]{2,1,0:T(8,128)(2,1)S(1)} %get-tuple-element.87), channel_id=1, source_target_pairs={{0,3},{1,0},{2,1},{3,2},{4,7},{5,4},{6,5},{7,6},{8,11},{9,8},{10,9... | collective-permute-start | bytes 442376 | tf_op jit(solution)/shard_map/ppermute | solution.py:46
  124.0 3.7 %attend_own.3 = (bf16[2,288,128]{2,1,0:T(8,128)(2,1)S(1)}, bf16[2,288,128]{2,1,0:T(8,128)(2,1)S(1)}, bf16[2,288,128]{2,1,0:T(8,128)(2,1)S(1)}, bf16[2,288,128]{2,1,0:T(8,128)(2,1)S(1)}) custom-call(s32[512]{0:T(512)S(1)} %fusion.9.row_ref, s32[1]{0:T(128)} %bitcast.15.rank_ref, bf16[4,1024,128]{2,1,0:T(8,128)(2,1)S(1)} %pad_maximum_fusion.q_ref, ...), custom_call_target="tpu_custom_call" | custom-call | flops 2147483648 | bytes 2097152 | tf_op jit(solution)/shard_map/attend_own/pallas_call | solution.py:201
  131.1 6.4 %collective-permute-done.40.refs_5_ = bf16[2,288,128]{2,1,0:T(8,128)(2,1)S(1)} collective-permute-done((bf16[2,288,128]{2,1,0:T(8,128)(2,1)S(1)}, bf16[2,288,128]{2,1,0:T(8,128)(2,1)S(1)}, u32[]{:S(2)}, u32[]{:S(2)}) %collective-permute-start.40) | collective-permute-done | bytes 147488 | tf_op jit(solution)/shard_map/ppermute | solution.py:46
  (124 shorter events, 58.4 us)
Async XLA Ops:
  4.2 16.4 %collective-permute-start.1 = (bf16[512,256]{1,0:T(8,128)(2,1)S(1)}, bf16[512,256]{1,0:T(8,128)(2,1)S(1)}, u32[]{:S(2)}, u32[]{:S(2)}) collective-permute-start(bf16[512,256]{1,0:T(8,128)(2,1)S(1)} %bitcast.39), channel_id=1, source_target_pairs={{0,1},{1,2},{2,3},{3,0},{4,5},{5,6},{6,7},{7,4},{8,9},{9,10},{10,1... | collective-permute-start | bytes 786440 | tf_op jit(solution)/shard_map/ppermute | solution.py:46
  5.8 14.8 %collective-permute-start.3 = (bf16[512,256]{1,0:T(8,128)(2,1)S(1)}, bf16[512,256]{1,0:T(8,128)(2,1)S(1)}, u32[]{:S(2)}, u32[]{:S(2)}) collective-permute-start(bf16[512,256]{1,0:T(8,128)(2,1)S(1)} %bitcast.38), channel_id=1, source_target_pairs={{0,3},{1,0},{2,1},{3,2},{4,7},{5,4},{6,5},{7,6},{8,11},{9,8},{10,9... | collective-permute-start | bytes 786440 | tf_op jit(solution)/shard_map/ppermute | solution.py:46
  7.9 12.6 %collective-permute-start.5 = (bf16[128,512]{1,0:T(8,128)(2,1)S(1)}, bf16[128,512]{1,0:T(8,128)(2,1)S(1)}, u32[]{:S(2)}, u32[]{:S(2)}) collective-permute-start(bf16[128,512]{1,0:T(8,128)(2,1)S(1)} %constant_dynamic-slice_fusion.refs_4_), channel_id=1, source_target_pairs={{0,2},{1,3},{2,0},{3,1},{4,6},{5,7},{6,4},{7,5},{8,10},{9,11},{10,... | collective-permute-start | bytes 393224 | tf_op jit(solution)/shard_map/ppermute | solution.py:46
  10.7 9.8 %collective-permute-start.6 = (bf16[128,512]{1,0:T(8,128)(2,1)S(1)}, bf16[128,512]{1,0:T(8,128)(2,1)S(1)}, u32[]{:S(2)}, u32[]{:S(2)}) collective-permute-start(bf16[128,512]{1,0:T(8,128)(2,1)S(1)} %constant_dynamic-slice_fusion.refs_4_), channel_id=1, source_target_pairs={{0,3},{1,0},{2,1},{3,2},{4,7},{5,4},{6,5},{7,6},{8,11},{9,8},{10,9... | collective-permute-start | bytes 393224 | tf_op jit(solution)/shard_map/ppermute | solution.py:46
  20.6 10.3 %collective-permute-start.7 = (bf16[4,128,512]{2,1,0:T(8,128)(2,1)S(1)}, bf16[4,128,512]{2,1,0:T(8,128)(2,1)S(1)}, u32[]{:S(2)}, u32[]{:S(2)}) collective-permute-start(bf16[4,128,512]{2,1,0:T(8,128)(2,1)S(1)} %pad_maximum_fusion.1), channel_id=1, source_target_pairs={{0,4},{4,0},{8,12},{12,8},{16,20},{20,16},{24,28},{28,24},{32,36},... | collective-permute-start | bytes 1572872 | tf_op jit(solution)/shard_map/ppermute | solution.py:42
  20.7 10.2 %collective-permute-start.2 = (bf16[512,256]{1,0:T(8,128)(2,1)S(1)}, bf16[512,256]{1,0:T(8,128)(2,1)S(1)}, u32[]{:S(2)}, u32[]{:S(2)}) collective-permute-start(bf16[512,256]{1,0:T(8,128)(2,1)S(1)} %bitcast.37), channel_id=1, source_target_pairs={{0,2},{1,3},{2,0},{3,1},{4,6},{5,7},{6,4},{7,5},{8,10},{9,11},{10,... | collective-permute-start | bytes 786440 | tf_op jit(solution)/shard_map/ppermute | solution.py:46
  32.2 12.6 %collective-permute-start.13 = (bf16[1024,128]{1,0:T(8,128)(2,1)S(1)}, bf16[1024,128]{1,0:T(8,128)(2,1)S(1)}, u32[]{:S(2)}, u32[]{:S(2)}) collective-permute-start(bf16[1024,128]{1,0:T(8,128)(2,1)S(1)} %copy-done.11), channel_id=1, source_target_pairs={{0,1},{1,2},{2,3},{3,0},{4,5},{5,6},{6,7},{7,4},{8,9},{9,10},{10,1... | collective-permute-start | bytes 786440 | tf_op jit(solution)/shard_map/ppermute | solution.py:46
  58.4 15.9 %collective-permute-start.23 = (bf16[16,32,512]{2,1,0:T(8,128)(2,1)S(1)}, bf16[16,32,512]{2,1,0:T(8,128)(2,1)S(1)}, u32[]{:S(2)}, u32[]{:S(2)}) collective-permute-start(bf16[16,32,512]{2,1,0:T(8,128)(2,1)S(1)} %pad_maximum_fusion.2.refs_0_), channel_id=1, source_target_pairs={{0,8},{4,12},{8,0},{12,4},{16,24},{20,28},{24,16},{28,20},{32,40},... | collective-permute-start | bytes 1572872 | tf_op jit(solution)/shard_map/ppermute | solution.py:42
  60.4 14.4 %collective-permute-start.24 = (bf16[16,32,512]{2,1,0:T(8,128)(2,1)S(1)}, bf16[16,32,512]{2,1,0:T(8,128)(2,1)S(1)}, u32[]{:S(2)}, u32[]{:S(2)}) collective-permute-start(bf16[16,32,512]{2,1,0:T(8,128)(2,1)S(1)} %pad_maximum_fusion.3.refs_1_), channel_id=1, source_target_pairs={{0,24},{4,28},{8,16},{12,20},{16,8},{20,12},{24,0},{28,4},{32,56},... | collective-permute-start | bytes 1572872 | tf_op jit(solution)/shard_map/ppermute | solution.py:42
  60.9 14.5 %collective-permute-start.25 = (bf16[16,32,512]{2,1,0:T(8,128)(2,1)}, bf16[16,32,512]{2,1,0:T(8,128)(2,1)S(1)}, u32[]{:S(2)}, u32[]{:S(2)}) collective-permute-start(bf16[16,32,512]{2,1,0:T(8,128)(2,1)} %pad_maximum_fusion.4.refs_2_), channel_id=1, source_target_pairs={{0,32},{4,36},{8,40},{12,44},{16,48},{20,52},{24,56},{28,60},{32,0... | collective-permute-start | bytes 1572872 | tf_op jit(solution)/shard_map/ppermute | solution.py:42
  62.9 16.0 %collective-permute-start.26 = (bf16[16,32,512]{2,1,0:T(8,128)(2,1)}, bf16[16,32,512]{2,1,0:T(8,128)(2,1)S(1)}, u32[]{:S(2)}, u32[]{:S(2)}) collective-permute-start(bf16[16,32,512]{2,1,0:T(8,128)(2,1)} %pad_maximum_fusion.5.refs_3_), channel_id=1, source_target_pairs={{0,96},{4,100},{8,104},{12,108},{16,112},{20,116},{24,120},{28,124... | collective-permute-start | bytes 1572872 | tf_op jit(solution)/shard_map/ppermute | solution.py:42
  71.7 11.3 %collective-permute-start.19 = (bf16[16,32,512]{2,1,0:T(8,128)(2,1)S(1)}, bf16[16,32,512]{2,1,0:T(8,128)(2,1)}, u32[]{:S(2)}, u32[]{:S(2)}) collective-permute-start(bf16[16,32,512]{2,1,0:T(8,128)(2,1)S(1)} %pad_maximum_fusion.2.refs_0_), channel_id=1, source_target_pairs={{0,24},{4,28},{8,16},{12,20},{16,8},{20,12},{24,0},{28,4},{32,56},... | collective-permute-start | bytes 1572872 | tf_op jit(solution)/shard_map/ppermute | solution.py:42
  74.3 10.5 %collective-permute-start.20 = (bf16[16,32,512]{2,1,0:T(8,128)(2,1)S(1)}, bf16[16,32,512]{2,1,0:T(8,128)(2,1)}, u32[]{:S(2)}, u32[]{:S(2)}) collective-permute-start(bf16[16,32,512]{2,1,0:T(8,128)(2,1)S(1)} %pad_maximum_fusion.3.refs_1_), channel_id=1, source_target_pairs={{0,8},{4,12},{8,0},{12,4},{16,24},{20,28},{24,16},{28,20},{32,40},... | collective-permute-start | bytes 1572872 | tf_op jit(solution)/shard_map/ppermute | solution.py:42
  74.8 10.7 %collective-permute-start.21 = (bf16[16,32,512]{2,1,0:T(8,128)(2,1)}, bf16[16,32,512]{2,1,0:T(8,128)(2,1)}, u32[]{:S(2)}, u32[]{:S(2)}) collective-permute-start(bf16[16,32,512]{2,1,0:T(8,128)(2,1)} %pad_maximum_fusion.4.refs_2_), channel_id=1, source_target_pairs={{0,96},{4,100},{8,104},{12,108},{16,112},{20,116},{24,120},{28,124... | collective-permute-start | bytes 1572872 | tf_op jit(solution)/shard_map/ppermute | solution.py:42
  75.5 11.6 %collective-permute-start.22 = (bf16[16,32,512]{2,1,0:T(8,128)(2,1)}, bf16[16,32,512]{2,1,0:T(8,128)(2,1)}, u32[]{:S(2)}, u32[]{:S(2)}) collective-permute-start(bf16[16,32,512]{2,1,0:T(8,128)(2,1)} %pad_maximum_fusion.5.refs_3_), channel_id=1, source_target_pairs={{0,32},{4,36},{8,40},{12,44},{16,48},{20,52},{24,56},{28,60},{32,0... | collective-permute-start | bytes 1572872 | tf_op jit(solution)/shard_map/ppermute | solution.py:42
  79.9 24.9 %collective-permute-start.32 = (bf16[4,1024,128]{2,1,0:T(8,128)(2,1)S(1)}, bf16[4,1024,128]{2,1,0:T(8,128)(2,1)S(1)}, u32[]{:S(2)}, u32[]{:S(2)}) collective-permute-start(bf16[4,1024,128]{2,1,0:T(8,128)(2,1)S(1)} %pad_maximum_fusion.q_ref), channel_id=1, source_target_pairs={{0,4},{4,0},{8,12},{12,8},{16,20},{20,16},{24,28},{28,24},{32,36},... | collective-permute-start | bytes 3145736 | tf_op jit(solution)/shard_map/ppermute | solution.py:42
  83.1 19.4 %collective-permute-start.28 = (bf16[16,32,512]{2,1,0:T(8,128)(2,1)}, bf16[16,32,512]{2,1,0:T(8,128)(2,1)}, u32[]{:S(2)}, u32[]{:S(2)}) collective-permute-start(bf16[16,32,512]{2,1,0:T(8,128)(2,1)} %copy-done.3), channel_id=1, source_target_pairs={{0,24},{4,28},{8,16},{12,20},{16,8},{20,12},{24,0},{28,4},{32,56},... | collective-permute-start | bytes 1572872 | tf_op jit(solution)/shard_map/ppermute | solution.py:42
  84.8 17.7 %collective-permute-start.29 = (bf16[16,32,512]{2,1,0:T(8,128)(2,1)}, bf16[16,32,512]{2,1,0:T(8,128)(2,1)}, u32[]{:S(2)}, u32[]{:S(2)}) collective-permute-start(bf16[16,32,512]{2,1,0:T(8,128)(2,1)} %copy-done.5), channel_id=1, source_target_pairs={{0,8},{4,12},{8,0},{12,4},{16,24},{20,28},{24,16},{28,20},{32,40},... | collective-permute-start | bytes 1572872 | tf_op jit(solution)/shard_map/ppermute | solution.py:42
  85.5 17.1 %collective-permute-start.30 = (bf16[16,32,512]{2,1,0:T(8,128)(2,1)}, bf16[16,32,512]{2,1,0:T(8,128)(2,1)}, u32[]{:S(2)}, u32[]{:S(2)}) collective-permute-start(bf16[16,32,512]{2,1,0:T(8,128)(2,1)} %copy-done.7), channel_id=1, source_target_pairs={{0,96},{4,100},{8,104},{12,108},{16,112},{20,116},{24,120},{28,124... | collective-permute-start | bytes 1572872 | tf_op jit(solution)/shard_map/ppermute | solution.py:42
  87.1 15.5 %collective-permute-start.31 = (bf16[16,32,512]{2,1,0:T(8,128)(2,1)}, bf16[16,32,512]{2,1,0:T(8,128)(2,1)}, u32[]{:S(2)}, u32[]{:S(2)}) collective-permute-start(bf16[16,32,512]{2,1,0:T(8,128)(2,1)} %copy-done.9), channel_id=1, source_target_pairs={{0,32},{4,36},{8,40},{12,44},{16,48},{20,52},{24,56},{28,60},{32,0... | collective-permute-start | bytes 1572872 | tf_op jit(solution)/shard_map/ppermute | solution.py:42
  111.8 12.2 %collective-permute-start.38 = (bf16[2,256,512]{2,1,0:T(8,128)(2,1)S(1)}, bf16[2,256,512]{2,1,0:T(8,128)(2,1)S(1)}, u32[]{:S(2)}, u32[]{:S(2)}) collective-permute-start(bf16[2,256,512]{2,1,0:T(8,128)(2,1)S(1)} %get-tuple-element.88), channel_id=1, source_target_pairs={{0,4},{4,0},{8,12},{12,8},{16,20},{20,16},{24,28},{28,24},{32,36},... | collective-permute-start | bytes 1572872 | tf_op jit(solution)/shard_map/ppermute | solution.py:42
  112.4 11.6 %collective-permute-start.39 = (f32[2,8,256]{2,1,0:T(8,128)S(1)}, f32[2,8,256]{2,1,0:T(8,128)S(1)}, u32[]{:S(2)}, u32[]{:S(2)}) collective-permute-start(f32[2,8,256]{2,1,0:T(8,128)S(1)} %get-tuple-element.89), channel_id=1, source_target_pairs={{0,4},{4,0},{8,12},{12,8},{16,20},{20,16},{24,28},{28,24},{32,36},... | collective-permute-start | bytes 49160 | tf_op jit(solution)/shard_map/ppermute | solution.py:42
  117.6 11.7 %collective-permute-start.35 = (bf16[2,288,128]{2,1,0:T(8,128)(2,1)S(1)}, bf16[2,288,128]{2,1,0:T(8,128)(2,1)S(1)}, u32[]{:S(2)}, u32[]{:S(2)}) collective-permute-start(bf16[2,288,128]{2,1,0:T(8,128)(2,1)S(1)} %get-tuple-element.85), channel_id=1, source_target_pairs={{0,1},{1,2},{2,3},{3,0},{4,5},{5,6},{6,7},{7,4},{8,9},{9,10},{10,1... | collective-permute-start | bytes 442376 | tf_op jit(solution)/shard_map/ppermute | solution.py:46
  119.7 11.4 %collective-permute-start.36 = (bf16[2,288,128]{2,1,0:T(8,128)(2,1)S(1)}, bf16[2,288,128]{2,1,0:T(8,128)(2,1)S(1)}, u32[]{:S(2)}, u32[]{:S(2)}) collective-permute-start(bf16[2,288,128]{2,1,0:T(8,128)(2,1)S(1)} %get-tuple-element.86), channel_id=1, source_target_pairs={{0,2},{1,3},{2,0},{3,1},{4,6},{5,7},{6,4},{7,5},{8,10},{9,11},{10,... | collective-permute-start | bytes 442376 | tf_op jit(solution)/shard_map/ppermute | solution.py:46
  (32 other events, 350.9 us)

commit v9 on v8

--- a/solution.py
+++ b/solution.py
@@ -79,11 +79,14 @@
 PART = 2
 
 
-def one_block(rank, block, base, q_ref, lq_ref, row_ref, table, picked, scores):
+def one_block(rank, block, side, q_refs, lq_ref, row_ref, table, picked, scores, gathered):
+    base = side * 2 * PART
     for j in range(PICKS):
         picked[pl.ds(j * ROWS, ROWS), :] = table[row_ref[(base + block) * PICKS + j]]
     here = pl.ds(block * BLK, BLK)
-    query = jnp.concatenate([q_ref[lax.rem(rank + TP - s, TP), here] for s in range(TP)], axis=1)
+    for d in range(TP):
+        gathered[lax.rem(rank + TP - d, TP)] = q_refs[d][side, here]
+    query = jnp.concatenate([gathered[s] for s in range(TP)], axis=1)
     top = jnp.full((BLK, 128), LOW, jnp.float32)
     for n in range(COLS // TILE):
         cols = pl.ds(n * TILE, TILE)
@@ -146,12 +149,14 @@
     )(*pieces, *given)
 
 
-def first_kernel(start, row_ref, rank_ref, q_ref, lq_ref, table, *refs):
-    out_ref, stat_ref, picked, scores = refs
+def first_kernel(start, row_ref, rank_ref, *refs):
+    q_refs, (lq_ref, table) = refs[:TP], refs[TP : TP + 2]
+    out_ref, stat_ref, picked, scores, gathered = refs[TP + 2 :]
 
     for n in range(PART):
         top, total, acc = one_block(
-            rank_ref[0], start + n, 0, q_ref, lq_ref, row_ref, table, picked.at[n], scores.at[n]
+            rank_ref[0], start + n, 0, q_refs, lq_ref, row_ref, table,
+            picked.at[n], scores.at[n], gathered.at[n],
         )
         out_ref[n] = acc.astype(jnp.bfloat16)
         stat_ref[n] = rows_of(top, total)
@@ -171,14 +176,16 @@
     return jnp.concatenate(halves, axis=1)
 
 
-def second_kernel(start, row_ref, rank_ref, q_ref, lq_ref, table, *refs):
+def second_kernel(start, row_ref, rank_ref, *refs):
+    q_refs, (lq_ref, table), refs = refs[:TP], refs[TP : TP + 2], refs[TP + 2 :]
     other_ref, other_stat_ref, pos_ref = refs[:3]
     outs = refs[3:7]
-    picked, scores, quarters = refs[7:]
+    picked, scores, gathered, quarters = refs[7:]
 
     for n in range(PART):
         top, total, acc = one_block(
-            rank_ref[0], start + n, 2 * PART, q_ref, lq_ref, row_ref, table, picked.at[n], scores.at[n]
+            rank_ref[0], start + n, 1, q_refs, lq_ref, row_ref, table,
+            picked.at[n], scores.at[n], gathered.at[n],
         )
         theirs = jnp.transpose(jnp.concatenate([other_stat_ref[n]] * 16, axis=0))
         their_top, their_total = theirs[:, 0:1], theirs[:, 1:2]
@@ -206,6 +213,7 @@
         scratch_shapes=[
             pltpu.VMEM((PART, COLS, E), jnp.bfloat16),
             pltpu.VMEM((PART, BLK, COLS), jnp.float32),
+            pltpu.VMEM((PART, TP, BLK, 128), jnp.bfloat16),
         ]
         + scratch,
         compiler_params=pltpu.CompilerParams(vmem_limit_bytes=32 << 20),
@@ -284,19 +292,24 @@
 def spread(items, query):
     held = [items[n * 4 : n * 4 + 4] for n in range(4)]
     queries = [query]
-    for step in range(3):
+    for step in range(2):
         got = [send(h, **{st[step][0]: st[step][1]}) for h, st in zip(held, STREAMS)]
         got = together(*got, send_x(query, step + 1), query)
         queries.append(got[4])
         query = got[5]
-        if step < 2:
-            held = together(*[jnp.concatenate([h, g]) for h, g in zip(held, got)])
-    third = got[:4]
+        held = together(*[jnp.concatenate([h, g]) for h, g in zip(held, got)], query)
+        query = held.pop()
+    third = [send(h, **{st[2][0]: st[2][1]}) for h, st in zip(held, STREAMS)]
+    queries.append(send_x(query, 3))
+    held, third = zip(*[together(h, t) for h, t in zip(held, third)])
+    held, third = list(held), list(third)
     fourth = [send(h, **{st[3][0]: st[3][1]}) for h, st in zip(held, STREAMS)]
+    third, fourth = zip(*[together(t, f) for t, f in zip(third, fourth)])
+    third, fourth = list(third), list(fourth)
     fifth = [send(h, **{st[3][0]: st[3][1]}) for h, st in zip(third, STREAMS)]
     table = pack(held + third, (0, 4, 8, 12, 1, 5, 9, 13))
     table = pack(fourth + fifth, (2, 6, 10, 14, 3, 7, 11, 15), table)
-    return table, jnp.stack(queries)
+    return table, queries
 
 
 def place_of(flipped, first):
@@ -329,11 +342,11 @@
     hiddens = [piece(0)] + [send_x(piece(d), d) for d in (1, 2, 3)]
     theirs_w = send(together(jnp.stack(mine_w), hiddens[1], hiddens[3])[0], c=1)
     picks = jnp.concatenate([send(neg_blocks, c=1), neg_blocks])
+    both_query = jnp.stack([send(query_emb, c=1), query_emb])
     items, late_query, picks = together(
-        tower(core_id, hiddens, mine_w, theirs_w), query_emb, picks
+        tower(core_id, hiddens, mine_w, theirs_w), both_query, picks
     )
-    table, query = spread(items, late_query)
-    other_query = send(query, c=1)
+    table, queries = spread(items, late_query)
     pos_part = SCALE * jnp.sum(
         query_emb.astype(jnp.float32) * positive_emb.astype(jnp.float32), axis=1
     ).reshape(qblocks, 1, BLK)
@@ -367,7 +380,7 @@
             first_kernel,
             start,
             (rows, rank_id),
-            (other_query, lq, table),
+            (*queries, lq, table),
             raw,
             [],
             "attend_other",
@@ -379,7 +392,7 @@
             second_kernel,
             start,
             (rows, rank_id),
-            (query, lq, table, *other, pos_part),
+            (*queries, lq, table, *other, pos_part),
             (share,) * TP,
             [pltpu.VMEM((TP, BLK, 128), jnp.bfloat16)],
             "attend_own",

time: 140 us -> 143 us (1.021)
  waiting for transfers between devices: 42.1 us -> 53.6 us
  starting transfers between devices: 60.1 us -> 53.4 us
  local copies, waits for them, and re-layouts: 10.3 us -> 5.33 us
  Pallas kernels: 20.9 us -> 22.7 us
    ppermute x28, waiting for transfers between devices: 15.1 us -> 34.8 us  [send(): return lax.ppermute(value, 'cat', cat_perm(y, z, c))]
    ppermute x15, waiting for transfers between devices: 26.9 us -> 18.8 us  [send_x(): return lax.ppermute(value, 'tp', [(i, (i + d) % TP) for i in range(TP)])]
    ppermute x28, starting transfers between devices: 34.7 us -> 29.1 us  [send(): return lax.ppermute(value, 'cat', cat_perm(y, z, c))]
    unnamed x26 -> x10, local copies, waits for them, and re-layouts: 5 us -> 0.03 us
  transfers between devices with their start and end apart: 43 -> 43, of which waited for: 18 -> 25; matrix products, arithmetic and copies ran while one was open for 5% -> 6% of each run, Pallas kernels for 10% -> 11%
where the time goes in v9:
time: 143 us; the launch traced here: 142 us
  waiting for transfers between devices  53.6 us (37%)
  starting transfers between devices  53.4 us (37%)
  Pallas kernels  22.7 us (16%)
  other arithmetic  6.18 us (4%)
  local copies, waits for them, and re-layouts  5.33 us (4%)
    ppermute x28, waiting for transfers between devices, send(): return lax.ppermute(value, 'cat', cat_perm(y, z, c))  34.8 us
    ppermute x28, starting transfers between devices, send(): return lax.ppermute(value, 'cat', cat_perm(y, z, c))  29.1 us
    ppermute x15, starting transfers between devices, send_x(): return lax.ppermute(value, 'tp', [(i, (i + d) % TP) for i in range(TP)])  24.3 us
    ppermute x15, waiting for transfers between devices, send_x(): return lax.ppermute(value, 'tp', [(i, (i + d) % TP) for i in range(TP)])  18.8 us
    pallas_call x4, Pallas kernels, attend(): pl.pallas_call(functools.partial(body, start), in_specs=[pl.BlockSpec(mem...  15.5 us
    pallas_call x2, Pallas kernels, pack(): pl.pallas_call(functools.partial(pack_kernel, places), out_shape=jax.Shap...  4.14 us
  transfers between devices with their start and end apart: 43, of which 25 were waited for; matrix products, arithmetic and copies ran while one was open for 6% of the time, Pallas kernels for 11%

profile of v9, /device:TPU:0, one launch (start us, length us, event | category | flops | bytes accessed | tf_op | source)
XLA Modules:
  0.0 142.3 jit_solution(189815357888205042)
XLA Ops:
  11.5 7.0 %collective-permute-done.5.refs_6_ = bf16[128,512]{1,0:T(8,128)(2,1)S(1)} collective-permute-done((bf16[128,512]{1,0:T(8,128)(2,1)S(1)}, bf16[128,512]{1,0:T(8,128)(2,1)S(1)}, u32[]{:S(2)}, u32[]{:S(2)}) %collective-permute-start.5) | collective-permute-done | bytes 131104 | tf_op jit(solution)/shard_map/ppermute | solution.py:46
  20.2 2.7 %collective-permute-start.2 = (bf16[512,256]{1,0:T(8,128)(2,1)S(1)}, bf16[512,256]{1,0:T(8,128)(2,1)S(1)}, u32[]{:S(2)}, u32[]{:S(2)}) collective-permute-start(bf16[512,256]{1,0:T(8,128)(2,1)S(1)} %bitcast.35), channel_id=1, source_target_pairs={{0,2},{1,3},{2,0},{3,1},{4,6},{5,7},{6,4},{7,5},{8,10},{9,11},{10,... | collective-permute-start | bytes 786440 | tf_op jit(solution)/shard_map/ppermute | solution.py:46
  26.0 4.0 %collective-permute-done.2.refs_2_ = bf16[512,256]{1,0:T(8,128)(2,1)S(1)} collective-permute-done((bf16[512,256]{1,0:T(8,128)(2,1)S(1)}, bf16[512,256]{1,0:T(8,128)(2,1)S(1)}, u32[]{:S(2)}, u32[]{:S(2)}) %collective-permute-start.2) | collective-permute-done | bytes 262176 | tf_op jit(solution)/shard_map/ppermute | solution.py:46
  34.5 2.2 %collective-permute-start.11 = (bf16[4,32,512]{2,1,0:T(8,128)(2,1)S(1)}, bf16[4,32,512]{2,1,0:T(8,128)(2,1)S(1)}, u32[]{:S(2)}, u32[]{:S(2)}) collective-permute-start(bf16[4,32,512]{2,1,0:T(8,128)(2,1)S(1)} %get-tuple-element.130), channel_id=1, source_target_pairs={{0,96},{4,100},{8,104},{12,108},{16,112},{20,116},{24,120},{28,124... | collective-permute-start | bytes 393224 | tf_op jit(solution)/shard_map/ppermute | solution.py:42
  38.6 2.5 %collective-permute-start.13 = (bf16[4,32,512]{2,1,0:T(8,128)(2,1)S(1)}, bf16[4,32,512]{2,1,0:T(8,128)(2,1)S(1)}, u32[]{:S(2)}, u32[]{:S(2)}) collective-permute-start(bf16[4,32,512]{2,1,0:T(8,128)(2,1)S(1)} %get-tuple-element.128), channel_id=1, source_target_pairs={{0,24},{4,28},{8,16},{12,20},{16,8},{20,12},{24,0},{28,4},{32,56},... | collective-permute-start | bytes 393224 | tf_op jit(solution)/shard_map/ppermute | solution.py:42
  41.7 3.1 %collective-permute-done.13 = bf16[4,32,512]{2,1,0:T(8,128)(2,1)S(1)} collective-permute-done((bf16[4,32,512]{2,1,0:T(8,128)(2,1)S(1)}, bf16[4,32,512]{2,1,0:T(8,128)(2,1)S(1)}, u32[]{:S(2)}, u32[]{:S(2)}) %collective-permute-start.13) | collective-permute-done | bytes 131104 | tf_op jit(solution)/shard_map/ppermute | solution.py:42
  45.7 2.2 %collective-permute-start.19 = (bf16[2,1024,128]{2,1,0:T(8,128)(2,1)S(1)}, bf16[2,1024,128]{2,1,0:T(8,128)(2,1)S(1)}, u32[]{:S(2)}, u32[]{:S(2)}) collective-permute-start(bf16[2,1024,128]{2,1,0:T(8,128)(2,1)S(1)} %pad_maximum_fusion.1.refs_0_), channel_id=1, source_target_pairs={{0,2},{1,3},{2,0},{3,1},{4,6},{5,7},{6,4},{7,5},{8,10},{9,11},{10,... | collective-permute-start | bytes 1572872 | tf_op jit(solution)/shard_map/ppermute | solution.py:46
  47.9 2.4 %collective-permute-start.15 = (bf16[8,32,512]{2,1,0:T(8,128)(2,1)S(1)}, bf16[8,32,512]{2,1,0:T(8,128)(2,1)S(1)}, u32[]{:S(2)}, u32[]{:S(2)}) collective-permute-start(bf16[8,32,512]{2,1,0:T(8,128)(2,1)S(1)} %get-tuple-element.70), channel_id=1, source_target_pairs={{0,96},{4,100},{8,104},{12,108},{16,112},{20,116},{24,120},{28,124... | collective-permute-start | bytes 786440 | tf_op jit(solution)/shard_map/ppermute | solution.py:42
  50.5 4.0 %collective-permute-start.17 = (bf16[8,32,512]{2,1,0:T(8,128)(2,1)S(1)}, bf16[8,32,512]{2,1,0:T(8,128)(2,1)S(1)}, u32[]{:S(2)}, u32[]{:S(2)}) collective-permute-start(bf16[8,32,512]{2,1,0:T(8,128)(2,1)S(1)} %get-tuple-element.72), channel_id=1, source_target_pairs={{0,24},{4,28},{8,16},{12,20},{16,8},{20,12},{24,0},{28,4},{32,56},... | collective-permute-start | bytes 786440 | tf_op jit(solution)/shard_map/ppermute | solution.py:42
  56.7 2.2 %collective-permute-done.17 = bf16[8,32,512]{2,1,0:T(8,128)(2,1)S(1)} collective-permute-done((bf16[8,32,512]{2,1,0:T(8,128)(2,1)S(1)}, bf16[8,32,512]{2,1,0:T(8,128)(2,1)S(1)}, u32[]{:S(2)}, u32[]{:S(2)}) %collective-permute-start.17) | collective-permute-done | bytes 262176 | tf_op jit(solution)/shard_map/ppermute | solution.py:42
  58.9 2.0 %collective-permute-done.18 = bf16[8,32,512]{2,1,0:T(8,128)(2,1)S(1)} collective-permute-done((bf16[8,32,512]{2,1,0:T(8,128)(2,1)S(1)}, bf16[8,32,512]{2,1,0:T(8,128)(2,1)S(1)}, u32[]{:S(2)}, u32[]{:S(2)}) %collective-permute-start.18) | collective-permute-done | bytes 262176 | tf_op jit(solution)/shard_map/ppermute | solution.py:42
  64.6 3.9 %collective-permute-start.22 = (bf16[16,32,512]{2,1,0:T(8,128)(2,1)}, bf16[16,32,512]{2,1,0:T(8,128)(2,1)}, u32[]{:S(2)}, u32[]{:S(2)}) collective-permute-start(bf16[16,32,512]{2,1,0:T(8,128)(2,1)} %pad_maximum_fusion.3.refs_1_), channel_id=1, source_target_pairs={{0,24},{4,28},{8,16},{12,20},{16,8},{20,12},{24,0},{28,4},{32,56},... | collective-permute-start | bytes 1572872 | tf_op jit(solution)/shard_map/ppermute | solution.py:42
  68.7 5.7 %collective-permute-done.26.refs_7_ = bf16[16,32,512]{2,1,0:T(8,128)(2,1)} collective-permute-done((bf16[16,32,512]{2,1,0:T(8,128)(2,1)S(1)}, bf16[16,32,512]{2,1,0:T(8,128)(2,1)}, u32[]{:S(2)}, u32[]{:S(2)}) %collective-permute-start.26) | collective-permute-done | bytes 524320 | tf_op jit(solution)/shard_map/ppermute | solution.py:42
  74.9 3.2 %collective-permute-done.24.refs_6_ = bf16[16,32,512]{2,1,0:T(8,128)(2,1)} collective-permute-done((bf16[16,32,512]{2,1,0:T(8,128)(2,1)S(1)}, bf16[16,32,512]{2,1,0:T(8,128)(2,1)}, u32[]{:S(2)}, u32[]{:S(2)}) %collective-permute-start.24) | collective-permute-done | bytes 524320 | tf_op jit(solution)/shard_map/ppermute | solution.py:42
  84.1 2.5 %collective-permute-done.27.refs_3_ = bf16[16,32,512]{2,1,0:T(8,128)(2,1)} collective-permute-done((bf16[16,32,512]{2,1,0:T(8,128)(2,1)S(1)}, bf16[16,32,512]{2,1,0:T(8,128)(2,1)}, u32[]{:S(2)}, u32[]{:S(2)}) %collective-permute-start.27) | collective-permute-done | bytes 524320 | tf_op jit(solution)/shard_map/ppermute | solution.py:42
  96.4 2.6 %gather_fusion = s32[512,128]{1,0:T(8,128)} fusion(s32[512,128]{1,0:T(8,128)} %bitcast.30, s32[1024]{0:T(1024)S(1)} %pad_clamp_fusion), kind=kCustom, calls=%fused_computation | custom fusion | bytes 526336 | tf_op jit(solution)/shard_map/gather | solution.py:365
  105.6 2.2 %pack.3.refs_5_ = bf16[256,32,512]{2,1,0:T(8,128)(2,1)S(1)} custom-call(bf16[16,32,512]{2,1,0:T(8,128)(2,1)} %collective-permute-done.21.refs_0_, bf16[16,32,512]{2,1,0:T(8,128)(2,1)} %collective-permute-done.23.refs_1_, bf16[16,32,512]{2,1,0:T(8,128)(2,1)} %collective-permute-done.25.refs_2_, ...), custom_call_target="tpu_custom_call", output_to_operand_aliasing={{}: (8, {})} | custom-call | bytes 8388608 | tf_op jit(solution)/shard_map/pack/pallas_call | solution.py:139
  107.9 3.8 %attend_other.3 = (bf16[2,256,512]{2,1,0:T(8,128)(2,1)S(1)}, f32[2,8,256]{2,1,0:T(8,128)S(1)}) custom-call(s32[512]{0:T(512)S(1)} %fusion.9.row_ref, s32[1]{0:T(128)} %bitcast.17.rank_ref, bf16[2,1024,128]{2,1,0:T(8,128)(2,1)S(1)} %pad_maximum_fusion.1.refs_0_, bf16[2,1024,128]{2,1,0:T(8,128)(2,1)S(1)} %collective-permute-done.14.refs_1_, ...), custom_call_target="tpu_custom_call" | custom-call | flops 2147483648 | bytes 2097152 | tf_op jit(solution)/shard_map/attend_other/pallas_call | solution.py:208
  111.7 3.8 %attend_other.2 = (bf16[2,256,512]{2,1,0:T(8,128)(2,1)S(1)}, f32[2,8,256]{2,1,0:T(8,128)S(1)}) custom-call(s32[512]{0:T(512)S(1)} %fusion.9.row_ref, s32[1]{0:T(128)} %bitcast.17.rank_ref, bf16[2,1024,128]{2,1,0:T(8,128)(2,1)S(1)} %pad_maximum_fusion.1.refs_0_, bf16[2,1024,128]{2,1,0:T(8,128)(2,1)S(1)} %collective-permute-done.14.refs_1_, ...), custom_call_target="tpu_custom_call" | custom-call | flops 2147483648 | bytes 2097152 | tf_op jit(solution)/shard_map/attend_other/pallas_call | solution.py:208
  117.6 4.0 %attend_own.3 = (bf16[2,288,128]{2,1,0:T(8,128)(2,1)S(1)}, bf16[2,288,128]{2,1,0:T(8,128)(2,1)S(1)}, bf16[2,288,128]{2,1,0:T(8,128)(2,1)S(1)}, bf16[2,288,128]{2,1,0:T(8,128)(2,1)S(1)}) custom-call(s32[512]{0:T(512)S(1)} %fusion.9.row_ref, s32[1]{0:T(128)} %bitcast.17.rank_ref, bf16[2,1024,128]{2,1,0:T(8,128)(2,1)S(1)} %pad_maximum_fusion.1.refs_0_, ...), custom_call_target="tpu_custom_call" | custom-call | flops 2147483648 | bytes 2097152 | tf_op jit(solution)/shard_map/attend_own/pallas_call | solution.py:208
  122.2 2.4 %collective-permute-start.41 = (bf16[2,288,128]{2,1,0:T(8,128)(2,1)S(1)}, bf16[2,288,128]{2,1,0:T(8,128)(2,1)S(1)}, u32[]{:S(2)}, u32[]{:S(2)}) collective-permute-start(bf16[2,288,128]{2,1,0:T(8,128)(2,1)S(1)} %get-tuple-element.118), channel_id=1, source_target_pairs={{0,2},{1,3},{2,0},{3,1},{4,6},{5,7},{6,4},{7,5},{8,10},{9,11},{10,... | collective-permute-start | bytes 442376 | tf_op jit(solution)/shard_map/ppermute | solution.py:46
  126.1 4.0 %attend_own.2 = (bf16[2,288,128]{2,1,0:T(8,128)(2,1)S(1)}, bf16[2,288,128]{2,1,0:T(8,128)(2,1)S(1)}, bf16[2,288,128]{2,1,0:T(8,128)(2,1)S(1)}, bf16[2,288,128]{2,1,0:T(8,128)(2,1)S(1)}) custom-call(s32[512]{0:T(512)S(1)} %fusion.9.row_ref, s32[1]{0:T(128)} %bitcast.17.rank_ref, bf16[2,1024,128]{2,1,0:T(8,128)(2,1)S(1)} %pad_maximum_fusion.1.refs_0_, ...), custom_call_target="tpu_custom_call" | custom-call | flops 2147483648 | bytes 2097152 | tf_op jit(solution)/shard_map/attend_own/pallas_call | solution.py:208
  132.2 2.4 %collective-permute-start.37 = (bf16[2,288,128]{2,1,0:T(8,128)(2,1)S(1)}, bf16[2,288,128]{2,1,0:T(8,128)(2,1)S(1)}, u32[]{:S(2)}, u32[]{:S(2)}) collective-permute-start(bf16[2,288,128]{2,1,0:T(8,128)(2,1)S(1)} %get-tuple-element.113), channel_id=1, source_target_pairs={{0,3},{1,0},{2,1},{3,2},{4,7},{5,4},{6,5},{7,6},{8,11},{9,8},{10,9... | collective-permute-start | bytes 442376 | tf_op jit(solution)/shard_map/ppermute | solution.py:46
  134.6 5.2 %collective-permute-done.35.refs_1_ = bf16[2,288,128]{2,1,0:T(8,128)(2,1)S(1)} collective-permute-done((bf16[2,288,128]{2,1,0:T(8,128)(2,1)S(1)}, bf16[2,288,128]{2,1,0:T(8,128)(2,1)S(1)}, u32[]{:S(2)}, u32[]{:S(2)}) %collective-permute-start.35) | collective-permute-done | bytes 147488 | tf_op jit(solution)/shard_map/ppermute | solution.py:46
  (108 shorter events, 61.3 us)
Async XLA Ops:
  4.2 15.4 %collective-permute-start.1 = (bf16[512,256]{1,0:T(8,128)(2,1)S(1)}, bf16[512,256]{1,0:T(8,128)(2,1)S(1)}, u32[]{:S(2)}, u32[]{:S(2)}) collective-permute-start(bf16[512,256]{1,0:T(8,128)(2,1)S(1)} %bitcast.37), channel_id=1, source_target_pairs={{0,1},{1,2},{2,3},{3,0},{4,5},{5,6},{6,7},{7,4},{8,9},{9,10},{10,1... | collective-permute-start | bytes 786440 | tf_op jit(solution)/shard_map/ppermute | solution.py:46
  5.8 13.8 %collective-permute-start.3 = (bf16[512,256]{1,0:T(8,128)(2,1)S(1)}, bf16[512,256]{1,0:T(8,128)(2,1)S(1)}, u32[]{:S(2)}, u32[]{:S(2)}) collective-permute-start(bf16[512,256]{1,0:T(8,128)(2,1)S(1)} %bitcast.36), channel_id=1, source_target_pairs={{0,3},{1,0},{2,1},{3,2},{4,7},{5,4},{6,5},{7,6},{8,11},{9,8},{10,9... | collective-permute-start | bytes 786440 | tf_op jit(solution)/shard_map/ppermute | solution.py:46
  7.5 11.0 %collective-permute-start.5 = (bf16[128,512]{1,0:T(8,128)(2,1)S(1)}, bf16[128,512]{1,0:T(8,128)(2,1)S(1)}, u32[]{:S(2)}, u32[]{:S(2)}) collective-permute-start(bf16[128,512]{1,0:T(8,128)(2,1)S(1)} %constant_dynamic-slice_fusion.refs_4_), channel_id=1, source_target_pairs={{0,2},{1,3},{2,0},{3,1},{4,6},{5,7},{6,4},{7,5},{8,10},{9,11},{10,... | collective-permute-start | bytes 393224 | tf_op jit(solution)/shard_map/ppermute | solution.py:46
  9.5 10.0 %collective-permute-start.6 = (bf16[128,512]{1,0:T(8,128)(2,1)S(1)}, bf16[128,512]{1,0:T(8,128)(2,1)S(1)}, u32[]{:S(2)}, u32[]{:S(2)}) collective-permute-start(bf16[128,512]{1,0:T(8,128)(2,1)S(1)} %constant_dynamic-slice_fusion.refs_4_), channel_id=1, source_target_pairs={{0,3},{1,0},{2,1},{3,2},{4,7},{5,4},{6,5},{7,6},{8,11},{9,8},{10,9... | collective-permute-start | bytes 393224 | tf_op jit(solution)/shard_map/ppermute | solution.py:46
  19.6 10.4 %collective-permute-start.7 = (bf16[4,128,512]{2,1,0:T(8,128)(2,1)S(1)}, bf16[4,128,512]{2,1,0:T(8,128)(2,1)S(1)}, u32[]{:S(2)}, u32[]{:S(2)}) collective-permute-start(bf16[4,128,512]{2,1,0:T(8,128)(2,1)S(1)} %pad_maximum_fusion), channel_id=1, source_target_pairs={{0,4},{4,0},{8,12},{12,8},{16,20},{20,16},{24,28},{28,24},{32,36},... | collective-permute-start | bytes 1572872 | tf_op jit(solution)/shard_map/ppermute | solution.py:42
  31.3 14.4 %collective-permute-start.14 = (bf16[2,1024,128]{2,1,0:T(8,128)(2,1)S(1)}, bf16[2,1024,128]{2,1,0:T(8,128)(2,1)S(1)}, u32[]{:S(2)}, u32[]{:S(2)}) collective-permute-start(bf16[2,1024,128]{2,1,0:T(8,128)(2,1)S(1)} %pad_maximum_fusion.1.refs_0_), channel_id=1, source_target_pairs={{0,1},{1,2},{2,3},{3,0},{4,5},{5,6},{6,7},{7,4},{8,9},{9,10},{10,1... | collective-permute-start | bytes 1572872 | tf_op jit(solution)/shard_map/ppermute | solution.py:46
  45.7 15.2 %collective-permute-start.19 = (bf16[2,1024,128]{2,1,0:T(8,128)(2,1)S(1)}, bf16[2,1024,128]{2,1,0:T(8,128)(2,1)S(1)}, u32[]{:S(2)}, u32[]{:S(2)}) collective-permute-start(bf16[2,1024,128]{2,1,0:T(8,128)(2,1)S(1)} %pad_maximum_fusion.1.refs_0_), channel_id=1, source_target_pairs={{0,2},{1,3},{2,0},{3,1},{4,6},{5,7},{6,4},{7,5},{8,10},{9,11},{10,... | collective-permute-start | bytes 1572872 | tf_op jit(solution)/shard_map/ppermute | solution.py:46
  62.7 11.7 %collective-permute-start.26 = (bf16[16,32,512]{2,1,0:T(8,128)(2,1)S(1)}, bf16[16,32,512]{2,1,0:T(8,128)(2,1)}, u32[]{:S(2)}, u32[]{:S(2)}) collective-permute-start(bf16[16,32,512]{2,1,0:T(8,128)(2,1)S(1)} %pad_maximum_fusion.5.refs_3_), channel_id=1, source_target_pairs={{0,96},{4,100},{8,104},{12,108},{16,112},{20,116},{24,120},{28,124... | collective-permute-start | bytes 1572872 | tf_op jit(solution)/shard_map/ppermute | solution.py:42
  64.3 13.7 %collective-permute-start.24 = (bf16[16,32,512]{2,1,0:T(8,128)(2,1)S(1)}, bf16[16,32,512]{2,1,0:T(8,128)(2,1)}, u32[]{:S(2)}, u32[]{:S(2)}) collective-permute-start(bf16[16,32,512]{2,1,0:T(8,128)(2,1)S(1)} %pad_maximum_fusion.4.refs_2_), channel_id=1, source_target_pairs={{0,32},{4,36},{8,40},{12,44},{16,48},{20,52},{24,56},{28,60},{32,0... | collective-permute-start | bytes 1572872 | tf_op jit(solution)/shard_map/ppermute | solution.py:42
  64.6 13.5 %collective-permute-start.22 = (bf16[16,32,512]{2,1,0:T(8,128)(2,1)}, bf16[16,32,512]{2,1,0:T(8,128)(2,1)}, u32[]{:S(2)}, u32[]{:S(2)}) collective-permute-start(bf16[16,32,512]{2,1,0:T(8,128)(2,1)} %pad_maximum_fusion.3.refs_1_), channel_id=1, source_target_pairs={{0,24},{4,28},{8,16},{12,20},{16,8},{20,12},{24,0},{28,4},{32,56},... | collective-permute-start | bytes 1572872 | tf_op jit(solution)/shard_map/ppermute | solution.py:42
  68.5 13.0 %collective-permute-start.20 = (bf16[16,32,512]{2,1,0:T(8,128)(2,1)}, bf16[16,32,512]{2,1,0:T(8,128)(2,1)}, u32[]{:S(2)}, u32[]{:S(2)}) collective-permute-start(bf16[16,32,512]{2,1,0:T(8,128)(2,1)} %pad_maximum_fusion.2.refs_0_), channel_id=1, source_target_pairs={{0,8},{4,12},{8,0},{12,4},{16,24},{20,28},{24,16},{28,20},{32,40},... | collective-permute-start | bytes 1572872 | tf_op jit(solution)/shard_map/ppermute | solution.py:42
  74.4 12.3 %collective-permute-start.27 = (bf16[16,32,512]{2,1,0:T(8,128)(2,1)S(1)}, bf16[16,32,512]{2,1,0:T(8,128)(2,1)}, u32[]{:S(2)}, u32[]{:S(2)}) collective-permute-start(bf16[16,32,512]{2,1,0:T(8,128)(2,1)S(1)} %pad_maximum_fusion.5.refs_3_), channel_id=1, source_target_pairs={{0,32},{4,36},{8,40},{12,44},{16,48},{20,52},{24,56},{28,60},{32,0... | collective-permute-start | bytes 1572872 | tf_op jit(solution)/shard_map/ppermute | solution.py:42
  78.1 10.5 %collective-permute-start.25 = (bf16[16,32,512]{2,1,0:T(8,128)(2,1)S(1)}, bf16[16,32,512]{2,1,0:T(8,128)(2,1)}, u32[]{:S(2)}, u32[]{:S(2)}) collective-permute-start(bf16[16,32,512]{2,1,0:T(8,128)(2,1)S(1)} %pad_maximum_fusion.4.refs_2_), channel_id=1, source_target_pairs={{0,96},{4,100},{8,104},{12,108},{16,112},{20,116},{24,120},{28,124... | collective-permute-start | bytes 1572872 | tf_op jit(solution)/shard_map/ppermute | solution.py:42
  78.1 12.5 %collective-permute-start.23 = (bf16[16,32,512]{2,1,0:T(8,128)(2,1)}, bf16[16,32,512]{2,1,0:T(8,128)(2,1)}, u32[]{:S(2)}, u32[]{:S(2)}) collective-permute-start(bf16[16,32,512]{2,1,0:T(8,128)(2,1)} %pad_maximum_fusion.3.refs_1_), channel_id=1, source_target_pairs={{0,8},{4,12},{8,0},{12,4},{16,24},{20,28},{24,16},{28,20},{32,40},... | collective-permute-start | bytes 1572872 | tf_op jit(solution)/shard_map/ppermute | solution.py:42
  81.5 10.7 %collective-permute-start.21 = (bf16[16,32,512]{2,1,0:T(8,128)(2,1)}, bf16[16,32,512]{2,1,0:T(8,128)(2,1)}, u32[]{:S(2)}, u32[]{:S(2)}) collective-permute-start(bf16[16,32,512]{2,1,0:T(8,128)(2,1)} %pad_maximum_fusion.2.refs_0_), channel_id=1, source_target_pairs={{0,24},{4,28},{8,16},{12,20},{16,8},{20,12},{24,0},{28,4},{32,56},... | collective-permute-start | bytes 1572872 | tf_op jit(solution)/shard_map/ppermute | solution.py:42
  82.4 25.5 %collective-permute-start.32 = (bf16[2,1024,128]{2,1,0:T(8,128)(2,1)S(1)}, bf16[2,1024,128]{2,1,0:T(8,128)(2,1)S(1)}, u32[]{:S(2)}, u32[]{:S(2)}) collective-permute-start(bf16[2,1024,128]{2,1,0:T(8,128)(2,1)S(1)} %pad_maximum_fusion.1.refs_0_), channel_id=1, source_target_pairs={{0,3},{1,0},{2,1},{3,2},{4,7},{5,4},{6,5},{7,6},{8,11},{9,8},{10,9... | collective-permute-start | bytes 1572872 | tf_op jit(solution)/shard_map/ppermute | solution.py:46
  92.2 11.7 %collective-permute-start.31 = (bf16[16,32,512]{2,1,0:T(8,128)(2,1)}, bf16[16,32,512]{2,1,0:T(8,128)(2,1)}, u32[]{:S(2)}, u32[]{:S(2)}) collective-permute-start(bf16[16,32,512]{2,1,0:T(8,128)(2,1)} %collective-permute-done.26.refs_7_), channel_id=1, source_target_pairs={{0,32},{4,36},{8,40},{12,44},{16,48},{20,52},{24,56},{28,60},{32,0... | collective-permute-start | bytes 1572872 | tf_op jit(solution)/shard_map/ppermute | solution.py:42
  94.1 11.0 %collective-permute-start.30 = (bf16[16,32,512]{2,1,0:T(8,128)(2,1)}, bf16[16,32,512]{2,1,0:T(8,128)(2,1)}, u32[]{:S(2)}, u32[]{:S(2)}) collective-permute-start(bf16[16,32,512]{2,1,0:T(8,128)(2,1)} %collective-permute-done.24.refs_6_), channel_id=1, source_target_pairs={{0,96},{4,100},{8,104},{12,108},{16,112},{20,116},{24,120},{28,124... | collective-permute-start | bytes 1572872 | tf_op jit(solution)/shard_map/ppermute | solution.py:42
  94.9 10.1 %collective-permute-start.29 = (bf16[16,32,512]{2,1,0:T(8,128)(2,1)}, bf16[16,32,512]{2,1,0:T(8,128)(2,1)}, u32[]{:S(2)}, u32[]{:S(2)}) collective-permute-start(bf16[16,32,512]{2,1,0:T(8,128)(2,1)} %collective-permute-done.22.refs_5_), channel_id=1, source_target_pairs={{0,8},{4,12},{8,0},{12,4},{16,24},{20,28},{24,16},{28,20},{32,40},... | collective-permute-start | bytes 1572872 | tf_op jit(solution)/shard_map/ppermute | solution.py:42
  94.9 10.7 %collective-permute-start.28 = (bf16[16,32,512]{2,1,0:T(8,128)(2,1)}, bf16[16,32,512]{2,1,0:T(8,128)(2,1)}, u32[]{:S(2)}, u32[]{:S(2)}) collective-permute-start(bf16[16,32,512]{2,1,0:T(8,128)(2,1)} %collective-permute-done.20.refs_4_), channel_id=1, source_target_pairs={{0,24},{4,28},{8,16},{12,20},{16,8},{20,12},{24,0},{28,4},{32,56},... | collective-permute-start | bytes 1572872 | tf_op jit(solution)/shard_map/ppermute | solution.py:42
  115.5 10.6 %collective-permute-start.33 = (bf16[2,256,512]{2,1,0:T(8,128)(2,1)S(1)}, bf16[2,256,512]{2,1,0:T(8,128)(2,1)S(1)}, u32[]{:S(2)}, u32[]{:S(2)}) collective-permute-start(bf16[2,256,512]{2,1,0:T(8,128)(2,1)S(1)} %get-tuple-element.107), channel_id=1, source_target_pairs={{0,4},{4,0},{8,12},{12,8},{16,20},{20,16},{24,28},{28,24},{32,36},... | collective-permute-start | bytes 1572872 | tf_op jit(solution)/shard_map/ppermute | solution.py:42
  121.6 10.6 %collective-permute-start.40 = (bf16[2,288,128]{2,1,0:T(8,128)(2,1)S(1)}, bf16[2,288,128]{2,1,0:T(8,128)(2,1)S(1)}, u32[]{:S(2)}, u32[]{:S(2)}) collective-permute-start(bf16[2,288,128]{2,1,0:T(8,128)(2,1)S(1)} %get-tuple-element.117), channel_id=1, source_target_pairs={{0,1},{1,2},{2,3},{3,0},{4,5},{5,6},{6,7},{7,4},{8,9},{9,10},{10,1... | collective-permute-start | bytes 442376 | tf_op jit(solution)/shard_map/ppermute | solution.py:46
  122.2 12.4 %collective-permute-start.41 = (bf16[2,288,128]{2,1,0:T(8,128)(2,1)S(1)}, bf16[2,288,128]{2,1,0:T(8,128)(2,1)S(1)}, u32[]{:S(2)}, u32[]{:S(2)}) collective-permute-start(bf16[2,288,128]{2,1,0:T(8,128)(2,1)S(1)} %get-tuple-element.118), channel_id=1, source_target_pairs={{0,2},{1,3},{2,0},{3,1},{4,6},{5,7},{6,4},{7,5},{8,10},{9,11},{10,... | collective-permute-start | bytes 442376 | tf_op jit(solution)/shard_map/ppermute | solution.py:46
  124.6 10.0 %collective-permute-start.42 = (bf16[2,288,128]{2,1,0:T(8,128)(2,1)S(1)}, bf16[2,288,128]{2,1,0:T(8,128)(2,1)S(1)}, u32[]{:S(2)}, u32[]{:S(2)}) collective-permute-start(bf16[2,288,128]{2,1,0:T(8,128)(2,1)S(1)} %get-tuple-element.119), channel_id=1, source_target_pairs={{0,3},{1,0},{2,1},{3,2},{4,7},{5,4},{6,5},{7,6},{8,11},{9,8},{10,9... | collective-permute-start | bytes 442376 | tf_op jit(solution)/shard_map/ppermute | solution.py:46
  (24 other events, 370.6 us)

commit v10 on v9

--- a/solution.py
+++ b/solution.py
@@ -46,10 +46,10 @@
     return lax.ppermute(value, "tp", [(i, (i + d) % TP) for i in range(TP)])
 
 
-def tower_kernel(core_ref, *refs):
+def tower_kernel(core_ref, rank_ref, *refs):
     hidden = refs[0:4]
     mine, theirs = refs[4:8], refs[8]
-    out_ref = refs[9]
+    out_ref, quarters = refs[9:]
     core = core_ref[0]
     half = HID // TP // 2
     acc = jnp.zeros((NBD * 2 * ROWS, E), jnp.float32)
@@ -58,35 +58,37 @@
         high = jnp.where(core == 0, theirs[d], mine[d][...])
         acc += jnp.dot(hidden[d][:, :half], low, preferred_element_type=jnp.float32)
         acc += jnp.dot(hidden[d][:, half:], high, preferred_element_type=jnp.float32)
-    out_ref[...] = acc.astype(jnp.bfloat16).reshape(out_ref.shape)
-
-
-def tower(core, hidden, mine, theirs):
+    for s in range(TP):
+        quarters[s] = acc[:, s * 128 : (s + 1) * 128].astype(jnp.bfloat16).reshape(quarters.shape[1:])
+    for d in range(TP):
+        out_ref[:, :, d * 128 : (d + 1) * 128] = quarters[lax.rem(rank_ref[0] + TP - d, TP)]
+
+
+def tower(core, rank, hidden, mine, theirs):
     return pl.pallas_call(
         tower_kernel,
         out_shape=jax.ShapeDtypeStruct((2 * NBD, ROWS, E), jnp.bfloat16),
-        in_specs=[pl.BlockSpec(memory_space=pltpu.SMEM)]
+        in_specs=[pl.BlockSpec(memory_space=pltpu.SMEM)] * 2
         + [pl.BlockSpec(memory_space=pltpu.VMEM)] * 9,
+        scratch_shapes=[pltpu.VMEM((TP, 2 * NBD, ROWS, 128), jnp.bfloat16)],
         out_specs=pl.BlockSpec(memory_space=pltpu.VMEM),
         compiler_params=pltpu.CompilerParams(vmem_limit_bytes=40 << 20),
         cost_estimate=pl.CostEstimate(
             flops=2 * 512 * 1024 * 512, bytes_accessed=3 << 20, transcendentals=0
         ),
         name="tower",
-    )(core, *hidden, *mine, theirs)
+    )(core, rank, *hidden, *mine, theirs)
 
 
 PART = 2
 
 
-def one_block(rank, block, side, q_refs, lq_ref, row_ref, table, picked, scores, gathered):
+def one_block(block, side, q_refs, lq_ref, row_ref, table, picked, scores):
     base = side * 2 * PART
     for j in range(PICKS):
         picked[pl.ds(j * ROWS, ROWS), :] = table[row_ref[(base + block) * PICKS + j]]
     here = pl.ds(block * BLK, BLK)
-    for d in range(TP):
-        gathered[lax.rem(rank + TP - d, TP)] = q_refs[d][side, here]
-    query = jnp.concatenate([gathered[s] for s in range(TP)], axis=1)
+    query = jnp.concatenate([q_refs[d][side, here] for d in range(TP)], axis=1)
     top = jnp.full((BLK, 128), LOW, jnp.float32)
     for n in range(COLS // TILE):
         cols = pl.ds(n * TILE, TILE)
@@ -149,14 +151,14 @@
     )(*pieces, *given)
 
 
-def first_kernel(start, row_ref, rank_ref, *refs):
+def first_kernel(start, row_ref, *refs):
     q_refs, (lq_ref, table) = refs[:TP], refs[TP : TP + 2]
-    out_ref, stat_ref, picked, scores, gathered = refs[TP + 2 :]
+    out_ref, stat_ref, picked, scores = refs[TP + 2 :]
 
     for n in range(PART):
         top, total, acc = one_block(
-            rank_ref[0], start + n, 0, q_refs, lq_ref, row_ref, table,
-            picked.at[n], scores.at[n], gathered.at[n],
+            start + n, 0, q_refs, lq_ref, row_ref, table,
+            picked.at[n], scores.at[n],
         )
         out_ref[n] = acc.astype(jnp.bfloat16)
         stat_ref[n] = rows_of(top, total)
@@ -176,34 +178,33 @@
     return jnp.concatenate(halves, axis=1)
 
 
-def second_kernel(start, row_ref, rank_ref, *refs):
+def second_kernel(start, row_ref, *refs):
     q_refs, (lq_ref, table), refs = refs[:TP], refs[TP : TP + 2], refs[TP + 2 :]
     other_ref, other_stat_ref, pos_ref = refs[:3]
     outs = refs[3:7]
-    picked, scores, gathered, quarters = refs[7:]
+    picked, scores = refs[7:]
 
     for n in range(PART):
         top, total, acc = one_block(
-            rank_ref[0], start + n, 1, q_refs, lq_ref, row_ref, table,
-            picked.at[n], scores.at[n], gathered.at[n],
+            start + n, 1, q_refs, lq_ref, row_ref, table,
+            picked.at[n], scores.at[n],
         )
         theirs = jnp.transpose(jnp.concatenate([other_stat_ref[n]] * 16, axis=0))
         their_top, their_total = theirs[:, 0:1], theirs[:, 1:2]
         joint = jnp.maximum(top, their_top)
         mine_by, theirs_by = jnp.exp2(top - joint), jnp.exp2(their_top - joint)
         acc = acc * mine_by + other_ref[n].astype(jnp.float32) * theirs_by
-        for s in range(TP):
-            quarters[s] = acc[:, s * 128 : (s + 1) * 128].astype(jnp.bfloat16)
         stat = rows_of(joint, total * mine_by + their_total * theirs_by)
         rows = split_rows(stat[0:1]) + split_rows(stat[1:2]) + split_rows(pos_ref[start + n])
         rows.append(jnp.zeros((EXTRA - len(rows), 128), jnp.float32))
         tail = jnp.concatenate(rows, axis=0).astype(jnp.bfloat16)
         for d in range(TP):
-            outs[d][n, :BLK] = quarters[lax.rem(rank_ref[0] + d, TP)]
+            at = (TP - d) % TP * 128
+            outs[d][n, :BLK] = acc[:, at : at + 128].astype(jnp.bfloat16)
             outs[d][n, BLK:] = tail
 
 
-def attend(body, start, scalars, inputs, outs, scratch, name):
+def attend(body, start, scalars, inputs, outs, name):
     vmem = pl.BlockSpec(memory_space=pltpu.VMEM)
     return pl.pallas_call(
         functools.partial(body, start),
@@ -213,9 +214,7 @@
         scratch_shapes=[
             pltpu.VMEM((PART, COLS, E), jnp.bfloat16),
             pltpu.VMEM((PART, BLK, COLS), jnp.float32),
-            pltpu.VMEM((PART, TP, BLK, 128), jnp.bfloat16),
-        ]
-        + scratch,
+        ],
         compiler_params=pltpu.CompilerParams(vmem_limit_bytes=32 << 20),
         cost_estimate=pl.CostEstimate(
             flops=PART * 4 * BLK * COLS * E,
@@ -291,21 +290,22 @@
 
 def spread(items, query):
     held = [items[n * 4 : n * 4 + 4] for n in range(4)]
-    queries = [query]
-    for step in range(2):
-        got = [send(h, **{st[step][0]: st[step][1]}) for h, st in zip(held, STREAMS)]
-        got = together(*got, send_x(query, step + 1), query)
-        queries.append(got[4])
-        query = got[5]
-        held = together(*[jnp.concatenate([h, g]) for h, g in zip(held, got)], query)
-        query = held.pop()
+    got = [send(h, **{st[0][0]: st[0][1]}) for h, st in zip(held, STREAMS)]
+    query_1 = send_x(query, 1)
+    got = together(*got)
+    held = together(*[jnp.concatenate([h, g]) for h, g in zip(held, got)])
+    got = [send(h, **{st[1][0]: st[1][1]}) for h, st in zip(held, STREAMS)]
+    *got, query_1, query = together(*got, query_1, query)
+    held = together(*[jnp.concatenate([h, g]) for h, g in zip(held, got)])
     third = [send(h, **{st[2][0]: st[2][1]}) for h, st in zip(held, STREAMS)]
-    queries.append(send_x(query, 3))
+    query_2 = send_x(query, 2)
     held, third = zip(*[together(h, t) for h, t in zip(held, third)])
+    fourth = [send(h, **{st[3][0]: st[3][1]}) for h, st in zip(held, STREAMS)]
     held, third = list(held), list(third)
-    fourth = [send(h, **{st[3][0]: st[3][1]}) for h, st in zip(held, STREAMS)]
     third, fourth = zip(*[together(t, f) for t, f in zip(third, fourth)])
     third, fourth = list(third), list(fourth)
+    query_2, query, fourth[0] = together(query_2, query, fourth[0])
+    queries = [query, query_1, query_2, send_x(query, 3)]
     fifth = [send(h, **{st[3][0]: st[3][1]}) for h, st in zip(third, STREAMS)]
     table = pack(held + third, (0, 4, 8, 12, 1, 5, 9, 13))
     table = pack(fourth + fifth, (2, 6, 10, 14, 3, 7, 11, 15), table)
@@ -344,7 +344,7 @@
     picks = jnp.concatenate([send(neg_blocks, c=1), neg_blocks])
     both_query = jnp.stack([send(query_emb, c=1), query_emb])
     items, late_query, picks = together(
-        tower(core_id, hiddens, mine_w, theirs_w), both_query, picks
+        tower(core_id, rank_id, hiddens, mine_w, theirs_w), both_query, picks
     )
     table, queries = spread(items, late_query)
     pos_part = SCALE * jnp.sum(
@@ -379,10 +379,9 @@
         made = attend(
             first_kernel,
             start,
-            (rows, rank_id),
+            (rows,),
             (*queries, lq, table),
             raw,
-            [],
             "attend_other",
         )
         others.append([send(one, c=1) for one in made])
@@ -391,10 +390,9 @@
         shares = attend(
             second_kernel,
             start,
-            (rows, rank_id),
+            (rows,),
             (*queries, lq, table, *other, pos_part),
             (share,) * TP,
-            [pltpu.VMEM((TP, BLK, 128), jnp.bfloat16)],
             "attend_own",
         )
         parts += [shares[0]] + [send_x(shares[d], d) for d in (1, 2, 3)]

time: 143 us -> 135 us (0.944)
  waiting for transfers between devices: 53.6 us -> 48.6 us
  starting transfers between devices: 53.4 us -> 50.3 us
    ppermute x28, waiting for transfers between devices: 34.8 us -> 29.9 us  [send(): return lax.ppermute(value, 'cat', cat_perm(y, z, c))]
    ppermute x15, starting transfers between devices: 24.3 us -> 22.7 us  [send_x(): return lax.ppermute(value, 'tp', [(i, (i + d) % TP) for i in range(TP)])]
    ppermute x28, starting transfers between devices: 29.1 us -> 27.6 us  [send(): return lax.ppermute(value, 'cat', cat_perm(y, z, c))]
  transfers between devices with their start and end apart: 43 -> 43, of which waited for: 25 -> 20; matrix products, arithmetic and copies ran while one was open for 6% -> 6% of each run, Pallas kernels for 11% -> 11%
where the time goes in v10:
time: 135 us; the launch traced here: 134 us
  starting transfers between devices  50.3 us (37%)
  waiting for transfers between devices  48.6 us (36%)
  Pallas kernels  22.2 us (16%)
  local copies, waits for them, and re-layouts  6.37 us (5%)
  other arithmetic  5.45 us (4%)
    ppermute x28, waiting for transfers between devices, send(): return lax.ppermute(value, 'cat', cat_perm(y, z, c))  29.9 us
    ppermute x28, starting transfers between devices, send(): return lax.ppermute(value, 'cat', cat_perm(y, z, c))  27.6 us
    ppermute x15, starting transfers between devices, send_x(): return lax.ppermute(value, 'tp', [(i, (i + d) % TP) for i in range(TP)])  22.7 us
    ppermute x15, waiting for transfers between devices, send_x(): return lax.ppermute(value, 'tp', [(i, (i + d) % TP) for i in range(TP)])  18.7 us
    pallas_call x4, Pallas kernels, attend(): pl.pallas_call(functools.partial(body, start), in_specs=[pl.BlockSpec(mem...  15 us
    pallas_call x2, Pallas kernels, pack(): pl.pallas_call(functools.partial(pack_kernel, places), out_shape=jax.Shap...  3.99 us
  transfers between devices with their start and end apart: 43, of which 20 were waited for; matrix products, arithmetic and copies ran while one was open for 6% of the time, Pallas kernels for 11%

profile of v10, /device:TPU:0, one launch (start us, length us, event | category | flops | bytes accessed | tf_op | source)
XLA Modules:
  0.0 134.0 jit_solution(9877199618379765264)
XLA Ops:
  7.9 2.7 %collective-permute-start.5 = (bf16[128,512]{1,0:T(8,128)(2,1)S(1)}, bf16[128,512]{1,0:T(8,128)(2,1)S(1)}, u32[]{:S(2)}, u32[]{:S(2)}) collective-permute-start(bf16[128,512]{1,0:T(8,128)(2,1)S(1)} %constant_dynamic-slice_fusion.refs_4_), channel_id=1, source_target_pairs={{0,2},{1,3},{2,0},{3,1},{4,6},{5,7},{6,4},{7,5},{8,10},{9,11},{10,... | collective-permute-start | bytes 393224 | tf_op jit(solution)/shard_map/ppermute | solution.py:46
  12.1 4.5 %collective-permute-done.4.refs_5_ = bf16[128,512]{1,0:T(8,128)(2,1)S(1)} collective-permute-done((bf16[128,512]{1,0:T(8,128)(2,1)S(1)}, bf16[128,512]{1,0:T(8,128)(2,1)S(1)}, u32[]{:S(2)}, u32[]{:S(2)}) %collective-permute-start.4) | collective-permute-done | bytes 131104 | tf_op jit(solution)/shard_map/ppermute | solution.py:46
  16.6 3.9 %collective-permute-done.5.refs_6_ = bf16[128,512]{1,0:T(8,128)(2,1)S(1)} collective-permute-done((bf16[128,512]{1,0:T(8,128)(2,1)S(1)}, bf16[128,512]{1,0:T(8,128)(2,1)S(1)}, u32[]{:S(2)}, u32[]{:S(2)}) %collective-permute-start.5) | collective-permute-done | bytes 131104 | tf_op jit(solution)/shard_map/ppermute | solution.py:46
  26.0 5.0 %collective-permute-done.2.refs_2_ = bf16[512,256]{1,0:T(8,128)(2,1)S(1)} collective-permute-done((bf16[512,256]{1,0:T(8,128)(2,1)S(1)}, bf16[512,256]{1,0:T(8,128)(2,1)S(1)}, u32[]{:S(2)}, u32[]{:S(2)}) %collective-permute-start.2) | collective-permute-done | bytes 262176 | tf_op jit(solution)/shard_map/ppermute | solution.py:46
  34.1 2.2 %collective-permute-start.11 = (bf16[4,32,512]{2,1,0:T(8,128)(2,1)S(1)}, bf16[4,32,512]{2,1,0:T(8,128)(2,1)S(1)}, u32[]{:S(2)}, u32[]{:S(2)}) collective-permute-start(bf16[4,32,512]{2,1,0:T(8,128)(2,1)S(1)} %get-tuple-element.128), channel_id=1, source_target_pairs={{0,96},{4,100},{8,104},{12,108},{16,112},{20,116},{24,120},{28,124... | collective-permute-start | bytes 393224 | tf_op jit(solution)/shard_map/ppermute | solution.py:42
  38.2 2.5 %collective-permute-start.13 = (bf16[4,32,512]{2,1,0:T(8,128)(2,1)S(1)}, bf16[4,32,512]{2,1,0:T(8,128)(2,1)S(1)}, u32[]{:S(2)}, u32[]{:S(2)}) collective-permute-start(bf16[4,32,512]{2,1,0:T(8,128)(2,1)S(1)} %get-tuple-element.126), channel_id=1, source_target_pairs={{0,24},{4,28},{8,16},{12,20},{16,8},{20,12},{24,0},{28,4},{32,56},... | collective-permute-start | bytes 393224 | tf_op jit(solution)/shard_map/ppermute | solution.py:42
  41.3 3.1 %collective-permute-done.13 = bf16[4,32,512]{2,1,0:T(8,128)(2,1)S(1)} collective-permute-done((bf16[4,32,512]{2,1,0:T(8,128)(2,1)S(1)}, bf16[4,32,512]{2,1,0:T(8,128)(2,1)S(1)}, u32[]{:S(2)}, u32[]{:S(2)}) %collective-permute-start.13) | collective-permute-done | bytes 131104 | tf_op jit(solution)/shard_map/ppermute | solution.py:42
  45.6 2.5 %collective-permute-start.16 = (bf16[8,32,512]{2,1,0:T(8,128)(2,1)S(1)}, bf16[8,32,512]{2,1,0:T(8,128)(2,1)S(1)}, u32[]{:S(2)}, u32[]{:S(2)}) collective-permute-start(bf16[8,32,512]{2,1,0:T(8,128)(2,1)S(1)} %get-tuple-element.69), channel_id=1, source_target_pairs={{0,24},{4,28},{8,16},{12,20},{16,8},{20,12},{24,0},{28,4},{32,56},... | collective-permute-start | bytes 786440 | tf_op jit(solution)/shard_map/ppermute | solution.py:42
  48.1 4.0 %collective-permute-done.14 = bf16[8,32,512]{2,1,0:T(8,128)(2,1)S(1)} collective-permute-done((bf16[8,32,512]{2,1,0:T(8,128)(2,1)S(1)}, bf16[8,32,512]{2,1,0:T(8,128)(2,1)S(1)}, u32[]{:S(2)}, u32[]{:S(2)}) %collective-permute-start.14) | collective-permute-done | bytes 262176 | tf_op jit(solution)/shard_map/ppermute | solution.py:42
  55.6 2.3 %collective-permute-start.26 = (bf16[16,32,512]{2,1,0:T(8,128)(2,1)S(1)}, bf16[16,32,512]{2,1,0:T(8,128)(2,1)}, u32[]{:S(2)}, u32[]{:S(2)}) collective-permute-start(bf16[16,32,512]{2,1,0:T(8,128)(2,1)S(1)} %pad_maximum_fusion.5.refs_3_), channel_id=1, source_target_pairs={{0,96},{4,100},{8,104},{12,108},{16,112},{20,116},{24,120},{28,124... | collective-permute-start | bytes 1572872 | tf_op jit(solution)/shard_map/ppermute | solution.py:42
  62.5 5.2 %collective-permute-done.26.refs_7_ = bf16[16,32,512]{2,1,0:T(8,128)(2,1)} collective-permute-done((bf16[16,32,512]{2,1,0:T(8,128)(2,1)S(1)}, bf16[16,32,512]{2,1,0:T(8,128)(2,1)}, u32[]{:S(2)}, u32[]{:S(2)}) %collective-permute-start.26) | collective-permute-done | bytes 524320 | tf_op jit(solution)/shard_map/ppermute | solution.py:42
  72.8 2.5 %collective-permute-start.21 = (bf16[16,32,512]{2,1,0:T(8,128)(2,1)}, bf16[16,32,512]{2,1,0:T(8,128)(2,1)}, u32[]{:S(2)}, u32[]{:S(2)}) collective-permute-start(bf16[16,32,512]{2,1,0:T(8,128)(2,1)} %pad_maximum_fusion.2.refs_0_), channel_id=1, source_target_pairs={{0,24},{4,28},{8,16},{12,20},{16,8},{20,12},{24,0},{28,4},{32,56},... | collective-permute-start | bytes 1572872 | tf_op jit(solution)/shard_map/ppermute | solution.py:42
  75.8 3.0 %collective-permute-done.27.refs_3_ = bf16[16,32,512]{2,1,0:T(8,128)(2,1)} collective-permute-done((bf16[16,32,512]{2,1,0:T(8,128)(2,1)S(1)}, bf16[16,32,512]{2,1,0:T(8,128)(2,1)}, u32[]{:S(2)}, u32[]{:S(2)}) %collective-permute-start.27) | collective-permute-done | bytes 524320 | tf_op jit(solution)/shard_map/ppermute | solution.py:42
  81.9 3.0 %collective-permute-done.21.refs_0_ = bf16[16,32,512]{2,1,0:T(8,128)(2,1)} collective-permute-done((bf16[16,32,512]{2,1,0:T(8,128)(2,1)}, bf16[16,32,512]{2,1,0:T(8,128)(2,1)}, u32[]{:S(2)}, u32[]{:S(2)}) %collective-permute-start.21) | collective-permute-done | bytes 524320 | tf_op jit(solution)/shard_map/ppermute | solution.py:42
  85.5 2.6 %collective-permute-start.28 = (bf16[16,32,512]{2,1,0:T(8,128)(2,1)}, bf16[16,32,512]{2,1,0:T(8,128)(2,1)}, u32[]{:S(2)}, u32[]{:S(2)}) collective-permute-start(bf16[16,32,512]{2,1,0:T(8,128)(2,1)} %collective-permute-done.20.refs_4_), channel_id=1, source_target_pairs={{0,24},{4,28},{8,16},{12,20},{16,8},{20,12},{24,0},{28,4},{32,56},... | collective-permute-start | bytes 1572872 | tf_op jit(solution)/shard_map/ppermute | solution.py:42
  88.1 2.2 %collective-permute-start.32 = (bf16[2,1024,128]{2,1,0:T(8,128)(2,1)S(1)}, bf16[2,1024,128]{2,1,0:T(8,128)(2,1)S(1)}, u32[]{:S(2)}, u32[]{:S(2)}) collective-permute-start(bf16[2,1024,128]{2,1,0:T(8,128)(2,1)S(1)} %pad_maximum_fusion.1.refs_0_), channel_id=1, source_target_pairs={{0,3},{1,0},{2,1},{3,2},{4,7},{5,4},{6,5},{7,6},{8,11},{9,8},{10,9... | collective-permute-start | bytes 1572872 | tf_op jit(solution)/shard_map/ppermute | solution.py:46
  90.3 2.6 %gather_fusion = s32[512,128]{1,0:T(8,128)} fusion(s32[512,128]{1,0:T(8,128)} %bitcast.30, s32[1024]{0:T(1024)S(1)} %pad_clamp_fusion), kind=kCustom, calls=%fused_computation | custom fusion | bytes 526336 | tf_op jit(solution)/shard_map/gather | solution.py:365
  98.8 2.2 %pack.3.refs_5_ = bf16[256,32,512]{2,1,0:T(8,128)(2,1)S(1)} custom-call(bf16[16,32,512]{2,1,0:T(8,128)(2,1)} %collective-permute-done.21.refs_0_, bf16[16,32,512]{2,1,0:T(8,128)(2,1)} %collective-permute-done.23.refs_1_, bf16[16,32,512]{2,1,0:T(8,128)(2,1)} %collective-permute-done.25.refs_2_, ...), custom_call_target="tpu_custom_call", output_to_operand_aliasing={{}: (8, {})} | custom-call | bytes 8388608 | tf_op jit(solution)/shard_map/pack/pallas_call | solution.py:141
  101.0 3.7 %attend_other.3 = (bf16[2,256,512]{2,1,0:T(8,128)(2,1)S(1)}, f32[2,8,256]{2,1,0:T(8,128)S(1)}) custom-call(s32[512]{0:T(512)S(1)} %fusion.9.row_ref, bf16[2,1024,128]{2,1,0:T(8,128)(2,1)S(1)} %pad_maximum_fusion.1.refs_0_, bf16[2,1024,128]{2,1,0:T(8,128)(2,1)S(1)} %collective-permute-done.18.refs_1_, ...), custom_call_target="tpu_custom_call" | custom-call | flops 2147483648 | bytes 2097152 | tf_op jit(solution)/shard_map/attend_other/pallas_call | solution.py:209
  104.8 3.7 %attend_other.2 = (bf16[2,256,512]{2,1,0:T(8,128)(2,1)S(1)}, f32[2,8,256]{2,1,0:T(8,128)S(1)}) custom-call(s32[512]{0:T(512)S(1)} %fusion.9.row_ref, bf16[2,1024,128]{2,1,0:T(8,128)(2,1)S(1)} %pad_maximum_fusion.1.refs_0_, bf16[2,1024,128]{2,1,0:T(8,128)(2,1)S(1)} %collective-permute-done.18.refs_1_, ...), custom_call_target="tpu_custom_call" | custom-call | flops 2147483648 | bytes 2097152 | tf_op jit(solution)/shard_map/attend_other/pallas_call | solution.py:209
  110.7 3.8 %attend_own.3 = (bf16[2,288,128]{2,1,0:T(8,128)(2,1)S(1)}, bf16[2,288,128]{2,1,0:T(8,128)(2,1)S(1)}, bf16[2,288,128]{2,1,0:T(8,128)(2,1)S(1)}, bf16[2,288,128]{2,1,0:T(8,128)(2,1)S(1)}) custom-call(s32[512]{0:T(512)S(1)} %fusion.9.row_ref, bf16[2,1024,128]{2,1,0:T(8,128)(2,1)S(1)} %pad_maximum_fusion.1.refs_0_, ...), custom_call_target="tpu_custom_call" | custom-call | flops 2147483648 | bytes 2097152 | tf_op jit(solution)/shard_map/attend_own/pallas_call | solution.py:209
  117.8 3.8 %attend_own.2 = (bf16[2,288,128]{2,1,0:T(8,128)(2,1)S(1)}, bf16[2,288,128]{2,1,0:T(8,128)(2,1)S(1)}, bf16[2,288,128]{2,1,0:T(8,128)(2,1)S(1)}, bf16[2,288,128]{2,1,0:T(8,128)(2,1)S(1)}) custom-call(s32[512]{0:T(512)S(1)} %fusion.9.row_ref, bf16[2,1024,128]{2,1,0:T(8,128)(2,1)S(1)} %pad_maximum_fusion.1.refs_0_, ...), custom_call_target="tpu_custom_call" | custom-call | flops 2147483648 | bytes 2097152 | tf_op jit(solution)/shard_map/attend_own/pallas_call | solution.py:209
  125.0 2.2 %collective-permute-start.37 = (bf16[2,288,128]{2,1,0:T(8,128)(2,1)S(1)}, bf16[2,288,128]{2,1,0:T(8,128)(2,1)S(1)}, u32[]{:S(2)}, u32[]{:S(2)}) collective-permute-start(bf16[2,288,128]{2,1,0:T(8,128)(2,1)S(1)} %get-tuple-element.111), channel_id=1, source_target_pairs={{0,3},{1,0},{2,1},{3,2},{4,7},{5,4},{6,5},{7,6},{8,11},{9,8},{10,9... | collective-permute-start | bytes 442376 | tf_op jit(solution)/shard_map/ppermute | solution.py:46
  127.2 4.4 %collective-permute-done.35.refs_1_ = bf16[2,288,128]{2,1,0:T(8,128)(2,1)S(1)} collective-permute-done((bf16[2,288,128]{2,1,0:T(8,128)(2,1)S(1)}, bf16[2,288,128]{2,1,0:T(8,128)(2,1)S(1)}, u32[]{:S(2)}, u32[]{:S(2)}) %collective-permute-start.35) | collective-permute-done | bytes 147488 | tf_op jit(solution)/shard_map/ppermute | solution.py:46
  (112 shorter events, 55.3 us)
Async XLA Ops:
  4.2 16.4 %collective-permute-start.1 = (bf16[512,256]{1,0:T(8,128)(2,1)S(1)}, bf16[512,256]{1,0:T(8,128)(2,1)S(1)}, u32[]{:S(2)}, u32[]{:S(2)}) collective-permute-start(bf16[512,256]{1,0:T(8,128)(2,1)S(1)} %bitcast.37), channel_id=1, source_target_pairs={{0,1},{1,2},{2,3},{3,0},{4,5},{5,6},{6,7},{7,4},{8,9},{9,10},{10,1... | collective-permute-start | bytes 786440 | tf_op jit(solution)/shard_map/ppermute | solution.py:46
  5.8 14.8 %collective-permute-start.3 = (bf16[512,256]{1,0:T(8,128)(2,1)S(1)}, bf16[512,256]{1,0:T(8,128)(2,1)S(1)}, u32[]{:S(2)}, u32[]{:S(2)}) collective-permute-start(bf16[512,256]{1,0:T(8,128)(2,1)S(1)} %bitcast.36), channel_id=1, source_target_pairs={{0,3},{1,0},{2,1},{3,2},{4,7},{5,4},{6,5},{7,6},{8,11},{9,8},{10,9... | collective-permute-start | bytes 786440 | tf_op jit(solution)/shard_map/ppermute | solution.py:46
  7.9 12.6 %collective-permute-start.5 = (bf16[128,512]{1,0:T(8,128)(2,1)S(1)}, bf16[128,512]{1,0:T(8,128)(2,1)S(1)}, u32[]{:S(2)}, u32[]{:S(2)}) collective-permute-start(bf16[128,512]{1,0:T(8,128)(2,1)S(1)} %constant_dynamic-slice_fusion.refs_4_), channel_id=1, source_target_pairs={{0,2},{1,3},{2,0},{3,1},{4,6},{5,7},{6,4},{7,5},{8,10},{9,11},{10,... | collective-permute-start | bytes 393224 | tf_op jit(solution)/shard_map/ppermute | solution.py:46
  10.7 9.8 %collective-permute-start.6 = (bf16[128,512]{1,0:T(8,128)(2,1)S(1)}, bf16[128,512]{1,0:T(8,128)(2,1)S(1)}, u32[]{:S(2)}, u32[]{:S(2)}) collective-permute-start(bf16[128,512]{1,0:T(8,128)(2,1)S(1)} %constant_dynamic-slice_fusion.refs_4_), channel_id=1, source_target_pairs={{0,3},{1,0},{2,1},{3,2},{4,7},{5,4},{6,5},{7,6},{8,11},{9,8},{10,9... | collective-permute-start | bytes 393224 | tf_op jit(solution)/shard_map/ppermute | solution.py:46
  20.6 10.4 %collective-permute-start.7 = (bf16[4,128,512]{2,1,0:T(8,128)(2,1)S(1)}, bf16[4,128,512]{2,1,0:T(8,128)(2,1)S(1)}, u32[]{:S(2)}, u32[]{:S(2)}) collective-permute-start(bf16[4,128,512]{2,1,0:T(8,128)(2,1)S(1)} %pad_maximum_fusion), channel_id=1, source_target_pairs={{0,4},{4,0},{8,12},{12,8},{16,20},{20,16},{24,28},{28,24},{32,36},... | collective-permute-start | bytes 1572872 | tf_op jit(solution)/shard_map/ppermute | solution.py:42
  40.7 13.8 %collective-permute-start.18 = (bf16[2,1024,128]{2,1,0:T(8,128)(2,1)S(1)}, bf16[2,1024,128]{2,1,0:T(8,128)(2,1)S(1)}, u32[]{:S(2)}, u32[]{:S(2)}) collective-permute-start(bf16[2,1024,128]{2,1,0:T(8,128)(2,1)S(1)} %pad_maximum_fusion.1.refs_0_), channel_id=1, source_target_pairs={{0,1},{1,2},{2,3},{3,0},{4,5},{5,6},{6,7},{7,4},{8,9},{9,10},{10,1... | collective-permute-start | bytes 1572872 | tf_op jit(solution)/shard_map/ppermute | solution.py:46
  55.6 12.1 %collective-permute-start.26 = (bf16[16,32,512]{2,1,0:T(8,128)(2,1)S(1)}, bf16[16,32,512]{2,1,0:T(8,128)(2,1)}, u32[]{:S(2)}, u32[]{:S(2)}) collective-permute-start(bf16[16,32,512]{2,1,0:T(8,128)(2,1)S(1)} %pad_maximum_fusion.5.refs_3_), channel_id=1, source_target_pairs={{0,96},{4,100},{8,104},{12,108},{16,112},{20,116},{24,120},{28,124... | collective-permute-start | bytes 1572872 | tf_op jit(solution)/shard_map/ppermute | solution.py:42
  57.9 11.4 %collective-permute-start.24 = (bf16[16,32,512]{2,1,0:T(8,128)(2,1)S(1)}, bf16[16,32,512]{2,1,0:T(8,128)(2,1)}, u32[]{:S(2)}, u32[]{:S(2)}) collective-permute-start(bf16[16,32,512]{2,1,0:T(8,128)(2,1)S(1)} %pad_maximum_fusion.4.refs_2_), channel_id=1, source_target_pairs={{0,32},{4,36},{8,40},{12,44},{16,48},{20,52},{24,56},{28,60},{32,0... | collective-permute-start | bytes 1572872 | tf_op jit(solution)/shard_map/ppermute | solution.py:42
  59.2 12.1 %collective-permute-start.22 = (bf16[16,32,512]{2,1,0:T(8,128)(2,1)S(1)}, bf16[16,32,512]{2,1,0:T(8,128)(2,1)}, u32[]{:S(2)}, u32[]{:S(2)}) collective-permute-start(bf16[16,32,512]{2,1,0:T(8,128)(2,1)S(1)} %pad_maximum_fusion.3.refs_1_), channel_id=1, source_target_pairs={{0,24},{4,28},{8,16},{12,20},{16,8},{20,12},{24,0},{28,4},{32,56},... | collective-permute-start | bytes 1572872 | tf_op jit(solution)/shard_map/ppermute | solution.py:42
  60.4 12.4 %collective-permute-start.20 = (bf16[16,32,512]{2,1,0:T(8,128)(2,1)}, bf16[16,32,512]{2,1,0:T(8,128)(2,1)}, u32[]{:S(2)}, u32[]{:S(2)}) collective-permute-start(bf16[16,32,512]{2,1,0:T(8,128)(2,1)} %pad_maximum_fusion.2.refs_0_), channel_id=1, source_target_pairs={{0,8},{4,12},{8,0},{12,4},{16,24},{20,28},{24,16},{28,20},{32,40},... | collective-permute-start | bytes 1572872 | tf_op jit(solution)/shard_map/ppermute | solution.py:42
  60.7 27.4 %collective-permute-start.19 = (bf16[2,1024,128]{2,1,0:T(8,128)(2,1)S(1)}, bf16[2,1024,128]{2,1,0:T(8,128)(2,1)S(1)}, u32[]{:S(2)}, u32[]{:S(2)}) collective-permute-start(bf16[2,1024,128]{2,1,0:T(8,128)(2,1)S(1)} %pad_maximum_fusion.1.refs_0_), channel_id=1, source_target_pairs={{0,2},{1,3},{2,0},{3,1},{4,6},{5,7},{6,4},{7,5},{8,10},{9,11},{10,... | collective-permute-start | bytes 1572872 | tf_op jit(solution)/shard_map/ppermute | solution.py:46
  67.7 11.1 %collective-permute-start.27 = (bf16[16,32,512]{2,1,0:T(8,128)(2,1)S(1)}, bf16[16,32,512]{2,1,0:T(8,128)(2,1)}, u32[]{:S(2)}, u32[]{:S(2)}) collective-permute-start(bf16[16,32,512]{2,1,0:T(8,128)(2,1)S(1)} %pad_maximum_fusion.5.refs_3_), channel_id=1, source_target_pairs={{0,32},{4,36},{8,40},{12,44},{16,48},{20,52},{24,56},{28,60},{32,0... | collective-permute-start | bytes 1572872 | tf_op jit(solution)/shard_map/ppermute | solution.py:42
  69.3 10.5 %collective-permute-start.25 = (bf16[16,32,512]{2,1,0:T(8,128)(2,1)S(1)}, bf16[16,32,512]{2,1,0:T(8,128)(2,1)}, u32[]{:S(2)}, u32[]{:S(2)}) collective-permute-start(bf16[16,32,512]{2,1,0:T(8,128)(2,1)S(1)} %pad_maximum_fusion.4.refs_2_), channel_id=1, source_target_pairs={{0,96},{4,100},{8,104},{12,108},{16,112},{20,116},{24,120},{28,124... | collective-permute-start | bytes 1572872 | tf_op jit(solution)/shard_map/ppermute | solution.py:42
  71.3 10.6 %collective-permute-start.23 = (bf16[16,32,512]{2,1,0:T(8,128)(2,1)S(1)}, bf16[16,32,512]{2,1,0:T(8,128)(2,1)}, u32[]{:S(2)}, u32[]{:S(2)}) collective-permute-start(bf16[16,32,512]{2,1,0:T(8,128)(2,1)S(1)} %pad_maximum_fusion.3.refs_1_), channel_id=1, source_target_pairs={{0,8},{4,12},{8,0},{12,4},{16,24},{20,28},{24,16},{28,20},{32,40},... | collective-permute-start | bytes 1572872 | tf_op jit(solution)/shard_map/ppermute | solution.py:42
  72.8 12.0 %collective-permute-start.21 = (bf16[16,32,512]{2,1,0:T(8,128)(2,1)}, bf16[16,32,512]{2,1,0:T(8,128)(2,1)}, u32[]{:S(2)}, u32[]{:S(2)}) collective-permute-start(bf16[16,32,512]{2,1,0:T(8,128)(2,1)} %pad_maximum_fusion.2.refs_0_), channel_id=1, source_target_pairs={{0,24},{4,28},{8,16},{12,20},{16,8},{20,12},{24,0},{28,4},{32,56},... | collective-permute-start | bytes 1572872 | tf_op jit(solution)/shard_map/ppermute | solution.py:42
  84.9 13.9 %collective-permute-start.31 = (bf16[16,32,512]{2,1,0:T(8,128)(2,1)}, bf16[16,32,512]{2,1,0:T(8,128)(2,1)}, u32[]{:S(2)}, u32[]{:S(2)}) collective-permute-start(bf16[16,32,512]{2,1,0:T(8,128)(2,1)} %collective-permute-done.26.refs_7_), channel_id=1, source_target_pairs={{0,32},{4,36},{8,40},{12,44},{16,48},{20,52},{24,56},{28,60},{32,0... | collective-permute-start | bytes 1572872 | tf_op jit(solution)/shard_map/ppermute | solution.py:42
  85.4 13.4 %collective-permute-start.30 = (bf16[16,32,512]{2,1,0:T(8,128)(2,1)}, bf16[16,32,512]{2,1,0:T(8,128)(2,1)}, u32[]{:S(2)}, u32[]{:S(2)}) collective-permute-start(bf16[16,32,512]{2,1,0:T(8,128)(2,1)} %collective-permute-done.24.refs_6_), channel_id=1, source_target_pairs={{0,96},{4,100},{8,104},{12,108},{16,112},{20,116},{24,120},{28,124... | collective-permute-start | bytes 1572872 | tf_op jit(solution)/shard_map/ppermute | solution.py:42
  85.4 13.4 %collective-permute-start.29 = (bf16[16,32,512]{2,1,0:T(8,128)(2,1)}, bf16[16,32,512]{2,1,0:T(8,128)(2,1)}, u32[]{:S(2)}, u32[]{:S(2)}) collective-permute-start(bf16[16,32,512]{2,1,0:T(8,128)(2,1)} %collective-permute-done.22.refs_5_), channel_id=1, source_target_pairs={{0,8},{4,12},{8,0},{12,4},{16,24},{20,28},{24,16},{28,20},{32,40},... | collective-permute-start | bytes 1572872 | tf_op jit(solution)/shard_map/ppermute | solution.py:42
  85.5 13.3 %collective-permute-start.28 = (bf16[16,32,512]{2,1,0:T(8,128)(2,1)}, bf16[16,32,512]{2,1,0:T(8,128)(2,1)}, u32[]{:S(2)}, u32[]{:S(2)}) collective-permute-start(bf16[16,32,512]{2,1,0:T(8,128)(2,1)} %collective-permute-done.20.refs_4_), channel_id=1, source_target_pairs={{0,24},{4,28},{8,16},{12,20},{16,8},{20,12},{24,0},{28,4},{32,56},... | collective-permute-start | bytes 1572872 | tf_op jit(solution)/shard_map/ppermute | solution.py:42
  88.1 12.9 %collective-permute-start.32 = (bf16[2,1024,128]{2,1,0:T(8,128)(2,1)S(1)}, bf16[2,1024,128]{2,1,0:T(8,128)(2,1)S(1)}, u32[]{:S(2)}, u32[]{:S(2)}) collective-permute-start(bf16[2,1024,128]{2,1,0:T(8,128)(2,1)S(1)} %pad_maximum_fusion.1.refs_0_), channel_id=1, source_target_pairs={{0,3},{1,0},{2,1},{3,2},{4,7},{5,4},{6,5},{7,6},{8,11},{9,8},{10,9... | collective-permute-start | bytes 1572872 | tf_op jit(solution)/shard_map/ppermute | solution.py:46
  114.5 10.6 %collective-permute-start.40 = (bf16[2,288,128]{2,1,0:T(8,128)(2,1)S(1)}, bf16[2,288,128]{2,1,0:T(8,128)(2,1)S(1)}, u32[]{:S(2)}, u32[]{:S(2)}) collective-permute-start(bf16[2,288,128]{2,1,0:T(8,128)(2,1)S(1)} %get-tuple-element.115), channel_id=1, source_target_pairs={{0,1},{1,2},{2,3},{3,0},{4,5},{5,6},{6,7},{7,4},{8,9},{9,10},{10,1... | collective-permute-start | bytes 442376 | tf_op jit(solution)/shard_map/ppermute | solution.py:46
  114.5 12.7 %collective-permute-start.41 = (bf16[2,288,128]{2,1,0:T(8,128)(2,1)S(1)}, bf16[2,288,128]{2,1,0:T(8,128)(2,1)S(1)}, u32[]{:S(2)}, u32[]{:S(2)}) collective-permute-start(bf16[2,288,128]{2,1,0:T(8,128)(2,1)S(1)} %get-tuple-element.116), channel_id=1, source_target_pairs={{0,2},{1,3},{2,0},{3,1},{4,6},{5,7},{6,4},{7,5},{8,10},{9,11},{10,... | collective-permute-start | bytes 442376 | tf_op jit(solution)/shard_map/ppermute | solution.py:46
  116.5 10.7 %collective-permute-start.42 = (bf16[2,288,128]{2,1,0:T(8,128)(2,1)S(1)}, bf16[2,288,128]{2,1,0:T(8,128)(2,1)S(1)}, u32[]{:S(2)}, u32[]{:S(2)}) collective-permute-start(bf16[2,288,128]{2,1,0:T(8,128)(2,1)S(1)} %get-tuple-element.117), channel_id=1, source_target_pairs={{0,3},{1,0},{2,1},{3,2},{4,7},{5,4},{6,5},{7,6},{8,11},{9,8},{10,9... | collective-permute-start | bytes 442376 | tf_op jit(solution)/shard_map/ppermute | solution.py:46
  121.6 10.0 %collective-permute-start.35 = (bf16[2,288,128]{2,1,0:T(8,128)(2,1)S(1)}, bf16[2,288,128]{2,1,0:T(8,128)(2,1)S(1)}, u32[]{:S(2)}, u32[]{:S(2)}) collective-permute-start(bf16[2,288,128]{2,1,0:T(8,128)(2,1)S(1)} %get-tuple-element.109), channel_id=1, source_target_pairs={{0,1},{1,2},{2,3},{3,0},{4,5},{5,6},{6,7},{7,4},{8,9},{9,10},{10,1... | collective-permute-start | bytes 442376 | tf_op jit(solution)/shard_map/ppermute | solution.py:46
  (26 other events, 377.8 us)

commit v11 on v10

--- a/solution.py
+++ b/solution.py
@@ -23,6 +23,7 @@
 COLS = PICKS * ROWS
 TILE = 512
 HID = 1024
+TAIL = 16
 EXTRA = 32
 
 
@@ -153,24 +154,32 @@
 
 def first_kernel(start, row_ref, *refs):
     q_refs, (lq_ref, table) = refs[:TP], refs[TP : TP + 2]
-    out_ref, stat_ref, picked, scores = refs[TP + 2 :]
+    out_ref, picked, scores = refs[TP + 2 :]
 
     for n in range(PART):
         top, total, acc = one_block(
             start + n, 0, q_refs, lq_ref, row_ref, table,
             picked.at[n], scores.at[n],
         )
-        out_ref[n] = acc.astype(jnp.bfloat16)
-        stat_ref[n] = rows_of(top, total)
-
-
-def split_rows(row):
+        stat = rows_of(top, total)
+        parts = parts_of(stat[0:1]) + parts_of(stat[1:2])
+        rows = [jnp.concatenate(parts[at : at + 2], axis=1) for at in (0, 2, 4)]
+        rows.append(jnp.zeros((TAIL - 3, E), jnp.float32))
+        out_ref[n, :BLK] = acc.astype(jnp.bfloat16)
+        out_ref[n, BLK:] = jnp.concatenate(rows, axis=0).astype(jnp.bfloat16)
+
+
+def parts_of(row):
     out = []
     for _ in range(3):
         part = row.astype(jnp.bfloat16).astype(jnp.float32)
-        out += [part[:, :128], part[:, 128:]]
+        out.append(part)
         row = row - part
     return out
+
+
+def split_rows(row):
+    return [part[:, at : at + 128] for part in parts_of(row) for at in (0, 128)]
 
 
 def joined_row(rows):
@@ -180,20 +189,26 @@
 
 def second_kernel(start, row_ref, *refs):
     q_refs, (lq_ref, table), refs = refs[:TP], refs[TP : TP + 2], refs[TP + 2 :]
-    other_ref, other_stat_ref, pos_ref = refs[:3]
-    outs = refs[3:7]
-    picked, scores = refs[7:]
+    other_ref, pos_ref = refs[:2]
+    outs = refs[2:6]
+    picked, scores = refs[6:]
 
     for n in range(PART):
         top, total, acc = one_block(
             start + n, 1, q_refs, lq_ref, row_ref, table,
             picked.at[n], scores.at[n],
         )
-        theirs = jnp.transpose(jnp.concatenate([other_stat_ref[n]] * 16, axis=0))
+        tail = other_ref[n, BLK:].astype(jnp.float32)
+        left, right = tail[:, :BLK], tail[:, BLK:]
+        row = lax.broadcasted_iota(jnp.int32, (128, BLK), 0)
+        their_top = left[0:1] + (right[0:1] + left[1:2])
+        their_total = right[1:2] + (left[2:3] + right[2:3])
+        theirs = jnp.where(row == 0, their_top, jnp.where(row == 1, their_total, 0.0))
+        theirs = jnp.transpose(theirs)
         their_top, their_total = theirs[:, 0:1], theirs[:, 1:2]
         joint = jnp.maximum(top, their_top)
         mine_by, theirs_by = jnp.exp2(top - joint), jnp.exp2(their_top - joint)
-        acc = acc * mine_by + other_ref[n].astype(jnp.float32) * theirs_by
+        acc = acc * mine_by + other_ref[n, :BLK].astype(jnp.float32) * theirs_by
         stat = rows_of(joint, total * mine_by + their_total * theirs_by)
         rows = split_rows(stat[0:1]) + split_rows(stat[1:2]) + split_rows(pos_ref[start + n])
         rows.append(jnp.zeros((EXTRA - len(rows), 128), jnp.float32))
@@ -369,10 +384,7 @@
     rows = rows.reshape(-1)
     table, pos_part, rows, lq = together(table, pos_part, rows, lq)
 
-    raw = (
-        jax.ShapeDtypeStruct((PART, BLK, E), jnp.bfloat16),
-        jax.ShapeDtypeStruct((PART, 8, BLK), jnp.float32),
-    )
+    raw = (jax.ShapeDtypeStruct((PART, BLK + TAIL, E), jnp.bfloat16),)
     share = jax.ShapeDtypeStruct((PART, BLK + EXTRA, 128), jnp.bfloat16)
     others = []
     for start in (0, PART):

time: 135 us -> 134 us (level)
  waiting for transfers between devices: 48.6 us -> 46.8 us
    ppermute x28 -> x26, waiting for transfers between devices: 29.9 us -> 28.8 us  [send(): return lax.ppermute(value, 'cat', cat_perm(y, z, c))]
    ppermute x28 -> x26, starting transfers between devices: 27.6 us -> 27.1 us  [send(): return lax.ppermute(value, 'cat', cat_perm(y, z, c))]
  transfers between devices with their start and end apart: 43 -> 41, of which waited for: 20 -> 18; matrix products, arithmetic and copies ran while one was open for 6% -> 6% of each run, Pallas kernels for 11% -> 12%
where the time goes in v11:
time: 134 us; the launch traced here: 132 us
  starting transfers between devices  50.1 us (37%)
  waiting for transfers between devices  46.8 us (35%)
  Pallas kernels  22.3 us (17%)
  local copies, waits for them, and re-layouts  6.37 us (5%)
  other arithmetic  5.42 us (4%)
    ppermute x26, waiting for transfers between devices, send(): return lax.ppermute(value, 'cat', cat_perm(y, z, c))  28.8 us
    ppermute x26, starting transfers between devices, send(): return lax.ppermute(value, 'cat', cat_perm(y, z, c))  27.1 us
    ppermute x15, starting transfers between devices, send_x(): return lax.ppermute(value, 'tp', [(i, (i + d) % TP) for i in range(TP)])  23.1 us
    ppermute x15, waiting for transfers between devices, send_x(): return lax.ppermute(value, 'tp', [(i, (i + d) % TP) for i in range(TP)])  18 us
    pallas_call x4, Pallas kernels, attend(): pl.pallas_call(functools.partial(body, start), in_specs=[pl.BlockSpec(mem...  15.1 us
    pallas_call x2, Pallas kernels, pack(): pl.pallas_call(functools.partial(pack_kernel, places), out_shape=jax.Shap...  3.99 us
  transfers between devices with their start and end apart: 41, of which 18 were waited for; matrix products, arithmetic and copies ran while one was open for 6% of the time, Pallas kernels for 12%

profile of v11, /device:TPU:0, one launch (start us, length us, event | category | flops | bytes accessed | tf_op | source)
XLA Modules:
  0.0 132.2 jit_solution(16471470705334480172)
XLA Ops:
  7.9 2.7 %collective-permute-start.5 = (bf16[128,512]{1,0:T(8,128)(2,1)S(1)}, bf16[128,512]{1,0:T(8,128)(2,1)S(1)}, u32[]{:S(2)}, u32[]{:S(2)}) collective-permute-start(bf16[128,512]{1,0:T(8,128)(2,1)S(1)} %constant_dynamic-slice_fusion.refs_4_), channel_id=1, source_target_pairs={{0,2},{1,3},{2,0},{3,1},{4,6},{5,7},{6,4},{7,5},{8,10},{9,11},{10,... | collective-permute-start | bytes 393224 | tf_op jit(solution)/shard_map/ppermute | solution.py:47
  12.1 4.5 %collective-permute-done.4.refs_5_ = bf16[128,512]{1,0:T(8,128)(2,1)S(1)} collective-permute-done((bf16[128,512]{1,0:T(8,128)(2,1)S(1)}, bf16[128,512]{1,0:T(8,128)(2,1)S(1)}, u32[]{:S(2)}, u32[]{:S(2)}) %collective-permute-start.4) | collective-permute-done | bytes 131104 | tf_op jit(solution)/shard_map/ppermute | solution.py:47
  16.6 3.9 %collective-permute-done.5.refs_6_ = bf16[128,512]{1,0:T(8,128)(2,1)S(1)} collective-permute-done((bf16[128,512]{1,0:T(8,128)(2,1)S(1)}, bf16[128,512]{1,0:T(8,128)(2,1)S(1)}, u32[]{:S(2)}, u32[]{:S(2)}) %collective-permute-start.5) | collective-permute-done | bytes 131104 | tf_op jit(solution)/shard_map/ppermute | solution.py:47
  26.0 5.0 %collective-permute-done.2.refs_2_ = bf16[512,256]{1,0:T(8,128)(2,1)S(1)} collective-permute-done((bf16[512,256]{1,0:T(8,128)(2,1)S(1)}, bf16[512,256]{1,0:T(8,128)(2,1)S(1)}, u32[]{:S(2)}, u32[]{:S(2)}) %collective-permute-start.2) | collective-permute-done | bytes 262176 | tf_op jit(solution)/shard_map/ppermute | solution.py:47
  34.1 2.2 %collective-permute-start.11 = (bf16[4,32,512]{2,1,0:T(8,128)(2,1)S(1)}, bf16[4,32,512]{2,1,0:T(8,128)(2,1)S(1)}, u32[]{:S(2)}, u32[]{:S(2)}) collective-permute-start(bf16[4,32,512]{2,1,0:T(8,128)(2,1)S(1)} %get-tuple-element.120), channel_id=1, source_target_pairs={{0,96},{4,100},{8,104},{12,108},{16,112},{20,116},{24,120},{28,124... | collective-permute-start | bytes 393224 | tf_op jit(solution)/shard_map/ppermute | solution.py:43
  38.2 2.5 %collective-permute-start.13 = (bf16[4,32,512]{2,1,0:T(8,128)(2,1)S(1)}, bf16[4,32,512]{2,1,0:T(8,128)(2,1)S(1)}, u32[]{:S(2)}, u32[]{:S(2)}) collective-permute-start(bf16[4,32,512]{2,1,0:T(8,128)(2,1)S(1)} %get-tuple-element.118), channel_id=1, source_target_pairs={{0,24},{4,28},{8,16},{12,20},{16,8},{20,12},{24,0},{28,4},{32,56},... | collective-permute-start | bytes 393224 | tf_op jit(solution)/shard_map/ppermute | solution.py:43
  41.3 3.1 %collective-permute-done.13 = bf16[4,32,512]{2,1,0:T(8,128)(2,1)S(1)} collective-permute-done((bf16[4,32,512]{2,1,0:T(8,128)(2,1)S(1)}, bf16[4,32,512]{2,1,0:T(8,128)(2,1)S(1)}, u32[]{:S(2)}, u32[]{:S(2)}) %collective-permute-start.13) | collective-permute-done | bytes 131104 | tf_op jit(solution)/shard_map/ppermute | solution.py:43
  45.6 2.5 %collective-permute-start.16 = (bf16[8,32,512]{2,1,0:T(8,128)(2,1)S(1)}, bf16[8,32,512]{2,1,0:T(8,128)(2,1)S(1)}, u32[]{:S(2)}, u32[]{:S(2)}) collective-permute-start(bf16[8,32,512]{2,1,0:T(8,128)(2,1)S(1)} %get-tuple-element.65), channel_id=1, source_target_pairs={{0,24},{4,28},{8,16},{12,20},{16,8},{20,12},{24,0},{28,4},{32,56},... | collective-permute-start | bytes 786440 | tf_op jit(solution)/shard_map/ppermute | solution.py:43
  48.1 4.0 %collective-permute-done.14 = bf16[8,32,512]{2,1,0:T(8,128)(2,1)S(1)} collective-permute-done((bf16[8,32,512]{2,1,0:T(8,128)(2,1)S(1)}, bf16[8,32,512]{2,1,0:T(8,128)(2,1)S(1)}, u32[]{:S(2)}, u32[]{:S(2)}) %collective-permute-start.14) | collective-permute-done | bytes 262176 | tf_op jit(solution)/shard_map/ppermute | solution.py:43
  55.6 2.3 %collective-permute-start.26 = (bf16[16,32,512]{2,1,0:T(8,128)(2,1)S(1)}, bf16[16,32,512]{2,1,0:T(8,128)(2,1)}, u32[]{:S(2)}, u32[]{:S(2)}) collective-permute-start(bf16[16,32,512]{2,1,0:T(8,128)(2,1)S(1)} %pad_maximum_fusion.5.refs_3_), channel_id=1, source_target_pairs={{0,96},{4,100},{8,104},{12,108},{16,112},{20,116},{24,120},{28,124... | collective-permute-start | bytes 1572872 | tf_op jit(solution)/shard_map/ppermute | solution.py:43
  62.5 5.2 %collective-permute-done.26.refs_7_ = bf16[16,32,512]{2,1,0:T(8,128)(2,1)} collective-permute-done((bf16[16,32,512]{2,1,0:T(8,128)(2,1)S(1)}, bf16[16,32,512]{2,1,0:T(8,128)(2,1)}, u32[]{:S(2)}, u32[]{:S(2)}) %collective-permute-start.26) | collective-permute-done | bytes 524320 | tf_op jit(solution)/shard_map/ppermute | solution.py:43
  72.8 2.5 %collective-permute-start.21 = (bf16[16,32,512]{2,1,0:T(8,128)(2,1)}, bf16[16,32,512]{2,1,0:T(8,128)(2,1)}, u32[]{:S(2)}, u32[]{:S(2)}) collective-permute-start(bf16[16,32,512]{2,1,0:T(8,128)(2,1)} %pad_maximum_fusion.2.refs_0_), channel_id=1, source_target_pairs={{0,24},{4,28},{8,16},{12,20},{16,8},{20,12},{24,0},{28,4},{32,56},... | collective-permute-start | bytes 1572872 | tf_op jit(solution)/shard_map/ppermute | solution.py:43
  75.8 3.0 %collective-permute-done.27.refs_3_ = bf16[16,32,512]{2,1,0:T(8,128)(2,1)} collective-permute-done((bf16[16,32,512]{2,1,0:T(8,128)(2,1)S(1)}, bf16[16,32,512]{2,1,0:T(8,128)(2,1)}, u32[]{:S(2)}, u32[]{:S(2)}) %collective-permute-start.27) | collective-permute-done | bytes 524320 | tf_op jit(solution)/shard_map/ppermute | solution.py:43
  81.8 3.0 %collective-permute-done.21.refs_0_ = bf16[16,32,512]{2,1,0:T(8,128)(2,1)} collective-permute-done((bf16[16,32,512]{2,1,0:T(8,128)(2,1)}, bf16[16,32,512]{2,1,0:T(8,128)(2,1)}, u32[]{:S(2)}, u32[]{:S(2)}) %collective-permute-start.21) | collective-permute-done | bytes 524320 | tf_op jit(solution)/shard_map/ppermute | solution.py:43
  85.5 2.6 %collective-permute-start.28 = (bf16[16,32,512]{2,1,0:T(8,128)(2,1)}, bf16[16,32,512]{2,1,0:T(8,128)(2,1)}, u32[]{:S(2)}, u32[]{:S(2)}) collective-permute-start(bf16[16,32,512]{2,1,0:T(8,128)(2,1)} %collective-permute-done.20.refs_4_), channel_id=1, source_target_pairs={{0,24},{4,28},{8,16},{12,20},{16,8},{20,12},{24,0},{28,4},{32,56},... | collective-permute-start | bytes 1572872 | tf_op jit(solution)/shard_map/ppermute | solution.py:43
  88.1 2.2 %collective-permute-start.32 = (bf16[2,1024,128]{2,1,0:T(8,128)(2,1)S(1)}, bf16[2,1024,128]{2,1,0:T(8,128)(2,1)S(1)}, u32[]{:S(2)}, u32[]{:S(2)}) collective-permute-start(bf16[2,1024,128]{2,1,0:T(8,128)(2,1)S(1)} %pad_maximum_fusion.1.refs_0_), channel_id=1, source_target_pairs={{0,3},{1,0},{2,1},{3,2},{4,7},{5,4},{6,5},{7,6},{8,11},{9,8},{10,9... | collective-permute-start | bytes 1572872 | tf_op jit(solution)/shard_map/ppermute | solution.py:47
  90.3 2.6 %gather_fusion = s32[512,128]{1,0:T(8,128)} fusion(s32[512,128]{1,0:T(8,128)} %bitcast.30, s32[1024]{0:T(1024)S(1)} %pad_clamp_fusion), kind=kCustom, calls=%fused_computation | custom fusion | bytes 526336 | tf_op jit(solution)/shard_map/gather | solution.py:380
  98.7 2.2 %pack.3.refs_5_ = bf16[256,32,512]{2,1,0:T(8,128)(2,1)S(1)} custom-call(bf16[16,32,512]{2,1,0:T(8,128)(2,1)} %collective-permute-done.21.refs_0_, bf16[16,32,512]{2,1,0:T(8,128)(2,1)} %collective-permute-done.23.refs_1_, bf16[16,32,512]{2,1,0:T(8,128)(2,1)} %collective-permute-done.25.refs_2_, ...), custom_call_target="tpu_custom_call", output_to_operand_aliasing={{}: (8, {})} | custom-call | bytes 8388608 | tf_op jit(solution)/shard_map/pack/pallas_call | solution.py:142
  101.0 3.7 %attend_other.3 = bf16[2,272,512]{2,1,0:T(8,128)(2,1)S(1)} custom-call(s32[512]{0:T(512)S(1)} %fusion.9.row_ref, bf16[2,1024,128]{2,1,0:T(8,128)(2,1)S(1)} %pad_maximum_fusion.1.refs_0_, bf16[2,1024,128]{2,1,0:T(8,128)(2,1)S(1)} %collective-permute-done.18.refs_1_, bf16[2,1024,128]{2,1,0:T(8,128)(2,1)S(1)} %collective-permute-done.19.refs_2_, ...), custom_call_target="tpu_custom_call" | custom-call | flops 2147483648 | bytes 2097152 | tf_op jit(solution)/shard_map/attend_other/pallas_call | solution.py:224
  104.8 3.7 %attend_other.2 = bf16[2,272,512]{2,1,0:T(8,128)(2,1)S(1)} custom-call(s32[512]{0:T(512)S(1)} %fusion.9.row_ref, bf16[2,1024,128]{2,1,0:T(8,128)(2,1)S(1)} %pad_maximum_fusion.1.refs_0_, bf16[2,1024,128]{2,1,0:T(8,128)(2,1)S(1)} %collective-permute-done.18.refs_1_, bf16[2,1024,128]{2,1,0:T(8,128)(2,1)S(1)} %collective-permute-done.19.refs_2_, ...), custom_call_target="tpu_custom_call" | custom-call | flops 2147483648 | bytes 2097152 | tf_op jit(solution)/shard_map/attend_other/pallas_call | solution.py:224
  109.1 3.9 %attend_own.3 = (bf16[2,288,128]{2,1,0:T(8,128)(2,1)S(1)}, bf16[2,288,128]{2,1,0:T(8,128)(2,1)S(1)}, bf16[2,288,128]{2,1,0:T(8,128)(2,1)S(1)}, bf16[2,288,128]{2,1,0:T(8,128)(2,1)S(1)}) custom-call(s32[512]{0:T(512)S(1)} %fusion.9.row_ref, bf16[2,1024,128]{2,1,0:T(8,128)(2,1)S(1)} %pad_maximum_fusion.1.refs_0_, ...), custom_call_target="tpu_custom_call" | custom-call | flops 2147483648 | bytes 2097152 | tf_op jit(solution)/shard_map/attend_own/pallas_call | solution.py:224
  116.2 3.9 %attend_own.2 = (bf16[2,288,128]{2,1,0:T(8,128)(2,1)S(1)}, bf16[2,288,128]{2,1,0:T(8,128)(2,1)S(1)}, bf16[2,288,128]{2,1,0:T(8,128)(2,1)S(1)}, bf16[2,288,128]{2,1,0:T(8,128)(2,1)S(1)}) custom-call(s32[512]{0:T(512)S(1)} %fusion.9.row_ref, bf16[2,1024,128]{2,1,0:T(8,128)(2,1)S(1)} %pad_maximum_fusion.1.refs_0_, ...), custom_call_target="tpu_custom_call" | custom-call | flops 2147483648 | bytes 2097152 | tf_op jit(solution)/shard_map/attend_own/pallas_call | solution.py:224
  123.2 2.5 %collective-permute-start.36 = (bf16[2,288,128]{2,1,0:T(8,128)(2,1)S(1)}, bf16[2,288,128]{2,1,0:T(8,128)(2,1)S(1)}, u32[]{:S(2)}, u32[]{:S(2)}) collective-permute-start(bf16[2,288,128]{2,1,0:T(8,128)(2,1)S(1)} %get-tuple-element.105), channel_id=1, source_target_pairs={{0,3},{1,0},{2,1},{3,2},{4,7},{5,4},{6,5},{7,6},{8,11},{9,8},{10,9... | collective-permute-start | bytes 442376 | tf_op jit(solution)/shard_map/ppermute | solution.py:47
  125.7 4.0 %collective-permute-done.34.refs_1_ = bf16[2,288,128]{2,1,0:T(8,128)(2,1)S(1)} collective-permute-done((bf16[2,288,128]{2,1,0:T(8,128)(2,1)S(1)}, bf16[2,288,128]{2,1,0:T(8,128)(2,1)S(1)}, u32[]{:S(2)}, u32[]{:S(2)}) %collective-permute-start.34) | collective-permute-done | bytes 147488 | tf_op jit(solution)/shard_map/ppermute | solution.py:47
  (108 shorter events, 53.4 us)
Async XLA Ops:
  4.2 16.4 %collective-permute-start.1 = (bf16[512,256]{1,0:T(8,128)(2,1)S(1)}, bf16[512,256]{1,0:T(8,128)(2,1)S(1)}, u32[]{:S(2)}, u32[]{:S(2)}) collective-permute-start(bf16[512,256]{1,0:T(8,128)(2,1)S(1)} %bitcast.37), channel_id=1, source_target_pairs={{0,1},{1,2},{2,3},{3,0},{4,5},{5,6},{6,7},{7,4},{8,9},{9,10},{10,1... | collective-permute-start | bytes 786440 | tf_op jit(solution)/shard_map/ppermute | solution.py:47
  5.8 14.8 %collective-permute-start.3 = (bf16[512,256]{1,0:T(8,128)(2,1)S(1)}, bf16[512,256]{1,0:T(8,128)(2,1)S(1)}, u32[]{:S(2)}, u32[]{:S(2)}) collective-permute-start(bf16[512,256]{1,0:T(8,128)(2,1)S(1)} %bitcast.36), channel_id=1, source_target_pairs={{0,3},{1,0},{2,1},{3,2},{4,7},{5,4},{6,5},{7,6},{8,11},{9,8},{10,9... | collective-permute-start | bytes 786440 | tf_op jit(solution)/shard_map/ppermute | solution.py:47
  7.9 12.6 %collective-permute-start.5 = (bf16[128,512]{1,0:T(8,128)(2,1)S(1)}, bf16[128,512]{1,0:T(8,128)(2,1)S(1)}, u32[]{:S(2)}, u32[]{:S(2)}) collective-permute-start(bf16[128,512]{1,0:T(8,128)(2,1)S(1)} %constant_dynamic-slice_fusion.refs_4_), channel_id=1, source_target_pairs={{0,2},{1,3},{2,0},{3,1},{4,6},{5,7},{6,4},{7,5},{8,10},{9,11},{10,... | collective-permute-start | bytes 393224 | tf_op jit(solution)/shard_map/ppermute | solution.py:47
  10.7 9.8 %collective-permute-start.6 = (bf16[128,512]{1,0:T(8,128)(2,1)S(1)}, bf16[128,512]{1,0:T(8,128)(2,1)S(1)}, u32[]{:S(2)}, u32[]{:S(2)}) collective-permute-start(bf16[128,512]{1,0:T(8,128)(2,1)S(1)} %constant_dynamic-slice_fusion.refs_4_), channel_id=1, source_target_pairs={{0,3},{1,0},{2,1},{3,2},{4,7},{5,4},{6,5},{7,6},{8,11},{9,8},{10,9... | collective-permute-start | bytes 393224 | tf_op jit(solution)/shard_map/ppermute | solution.py:47
  20.6 10.4 %collective-permute-start.7 = (bf16[4,128,512]{2,1,0:T(8,128)(2,1)S(1)}, bf16[4,128,512]{2,1,0:T(8,128)(2,1)S(1)}, u32[]{:S(2)}, u32[]{:S(2)}) collective-permute-start(bf16[4,128,512]{2,1,0:T(8,128)(2,1)S(1)} %pad_maximum_fusion), channel_id=1, source_target_pairs={{0,4},{4,0},{8,12},{12,8},{16,20},{20,16},{24,28},{28,24},{32,36},... | collective-permute-start | bytes 1572872 | tf_op jit(solution)/shard_map/ppermute | solution.py:43
  21.2 9.8 %collective-permute-start.2 = (bf16[512,256]{1,0:T(8,128)(2,1)S(1)}, bf16[512,256]{1,0:T(8,128)(2,1)S(1)}, u32[]{:S(2)}, u32[]{:S(2)}) collective-permute-start(bf16[512,256]{1,0:T(8,128)(2,1)S(1)} %bitcast.35), channel_id=1, source_target_pairs={{0,2},{1,3},{2,0},{3,1},{4,6},{5,7},{6,4},{7,5},{8,10},{9,11},{10,... | collective-permute-start | bytes 786440 | tf_op jit(solution)/shard_map/ppermute | solution.py:47
  40.7 13.8 %collective-permute-start.18 = (bf16[2,1024,128]{2,1,0:T(8,128)(2,1)S(1)}, bf16[2,1024,128]{2,1,0:T(8,128)(2,1)S(1)}, u32[]{:S(2)}, u32[]{:S(2)}) collective-permute-start(bf16[2,1024,128]{2,1,0:T(8,128)(2,1)S(1)} %pad_maximum_fusion.1.refs_0_), channel_id=1, source_target_pairs={{0,1},{1,2},{2,3},{3,0},{4,5},{5,6},{6,7},{7,4},{8,9},{9,10},{10,1... | collective-permute-start | bytes 1572872 | tf_op jit(solution)/shard_map/ppermute | solution.py:47
  55.6 12.1 %collective-permute-start.26 = (bf16[16,32,512]{2,1,0:T(8,128)(2,1)S(1)}, bf16[16,32,512]{2,1,0:T(8,128)(2,1)}, u32[]{:S(2)}, u32[]{:S(2)}) collective-permute-start(bf16[16,32,512]{2,1,0:T(8,128)(2,1)S(1)} %pad_maximum_fusion.5.refs_3_), channel_id=1, source_target_pairs={{0,96},{4,100},{8,104},{12,108},{16,112},{20,116},{24,120},{28,124... | collective-permute-start | bytes 1572872 | tf_op jit(solution)/shard_map/ppermute | solution.py:43
  57.9 11.4 %collective-permute-start.24 = (bf16[16,32,512]{2,1,0:T(8,128)(2,1)S(1)}, bf16[16,32,512]{2,1,0:T(8,128)(2,1)}, u32[]{:S(2)}, u32[]{:S(2)}) collective-permute-start(bf16[16,32,512]{2,1,0:T(8,128)(2,1)S(1)} %pad_maximum_fusion.4.refs_2_), channel_id=1, source_target_pairs={{0,32},{4,36},{8,40},{12,44},{16,48},{20,52},{24,56},{28,60},{32,0... | collective-permute-start | bytes 1572872 | tf_op jit(solution)/shard_map/ppermute | solution.py:43
  59.2 12.1 %collective-permute-start.22 = (bf16[16,32,512]{2,1,0:T(8,128)(2,1)S(1)}, bf16[16,32,512]{2,1,0:T(8,128)(2,1)}, u32[]{:S(2)}, u32[]{:S(2)}) collective-permute-start(bf16[16,32,512]{2,1,0:T(8,128)(2,1)S(1)} %pad_maximum_fusion.3.refs_1_), channel_id=1, source_target_pairs={{0,24},{4,28},{8,16},{12,20},{16,8},{20,12},{24,0},{28,4},{32,56},... | collective-permute-start | bytes 1572872 | tf_op jit(solution)/shard_map/ppermute | solution.py:43
  60.4 12.4 %collective-permute-start.20 = (bf16[16,32,512]{2,1,0:T(8,128)(2,1)}, bf16[16,32,512]{2,1,0:T(8,128)(2,1)}, u32[]{:S(2)}, u32[]{:S(2)}) collective-permute-start(bf16[16,32,512]{2,1,0:T(8,128)(2,1)} %pad_maximum_fusion.2.refs_0_), channel_id=1, source_target_pairs={{0,8},{4,12},{8,0},{12,4},{16,24},{20,28},{24,16},{28,20},{32,40},... | collective-permute-start | bytes 1572872 | tf_op jit(solution)/shard_map/ppermute | solution.py:43
  60.7 27.4 %collective-permute-start.19 = (bf16[2,1024,128]{2,1,0:T(8,128)(2,1)S(1)}, bf16[2,1024,128]{2,1,0:T(8,128)(2,1)S(1)}, u32[]{:S(2)}, u32[]{:S(2)}) collective-permute-start(bf16[2,1024,128]{2,1,0:T(8,128)(2,1)S(1)} %pad_maximum_fusion.1.refs_0_), channel_id=1, source_target_pairs={{0,2},{1,3},{2,0},{3,1},{4,6},{5,7},{6,4},{7,5},{8,10},{9,11},{10,... | collective-permute-start | bytes 1572872 | tf_op jit(solution)/shard_map/ppermute | solution.py:47
  67.7 11.1 %collective-permute-start.27 = (bf16[16,32,512]{2,1,0:T(8,128)(2,1)S(1)}, bf16[16,32,512]{2,1,0:T(8,128)(2,1)}, u32[]{:S(2)}, u32[]{:S(2)}) collective-permute-start(bf16[16,32,512]{2,1,0:T(8,128)(2,1)S(1)} %pad_maximum_fusion.5.refs_3_), channel_id=1, source_target_pairs={{0,32},{4,36},{8,40},{12,44},{16,48},{20,52},{24,56},{28,60},{32,0... | collective-permute-start | bytes 1572872 | tf_op jit(solution)/shard_map/ppermute | solution.py:43
  69.3 10.5 %collective-permute-start.25 = (bf16[16,32,512]{2,1,0:T(8,128)(2,1)S(1)}, bf16[16,32,512]{2,1,0:T(8,128)(2,1)}, u32[]{:S(2)}, u32[]{:S(2)}) collective-permute-start(bf16[16,32,512]{2,1,0:T(8,128)(2,1)S(1)} %pad_maximum_fusion.4.refs_2_), channel_id=1, source_target_pairs={{0,96},{4,100},{8,104},{12,108},{16,112},{20,116},{24,120},{28,124... | collective-permute-start | bytes 1572872 | tf_op jit(solution)/shard_map/ppermute | solution.py:43
  71.3 10.6 %collective-permute-start.23 = (bf16[16,32,512]{2,1,0:T(8,128)(2,1)S(1)}, bf16[16,32,512]{2,1,0:T(8,128)(2,1)}, u32[]{:S(2)}, u32[]{:S(2)}) collective-permute-start(bf16[16,32,512]{2,1,0:T(8,128)(2,1)S(1)} %pad_maximum_fusion.3.refs_1_), channel_id=1, source_target_pairs={{0,8},{4,12},{8,0},{12,4},{16,24},{20,28},{24,16},{28,20},{32,40},... | collective-permute-start | bytes 1572872 | tf_op jit(solution)/shard_map/ppermute | solution.py:43
  72.8 12.0 %collective-permute-start.21 = (bf16[16,32,512]{2,1,0:T(8,128)(2,1)}, bf16[16,32,512]{2,1,0:T(8,128)(2,1)}, u32[]{:S(2)}, u32[]{:S(2)}) collective-permute-start(bf16[16,32,512]{2,1,0:T(8,128)(2,1)} %pad_maximum_fusion.2.refs_0_), channel_id=1, source_target_pairs={{0,24},{4,28},{8,16},{12,20},{16,8},{20,12},{24,0},{28,4},{32,56},... | collective-permute-start | bytes 1572872 | tf_op jit(solution)/shard_map/ppermute | solution.py:43
  84.9 13.8 %collective-permute-start.31 = (bf16[16,32,512]{2,1,0:T(8,128)(2,1)}, bf16[16,32,512]{2,1,0:T(8,128)(2,1)}, u32[]{:S(2)}, u32[]{:S(2)}) collective-permute-start(bf16[16,32,512]{2,1,0:T(8,128)(2,1)} %collective-permute-done.26.refs_7_), channel_id=1, source_target_pairs={{0,32},{4,36},{8,40},{12,44},{16,48},{20,52},{24,56},{28,60},{32,0... | collective-permute-start | bytes 1572872 | tf_op jit(solution)/shard_map/ppermute | solution.py:43
  85.4 13.3 %collective-permute-start.30 = (bf16[16,32,512]{2,1,0:T(8,128)(2,1)}, bf16[16,32,512]{2,1,0:T(8,128)(2,1)}, u32[]{:S(2)}, u32[]{:S(2)}) collective-permute-start(bf16[16,32,512]{2,1,0:T(8,128)(2,1)} %collective-permute-done.24.refs_6_), channel_id=1, source_target_pairs={{0,96},{4,100},{8,104},{12,108},{16,112},{20,116},{24,120},{28,124... | collective-permute-start | bytes 1572872 | tf_op jit(solution)/shard_map/ppermute | solution.py:43
  85.4 13.3 %collective-permute-start.29 = (bf16[16,32,512]{2,1,0:T(8,128)(2,1)}, bf16[16,32,512]{2,1,0:T(8,128)(2,1)}, u32[]{:S(2)}, u32[]{:S(2)}) collective-permute-start(bf16[16,32,512]{2,1,0:T(8,128)(2,1)} %collective-permute-done.22.refs_5_), channel_id=1, source_target_pairs={{0,8},{4,12},{8,0},{12,4},{16,24},{20,28},{24,16},{28,20},{32,40},... | collective-permute-start | bytes 1572872 | tf_op jit(solution)/shard_map/ppermute | solution.py:43
  85.5 13.3 %collective-permute-start.28 = (bf16[16,32,512]{2,1,0:T(8,128)(2,1)}, bf16[16,32,512]{2,1,0:T(8,128)(2,1)}, u32[]{:S(2)}, u32[]{:S(2)}) collective-permute-start(bf16[16,32,512]{2,1,0:T(8,128)(2,1)} %collective-permute-done.20.refs_4_), channel_id=1, source_target_pairs={{0,24},{4,28},{8,16},{12,20},{16,8},{20,12},{24,0},{28,4},{32,56},... | collective-permute-start | bytes 1572872 | tf_op jit(solution)/shard_map/ppermute | solution.py:43
  88.1 12.9 %collective-permute-start.32 = (bf16[2,1024,128]{2,1,0:T(8,128)(2,1)S(1)}, bf16[2,1024,128]{2,1,0:T(8,128)(2,1)S(1)}, u32[]{:S(2)}, u32[]{:S(2)}) collective-permute-start(bf16[2,1024,128]{2,1,0:T(8,128)(2,1)S(1)} %pad_maximum_fusion.1.refs_0_), channel_id=1, source_target_pairs={{0,3},{1,0},{2,1},{3,2},{4,7},{5,4},{6,5},{7,6},{8,11},{9,8},{10,9... | collective-permute-start | bytes 1572872 | tf_op jit(solution)/shard_map/ppermute | solution.py:47
  112.9 10.3 %collective-permute-start.38 = (bf16[2,288,128]{2,1,0:T(8,128)(2,1)S(1)}, bf16[2,288,128]{2,1,0:T(8,128)(2,1)S(1)}, u32[]{:S(2)}, u32[]{:S(2)}) collective-permute-start(bf16[2,288,128]{2,1,0:T(8,128)(2,1)S(1)} %get-tuple-element.107), channel_id=1, source_target_pairs={{0,1},{1,2},{2,3},{3,0},{4,5},{5,6},{6,7},{7,4},{8,9},{9,10},{10,1... | collective-permute-start | bytes 442376 | tf_op jit(solution)/shard_map/ppermute | solution.py:47
  113.0 12.7 %collective-permute-start.39 = (bf16[2,288,128]{2,1,0:T(8,128)(2,1)S(1)}, bf16[2,288,128]{2,1,0:T(8,128)(2,1)S(1)}, u32[]{:S(2)}, u32[]{:S(2)}) collective-permute-start(bf16[2,288,128]{2,1,0:T(8,128)(2,1)S(1)} %get-tuple-element.108), channel_id=1, source_target_pairs={{0,2},{1,3},{2,0},{3,1},{4,6},{5,7},{6,4},{7,5},{8,10},{9,11},{10,... | collective-permute-start | bytes 442376 | tf_op jit(solution)/shard_map/ppermute | solution.py:47
  115.0 10.8 %collective-permute-start.40 = (bf16[2,288,128]{2,1,0:T(8,128)(2,1)S(1)}, bf16[2,288,128]{2,1,0:T(8,128)(2,1)S(1)}, u32[]{:S(2)}, u32[]{:S(2)}) collective-permute-start(bf16[2,288,128]{2,1,0:T(8,128)(2,1)S(1)} %get-tuple-element.109), channel_id=1, source_target_pairs={{0,3},{1,0},{2,1},{3,2},{4,7},{5,4},{6,5},{7,6},{8,11},{9,8},{10,9... | collective-permute-start | bytes 442376 | tf_op jit(solution)/shard_map/ppermute | solution.py:47
  (24 other events, 362.9 us)

commit v12 on v11

--- a/solution.py
+++ b/solution.py
@@ -305,13 +305,11 @@
 
 def spread(items, query):
     held = [items[n * 4 : n * 4 + 4] for n in range(4)]
-    got = [send(h, **{st[0][0]: st[0][1]}) for h, st in zip(held, STREAMS)]
     query_1 = send_x(query, 1)
-    got = together(*got)
-    held = together(*[jnp.concatenate([h, g]) for h, g in zip(held, got)])
-    got = [send(h, **{st[1][0]: st[1][1]}) for h, st in zip(held, STREAMS)]
-    *got, query_1, query = together(*got, query_1, query)
-    held = together(*[jnp.concatenate([h, g]) for h, g in zip(held, got)])
+    for step in range(2):
+        got = [send(h, **{st[step][0]: st[step][1]}) for h, st in zip(held, STREAMS)]
+        held = [jnp.concatenate(together(h, g)) for h, g in zip(held, got)]
+    held[3], query_1, query = together(held[3], query_1, query)
     third = [send(h, **{st[2][0]: st[2][1]}) for h, st in zip(held, STREAMS)]
     query_2 = send_x(query, 2)
     held, third = zip(*[together(h, t) for h, t in zip(held, third)])

time: 134 us -> 136 us (1.015)
  starting transfers between devices: 50.1 us -> 59.9 us
  waiting for transfers between devices: 46.8 us -> 39.4 us
  local copies, waits for them, and re-layouts: 6.37 us -> 7.96 us
    ppermute x26, waiting for transfers between devices: 28.8 us -> 21.3 us  [send(): return lax.ppermute(value, 'cat', cat_perm(y, z, c))]
    ppermute x26, starting transfers between devices: 27.1 us -> 32.8 us  [send(): return lax.ppermute(value, 'cat', cat_perm(y, z, c))]
    ppermute x15, starting transfers between devices: 23.1 us -> 27.1 us  [send_x(): return lax.ppermute(value, 'tp', [(i, (i + d) % TP) for i in range(TP)])]
  transfers between devices with their start and end apart: 41 -> 41, of which waited for: 18 -> 15; matrix products, arithmetic and copies ran while one was open for 6% -> 7% of each run, Pallas kernels for 12% -> 11%
where the time goes in v12:
time: 136 us; the launch traced here: 135 us
  starting transfers between devices  59.9 us (44%)
  waiting for transfers between devices  39.4 us (29%)
  Pallas kernels  22.3 us (16%)
  local copies, waits for them, and re-layouts  7.96 us (6%)
  other arithmetic  4.3 us (3%)
    ppermute x26, starting transfers between devices, send(): return lax.ppermute(value, 'cat', cat_perm(y, z, c))  32.8 us
    ppermute x15, starting transfers between devices, send_x(): return lax.ppermute(value, 'tp', [(i, (i + d) % TP) for i in range(TP)])  27.1 us
    ppermute x26, waiting for transfers between devices, send(): return lax.ppermute(value, 'cat', cat_perm(y, z, c))  21.3 us
    ppermute x15, waiting for transfers between devices, send_x(): return lax.ppermute(value, 'tp', [(i, (i + d) % TP) for i in range(TP)])  18.1 us
    pallas_call x4, Pallas kernels, attend(): pl.pallas_call(functools.partial(body, start), in_specs=[pl.BlockSpec(mem...  15.1 us
    pallas_call x2, Pallas kernels, pack(): pl.pallas_call(functools.partial(pack_kernel, places), out_shape=jax.Shap...  3.99 us
  transfers between devices with their start and end apart: 41, of which 15 were waited for; matrix products, arithmetic and copies ran while one was open for 7% of the time, Pallas kernels for 11%

profile of v12, /device:TPU:0, one launch (start us, length us, event | category | flops | bytes accessed | tf_op | source)
XLA Modules:
  0.0 135.0 jit_solution(14983021528705772506)
XLA Ops:
  7.9 2.7 %collective-permute-start.5 = (bf16[128,512]{1,0:T(8,128)(2,1)S(1)}, bf16[128,512]{1,0:T(8,128)(2,1)S(1)}, u32[]{:S(2)}, u32[]{:S(2)}) collective-permute-start(bf16[128,512]{1,0:T(8,128)(2,1)S(1)} %constant_dynamic-slice_fusion.refs_4_), channel_id=1, source_target_pairs={{0,2},{1,3},{2,0},{3,1},{4,6},{5,7},{6,4},{7,5},{8,10},{9,11},{10,... | collective-permute-start | bytes 393224 | tf_op jit(solution)/shard_map/ppermute | solution.py:47
  12.1 4.5 %collective-permute-done.4.refs_5_ = bf16[128,512]{1,0:T(8,128)(2,1)S(1)} collective-permute-done((bf16[128,512]{1,0:T(8,128)(2,1)S(1)}, bf16[128,512]{1,0:T(8,128)(2,1)S(1)}, u32[]{:S(2)}, u32[]{:S(2)}) %collective-permute-start.4) | collective-permute-done | bytes 131104 | tf_op jit(solution)/shard_map/ppermute | solution.py:47
  16.6 3.9 %collective-permute-done.5.refs_6_ = bf16[128,512]{1,0:T(8,128)(2,1)S(1)} collective-permute-done((bf16[128,512]{1,0:T(8,128)(2,1)S(1)}, bf16[128,512]{1,0:T(8,128)(2,1)S(1)}, u32[]{:S(2)}, u32[]{:S(2)}) %collective-permute-start.5) | collective-permute-done | bytes 131104 | tf_op jit(solution)/shard_map/ppermute | solution.py:47
  26.0 5.0 %collective-permute-done.2.refs_2_ = bf16[512,256]{1,0:T(8,128)(2,1)S(1)} collective-permute-done((bf16[512,256]{1,0:T(8,128)(2,1)S(1)}, bf16[512,256]{1,0:T(8,128)(2,1)S(1)}, u32[]{:S(2)}, u32[]{:S(2)}) %collective-permute-start.2) | collective-permute-done | bytes 262176 | tf_op jit(solution)/shard_map/ppermute | solution.py:47
  32.4 4.1 %collective-permute-start.10 = (bf16[4,32,512]{2,1,0:T(8,128)(2,1)S(1)}, bf16[4,32,512]{2,1,0:T(8,128)(2,1)S(1)}, u32[]{:S(2)}, u32[]{:S(2)}) collective-permute-start(bf16[4,32,512]{2,1,0:T(8,128)(2,1)S(1)} %get-tuple-element.60), channel_id=1, source_target_pairs={{0,24},{4,28},{8,16},{12,20},{16,8},{20,12},{24,0},{28,4},{32,56},... | collective-permute-start | bytes 393224 | tf_op jit(solution)/shard_map/ppermute | solution.py:43
  37.1 3.0 %collective-permute-start.18 = (bf16[4,32,512]{2,1,0:T(8,128)(2,1)S(1)}, bf16[4,32,512]{2,1,0:T(8,128)(2,1)S(1)}, u32[]{:S(2)}, u32[]{:S(2)}) collective-permute-start(bf16[4,32,512]{2,1,0:T(8,128)(2,1)S(1)} %get-tuple-element.74), channel_id=1, source_target_pairs={{0,96},{4,100},{8,104},{12,108},{16,112},{20,116},{24,120},{28,124... | collective-permute-start | bytes 393224 | tf_op jit(solution)/shard_map/ppermute | solution.py:43
  47.6 3.1 %collective-permute-done.23 = bf16[8,32,512]{2,1,0:T(8,128)(2,1)S(1)} collective-permute-done((bf16[8,32,512]{2,1,0:T(8,128)(2,1)S(1)}, bf16[8,32,512]{2,1,0:T(8,128)(2,1)S(1)}, u32[]{:S(2)}, u32[]{:S(2)}) %collective-permute-start.23) | collective-permute-done | bytes 262176 | tf_op jit(solution)/shard_map/ppermute | solution.py:43
  52.2 3.0 %collective-permute-start.20 = (bf16[16,32,512]{2,1,0:T(8,128)(2,1)S(1)}, bf16[16,32,512]{2,1,0:T(8,128)(2,1)}, u32[]{:S(2)}, u32[]{:S(2)}) collective-permute-start(bf16[16,32,512]{2,1,0:T(8,128)(2,1)S(1)} %constant_dynamic-update-slice_fusion.8.refs_1_), channel_id=1, source_target_pairs={{0,24},{4,28},{8,16},{12,20},{16,8},{20,12},{24,0},{28,4},{32,56},... | collective-permute-start | bytes 1572872 | tf_op jit(solution)/shard_map/ppermute | solution.py:43
  57.7 3.1 %collective-permute-start.26 = (bf16[16,32,512]{2,1,0:T(8,128)(2,1)S(1)}, bf16[16,32,512]{2,1,0:T(8,128)(2,1)}, u32[]{:S(2)}, u32[]{:S(2)}) collective-permute-start(bf16[16,32,512]{2,1,0:T(8,128)(2,1)S(1)} %pad_maximum_fusion.2.refs_3_), channel_id=1, source_target_pairs={{0,96},{4,100},{8,104},{12,108},{16,112},{20,116},{24,120},{28,124... | collective-permute-start | bytes 1572872 | tf_op jit(solution)/shard_map/ppermute | solution.py:43
  60.9 3.2 %collective-permute-start.13 = (bf16[2,1024,128]{2,1,0:T(8,128)(2,1)S(1)}, bf16[2,1024,128]{2,1,0:T(8,128)(2,1)S(1)}, u32[]{:S(2)}, u32[]{:S(2)}) collective-permute-start(bf16[2,1024,128]{2,1,0:T(8,128)(2,1)S(1)} %pad_maximum_fusion.1.refs_0_), channel_id=1, source_target_pairs={{0,2},{1,3},{2,0},{3,1},{4,6},{5,7},{6,4},{7,5},{8,10},{9,11},{10,... | collective-permute-start | bytes 1572872 | tf_op jit(solution)/shard_map/ppermute | solution.py:47
  66.3 2.2 %collective-permute-done.16.refs_4_ = bf16[16,32,512]{2,1,0:T(8,128)(2,1)} collective-permute-done((bf16[16,32,512]{2,1,0:T(8,128)(2,1)}, bf16[16,32,512]{2,1,0:T(8,128)(2,1)}, u32[]{:S(2)}, u32[]{:S(2)}) %collective-permute-start.16) | collective-permute-done | bytes 524320 | tf_op jit(solution)/shard_map/ppermute | solution.py:43
  68.5 4.9 %collective-permute-done.26.refs_7_ = bf16[16,32,512]{2,1,0:T(8,128)(2,1)} collective-permute-done((bf16[16,32,512]{2,1,0:T(8,128)(2,1)S(1)}, bf16[16,32,512]{2,1,0:T(8,128)(2,1)}, u32[]{:S(2)}, u32[]{:S(2)}) %collective-permute-start.26) | collective-permute-done | bytes 524320 | tf_op jit(solution)/shard_map/ppermute | solution.py:43
  73.8 5.2 %collective-permute-done.25.refs_2_ = bf16[16,32,512]{2,1,0:T(8,128)(2,1)} collective-permute-done((bf16[16,32,512]{2,1,0:T(8,128)(2,1)S(1)}, bf16[16,32,512]{2,1,0:T(8,128)(2,1)}, u32[]{:S(2)}, u32[]{:S(2)}) %collective-permute-start.25) | collective-permute-done | bytes 524320 | tf_op jit(solution)/shard_map/ppermute | solution.py:43
  79.2 6.2 %collective-permute-start.30 = (bf16[16,32,512]{2,1,0:T(8,128)(2,1)}, bf16[16,32,512]{2,1,0:T(8,128)(2,1)}, u32[]{:S(2)}, u32[]{:S(2)}) collective-permute-start(bf16[16,32,512]{2,1,0:T(8,128)(2,1)} %collective-permute-done.24.refs_6_), channel_id=1, source_target_pairs={{0,96},{4,100},{8,104},{12,108},{16,112},{20,116},{24,120},{28,124... | collective-permute-start | bytes 1572872 | tf_op jit(solution)/shard_map/ppermute | solution.py:43
  85.5 4.8 %collective-permute-start.32 = (bf16[2,1024,128]{2,1,0:T(8,128)(2,1)S(1)}, bf16[2,1024,128]{2,1,0:T(8,128)(2,1)S(1)}, u32[]{:S(2)}, u32[]{:S(2)}) collective-permute-start(bf16[2,1024,128]{2,1,0:T(8,128)(2,1)S(1)} %pad_maximum_fusion.1.refs_0_), channel_id=1, source_target_pairs={{0,3},{1,0},{2,1},{3,2},{4,7},{5,4},{6,5},{7,6},{8,11},{9,8},{10,9... | collective-permute-start | bytes 1572872 | tf_op jit(solution)/shard_map/ppermute | solution.py:47
  90.3 2.6 %collective-permute-start.31 = (bf16[16,32,512]{2,1,0:T(8,128)(2,1)}, bf16[16,32,512]{2,1,0:T(8,128)(2,1)}, u32[]{:S(2)}, u32[]{:S(2)}) collective-permute-start(bf16[16,32,512]{2,1,0:T(8,128)(2,1)} %collective-permute-done.26.refs_7_), channel_id=1, source_target_pairs={{0,32},{4,36},{8,40},{12,44},{16,48},{20,52},{24,56},{28,60},{32,0... | collective-permute-start | bytes 1572872 | tf_op jit(solution)/shard_map/ppermute | solution.py:43
  93.0 2.6 %gather_fusion = s32[512,128]{1,0:T(8,128)} fusion(s32[512,128]{1,0:T(8,128)} %bitcast.30, s32[1024]{0:T(1024)S(1)} %pad_clamp_fusion), kind=kCustom, calls=%fused_computation | custom fusion | bytes 526336 | tf_op jit(solution)/shard_map/gather | solution.py:378
  101.4 2.2 %pack.3.refs_5_ = bf16[256,32,512]{2,1,0:T(8,128)(2,1)S(1)} custom-call(bf16[16,32,512]{2,1,0:T(8,128)(2,1)} %collective-permute-done.17.refs_0_, bf16[16,32,512]{2,1,0:T(8,128)(2,1)} %collective-permute-done.21.refs_1_, bf16[16,32,512]{2,1,0:T(8,128)(2,1)} %collective-permute-done.25.refs_2_, ...), custom_call_target="tpu_custom_call", output_to_operand_aliasing={{}: (8, {})} | custom-call | bytes 8388608 | tf_op jit(solution)/shard_map/pack/pallas_call | solution.py:142
  103.7 3.7 %attend_other.3 = bf16[2,272,512]{2,1,0:T(8,128)(2,1)S(1)} custom-call(s32[512]{0:T(512)S(1)} %fusion.9.row_ref, bf16[2,1024,128]{2,1,0:T(8,128)(2,1)S(1)} %pad_maximum_fusion.1.refs_0_, bf16[2,1024,128]{2,1,0:T(8,128)(2,1)S(1)} %collective-permute-done.12.refs_1_, bf16[2,1024,128]{2,1,0:T(8,128)(2,1)S(1)} %collective-permute-done.13.refs_2_, ...), custom_call_target="tpu_custom_call" | custom-call | flops 2147483648 | bytes 2097152 | tf_op jit(solution)/shard_map/attend_other/pallas_call | solution.py:224
  107.5 3.7 %attend_other.2 = bf16[2,272,512]{2,1,0:T(8,128)(2,1)S(1)} custom-call(s32[512]{0:T(512)S(1)} %fusion.9.row_ref, bf16[2,1024,128]{2,1,0:T(8,128)(2,1)S(1)} %pad_maximum_fusion.1.refs_0_, bf16[2,1024,128]{2,1,0:T(8,128)(2,1)S(1)} %collective-permute-done.12.refs_1_, bf16[2,1024,128]{2,1,0:T(8,128)(2,1)S(1)} %collective-permute-done.13.refs_2_, ...), custom_call_target="tpu_custom_call" | custom-call | flops 2147483648 | bytes 2097152 | tf_op jit(solution)/shard_map/attend_other/pallas_call | solution.py:224
  111.8 3.9 %attend_own.3 = (bf16[2,288,128]{2,1,0:T(8,128)(2,1)S(1)}, bf16[2,288,128]{2,1,0:T(8,128)(2,1)S(1)}, bf16[2,288,128]{2,1,0:T(8,128)(2,1)S(1)}, bf16[2,288,128]{2,1,0:T(8,128)(2,1)S(1)}) custom-call(s32[512]{0:T(512)S(1)} %fusion.9.row_ref, bf16[2,1024,128]{2,1,0:T(8,128)(2,1)S(1)} %pad_maximum_fusion.1.refs_0_, ...), custom_call_target="tpu_custom_call" | custom-call | flops 2147483648 | bytes 2097152 | tf_op jit(solution)/shard_map/attend_own/pallas_call | solution.py:224
  119.3 3.9 %attend_own.2 = (bf16[2,288,128]{2,1,0:T(8,128)(2,1)S(1)}, bf16[2,288,128]{2,1,0:T(8,128)(2,1)S(1)}, bf16[2,288,128]{2,1,0:T(8,128)(2,1)S(1)}, bf16[2,288,128]{2,1,0:T(8,128)(2,1)S(1)}) custom-call(s32[512]{0:T(512)S(1)} %fusion.9.row_ref, bf16[2,1024,128]{2,1,0:T(8,128)(2,1)S(1)} %pad_maximum_fusion.1.refs_0_, ...), custom_call_target="tpu_custom_call" | custom-call | flops 2147483648 | bytes 2097152 | tf_op jit(solution)/shard_map/attend_own/pallas_call | solution.py:224
  125.9 2.5 %collective-permute-start.36 = (bf16[2,288,128]{2,1,0:T(8,128)(2,1)S(1)}, bf16[2,288,128]{2,1,0:T(8,128)(2,1)S(1)}, u32[]{:S(2)}, u32[]{:S(2)}) collective-permute-start(bf16[2,288,128]{2,1,0:T(8,128)(2,1)S(1)} %get-tuple-element.107), channel_id=1, source_target_pairs={{0,3},{1,0},{2,1},{3,2},{4,7},{5,4},{6,5},{7,6},{8,11},{9,8},{10,9... | collective-permute-start | bytes 442376 | tf_op jit(solution)/shard_map/ppermute | solution.py:47
  128.4 4.1 %collective-permute-done.34.refs_1_ = bf16[2,288,128]{2,1,0:T(8,128)(2,1)S(1)} collective-permute-done((bf16[2,288,128]{2,1,0:T(8,128)(2,1)S(1)}, bf16[2,288,128]{2,1,0:T(8,128)(2,1)S(1)}, u32[]{:S(2)}, u32[]{:S(2)}) %collective-permute-start.34) | collective-permute-done | bytes 147488 | tf_op jit(solution)/shard_map/ppermute | solution.py:47
  (117 shorter events, 45.9 us)
Async XLA Ops:
  4.2 16.4 %collective-permute-start.1 = (bf16[512,256]{1,0:T(8,128)(2,1)S(1)}, bf16[512,256]{1,0:T(8,128)(2,1)S(1)}, u32[]{:S(2)}, u32[]{:S(2)}) collective-permute-start(bf16[512,256]{1,0:T(8,128)(2,1)S(1)} %bitcast.37), channel_id=1, source_target_pairs={{0,1},{1,2},{2,3},{3,0},{4,5},{5,6},{6,7},{7,4},{8,9},{9,10},{10,1... | collective-permute-start | bytes 786440 | tf_op jit(solution)/shard_map/ppermute | solution.py:47
  5.8 14.8 %collective-permute-start.3 = (bf16[512,256]{1,0:T(8,128)(2,1)S(1)}, bf16[512,256]{1,0:T(8,128)(2,1)S(1)}, u32[]{:S(2)}, u32[]{:S(2)}) collective-permute-start(bf16[512,256]{1,0:T(8,128)(2,1)S(1)} %bitcast.36), channel_id=1, source_target_pairs={{0,3},{1,0},{2,1},{3,2},{4,7},{5,4},{6,5},{7,6},{8,11},{9,8},{10,9... | collective-permute-start | bytes 786440 | tf_op jit(solution)/shard_map/ppermute | solution.py:47
  7.9 12.6 %collective-permute-start.5 = (bf16[128,512]{1,0:T(8,128)(2,1)S(1)}, bf16[128,512]{1,0:T(8,128)(2,1)S(1)}, u32[]{:S(2)}, u32[]{:S(2)}) collective-permute-start(bf16[128,512]{1,0:T(8,128)(2,1)S(1)} %constant_dynamic-slice_fusion.refs_4_), channel_id=1, source_target_pairs={{0,2},{1,3},{2,0},{3,1},{4,6},{5,7},{6,4},{7,5},{8,10},{9,11},{10,... | collective-permute-start | bytes 393224 | tf_op jit(solution)/shard_map/ppermute | solution.py:47
  10.7 9.8 %collective-permute-start.6 = (bf16[128,512]{1,0:T(8,128)(2,1)S(1)}, bf16[128,512]{1,0:T(8,128)(2,1)S(1)}, u32[]{:S(2)}, u32[]{:S(2)}) collective-permute-start(bf16[128,512]{1,0:T(8,128)(2,1)S(1)} %constant_dynamic-slice_fusion.refs_4_), channel_id=1, source_target_pairs={{0,3},{1,0},{2,1},{3,2},{4,7},{5,4},{6,5},{7,6},{8,11},{9,8},{10,9... | collective-permute-start | bytes 393224 | tf_op jit(solution)/shard_map/ppermute | solution.py:47
  20.6 10.4 %collective-permute-start.7 = (bf16[4,128,512]{2,1,0:T(8,128)(2,1)S(1)}, bf16[4,128,512]{2,1,0:T(8,128)(2,1)S(1)}, u32[]{:S(2)}, u32[]{:S(2)}) collective-permute-start(bf16[4,128,512]{2,1,0:T(8,128)(2,1)S(1)} %pad_maximum_fusion), channel_id=1, source_target_pairs={{0,4},{4,0},{8,12},{12,8},{16,20},{20,16},{24,28},{28,24},{32,36},... | collective-permute-start | bytes 1572872 | tf_op jit(solution)/shard_map/ppermute | solution.py:43
  36.6 21.1 %collective-permute-start.12 = (bf16[2,1024,128]{2,1,0:T(8,128)(2,1)S(1)}, bf16[2,1024,128]{2,1,0:T(8,128)(2,1)S(1)}, u32[]{:S(2)}, u32[]{:S(2)}) collective-permute-start(bf16[2,1024,128]{2,1,0:T(8,128)(2,1)S(1)} %pad_maximum_fusion.1.refs_0_), channel_id=1, source_target_pairs={{0,1},{1,2},{2,3},{3,0},{4,5},{5,6},{6,7},{7,4},{8,9},{9,10},{10,1... | collective-permute-start | bytes 1572872 | tf_op jit(solution)/shard_map/ppermute | solution.py:47
  40.3 10.4 %collective-permute-start.11 = (bf16[8,32,512]{2,1,0:T(8,128)(2,1)S(1)}, bf16[8,32,512]{2,1,0:T(8,128)(2,1)S(1)}, u32[]{:S(2)}, u32[]{:S(2)}) collective-permute-start(bf16[8,32,512]{2,1,0:T(8,128)(2,1)S(1)} %constant_dynamic-update-slice_fusion), channel_id=1, source_target_pairs={{0,8},{4,12},{8,0},{12,4},{16,24},{20,28},{24,16},{28,20},{32,40},... | collective-permute-start | bytes 786440 | tf_op jit(solution)/shard_map/ppermute | solution.py:43
  50.7 13.4 %collective-permute-start.24 = (bf16[16,32,512]{2,1,0:T(8,128)(2,1)S(1)}, bf16[16,32,512]{2,1,0:T(8,128)(2,1)}, u32[]{:S(2)}, u32[]{:S(2)}) collective-permute-start(bf16[16,32,512]{2,1,0:T(8,128)(2,1)S(1)} %constant_dynamic-update-slice_fusion.12.refs_2_), channel_id=1, source_target_pairs={{0,32},{4,36},{8,40},{12,44},{16,48},{20,52},{24,56},{28,60},{32,0... | collective-permute-start | bytes 1572872 | tf_op jit(solution)/shard_map/ppermute | solution.py:43
  52.2 12.2 %collective-permute-start.20 = (bf16[16,32,512]{2,1,0:T(8,128)(2,1)S(1)}, bf16[16,32,512]{2,1,0:T(8,128)(2,1)}, u32[]{:S(2)}, u32[]{:S(2)}) collective-permute-start(bf16[16,32,512]{2,1,0:T(8,128)(2,1)S(1)} %constant_dynamic-update-slice_fusion.8.refs_1_), channel_id=1, source_target_pairs={{0,24},{4,28},{8,16},{12,20},{16,8},{20,12},{24,0},{28,4},{32,56},... | collective-permute-start | bytes 1572872 | tf_op jit(solution)/shard_map/ppermute | solution.py:43
  56.6 11.9 %collective-permute-start.16 = (bf16[16,32,512]{2,1,0:T(8,128)(2,1)}, bf16[16,32,512]{2,1,0:T(8,128)(2,1)}, u32[]{:S(2)}, u32[]{:S(2)}) collective-permute-start(bf16[16,32,512]{2,1,0:T(8,128)(2,1)} %constant_dynamic-update-slice_fusion.4.refs_0_), channel_id=1, source_target_pairs={{0,8},{4,12},{8,0},{12,4},{16,24},{20,28},{24,16},{28,20},{32,40},... | collective-permute-start | bytes 1572872 | tf_op jit(solution)/shard_map/ppermute | solution.py:43
  57.7 15.7 %collective-permute-start.26 = (bf16[16,32,512]{2,1,0:T(8,128)(2,1)S(1)}, bf16[16,32,512]{2,1,0:T(8,128)(2,1)}, u32[]{:S(2)}, u32[]{:S(2)}) collective-permute-start(bf16[16,32,512]{2,1,0:T(8,128)(2,1)S(1)} %pad_maximum_fusion.2.refs_3_), channel_id=1, source_target_pairs={{0,96},{4,100},{8,104},{12,108},{16,112},{20,116},{24,120},{28,124... | collective-permute-start | bytes 1572872 | tf_op jit(solution)/shard_map/ppermute | solution.py:43
  60.9 24.6 %collective-permute-start.13 = (bf16[2,1024,128]{2,1,0:T(8,128)(2,1)S(1)}, bf16[2,1024,128]{2,1,0:T(8,128)(2,1)S(1)}, u32[]{:S(2)}, u32[]{:S(2)}) collective-permute-start(bf16[2,1024,128]{2,1,0:T(8,128)(2,1)S(1)} %pad_maximum_fusion.1.refs_0_), channel_id=1, source_target_pairs={{0,2},{1,3},{2,0},{3,1},{4,6},{5,7},{6,4},{7,5},{8,10},{9,11},{10,... | collective-permute-start | bytes 1572872 | tf_op jit(solution)/shard_map/ppermute | solution.py:47
  64.1 14.9 %collective-permute-start.25 = (bf16[16,32,512]{2,1,0:T(8,128)(2,1)S(1)}, bf16[16,32,512]{2,1,0:T(8,128)(2,1)}, u32[]{:S(2)}, u32[]{:S(2)}) collective-permute-start(bf16[16,32,512]{2,1,0:T(8,128)(2,1)S(1)} %constant_dynamic-update-slice_fusion.12.refs_2_), channel_id=1, source_target_pairs={{0,96},{4,100},{8,104},{12,108},{16,112},{20,116},{24,120},{28,124... | collective-permute-start | bytes 1572872 | tf_op jit(solution)/shard_map/ppermute | solution.py:43
  64.4 14.6 %collective-permute-start.21 = (bf16[16,32,512]{2,1,0:T(8,128)(2,1)S(1)}, bf16[16,32,512]{2,1,0:T(8,128)(2,1)}, u32[]{:S(2)}, u32[]{:S(2)}) collective-permute-start(bf16[16,32,512]{2,1,0:T(8,128)(2,1)S(1)} %constant_dynamic-update-slice_fusion.8.refs_1_), channel_id=1, source_target_pairs={{0,8},{4,12},{8,0},{12,4},{16,24},{20,28},{24,16},{28,20},{32,40},... | collective-permute-start | bytes 1572872 | tf_op jit(solution)/shard_map/ppermute | solution.py:43
  68.5 10.7 %collective-permute-start.17 = (bf16[16,32,512]{2,1,0:T(8,128)(2,1)}, bf16[16,32,512]{2,1,0:T(8,128)(2,1)}, u32[]{:S(2)}, u32[]{:S(2)}) collective-permute-start(bf16[16,32,512]{2,1,0:T(8,128)(2,1)} %constant_dynamic-update-slice_fusion.4.refs_0_), channel_id=1, source_target_pairs={{0,24},{4,28},{8,16},{12,20},{16,8},{20,12},{24,0},{28,4},{32,56},... | collective-permute-start | bytes 1572872 | tf_op jit(solution)/shard_map/ppermute | solution.py:43
  73.4 16.9 %collective-permute-start.27 = (bf16[16,32,512]{2,1,0:T(8,128)(2,1)S(1)}, bf16[16,32,512]{2,1,0:T(8,128)(2,1)}, u32[]{:S(2)}, u32[]{:S(2)}) collective-permute-start(bf16[16,32,512]{2,1,0:T(8,128)(2,1)S(1)} %pad_maximum_fusion.2.refs_3_), channel_id=1, source_target_pairs={{0,32},{4,36},{8,40},{12,44},{16,48},{20,52},{24,56},{28,60},{32,0... | collective-permute-start | bytes 1572872 | tf_op jit(solution)/shard_map/ppermute | solution.py:43
  79.2 22.2 %collective-permute-start.30 = (bf16[16,32,512]{2,1,0:T(8,128)(2,1)}, bf16[16,32,512]{2,1,0:T(8,128)(2,1)}, u32[]{:S(2)}, u32[]{:S(2)}) collective-permute-start(bf16[16,32,512]{2,1,0:T(8,128)(2,1)} %collective-permute-done.24.refs_6_), channel_id=1, source_target_pairs={{0,96},{4,100},{8,104},{12,108},{16,112},{20,116},{24,120},{28,124... | collective-permute-start | bytes 1572872 | tf_op jit(solution)/shard_map/ppermute | solution.py:43
  85.4 16.0 %collective-permute-start.29 = (bf16[16,32,512]{2,1,0:T(8,128)(2,1)}, bf16[16,32,512]{2,1,0:T(8,128)(2,1)}, u32[]{:S(2)}, u32[]{:S(2)}) collective-permute-start(bf16[16,32,512]{2,1,0:T(8,128)(2,1)} %collective-permute-done.20.refs_5_), channel_id=1, source_target_pairs={{0,8},{4,12},{8,0},{12,4},{16,24},{20,28},{24,16},{28,20},{32,40},... | collective-permute-start | bytes 1572872 | tf_op jit(solution)/shard_map/ppermute | solution.py:43
  85.4 16.1 %collective-permute-start.28 = (bf16[16,32,512]{2,1,0:T(8,128)(2,1)}, bf16[16,32,512]{2,1,0:T(8,128)(2,1)}, u32[]{:S(2)}, u32[]{:S(2)}) collective-permute-start(bf16[16,32,512]{2,1,0:T(8,128)(2,1)} %collective-permute-done.16.refs_4_), channel_id=1, source_target_pairs={{0,24},{4,28},{8,16},{12,20},{16,8},{20,12},{24,0},{28,4},{32,56},... | collective-permute-start | bytes 1572872 | tf_op jit(solution)/shard_map/ppermute | solution.py:43
  85.5 18.1 %collective-permute-start.32 = (bf16[2,1024,128]{2,1,0:T(8,128)(2,1)S(1)}, bf16[2,1024,128]{2,1,0:T(8,128)(2,1)S(1)}, u32[]{:S(2)}, u32[]{:S(2)}) collective-permute-start(bf16[2,1024,128]{2,1,0:T(8,128)(2,1)S(1)} %pad_maximum_fusion.1.refs_0_), channel_id=1, source_target_pairs={{0,3},{1,0},{2,1},{3,2},{4,7},{5,4},{6,5},{7,6},{8,11},{9,8},{10,9... | collective-permute-start | bytes 1572872 | tf_op jit(solution)/shard_map/ppermute | solution.py:47
  90.3 11.1 %collective-permute-start.31 = (bf16[16,32,512]{2,1,0:T(8,128)(2,1)}, bf16[16,32,512]{2,1,0:T(8,128)(2,1)}, u32[]{:S(2)}, u32[]{:S(2)}) collective-permute-start(bf16[16,32,512]{2,1,0:T(8,128)(2,1)} %collective-permute-done.26.refs_7_), channel_id=1, source_target_pairs={{0,32},{4,36},{8,40},{12,44},{16,48},{20,52},{24,56},{28,60},{32,0... | collective-permute-start | bytes 1572872 | tf_op jit(solution)/shard_map/ppermute | solution.py:43
  115.6 10.3 %collective-permute-start.38 = (bf16[2,288,128]{2,1,0:T(8,128)(2,1)S(1)}, bf16[2,288,128]{2,1,0:T(8,128)(2,1)S(1)}, u32[]{:S(2)}, u32[]{:S(2)}) collective-permute-start(bf16[2,288,128]{2,1,0:T(8,128)(2,1)S(1)} %get-tuple-element.109), channel_id=1, source_target_pairs={{0,1},{1,2},{2,3},{3,0},{4,5},{5,6},{6,7},{7,4},{8,9},{9,10},{10,1... | collective-permute-start | bytes 442376 | tf_op jit(solution)/shard_map/ppermute | solution.py:47
  116.2 12.2 %collective-permute-start.39 = (bf16[2,288,128]{2,1,0:T(8,128)(2,1)S(1)}, bf16[2,288,128]{2,1,0:T(8,128)(2,1)S(1)}, u32[]{:S(2)}, u32[]{:S(2)}) collective-permute-start(bf16[2,288,128]{2,1,0:T(8,128)(2,1)S(1)} %get-tuple-element.110), channel_id=1, source_target_pairs={{0,2},{1,3},{2,0},{3,1},{4,6},{5,7},{6,4},{7,5},{8,10},{9,11},{10,... | collective-permute-start | bytes 442376 | tf_op jit(solution)/shard_map/ppermute | solution.py:47
  118.4 10.0 %collective-permute-start.40 = (bf16[2,288,128]{2,1,0:T(8,128)(2,1)S(1)}, bf16[2,288,128]{2,1,0:T(8,128)(2,1)S(1)}, u32[]{:S(2)}, u32[]{:S(2)}) collective-permute-start(bf16[2,288,128]{2,1,0:T(8,128)(2,1)S(1)} %get-tuple-element.111), channel_id=1, source_target_pairs={{0,3},{1,0},{2,1},{3,2},{4,7},{5,4},{6,5},{7,6},{8,11},{9,8},{10,9... | collective-permute-start | bytes 442376 | tf_op jit(solution)/shard_map/ppermute | solution.py:47
  (24 other events, 367.2 us)

commit v13 on v12

--- a/solution.py
+++ b/solution.py
@@ -317,7 +317,7 @@
     held, third = list(held), list(third)
     third, fourth = zip(*[together(t, f) for t, f in zip(third, fourth)])
     third, fourth = list(third), list(fourth)
-    query_2, query, fourth[0] = together(query_2, query, fourth[0])
+    query_2, query, *fourth = together(query_2, query, *fourth)
     queries = [query, query_1, query_2, send_x(query, 3)]
     fifth = [send(h, **{st[3][0]: st[3][1]}) for h, st in zip(third, STREAMS)]
     table = pack(held + third, (0, 4, 8, 12, 1, 5, 9, 13))

time: 136 us -> 136 us (level)
    ppermute x26, starting transfers between devices: 32.8 us -> 36.1 us  [send(): return lax.ppermute(value, 'cat', cat_perm(y, z, c))]
    ppermute x15, starting transfers between devices: 27.1 us -> 23.8 us  [send_x(): return lax.ppermute(value, 'tp', [(i, (i + d) % TP) for i in range(TP)])]
where the time goes in v13:
time: 136 us; the launch traced here: 135 us
  starting transfers between devices  59.9 us (44%)
  waiting for transfers between devices  39.4 us (29%)
  Pallas kernels  22.3 us (16%)
  local copies, waits for them, and re-layouts  7.96 us (6%)
  other arithmetic  4.3 us (3%)
    ppermute x26, starting transfers between devices, send(): return lax.ppermute(value, 'cat', cat_perm(y, z, c))  36.1 us
    ppermute x15, starting transfers between devices, send_x(): return lax.ppermute(value, 'tp', [(i, (i + d) % TP) for i in range(TP)])  23.8 us
    ppermute x26, waiting for transfers between devices, send(): return lax.ppermute(value, 'cat', cat_perm(y, z, c))  21.3 us
    ppermute x15, waiting for transfers between devices, send_x(): return lax.ppermute(value, 'tp', [(i, (i + d) % TP) for i in range(TP)])  18.1 us
    pallas_call x4, Pallas kernels, attend(): pl.pallas_call(functools.partial(body, start), in_specs=[pl.BlockSpec(mem...  15.1 us
    pallas_call x2, Pallas kernels, pack(): pl.pallas_call(functools.partial(pack_kernel, places), out_shape=jax.Shap...  3.99 us
  transfers between devices with their start and end apart: 41, of which 15 were waited for; matrix products, arithmetic and copies ran while one was open for 7% of the time, Pallas kernels for 11%

profile of v13, /device:TPU:0, one launch (start us, length us, event | category | flops | bytes accessed | tf_op | source)
XLA Modules:
  0.0 135.0 jit_solution(9819392449255383137)
XLA Ops:
  7.9 2.7 %collective-permute-start.5 = (bf16[128,512]{1,0:T(8,128)(2,1)S(1)}, bf16[128,512]{1,0:T(8,128)(2,1)S(1)}, u32[]{:S(2)}, u32[]{:S(2)}) collective-permute-start(bf16[128,512]{1,0:T(8,128)(2,1)S(1)} %constant_dynamic-slice_fusion.refs_4_), channel_id=1, source_target_pairs={{0,2},{1,3},{2,0},{3,1},{4,6},{5,7},{6,4},{7,5},{8,10},{9,11},{10,... | collective-permute-start | bytes 393224 | tf_op jit(solution)/shard_map/ppermute | solution.py:47
  12.1 4.5 %collective-permute-done.4.refs_5_ = bf16[128,512]{1,0:T(8,128)(2,1)S(1)} collective-permute-done((bf16[128,512]{1,0:T(8,128)(2,1)S(1)}, bf16[128,512]{1,0:T(8,128)(2,1)S(1)}, u32[]{:S(2)}, u32[]{:S(2)}) %collective-permute-start.4) | collective-permute-done | bytes 131104 | tf_op jit(solution)/shard_map/ppermute | solution.py:47
  16.6 3.9 %collective-permute-done.5.refs_6_ = bf16[128,512]{1,0:T(8,128)(2,1)S(1)} collective-permute-done((bf16[128,512]{1,0:T(8,128)(2,1)S(1)}, bf16[128,512]{1,0:T(8,128)(2,1)S(1)}, u32[]{:S(2)}, u32[]{:S(2)}) %collective-permute-start.5) | collective-permute-done | bytes 131104 | tf_op jit(solution)/shard_map/ppermute | solution.py:47
  26.0 5.0 %collective-permute-done.2.refs_2_ = bf16[512,256]{1,0:T(8,128)(2,1)S(1)} collective-permute-done((bf16[512,256]{1,0:T(8,128)(2,1)S(1)}, bf16[512,256]{1,0:T(8,128)(2,1)S(1)}, u32[]{:S(2)}, u32[]{:S(2)}) %collective-permute-start.2) | collective-permute-done | bytes 262176 | tf_op jit(solution)/shard_map/ppermute | solution.py:47
  32.4 4.1 %collective-permute-start.10 = (bf16[4,32,512]{2,1,0:T(8,128)(2,1)S(1)}, bf16[4,32,512]{2,1,0:T(8,128)(2,1)S(1)}, u32[]{:S(2)}, u32[]{:S(2)}) collective-permute-start(bf16[4,32,512]{2,1,0:T(8,128)(2,1)S(1)} %get-tuple-element.63), channel_id=1, source_target_pairs={{0,24},{4,28},{8,16},{12,20},{16,8},{20,12},{24,0},{28,4},{32,56},... | collective-permute-start | bytes 393224 | tf_op jit(solution)/shard_map/ppermute | solution.py:43
  37.1 3.0 %collective-permute-start.18 = (bf16[4,32,512]{2,1,0:T(8,128)(2,1)S(1)}, bf16[4,32,512]{2,1,0:T(8,128)(2,1)S(1)}, u32[]{:S(2)}, u32[]{:S(2)}) collective-permute-start(bf16[4,32,512]{2,1,0:T(8,128)(2,1)S(1)} %get-tuple-element.76), channel_id=1, source_target_pairs={{0,96},{4,100},{8,104},{12,108},{16,112},{20,116},{24,120},{28,124... | collective-permute-start | bytes 393224 | tf_op jit(solution)/shard_map/ppermute | solution.py:43
  47.6 3.1 %collective-permute-done.23 = bf16[8,32,512]{2,1,0:T(8,128)(2,1)S(1)} collective-permute-done((bf16[8,32,512]{2,1,0:T(8,128)(2,1)S(1)}, bf16[8,32,512]{2,1,0:T(8,128)(2,1)S(1)}, u32[]{:S(2)}, u32[]{:S(2)}) %collective-permute-start.23) | collective-permute-done | bytes 262176 | tf_op jit(solution)/shard_map/ppermute | solution.py:43
  52.2 3.0 %collective-permute-start.20 = (bf16[16,32,512]{2,1,0:T(8,128)(2,1)S(1)}, bf16[16,32,512]{2,1,0:T(8,128)(2,1)}, u32[]{:S(2)}, u32[]{:S(2)}) collective-permute-start(bf16[16,32,512]{2,1,0:T(8,128)(2,1)S(1)} %constant_dynamic-update-slice_fusion.8.refs_1_), channel_id=1, source_target_pairs={{0,24},{4,28},{8,16},{12,20},{16,8},{20,12},{24,0},{28,4},{32,56},... | collective-permute-start | bytes 1572872 | tf_op jit(solution)/shard_map/ppermute | solution.py:43
  57.7 3.1 %collective-permute-start.26 = (bf16[16,32,512]{2,1,0:T(8,128)(2,1)S(1)}, bf16[16,32,512]{2,1,0:T(8,128)(2,1)}, u32[]{:S(2)}, u32[]{:S(2)}) collective-permute-start(bf16[16,32,512]{2,1,0:T(8,128)(2,1)S(1)} %pad_maximum_fusion.2.refs_3_), channel_id=1, source_target_pairs={{0,96},{4,100},{8,104},{12,108},{16,112},{20,116},{24,120},{28,124... | collective-permute-start | bytes 1572872 | tf_op jit(solution)/shard_map/ppermute | solution.py:43
  60.9 3.2 %collective-permute-start.13 = (bf16[2,1024,128]{2,1,0:T(8,128)(2,1)S(1)}, bf16[2,1024,128]{2,1,0:T(8,128)(2,1)S(1)}, u32[]{:S(2)}, u32[]{:S(2)}) collective-permute-start(bf16[2,1024,128]{2,1,0:T(8,128)(2,1)S(1)} %pad_maximum_fusion.1.refs_0_), channel_id=1, source_target_pairs={{0,2},{1,3},{2,0},{3,1},{4,6},{5,7},{6,4},{7,5},{8,10},{9,11},{10,... | collective-permute-start | bytes 1572872 | tf_op jit(solution)/shard_map/ppermute | solution.py:47
  66.3 2.2 %collective-permute-done.16.refs_4_ = bf16[16,32,512]{2,1,0:T(8,128)(2,1)} collective-permute-done((bf16[16,32,512]{2,1,0:T(8,128)(2,1)}, bf16[16,32,512]{2,1,0:T(8,128)(2,1)}, u32[]{:S(2)}, u32[]{:S(2)}) %collective-permute-start.16) | collective-permute-done | bytes 524320 | tf_op jit(solution)/shard_map/ppermute | solution.py:43
  68.5 4.9 %collective-permute-done.26.refs_7_ = bf16[16,32,512]{2,1,0:T(8,128)(2,1)} collective-permute-done((bf16[16,32,512]{2,1,0:T(8,128)(2,1)S(1)}, bf16[16,32,512]{2,1,0:T(8,128)(2,1)}, u32[]{:S(2)}, u32[]{:S(2)}) %collective-permute-start.26) | collective-permute-done | bytes 524320 | tf_op jit(solution)/shard_map/ppermute | solution.py:43
  73.8 5.2 %collective-permute-done.25.refs_2_ = bf16[16,32,512]{2,1,0:T(8,128)(2,1)} collective-permute-done((bf16[16,32,512]{2,1,0:T(8,128)(2,1)S(1)}, bf16[16,32,512]{2,1,0:T(8,128)(2,1)}, u32[]{:S(2)}, u32[]{:S(2)}) %collective-permute-start.25) | collective-permute-done | bytes 524320 | tf_op jit(solution)/shard_map/ppermute | solution.py:43
  79.2 6.2 %collective-permute-start.30 = (bf16[16,32,512]{2,1,0:T(8,128)(2,1)}, bf16[16,32,512]{2,1,0:T(8,128)(2,1)}, u32[]{:S(2)}, u32[]{:S(2)}) collective-permute-start(bf16[16,32,512]{2,1,0:T(8,128)(2,1)} %collective-permute-done.24.refs_6_), channel_id=1, source_target_pairs={{0,96},{4,100},{8,104},{12,108},{16,112},{20,116},{24,120},{28,124... | collective-permute-start | bytes 1572872 | tf_op jit(solution)/shard_map/ppermute | solution.py:43
  85.5 5.9 %collective-permute-start.31 = (bf16[16,32,512]{2,1,0:T(8,128)(2,1)}, bf16[16,32,512]{2,1,0:T(8,128)(2,1)}, u32[]{:S(2)}, u32[]{:S(2)}) collective-permute-start(bf16[16,32,512]{2,1,0:T(8,128)(2,1)} %collective-permute-done.26.refs_7_), channel_id=1, source_target_pairs={{0,32},{4,36},{8,40},{12,44},{16,48},{20,52},{24,56},{28,60},{32,0... | collective-permute-start | bytes 1572872 | tf_op jit(solution)/shard_map/ppermute | solution.py:43
  93.0 2.6 %gather_fusion = s32[512,128]{1,0:T(8,128)} fusion(s32[512,128]{1,0:T(8,128)} %bitcast.30, s32[1024]{0:T(1024)S(1)} %pad_clamp_fusion), kind=kCustom, calls=%fused_computation | custom fusion | bytes 526336 | tf_op jit(solution)/shard_map/gather | solution.py:378
  101.4 2.2 %pack.3.refs_5_ = bf16[256,32,512]{2,1,0:T(8,128)(2,1)S(1)} custom-call(bf16[16,32,512]{2,1,0:T(8,128)(2,1)} %collective-permute-done.17.refs_0_, bf16[16,32,512]{2,1,0:T(8,128)(2,1)} %collective-permute-done.21.refs_1_, bf16[16,32,512]{2,1,0:T(8,128)(2,1)} %collective-permute-done.25.refs_2_, ...), custom_call_target="tpu_custom_call", output_to_operand_aliasing={{}: (8, {})} | custom-call | bytes 8388608 | tf_op jit(solution)/shard_map/pack/pallas_call | solution.py:142
  103.7 3.7 %attend_other.3 = bf16[2,272,512]{2,1,0:T(8,128)(2,1)S(1)} custom-call(s32[512]{0:T(512)S(1)} %fusion.9.row_ref, bf16[2,1024,128]{2,1,0:T(8,128)(2,1)S(1)} %pad_maximum_fusion.1.refs_0_, bf16[2,1024,128]{2,1,0:T(8,128)(2,1)S(1)} %collective-permute-done.12.refs_1_, bf16[2,1024,128]{2,1,0:T(8,128)(2,1)S(1)} %collective-permute-done.13.refs_2_, ...), custom_call_target="tpu_custom_call" | custom-call | flops 2147483648 | bytes 2097152 | tf_op jit(solution)/shard_map/attend_other/pallas_call | solution.py:224
  107.5 3.7 %attend_other.2 = bf16[2,272,512]{2,1,0:T(8,128)(2,1)S(1)} custom-call(s32[512]{0:T(512)S(1)} %fusion.9.row_ref, bf16[2,1024,128]{2,1,0:T(8,128)(2,1)S(1)} %pad_maximum_fusion.1.refs_0_, bf16[2,1024,128]{2,1,0:T(8,128)(2,1)S(1)} %collective-permute-done.12.refs_1_, bf16[2,1024,128]{2,1,0:T(8,128)(2,1)S(1)} %collective-permute-done.13.refs_2_, ...), custom_call_target="tpu_custom_call" | custom-call | flops 2147483648 | bytes 2097152 | tf_op jit(solution)/shard_map/attend_other/pallas_call | solution.py:224
  111.8 3.9 %attend_own.3 = (bf16[2,288,128]{2,1,0:T(8,128)(2,1)S(1)}, bf16[2,288,128]{2,1,0:T(8,128)(2,1)S(1)}, bf16[2,288,128]{2,1,0:T(8,128)(2,1)S(1)}, bf16[2,288,128]{2,1,0:T(8,128)(2,1)S(1)}) custom-call(s32[512]{0:T(512)S(1)} %fusion.9.row_ref, bf16[2,1024,128]{2,1,0:T(8,128)(2,1)S(1)} %pad_maximum_fusion.1.refs_0_, ...), custom_call_target="tpu_custom_call" | custom-call | flops 2147483648 | bytes 2097152 | tf_op jit(solution)/shard_map/attend_own/pallas_call | solution.py:224
  116.2 2.2 %collective-permute-start.39 = (bf16[2,288,128]{2,1,0:T(8,128)(2,1)S(1)}, bf16[2,288,128]{2,1,0:T(8,128)(2,1)S(1)}, u32[]{:S(2)}, u32[]{:S(2)}) collective-permute-start(bf16[2,288,128]{2,1,0:T(8,128)(2,1)S(1)} %get-tuple-element.116), channel_id=1, source_target_pairs={{0,2},{1,3},{2,0},{3,1},{4,6},{5,7},{6,4},{7,5},{8,10},{9,11},{10,... | collective-permute-start | bytes 442376 | tf_op jit(solution)/shard_map/ppermute | solution.py:47
  119.1 3.9 %attend_own.2 = (bf16[2,288,128]{2,1,0:T(8,128)(2,1)S(1)}, bf16[2,288,128]{2,1,0:T(8,128)(2,1)S(1)}, bf16[2,288,128]{2,1,0:T(8,128)(2,1)S(1)}, bf16[2,288,128]{2,1,0:T(8,128)(2,1)S(1)}) custom-call(s32[512]{0:T(512)S(1)} %fusion.9.row_ref, bf16[2,1024,128]{2,1,0:T(8,128)(2,1)S(1)} %pad_maximum_fusion.1.refs_0_, ...), custom_call_target="tpu_custom_call" | custom-call | flops 2147483648 | bytes 2097152 | tf_op jit(solution)/shard_map/attend_own/pallas_call | solution.py:224
  125.9 2.5 %collective-permute-start.36 = (bf16[2,288,128]{2,1,0:T(8,128)(2,1)S(1)}, bf16[2,288,128]{2,1,0:T(8,128)(2,1)S(1)}, u32[]{:S(2)}, u32[]{:S(2)}) collective-permute-start(bf16[2,288,128]{2,1,0:T(8,128)(2,1)S(1)} %get-tuple-element.113), channel_id=1, source_target_pairs={{0,3},{1,0},{2,1},{3,2},{4,7},{5,4},{6,5},{7,6},{8,11},{9,8},{10,9... | collective-permute-start | bytes 442376 | tf_op jit(solution)/shard_map/ppermute | solution.py:47
  128.4 4.1 %collective-permute-done.34.refs_1_ = bf16[2,288,128]{2,1,0:T(8,128)(2,1)S(1)} collective-permute-done((bf16[2,288,128]{2,1,0:T(8,128)(2,1)S(1)}, bf16[2,288,128]{2,1,0:T(8,128)(2,1)S(1)}, u32[]{:S(2)}, u32[]{:S(2)}) %collective-permute-start.34) | collective-permute-done | bytes 147488 | tf_op jit(solution)/shard_map/ppermute | solution.py:47
  (117 shorter events, 45.2 us)
Async XLA Ops:
  4.2 16.4 %collective-permute-start.1 = (bf16[512,256]{1,0:T(8,128)(2,1)S(1)}, bf16[512,256]{1,0:T(8,128)(2,1)S(1)}, u32[]{:S(2)}, u32[]{:S(2)}) collective-permute-start(bf16[512,256]{1,0:T(8,128)(2,1)S(1)} %bitcast.37), channel_id=1, source_target_pairs={{0,1},{1,2},{2,3},{3,0},{4,5},{5,6},{6,7},{7,4},{8,9},{9,10},{10,1... | collective-permute-start | bytes 786440 | tf_op jit(solution)/shard_map/ppermute | solution.py:47
  5.8 14.8 %collective-permute-start.3 = (bf16[512,256]{1,0:T(8,128)(2,1)S(1)}, bf16[512,256]{1,0:T(8,128)(2,1)S(1)}, u32[]{:S(2)}, u32[]{:S(2)}) collective-permute-start(bf16[512,256]{1,0:T(8,128)(2,1)S(1)} %bitcast.36), channel_id=1, source_target_pairs={{0,3},{1,0},{2,1},{3,2},{4,7},{5,4},{6,5},{7,6},{8,11},{9,8},{10,9... | collective-permute-start | bytes 786440 | tf_op jit(solution)/shard_map/ppermute | solution.py:47
  7.9 12.6 %collective-permute-start.5 = (bf16[128,512]{1,0:T(8,128)(2,1)S(1)}, bf16[128,512]{1,0:T(8,128)(2,1)S(1)}, u32[]{:S(2)}, u32[]{:S(2)}) collective-permute-start(bf16[128,512]{1,0:T(8,128)(2,1)S(1)} %constant_dynamic-slice_fusion.refs_4_), channel_id=1, source_target_pairs={{0,2},{1,3},{2,0},{3,1},{4,6},{5,7},{6,4},{7,5},{8,10},{9,11},{10,... | collective-permute-start | bytes 393224 | tf_op jit(solution)/shard_map/ppermute | solution.py:47
  10.7 9.8 %collective-permute-start.6 = (bf16[128,512]{1,0:T(8,128)(2,1)S(1)}, bf16[128,512]{1,0:T(8,128)(2,1)S(1)}, u32[]{:S(2)}, u32[]{:S(2)}) collective-permute-start(bf16[128,512]{1,0:T(8,128)(2,1)S(1)} %constant_dynamic-slice_fusion.refs_4_), channel_id=1, source_target_pairs={{0,3},{1,0},{2,1},{3,2},{4,7},{5,4},{6,5},{7,6},{8,11},{9,8},{10,9... | collective-permute-start | bytes 393224 | tf_op jit(solution)/shard_map/ppermute | solution.py:47
  20.6 10.4 %collective-permute-start.7 = (bf16[4,128,512]{2,1,0:T(8,128)(2,1)S(1)}, bf16[4,128,512]{2,1,0:T(8,128)(2,1)S(1)}, u32[]{:S(2)}, u32[]{:S(2)}) collective-permute-start(bf16[4,128,512]{2,1,0:T(8,128)(2,1)S(1)} %pad_maximum_fusion), channel_id=1, source_target_pairs={{0,4},{4,0},{8,12},{12,8},{16,20},{20,16},{24,28},{28,24},{32,36},... | collective-permute-start | bytes 1572872 | tf_op jit(solution)/shard_map/ppermute | solution.py:43
  36.6 21.1 %collective-permute-start.12 = (bf16[2,1024,128]{2,1,0:T(8,128)(2,1)S(1)}, bf16[2,1024,128]{2,1,0:T(8,128)(2,1)S(1)}, u32[]{:S(2)}, u32[]{:S(2)}) collective-permute-start(bf16[2,1024,128]{2,1,0:T(8,128)(2,1)S(1)} %pad_maximum_fusion.1.refs_0_), channel_id=1, source_target_pairs={{0,1},{1,2},{2,3},{3,0},{4,5},{5,6},{6,7},{7,4},{8,9},{9,10},{10,1... | collective-permute-start | bytes 1572872 | tf_op jit(solution)/shard_map/ppermute | solution.py:47
  40.3 10.4 %collective-permute-start.11 = (bf16[8,32,512]{2,1,0:T(8,128)(2,1)S(1)}, bf16[8,32,512]{2,1,0:T(8,128)(2,1)S(1)}, u32[]{:S(2)}, u32[]{:S(2)}) collective-permute-start(bf16[8,32,512]{2,1,0:T(8,128)(2,1)S(1)} %constant_dynamic-update-slice_fusion), channel_id=1, source_target_pairs={{0,8},{4,12},{8,0},{12,4},{16,24},{20,28},{24,16},{28,20},{32,40},... | collective-permute-start | bytes 786440 | tf_op jit(solution)/shard_map/ppermute | solution.py:43
  50.7 13.4 %collective-permute-start.24 = (bf16[16,32,512]{2,1,0:T(8,128)(2,1)S(1)}, bf16[16,32,512]{2,1,0:T(8,128)(2,1)}, u32[]{:S(2)}, u32[]{:S(2)}) collective-permute-start(bf16[16,32,512]{2,1,0:T(8,128)(2,1)S(1)} %constant_dynamic-update-slice_fusion.12.refs_2_), channel_id=1, source_target_pairs={{0,32},{4,36},{8,40},{12,44},{16,48},{20,52},{24,56},{28,60},{32,0... | collective-permute-start | bytes 1572872 | tf_op jit(solution)/shard_map/ppermute | solution.py:43
  52.2 12.2 %collective-permute-start.20 = (bf16[16,32,512]{2,1,0:T(8,128)(2,1)S(1)}, bf16[16,32,512]{2,1,0:T(8,128)(2,1)}, u32[]{:S(2)}, u32[]{:S(2)}) collective-permute-start(bf16[16,32,512]{2,1,0:T(8,128)(2,1)S(1)} %constant_dynamic-update-slice_fusion.8.refs_1_), channel_id=1, source_target_pairs={{0,24},{4,28},{8,16},{12,20},{16,8},{20,12},{24,0},{28,4},{32,56},... | collective-permute-start | bytes 1572872 | tf_op jit(solution)/shard_map/ppermute | solution.py:43
  56.6 11.9 %collective-permute-start.16 = (bf16[16,32,512]{2,1,0:T(8,128)(2,1)}, bf16[16,32,512]{2,1,0:T(8,128)(2,1)}, u32[]{:S(2)}, u32[]{:S(2)}) collective-permute-start(bf16[16,32,512]{2,1,0:T(8,128)(2,1)} %constant_dynamic-update-slice_fusion.4.refs_0_), channel_id=1, source_target_pairs={{0,8},{4,12},{8,0},{12,4},{16,24},{20,28},{24,16},{28,20},{32,40},... | collective-permute-start | bytes 1572872 | tf_op jit(solution)/shard_map/ppermute | solution.py:43
  57.7 15.7 %collective-permute-start.26 = (bf16[16,32,512]{2,1,0:T(8,128)(2,1)S(1)}, bf16[16,32,512]{2,1,0:T(8,128)(2,1)}, u32[]{:S(2)}, u32[]{:S(2)}) collective-permute-start(bf16[16,32,512]{2,1,0:T(8,128)(2,1)S(1)} %pad_maximum_fusion.2.refs_3_), channel_id=1, source_target_pairs={{0,96},{4,100},{8,104},{12,108},{16,112},{20,116},{24,120},{28,124... | collective-permute-start | bytes 1572872 | tf_op jit(solution)/shard_map/ppermute | solution.py:43
  60.9 30.5 %collective-permute-start.13 = (bf16[2,1024,128]{2,1,0:T(8,128)(2,1)S(1)}, bf16[2,1024,128]{2,1,0:T(8,128)(2,1)S(1)}, u32[]{:S(2)}, u32[]{:S(2)}) collective-permute-start(bf16[2,1024,128]{2,1,0:T(8,128)(2,1)S(1)} %pad_maximum_fusion.1.refs_0_), channel_id=1, source_target_pairs={{0,2},{1,3},{2,0},{3,1},{4,6},{5,7},{6,4},{7,5},{8,10},{9,11},{10,... | collective-permute-start | bytes 1572872 | tf_op jit(solution)/shard_map/ppermute | solution.py:47
  64.1 14.9 %collective-permute-start.25 = (bf16[16,32,512]{2,1,0:T(8,128)(2,1)S(1)}, bf16[16,32,512]{2,1,0:T(8,128)(2,1)}, u32[]{:S(2)}, u32[]{:S(2)}) collective-permute-start(bf16[16,32,512]{2,1,0:T(8,128)(2,1)S(1)} %constant_dynamic-update-slice_fusion.12.refs_2_), channel_id=1, source_target_pairs={{0,96},{4,100},{8,104},{12,108},{16,112},{20,116},{24,120},{28,124... | collective-permute-start | bytes 1572872 | tf_op jit(solution)/shard_map/ppermute | solution.py:43
  64.4 14.6 %collective-permute-start.21 = (bf16[16,32,512]{2,1,0:T(8,128)(2,1)S(1)}, bf16[16,32,512]{2,1,0:T(8,128)(2,1)}, u32[]{:S(2)}, u32[]{:S(2)}) collective-permute-start(bf16[16,32,512]{2,1,0:T(8,128)(2,1)S(1)} %constant_dynamic-update-slice_fusion.8.refs_1_), channel_id=1, source_target_pairs={{0,8},{4,12},{8,0},{12,4},{16,24},{20,28},{24,16},{28,20},{32,40},... | collective-permute-start | bytes 1572872 | tf_op jit(solution)/shard_map/ppermute | solution.py:43
  68.5 10.7 %collective-permute-start.17 = (bf16[16,32,512]{2,1,0:T(8,128)(2,1)}, bf16[16,32,512]{2,1,0:T(8,128)(2,1)}, u32[]{:S(2)}, u32[]{:S(2)}) collective-permute-start(bf16[16,32,512]{2,1,0:T(8,128)(2,1)} %constant_dynamic-update-slice_fusion.4.refs_0_), channel_id=1, source_target_pairs={{0,24},{4,28},{8,16},{12,20},{16,8},{20,12},{24,0},{28,4},{32,56},... | collective-permute-start | bytes 1572872 | tf_op jit(solution)/shard_map/ppermute | solution.py:43
  73.4 12.1 %collective-permute-start.27 = (bf16[16,32,512]{2,1,0:T(8,128)(2,1)S(1)}, bf16[16,32,512]{2,1,0:T(8,128)(2,1)}, u32[]{:S(2)}, u32[]{:S(2)}) collective-permute-start(bf16[16,32,512]{2,1,0:T(8,128)(2,1)S(1)} %pad_maximum_fusion.2.refs_3_), channel_id=1, source_target_pairs={{0,32},{4,36},{8,40},{12,44},{16,48},{20,52},{24,56},{28,60},{32,0... | collective-permute-start | bytes 1572872 | tf_op jit(solution)/shard_map/ppermute | solution.py:43
  79.2 22.2 %collective-permute-start.30 = (bf16[16,32,512]{2,1,0:T(8,128)(2,1)}, bf16[16,32,512]{2,1,0:T(8,128)(2,1)}, u32[]{:S(2)}, u32[]{:S(2)}) collective-permute-start(bf16[16,32,512]{2,1,0:T(8,128)(2,1)} %collective-permute-done.24.refs_6_), channel_id=1, source_target_pairs={{0,96},{4,100},{8,104},{12,108},{16,112},{20,116},{24,120},{28,124... | collective-permute-start | bytes 1572872 | tf_op jit(solution)/shard_map/ppermute | solution.py:43
  85.4 16.1 %collective-permute-start.29 = (bf16[16,32,512]{2,1,0:T(8,128)(2,1)}, bf16[16,32,512]{2,1,0:T(8,128)(2,1)}, u32[]{:S(2)}, u32[]{:S(2)}) collective-permute-start(bf16[16,32,512]{2,1,0:T(8,128)(2,1)} %collective-permute-done.20.refs_5_), channel_id=1, source_target_pairs={{0,8},{4,12},{8,0},{12,4},{16,24},{20,28},{24,16},{28,20},{32,40},... | collective-permute-start | bytes 1572872 | tf_op jit(solution)/shard_map/ppermute | solution.py:43
  85.4 16.1 %collective-permute-start.28 = (bf16[16,32,512]{2,1,0:T(8,128)(2,1)}, bf16[16,32,512]{2,1,0:T(8,128)(2,1)}, u32[]{:S(2)}, u32[]{:S(2)}) collective-permute-start(bf16[16,32,512]{2,1,0:T(8,128)(2,1)} %collective-permute-done.16.refs_4_), channel_id=1, source_target_pairs={{0,24},{4,28},{8,16},{12,20},{16,8},{20,12},{24,0},{28,4},{32,56},... | collective-permute-start | bytes 1572872 | tf_op jit(solution)/shard_map/ppermute | solution.py:43
  85.5 15.9 %collective-permute-start.31 = (bf16[16,32,512]{2,1,0:T(8,128)(2,1)}, bf16[16,32,512]{2,1,0:T(8,128)(2,1)}, u32[]{:S(2)}, u32[]{:S(2)}) collective-permute-start(bf16[16,32,512]{2,1,0:T(8,128)(2,1)} %collective-permute-done.26.refs_7_), channel_id=1, source_target_pairs={{0,32},{4,36},{8,40},{12,44},{16,48},{20,52},{24,56},{28,60},{32,0... | collective-permute-start | bytes 1572872 | tf_op jit(solution)/shard_map/ppermute | solution.py:43
  91.5 12.2 %collective-permute-start.32 = (bf16[2,1024,128]{2,1,0:T(8,128)(2,1)S(1)}, bf16[2,1024,128]{2,1,0:T(8,128)(2,1)S(1)}, u32[]{:S(2)}, u32[]{:S(2)}) collective-permute-start(bf16[2,1024,128]{2,1,0:T(8,128)(2,1)S(1)} %pad_maximum_fusion.1.refs_0_), channel_id=1, source_target_pairs={{0,3},{1,0},{2,1},{3,2},{4,7},{5,4},{6,5},{7,6},{8,11},{9,8},{10,9... | collective-permute-start | bytes 1572872 | tf_op jit(solution)/shard_map/ppermute | solution.py:47
  115.6 10.3 %collective-permute-start.38 = (bf16[2,288,128]{2,1,0:T(8,128)(2,1)S(1)}, bf16[2,288,128]{2,1,0:T(8,128)(2,1)S(1)}, u32[]{:S(2)}, u32[]{:S(2)}) collective-permute-start(bf16[2,288,128]{2,1,0:T(8,128)(2,1)S(1)} %get-tuple-element.115), channel_id=1, source_target_pairs={{0,1},{1,2},{2,3},{3,0},{4,5},{5,6},{6,7},{7,4},{8,9},{9,10},{10,1... | collective-permute-start | bytes 442376 | tf_op jit(solution)/shard_map/ppermute | solution.py:47
  116.2 12.2 %collective-permute-start.39 = (bf16[2,288,128]{2,1,0:T(8,128)(2,1)S(1)}, bf16[2,288,128]{2,1,0:T(8,128)(2,1)S(1)}, u32[]{:S(2)}, u32[]{:S(2)}) collective-permute-start(bf16[2,288,128]{2,1,0:T(8,128)(2,1)S(1)} %get-tuple-element.116), channel_id=1, source_target_pairs={{0,2},{1,3},{2,0},{3,1},{4,6},{5,7},{6,4},{7,5},{8,10},{9,11},{10,... | collective-permute-start | bytes 442376 | tf_op jit(solution)/shard_map/ppermute | solution.py:47
  118.4 10.0 %collective-permute-start.40 = (bf16[2,288,128]{2,1,0:T(8,128)(2,1)S(1)}, bf16[2,288,128]{2,1,0:T(8,128)(2,1)S(1)}, u32[]{:S(2)}, u32[]{:S(2)}) collective-permute-start(bf16[2,288,128]{2,1,0:T(8,128)(2,1)S(1)} %get-tuple-element.117), channel_id=1, source_target_pairs={{0,3},{1,0},{2,1},{3,2},{4,7},{5,4},{6,5},{7,6},{8,11},{9,8},{10,9... | collective-permute-start | bytes 442376 | tf_op jit(solution)/shard_map/ppermute | solution.py:47
  (24 other events, 373.1 us)

commit v14 on v11

--- a/solution.py
+++ b/solution.py
@@ -303,7 +303,7 @@
     return list(lax.optimization_barrier(tuple(values)))
 
 
-def spread(items, query):
+def spread(items, query, lq):
     held = [items[n * 4 : n * 4 + 4] for n in range(4)]
     got = [send(h, **{st[0][0]: st[0][1]}) for h, st in zip(held, STREAMS)]
     query_1 = send_x(query, 1)
@@ -319,12 +319,12 @@
     held, third = list(held), list(third)
     third, fourth = zip(*[together(t, f) for t, f in zip(third, fourth)])
     third, fourth = list(third), list(fourth)
-    query_2, query, fourth[0] = together(query_2, query, fourth[0])
+    query_2, query, fourth[0], lq = together(query_2, query, fourth[0], lq)
     queries = [query, query_1, query_2, send_x(query, 3)]
     fifth = [send(h, **{st[3][0]: st[3][1]}) for h, st in zip(third, STREAMS)]
     table = pack(held + third, (0, 4, 8, 12, 1, 5, 9, 13))
     table = pack(fourth + fifth, (2, 6, 10, 14, 3, 7, 11, 15), table)
-    return table, queries
+    return table, queries, lq
 
 
 def place_of(flipped, first):
@@ -361,7 +361,6 @@
     items, late_query, picks = together(
         tower(core_id, rank_id, hiddens, mine_w, theirs_w), both_query, picks
     )
-    table, queries = spread(items, late_query)
     pos_part = SCALE * jnp.sum(
         query_emb.astype(jnp.float32) * positive_emb.astype(jnp.float32), axis=1
     ).reshape(qblocks, 1, BLK)
@@ -381,6 +380,7 @@
     counts = lax.dynamic_slice_in_dim(count_rows, (rank % 2 * 2 + core) * ROWS, ROWS, 1)
     lq = (jnp.log(counts.astype(jnp.float32)) * LOG2E).reshape(2 * qblocks, COLS)
 
+    table, queries, lq = spread(items, late_query, lq)
     rows = rows.reshape(-1)
     table, pos_part, rows, lq = together(table, pos_part, rows, lq)
 

time: 134 us -> 133 us (level)
  waiting for transfers between devices: 46.8 us -> 44.7 us
    ppermute x26, waiting for transfers between devices: 28.8 us -> 25.3 us  [send(): return lax.ppermute(value, 'cat', cat_perm(y, z, c))]
    ppermute x15, waiting for transfers between devices: 18 us -> 19.4 us  [send_x(): return lax.ppermute(value, 'tp', [(i, (i + d) % TP) for i in range(TP)])]
  transfers between devices with their start and end apart: 41 -> 41, of which waited for: 18 -> 18; matrix products, arithmetic and copies ran while one was open for 6% -> 7% of each run, Pallas kernels for 12% -> 12%
where the time goes in v14:
time: 133 us; the launch traced here: 132 us
  starting transfers between devices  50.6 us (38%)
  waiting for transfers between devices  44.7 us (34%)
  Pallas kernels  22.3 us (17%)
  other arithmetic  6.48 us (5%)
  local copies, waits for them, and re-layouts  6.36 us (5%)
    ppermute x26, starting transfers between devices, send(): return lax.ppermute(value, 'cat', cat_perm(y, z, c))  27.1 us
    ppermute x26, waiting for transfers between devices, send(): return lax.ppermute(value, 'cat', cat_perm(y, z, c))  25.3 us
    ppermute x15, starting transfers between devices, send_x(): return lax.ppermute(value, 'tp', [(i, (i + d) % TP) for i in range(TP)])  23.5 us
    ppermute x15, waiting for transfers between devices, send_x(): return lax.ppermute(value, 'tp', [(i, (i + d) % TP) for i in range(TP)])  19.4 us
    pallas_call x4, Pallas kernels, attend(): pl.pallas_call(functools.partial(body, start), in_specs=[pl.BlockSpec(mem...  15.1 us
    pallas_call x2, Pallas kernels, pack(): pl.pallas_call(functools.partial(pack_kernel, places), out_shape=jax.Shap...  3.98 us
  transfers between devices with their start and end apart: 41, of which 18 were waited for; matrix products, arithmetic and copies ran while one was open for 7% of the time, Pallas kernels for 12%

profile of v14, /device:TPU:0, one launch (start us, length us, event | category | flops | bytes accessed | tf_op | source)
XLA Modules:
  0.0 131.5 jit_solution(3337336962169581806)
XLA Ops:
  7.9 2.7 %collective-permute-start.5 = (bf16[128,512]{1,0:T(8,128)(2,1)S(1)}, bf16[128,512]{1,0:T(8,128)(2,1)S(1)}, u32[]{:S(2)}, u32[]{:S(2)}) collective-permute-start(bf16[128,512]{1,0:T(8,128)(2,1)S(1)} %constant_dynamic-slice_fusion.refs_4_), channel_id=1, source_target_pairs={{0,2},{1,3},{2,0},{3,1},{4,6},{5,7},{6,4},{7,5},{8,10},{9,11},{10,... | collective-permute-start | bytes 393224 | tf_op jit(solution)/shard_map/ppermute | solution.py:47
  12.1 4.5 %collective-permute-done.4.refs_5_ = bf16[128,512]{1,0:T(8,128)(2,1)S(1)} collective-permute-done((bf16[128,512]{1,0:T(8,128)(2,1)S(1)}, bf16[128,512]{1,0:T(8,128)(2,1)S(1)}, u32[]{:S(2)}, u32[]{:S(2)}) %collective-permute-start.4) | collective-permute-done | bytes 131104 | tf_op jit(solution)/shard_map/ppermute | solution.py:47
  16.6 3.9 %collective-permute-done.5.refs_6_ = bf16[128,512]{1,0:T(8,128)(2,1)S(1)} collective-permute-done((bf16[128,512]{1,0:T(8,128)(2,1)S(1)}, bf16[128,512]{1,0:T(8,128)(2,1)S(1)}, u32[]{:S(2)}, u32[]{:S(2)}) %collective-permute-start.5) | collective-permute-done | bytes 131104 | tf_op jit(solution)/shard_map/ppermute | solution.py:47
  26.0 5.0 %collective-permute-done.2.refs_2_ = bf16[512,256]{1,0:T(8,128)(2,1)S(1)} collective-permute-done((bf16[512,256]{1,0:T(8,128)(2,1)S(1)}, bf16[512,256]{1,0:T(8,128)(2,1)S(1)}, u32[]{:S(2)}, u32[]{:S(2)}) %collective-permute-start.2) | collective-permute-done | bytes 262176 | tf_op jit(solution)/shard_map/ppermute | solution.py:47
  34.1 2.2 %collective-permute-start.11 = (bf16[4,32,512]{2,1,0:T(8,128)(2,1)S(1)}, bf16[4,32,512]{2,1,0:T(8,128)(2,1)S(1)}, u32[]{:S(2)}, u32[]{:S(2)}) collective-permute-start(bf16[4,32,512]{2,1,0:T(8,128)(2,1)S(1)} %get-tuple-element.122), channel_id=1, source_target_pairs={{0,96},{4,100},{8,104},{12,108},{16,112},{20,116},{24,120},{28,124... | collective-permute-start | bytes 393224 | tf_op jit(solution)/shard_map/ppermute | solution.py:43
  38.2 2.5 %collective-permute-start.13 = (bf16[4,32,512]{2,1,0:T(8,128)(2,1)S(1)}, bf16[4,32,512]{2,1,0:T(8,128)(2,1)S(1)}, u32[]{:S(2)}, u32[]{:S(2)}) collective-permute-start(bf16[4,32,512]{2,1,0:T(8,128)(2,1)S(1)} %get-tuple-element.120), channel_id=1, source_target_pairs={{0,24},{4,28},{8,16},{12,20},{16,8},{20,12},{24,0},{28,4},{32,56},... | collective-permute-start | bytes 393224 | tf_op jit(solution)/shard_map/ppermute | solution.py:43
  41.2 3.1 %collective-permute-done.13 = bf16[4,32,512]{2,1,0:T(8,128)(2,1)S(1)} collective-permute-done((bf16[4,32,512]{2,1,0:T(8,128)(2,1)S(1)}, bf16[4,32,512]{2,1,0:T(8,128)(2,1)S(1)}, u32[]{:S(2)}, u32[]{:S(2)}) %collective-permute-start.13) | collective-permute-done | bytes 131104 | tf_op jit(solution)/shard_map/ppermute | solution.py:43
  45.6 2.5 %collective-permute-start.16 = (bf16[8,32,512]{2,1,0:T(8,128)(2,1)S(1)}, bf16[8,32,512]{2,1,0:T(8,128)(2,1)S(1)}, u32[]{:S(2)}, u32[]{:S(2)}) collective-permute-start(bf16[8,32,512]{2,1,0:T(8,128)(2,1)S(1)} %get-tuple-element.66), channel_id=1, source_target_pairs={{0,24},{4,28},{8,16},{12,20},{16,8},{20,12},{24,0},{28,4},{32,56},... | collective-permute-start | bytes 786440 | tf_op jit(solution)/shard_map/ppermute | solution.py:43
  48.1 4.0 %collective-permute-done.14 = bf16[8,32,512]{2,1,0:T(8,128)(2,1)S(1)} collective-permute-done((bf16[8,32,512]{2,1,0:T(8,128)(2,1)S(1)}, bf16[8,32,512]{2,1,0:T(8,128)(2,1)S(1)}, u32[]{:S(2)}, u32[]{:S(2)}) %collective-permute-start.14) | collective-permute-done | bytes 262176 | tf_op jit(solution)/shard_map/ppermute | solution.py:43
  55.6 2.2 %collective-permute-start.26 = (bf16[16,32,512]{2,1,0:T(8,128)(2,1)S(1)}, bf16[16,32,512]{2,1,0:T(8,128)(2,1)}, u32[]{:S(2)}, u32[]{:S(2)}) collective-permute-start(bf16[16,32,512]{2,1,0:T(8,128)(2,1)S(1)} %pad_maximum_fusion.5.refs_3_), channel_id=1, source_target_pairs={{0,96},{4,100},{8,104},{12,108},{16,112},{20,116},{24,120},{28,124... | collective-permute-start | bytes 1572872 | tf_op jit(solution)/shard_map/ppermute | solution.py:43
  62.6 5.1 %collective-permute-done.26.refs_7_ = bf16[16,32,512]{2,1,0:T(8,128)(2,1)} collective-permute-done((bf16[16,32,512]{2,1,0:T(8,128)(2,1)S(1)}, bf16[16,32,512]{2,1,0:T(8,128)(2,1)}, u32[]{:S(2)}, u32[]{:S(2)}) %collective-permute-start.26) | collective-permute-done | bytes 524320 | tf_op jit(solution)/shard_map/ppermute | solution.py:43
  72.8 2.5 %collective-permute-start.21 = (bf16[16,32,512]{2,1,0:T(8,128)(2,1)}, bf16[16,32,512]{2,1,0:T(8,128)(2,1)}, u32[]{:S(2)}, u32[]{:S(2)}) collective-permute-start(bf16[16,32,512]{2,1,0:T(8,128)(2,1)} %pad_maximum_fusion.2.refs_0_), channel_id=1, source_target_pairs={{0,24},{4,28},{8,16},{12,20},{16,8},{20,12},{24,0},{28,4},{32,56},... | collective-permute-start | bytes 1572872 | tf_op jit(solution)/shard_map/ppermute | solution.py:43
  75.5 2.6 %gather_fusion = s32[512,128]{1,0:T(8,128)} fusion(s32[512,128]{1,0:T(8,128)} %bitcast.30, s32[1024]{0:T(1024)S(1)} %pad_clamp_fusion), kind=kCustom, calls=%fused_computation | custom fusion | bytes 526336 | tf_op jit(solution)/shard_map/gather | solution.py:379
  81.9 3.0 %collective-permute-done.21.refs_0_ = bf16[16,32,512]{2,1,0:T(8,128)(2,1)} collective-permute-done((bf16[16,32,512]{2,1,0:T(8,128)(2,1)}, bf16[16,32,512]{2,1,0:T(8,128)(2,1)}, u32[]{:S(2)}, u32[]{:S(2)}) %collective-permute-start.21) | collective-permute-done | bytes 524320 | tf_op jit(solution)/shard_map/ppermute | solution.py:43
  85.5 2.6 %collective-permute-start.28 = (bf16[16,32,512]{2,1,0:T(8,128)(2,1)}, bf16[16,32,512]{2,1,0:T(8,128)(2,1)}, u32[]{:S(2)}, u32[]{:S(2)}) collective-permute-start(bf16[16,32,512]{2,1,0:T(8,128)(2,1)} %collective-permute-done.20.refs_4_), channel_id=1, source_target_pairs={{0,24},{4,28},{8,16},{12,20},{16,8},{20,12},{24,0},{28,4},{32,56},... | collective-permute-start | bytes 1572872 | tf_op jit(solution)/shard_map/ppermute | solution.py:43
  88.1 2.1 %collective-permute-start.32 = (bf16[2,1024,128]{2,1,0:T(8,128)(2,1)S(1)}, bf16[2,1024,128]{2,1,0:T(8,128)(2,1)S(1)}, u32[]{:S(2)}, u32[]{:S(2)}) collective-permute-start(bf16[2,1024,128]{2,1,0:T(8,128)(2,1)S(1)} %pad_maximum_fusion.1.refs_0_), channel_id=1, source_target_pairs={{0,3},{1,0},{2,1},{3,2},{4,7},{5,4},{6,5},{7,6},{8,11},{9,8},{10,9... | collective-permute-start | bytes 1572872 | tf_op jit(solution)/shard_map/ppermute | solution.py:47
  96.2 2.2 %pack.3.refs_5_ = bf16[256,32,512]{2,1,0:T(8,128)(2,1)S(1)} custom-call(bf16[16,32,512]{2,1,0:T(8,128)(2,1)} %collective-permute-done.21.refs_0_, bf16[16,32,512]{2,1,0:T(8,128)(2,1)} %collective-permute-done.23.refs_1_, bf16[16,32,512]{2,1,0:T(8,128)(2,1)} %collective-permute-done.25.refs_2_, ...), custom_call_target="tpu_custom_call", output_to_operand_aliasing={{}: (8, {})} | custom-call | bytes 8388608 | tf_op jit(solution)/shard_map/pack/pallas_call | solution.py:142
  98.4 3.7 %attend_other.3 = bf16[2,272,512]{2,1,0:T(8,128)(2,1)S(1)} custom-call(s32[512]{0:T(512)S(1)} %fusion.9.row_ref, bf16[2,1024,128]{2,1,0:T(8,128)(2,1)S(1)} %pad_maximum_fusion.1.refs_0_, bf16[2,1024,128]{2,1,0:T(8,128)(2,1)S(1)} %collective-permute-done.18.refs_1_, bf16[2,1024,128]{2,1,0:T(8,128)(2,1)S(1)} %collective-permute-done.19.refs_2_, ...), custom_call_target="tpu_custom_call" | custom-call | flops 2147483648 | bytes 2097152 | tf_op jit(solution)/shard_map/attend_other/pallas_call | solution.py:224
  102.2 3.7 %attend_other.2 = bf16[2,272,512]{2,1,0:T(8,128)(2,1)S(1)} custom-call(s32[512]{0:T(512)S(1)} %fusion.9.row_ref, bf16[2,1024,128]{2,1,0:T(8,128)(2,1)S(1)} %pad_maximum_fusion.1.refs_0_, bf16[2,1024,128]{2,1,0:T(8,128)(2,1)S(1)} %collective-permute-done.18.refs_1_, bf16[2,1024,128]{2,1,0:T(8,128)(2,1)S(1)} %collective-permute-done.19.refs_2_, ...), custom_call_target="tpu_custom_call" | custom-call | flops 2147483648 | bytes 2097152 | tf_op jit(solution)/shard_map/attend_other/pallas_call | solution.py:224
  106.5 3.8 %attend_own.3 = (bf16[2,288,128]{2,1,0:T(8,128)(2,1)S(1)}, bf16[2,288,128]{2,1,0:T(8,128)(2,1)S(1)}, bf16[2,288,128]{2,1,0:T(8,128)(2,1)S(1)}, bf16[2,288,128]{2,1,0:T(8,128)(2,1)S(1)}) custom-call(s32[512]{0:T(512)S(1)} %fusion.9.row_ref, bf16[2,1024,128]{2,1,0:T(8,128)(2,1)S(1)} %pad_maximum_fusion.1.refs_0_, ...), custom_call_target="tpu_custom_call" | custom-call | flops 2147483648 | bytes 2097152 | tf_op jit(solution)/shard_map/attend_own/pallas_call | solution.py:224
  112.0 2.9 %collective-permute-start.39 = (bf16[2,288,128]{2,1,0:T(8,128)(2,1)S(1)}, bf16[2,288,128]{2,1,0:T(8,128)(2,1)S(1)}, u32[]{:S(2)}, u32[]{:S(2)}) collective-permute-start(bf16[2,288,128]{2,1,0:T(8,128)(2,1)S(1)} %get-tuple-element.110), channel_id=1, source_target_pairs={{0,2},{1,3},{2,0},{3,1},{4,6},{5,7},{6,4},{7,5},{8,10},{9,11},{10,... | collective-permute-start | bytes 442376 | tf_op jit(solution)/shard_map/ppermute | solution.py:47
  115.8 3.9 %attend_own.2 = (bf16[2,288,128]{2,1,0:T(8,128)(2,1)S(1)}, bf16[2,288,128]{2,1,0:T(8,128)(2,1)S(1)}, bf16[2,288,128]{2,1,0:T(8,128)(2,1)S(1)}, bf16[2,288,128]{2,1,0:T(8,128)(2,1)S(1)}) custom-call(s32[512]{0:T(512)S(1)} %fusion.9.row_ref, bf16[2,1024,128]{2,1,0:T(8,128)(2,1)S(1)} %pad_maximum_fusion.1.refs_0_, ...), custom_call_target="tpu_custom_call" | custom-call | flops 2147483648 | bytes 2097152 | tf_op jit(solution)/shard_map/attend_own/pallas_call | solution.py:224
  121.5 2.2 %collective-permute-start.36 = (bf16[2,288,128]{2,1,0:T(8,128)(2,1)S(1)}, bf16[2,288,128]{2,1,0:T(8,128)(2,1)S(1)}, u32[]{:S(2)}, u32[]{:S(2)}) collective-permute-start(bf16[2,288,128]{2,1,0:T(8,128)(2,1)S(1)} %get-tuple-element.107), channel_id=1, source_target_pairs={{0,3},{1,0},{2,1},{3,2},{4,7},{5,4},{6,5},{7,6},{8,11},{9,8},{10,9... | collective-permute-start | bytes 442376 | tf_op jit(solution)/shard_map/ppermute | solution.py:47
  123.6 5.4 %collective-permute-done.34.refs_1_ = bf16[2,288,128]{2,1,0:T(8,128)(2,1)S(1)} collective-permute-done((bf16[2,288,128]{2,1,0:T(8,128)(2,1)S(1)}, bf16[2,288,128]{2,1,0:T(8,128)(2,1)S(1)}, u32[]{:S(2)}, u32[]{:S(2)}) %collective-permute-start.34) | collective-permute-done | bytes 147488 | tf_op jit(solution)/shard_map/ppermute | solution.py:47
  (104 shorter events, 52.0 us)
Async XLA Ops:
  4.2 16.4 %collective-permute-start.1 = (bf16[512,256]{1,0:T(8,128)(2,1)S(1)}, bf16[512,256]{1,0:T(8,128)(2,1)S(1)}, u32[]{:S(2)}, u32[]{:S(2)}) collective-permute-start(bf16[512,256]{1,0:T(8,128)(2,1)S(1)} %bitcast.37), channel_id=1, source_target_pairs={{0,1},{1,2},{2,3},{3,0},{4,5},{5,6},{6,7},{7,4},{8,9},{9,10},{10,1... | collective-permute-start | bytes 786440 | tf_op jit(solution)/shard_map/ppermute | solution.py:47
  5.8 14.8 %collective-permute-start.3 = (bf16[512,256]{1,0:T(8,128)(2,1)S(1)}, bf16[512,256]{1,0:T(8,128)(2,1)S(1)}, u32[]{:S(2)}, u32[]{:S(2)}) collective-permute-start(bf16[512,256]{1,0:T(8,128)(2,1)S(1)} %bitcast.36), channel_id=1, source_target_pairs={{0,3},{1,0},{2,1},{3,2},{4,7},{5,4},{6,5},{7,6},{8,11},{9,8},{10,9... | collective-permute-start | bytes 786440 | tf_op jit(solution)/shard_map/ppermute | solution.py:47
  7.9 12.6 %collective-permute-start.5 = (bf16[128,512]{1,0:T(8,128)(2,1)S(1)}, bf16[128,512]{1,0:T(8,128)(2,1)S(1)}, u32[]{:S(2)}, u32[]{:S(2)}) collective-permute-start(bf16[128,512]{1,0:T(8,128)(2,1)S(1)} %constant_dynamic-slice_fusion.refs_4_), channel_id=1, source_target_pairs={{0,2},{1,3},{2,0},{3,1},{4,6},{5,7},{6,4},{7,5},{8,10},{9,11},{10,... | collective-permute-start | bytes 393224 | tf_op jit(solution)/shard_map/ppermute | solution.py:47
  10.6 9.8 %collective-permute-start.6 = (bf16[128,512]{1,0:T(8,128)(2,1)S(1)}, bf16[128,512]{1,0:T(8,128)(2,1)S(1)}, u32[]{:S(2)}, u32[]{:S(2)}) collective-permute-start(bf16[128,512]{1,0:T(8,128)(2,1)S(1)} %constant_dynamic-slice_fusion.refs_4_), channel_id=1, source_target_pairs={{0,3},{1,0},{2,1},{3,2},{4,7},{5,4},{6,5},{7,6},{8,11},{9,8},{10,9... | collective-permute-start | bytes 393224 | tf_op jit(solution)/shard_map/ppermute | solution.py:47
  20.6 10.4 %collective-permute-start.7 = (bf16[4,128,512]{2,1,0:T(8,128)(2,1)S(1)}, bf16[4,128,512]{2,1,0:T(8,128)(2,1)S(1)}, u32[]{:S(2)}, u32[]{:S(2)}) collective-permute-start(bf16[4,128,512]{2,1,0:T(8,128)(2,1)S(1)} %pad_maximum_fusion), channel_id=1, source_target_pairs={{0,4},{4,0},{8,12},{12,8},{16,20},{20,16},{24,28},{28,24},{32,36},... | collective-permute-start | bytes 1572872 | tf_op jit(solution)/shard_map/ppermute | solution.py:43
  21.2 9.8 %collective-permute-start.2 = (bf16[512,256]{1,0:T(8,128)(2,1)S(1)}, bf16[512,256]{1,0:T(8,128)(2,1)S(1)}, u32[]{:S(2)}, u32[]{:S(2)}) collective-permute-start(bf16[512,256]{1,0:T(8,128)(2,1)S(1)} %bitcast.35), channel_id=1, source_target_pairs={{0,2},{1,3},{2,0},{3,1},{4,6},{5,7},{6,4},{7,5},{8,10},{9,11},{10,... | collective-permute-start | bytes 786440 | tf_op jit(solution)/shard_map/ppermute | solution.py:47
  40.7 13.8 %collective-permute-start.18 = (bf16[2,1024,128]{2,1,0:T(8,128)(2,1)S(1)}, bf16[2,1024,128]{2,1,0:T(8,128)(2,1)S(1)}, u32[]{:S(2)}, u32[]{:S(2)}) collective-permute-start(bf16[2,1024,128]{2,1,0:T(8,128)(2,1)S(1)} %pad_maximum_fusion.1.refs_0_), channel_id=1, source_target_pairs={{0,1},{1,2},{2,3},{3,0},{4,5},{5,6},{6,7},{7,4},{8,9},{9,10},{10,1... | collective-permute-start | bytes 1572872 | tf_op jit(solution)/shard_map/ppermute | solution.py:47
  55.6 12.1 %collective-permute-start.26 = (bf16[16,32,512]{2,1,0:T(8,128)(2,1)S(1)}, bf16[16,32,512]{2,1,0:T(8,128)(2,1)}, u32[]{:S(2)}, u32[]{:S(2)}) collective-permute-start(bf16[16,32,512]{2,1,0:T(8,128)(2,1)S(1)} %pad_maximum_fusion.5.refs_3_), channel_id=1, source_target_pairs={{0,96},{4,100},{8,104},{12,108},{16,112},{20,116},{24,120},{28,124... | collective-permute-start | bytes 1572872 | tf_op jit(solution)/shard_map/ppermute | solution.py:43
  57.9 11.4 %collective-permute-start.24 = (bf16[16,32,512]{2,1,0:T(8,128)(2,1)S(1)}, bf16[16,32,512]{2,1,0:T(8,128)(2,1)}, u32[]{:S(2)}, u32[]{:S(2)}) collective-permute-start(bf16[16,32,512]{2,1,0:T(8,128)(2,1)S(1)} %pad_maximum_fusion.4.refs_2_), channel_id=1, source_target_pairs={{0,32},{4,36},{8,40},{12,44},{16,48},{20,52},{24,56},{28,60},{32,0... | collective-permute-start | bytes 1572872 | tf_op jit(solution)/shard_map/ppermute | solution.py:43
  59.2 12.1 %collective-permute-start.22 = (bf16[16,32,512]{2,1,0:T(8,128)(2,1)S(1)}, bf16[16,32,512]{2,1,0:T(8,128)(2,1)}, u32[]{:S(2)}, u32[]{:S(2)}) collective-permute-start(bf16[16,32,512]{2,1,0:T(8,128)(2,1)S(1)} %pad_maximum_fusion.3.refs_1_), channel_id=1, source_target_pairs={{0,24},{4,28},{8,16},{12,20},{16,8},{20,12},{24,0},{28,4},{32,56},... | collective-permute-start | bytes 1572872 | tf_op jit(solution)/shard_map/ppermute | solution.py:43
  60.4 12.4 %collective-permute-start.20 = (bf16[16,32,512]{2,1,0:T(8,128)(2,1)}, bf16[16,32,512]{2,1,0:T(8,128)(2,1)}, u32[]{:S(2)}, u32[]{:S(2)}) collective-permute-start(bf16[16,32,512]{2,1,0:T(8,128)(2,1)} %pad_maximum_fusion.2.refs_0_), channel_id=1, source_target_pairs={{0,8},{4,12},{8,0},{12,4},{16,24},{20,28},{24,16},{28,20},{32,40},... | collective-permute-start | bytes 1572872 | tf_op jit(solution)/shard_map/ppermute | solution.py:43
  60.8 24.7 %collective-permute-start.19 = (bf16[2,1024,128]{2,1,0:T(8,128)(2,1)S(1)}, bf16[2,1024,128]{2,1,0:T(8,128)(2,1)S(1)}, u32[]{:S(2)}, u32[]{:S(2)}) collective-permute-start(bf16[2,1024,128]{2,1,0:T(8,128)(2,1)S(1)} %pad_maximum_fusion.1.refs_0_), channel_id=1, source_target_pairs={{0,2},{1,3},{2,0},{3,1},{4,6},{5,7},{6,4},{7,5},{8,10},{9,11},{10,... | collective-permute-start | bytes 1572872 | tf_op jit(solution)/shard_map/ppermute | solution.py:47
  67.7 13.3 %collective-permute-start.27 = (bf16[16,32,512]{2,1,0:T(8,128)(2,1)S(1)}, bf16[16,32,512]{2,1,0:T(8,128)(2,1)}, u32[]{:S(2)}, u32[]{:S(2)}) collective-permute-start(bf16[16,32,512]{2,1,0:T(8,128)(2,1)S(1)} %pad_maximum_fusion.5.refs_3_), channel_id=1, source_target_pairs={{0,32},{4,36},{8,40},{12,44},{16,48},{20,52},{24,56},{28,60},{32,0... | collective-permute-start | bytes 1572872 | tf_op jit(solution)/shard_map/ppermute | solution.py:43
  69.3 11.7 %collective-permute-start.25 = (bf16[16,32,512]{2,1,0:T(8,128)(2,1)S(1)}, bf16[16,32,512]{2,1,0:T(8,128)(2,1)}, u32[]{:S(2)}, u32[]{:S(2)}) collective-permute-start(bf16[16,32,512]{2,1,0:T(8,128)(2,1)S(1)} %pad_maximum_fusion.4.refs_2_), channel_id=1, source_target_pairs={{0,96},{4,100},{8,104},{12,108},{16,112},{20,116},{24,120},{28,124... | collective-permute-start | bytes 1572872 | tf_op jit(solution)/shard_map/ppermute | solution.py:43
  71.3 10.6 %collective-permute-start.23 = (bf16[16,32,512]{2,1,0:T(8,128)(2,1)S(1)}, bf16[16,32,512]{2,1,0:T(8,128)(2,1)}, u32[]{:S(2)}, u32[]{:S(2)}) collective-permute-start(bf16[16,32,512]{2,1,0:T(8,128)(2,1)S(1)} %pad_maximum_fusion.3.refs_1_), channel_id=1, source_target_pairs={{0,8},{4,12},{8,0},{12,4},{16,24},{20,28},{24,16},{28,20},{32,40},... | collective-permute-start | bytes 1572872 | tf_op jit(solution)/shard_map/ppermute | solution.py:43
  72.8 12.0 %collective-permute-start.21 = (bf16[16,32,512]{2,1,0:T(8,128)(2,1)}, bf16[16,32,512]{2,1,0:T(8,128)(2,1)}, u32[]{:S(2)}, u32[]{:S(2)}) collective-permute-start(bf16[16,32,512]{2,1,0:T(8,128)(2,1)} %pad_maximum_fusion.2.refs_0_), channel_id=1, source_target_pairs={{0,24},{4,28},{8,16},{12,20},{16,8},{20,12},{24,0},{28,4},{32,56},... | collective-permute-start | bytes 1572872 | tf_op jit(solution)/shard_map/ppermute | solution.py:43
  84.8 9.5 %collective-permute-start.31 = (bf16[16,32,512]{2,1,0:T(8,128)(2,1)}, bf16[16,32,512]{2,1,0:T(8,128)(2,1)}, u32[]{:S(2)}, u32[]{:S(2)}) collective-permute-start(bf16[16,32,512]{2,1,0:T(8,128)(2,1)} %collective-permute-done.26.refs_7_), channel_id=1, source_target_pairs={{0,32},{4,36},{8,40},{12,44},{16,48},{20,52},{24,56},{28,60},{32,0... | collective-permute-start | bytes 1572872 | tf_op jit(solution)/shard_map/ppermute | solution.py:43
  85.4 10.7 %collective-permute-start.30 = (bf16[16,32,512]{2,1,0:T(8,128)(2,1)}, bf16[16,32,512]{2,1,0:T(8,128)(2,1)}, u32[]{:S(2)}, u32[]{:S(2)}) collective-permute-start(bf16[16,32,512]{2,1,0:T(8,128)(2,1)} %collective-permute-done.24.refs_6_), channel_id=1, source_target_pairs={{0,96},{4,100},{8,104},{12,108},{16,112},{20,116},{24,120},{28,124... | collective-permute-start | bytes 1572872 | tf_op jit(solution)/shard_map/ppermute | solution.py:43
  85.4 10.7 %collective-permute-start.29 = (bf16[16,32,512]{2,1,0:T(8,128)(2,1)}, bf16[16,32,512]{2,1,0:T(8,128)(2,1)}, u32[]{:S(2)}, u32[]{:S(2)}) collective-permute-start(bf16[16,32,512]{2,1,0:T(8,128)(2,1)} %collective-permute-done.22.refs_5_), channel_id=1, source_target_pairs={{0,8},{4,12},{8,0},{12,4},{16,24},{20,28},{24,16},{28,20},{32,40},... | collective-permute-start | bytes 1572872 | tf_op jit(solution)/shard_map/ppermute | solution.py:43
  85.5 10.7 %collective-permute-start.28 = (bf16[16,32,512]{2,1,0:T(8,128)(2,1)}, bf16[16,32,512]{2,1,0:T(8,128)(2,1)}, u32[]{:S(2)}, u32[]{:S(2)}) collective-permute-start(bf16[16,32,512]{2,1,0:T(8,128)(2,1)} %collective-permute-done.20.refs_4_), channel_id=1, source_target_pairs={{0,24},{4,28},{8,16},{12,20},{16,8},{20,12},{24,0},{28,4},{32,56},... | collective-permute-start | bytes 1572872 | tf_op jit(solution)/shard_map/ppermute | solution.py:43
  88.1 10.4 %collective-permute-start.32 = (bf16[2,1024,128]{2,1,0:T(8,128)(2,1)S(1)}, bf16[2,1024,128]{2,1,0:T(8,128)(2,1)S(1)}, u32[]{:S(2)}, u32[]{:S(2)}) collective-permute-start(bf16[2,1024,128]{2,1,0:T(8,128)(2,1)S(1)} %pad_maximum_fusion.1.refs_0_), channel_id=1, source_target_pairs={{0,3},{1,0},{2,1},{3,2},{4,7},{5,4},{6,5},{7,6},{8,11},{9,8},{10,9... | collective-permute-start | bytes 1572872 | tf_op jit(solution)/shard_map/ppermute | solution.py:47
  105.9 9.9 %collective-permute-start.33 = (bf16[2,272,512]{2,1,0:T(8,128)(2,1)S(1)}, bf16[2,272,512]{2,1,0:T(8,128)(2,1)S(1)}, u32[]{:S(2)}, u32[]{:S(2)}) collective-permute-start(bf16[2,272,512]{2,1,0:T(8,128)(2,1)S(1)} %attend_other.2), channel_id=1, source_target_pairs={{0,4},{4,0},{8,12},{12,8},{16,20},{20,16},{24,28},{28,24},{32,36},... | collective-permute-start | bytes 1671176 | tf_op jit(solution)/shard_map/ppermute | solution.py:43
  110.4 11.1 %collective-permute-start.38 = (bf16[2,288,128]{2,1,0:T(8,128)(2,1)S(1)}, bf16[2,288,128]{2,1,0:T(8,128)(2,1)S(1)}, u32[]{:S(2)}, u32[]{:S(2)}) collective-permute-start(bf16[2,288,128]{2,1,0:T(8,128)(2,1)S(1)} %get-tuple-element.109), channel_id=1, source_target_pairs={{0,1},{1,2},{2,3},{3,0},{4,5},{5,6},{6,7},{7,4},{8,9},{9,10},{10,1... | collective-permute-start | bytes 442376 | tf_op jit(solution)/shard_map/ppermute | solution.py:47
  112.0 11.7 %collective-permute-start.39 = (bf16[2,288,128]{2,1,0:T(8,128)(2,1)S(1)}, bf16[2,288,128]{2,1,0:T(8,128)(2,1)S(1)}, u32[]{:S(2)}, u32[]{:S(2)}) collective-permute-start(bf16[2,288,128]{2,1,0:T(8,128)(2,1)S(1)} %get-tuple-element.110), channel_id=1, source_target_pairs={{0,2},{1,3},{2,0},{3,1},{4,6},{5,7},{6,4},{7,5},{8,10},{9,11},{10,... | collective-permute-start | bytes 442376 | tf_op jit(solution)/shard_map/ppermute | solution.py:47
  (22 other events, 231.8 us)
